TPU v7x, 32 devices: a whole 2x2x4 slice. The times are simulated.
32 devices in a mesh: groups: 2 (over y), dp: 4 (over z), heads: 4 (over x, core).
Axes of the slice: x: 2, y: 2, z: 4, core: 2. Of those that a mesh axis runs over, the one named last changes fastest.
Arguments:
- queries: bfloat16 [2048, 64, 128], P(('groups', 'dp'), 'heads'), parts along dimension 0, may hold values from -41 to 41
- out_grad: bfloat16 [2048, 64, 128], P(('groups', 'dp'), 'heads'), parts along dimension 0, may hold values from -24 to 24
- self_keys: bfloat16 [2048, 8, 128], P(('groups', 'dp'), 'heads'), parts along dimension 0, may hold values from -6 to 6
- self_values: bfloat16 [2048, 8, 128], P(('groups', 'dp'), 'heads'), parts along dimension 0, may hold values from -6 to 6
- cart_keys: bfloat16 [2048, 8, 128], P('groups', 'heads'), parts along dimension 0, may hold values from -17 to 17
- cart_values: bfloat16 [2048, 8, 128], P('groups', 'heads'), parts along dimension 0, may hold values from -6 to 6
- segment_ids: int32 [8, 256], P(('groups', 'dp')), parts along dimension 0, may hold values from 0 to 1, never falling along the last dimension, each value on 1 to 192 neighbouring positions
Outputs:
- cart_grads: float32 [2048, 2, 8, 128], P(('groups', 'dp'), None, 'heads'), parts along dimension 0
- self_grads: bfloat16 [2, 2048, 8, 128], P(None, ('groups', 'dp'), 'heads'), parts along dimension 1
- query_grads: bfloat16 [2048, 8192], P(('groups', 'dp', 'heads')), parts along dimension 0
There are 2 independent parts, one for each index of `groups`. A program takes and returns all parts, laid end to end along the dimension named above; each array names one. Nothing has to cross between parts.
Inputs may be any that keep to these rules, and one draw needn't show every extreme that they name: `segment_ids`: in each row ids never fall and both sequences occur; one sequence of a row may hold up to 192 positions.
All inputs are finite; a program needn't handle non-finite values.
Results may differ from a plain program's by a relative error of at most 0.0053.
Values may be sent and summed in bfloat16 or wider, within the bound.
No kernel may reach another device: no remote copies, remote signals or barrier semaphores. Data moves between devices by JAX's collectives and lax.ppermute only.
A program may use at most 64 MiB of HBM per device.

v0:
```python
import functools
import math

import jax
import jax.numpy as jnp
from jax import lax
from jax.experimental import pallas as pl
from jax.experimental.pallas import tpu as pltpu
from jax.sharding import PartitionSpec as P

masked_score = -1e30
vmem_bytes = 56 * 1024 * 1024
f32 = jnp.float32
bf16 = jnp.bfloat16


def dot_nt(left, right):
    return lax.dot_general(left, right, (((1,), (1,)), ((), ())), preferred_element_type=f32)


def dot_nn(left, right):
    return lax.dot_general(left, right, (((1,), (0,)), ((), ())), preferred_element_type=f32)


def fold_rows(values, op):
    rows, columns = values.shape
    return op(values.reshape(rows // 8, 8, columns), axis=0)


def head_kernel(
    kv_index, kv_local, width, block_tokens, chunk,
    q_ref, g_ref, sk_ref, sv_ref, ck_ref, cv_ref, seg_ref,
    dq_ref, cart_ref, self_ref,
    wide_ref, keys_ref, vals_ref, keys_t_ref, s_ref, d_ref, dk_ref, dv_ref, out_ref,
):
    head_dim = q_ref.shape[1]
    tokens = seg_ref.shape[1]
    cart_rows = ck_ref.shape[0] // kv_local
    all_keys = cart_rows + tokens
    rows = block_tokens * width
    scale = head_dim ** -0.5
    scale2 = scale * math.log2(math.e)

    def pick(ref, dst, at):
        count = ref.shape[0] // kv_local
        if kv_local == 1:
            dst[at : at + count, :] = ref[...]
        else:
            wide_ref[0 : ref.shape[0], :] = ref[...].astype(f32)
            dst[at : at + count, :] = wide_ref[pl.ds(kv_index, count, stride=kv_local), :].astype(bf16)

    pick(ck_ref, keys_ref, 0)
    pick(sk_ref, keys_ref, cart_rows)
    pick(cv_ref, vals_ref, 0)
    pick(sv_ref, vals_ref, cart_rows)
    keys_t_ref[...] = keys_ref[...].astype(f32).T.astype(bf16)
    first_count = jnp.sum((seg_ref[...] == 0).astype(f32), axis=1, keepdims=True).astype(jnp.int32)

    def rows_of(ref, block):
        span = block_tokens * kv_local * width
        wide = ref[block * span : (block + 1) * span, :]
        if kv_local == 1:
            return wide
        wide = wide.astype(f32).reshape(block_tokens, kv_local, width, head_dim)
        return wide[:, kv_index].reshape(rows, head_dim).astype(bf16)

    for block in range(tokens // block_tokens):
        query = rows_of(q_ref, block)
        grad = rows_of(g_ref, block)
        own_limit = (block + 1) * block_tokens
        own_limit = -(-own_limit // chunk) * chunk
        starts = list(range(0, cart_rows + own_limit, chunk))
        token = (lax.broadcasted_iota(jnp.int32, (1, rows), 1) + block * rows) // width
        begin = jnp.where(token >= first_count, first_count, 0)
        peak8 = jnp.full((8, rows), masked_score, f32)
        for start in starts:
            score = dot_nt(keys_ref[start : start + chunk, :], query)
            if start >= cart_rows:
                key_at = lax.broadcasted_iota(jnp.int32, (chunk, rows), 0) + (start - cart_rows)
                score = jnp.where((key_at >= begin) & (key_at <= token), score, masked_score)
            s_ref[start : start + chunk, :] = score
            peak8 = jnp.maximum(peak8, fold_rows(score, jnp.max))
        peak = jnp.max(peak8, axis=0, keepdims=True)
        total8 = jnp.zeros((8, rows), f32)
        center8 = jnp.zeros((8, rows), f32)
        for start in starts:
            weight = jnp.exp2((s_ref[start : start + chunk, :] - peak) * scale2)
            dprob = dot_nt(vals_ref[start : start + chunk, :], grad)
            s_ref[start : start + chunk, :] = weight
            d_ref[start : start + chunk, :] = dprob
            total8 = total8 + fold_rows(weight, jnp.sum)
            center8 = center8 + fold_rows(weight * dprob, jnp.sum)
        share = 1.0 / jnp.sum(total8, axis=0, keepdims=True)
        center = jnp.sum(center8, axis=0, keepdims=True) * share
        dq_t = jnp.zeros((head_dim, rows), f32)
        for start in starts:
            span = slice(start, start + chunk)
            prob = s_ref[span, :] * share
            dscore = (prob * (d_ref[span, :] - center)).astype(bf16)
            dv = dot_nn(prob.astype(bf16), grad)
            dk = dot_nn(dscore, query)
            first = block == 0 or start >= cart_rows + -(-block * block_tokens // chunk) * chunk
            if first:
                dv_ref[span, :] = dv
                dk_ref[span, :] = dk
            else:
                dv_ref[span, :] += dv
                dk_ref[span, :] += dk
            dq_t = dq_t + dot_nn(keys_t_ref[:, span], dscore)
        out_ref[...] = (dq_t * scale).T
        for head in range(width):
            dq_ref[block * block_tokens : (block + 1) * block_tokens, head * head_dim : (head + 1) * head_dim] = (
                out_ref[pl.ds(head, block_tokens, stride=width), :].astype(bf16)
            )
    parts, _, part_rows, _ = cart_ref.shape
    for part in range(parts):
        span = slice(part * part_rows, (part + 1) * part_rows)
        cart_ref[part, 0] = (dk_ref[span, :] * scale).astype(bf16)
        cart_ref[part, 1] = dv_ref[span, :].astype(bf16)
    self_ref[0] = (dk_ref[cart_rows:all_keys, :] * scale).astype(bf16)
    self_ref[1] = dv_ref[cart_rows:all_keys, :].astype(bf16)


def cart_kernel(kv_local, *refs):
    part_refs, out_ref = refs[:-1], refs[-1]
    count = part_refs[0].shape[0]
    part_rows = part_refs[0].shape[2]
    for kv_index, ref in enumerate(part_refs):
        for kind in range(2):
            total = ref[0, kind].astype(f32)
            for part in range(1, count):
                total = total + ref[part, kind].astype(f32)
            out_ref[pl.ds(kind * kv_local + kv_index, part_rows, stride=2 * kv_local), :] = total


def on_device(dp_size, heads_size, queries, out_grad, self_keys, self_values, cart_keys, cart_values, segment_ids):
    tokens, heads_local, head_dim = queries.shape
    kv_local = self_keys.shape[1]
    cart_rows = cart_keys.shape[0]
    width = heads_local // kv_local
    block_tokens = 64
    chunk = 128
    all_keys = cart_rows + tokens
    rows = block_tokens * width
    part_rows = cart_rows // dp_size
    flat = [array.reshape(-1, head_dim) for array in (queries, out_grad, self_keys, self_values, cart_keys, cart_values)]
    macs = tokens * width * all_keys * head_dim * 5
    query_list, cart_list, self_list = [], [], []
    for kv_index in range(kv_local):
        dq, cart, own = pl.pallas_call(
            functools.partial(head_kernel, kv_index, kv_local, width, block_tokens, chunk),
            out_shape=(
                jax.ShapeDtypeStruct((tokens, width * head_dim), bf16),
                jax.ShapeDtypeStruct((dp_size, 2, part_rows, head_dim), bf16),
                jax.ShapeDtypeStruct((2, tokens, head_dim), bf16),
            ),
            scratch_shapes=[
                pltpu.VMEM((cart_rows * kv_local, head_dim), f32),
                pltpu.VMEM((all_keys, head_dim), bf16),
                pltpu.VMEM((all_keys, head_dim), bf16),
                pltpu.VMEM((head_dim, all_keys), bf16),
                pltpu.VMEM((all_keys, rows), f32),
                pltpu.VMEM((all_keys, rows), f32),
                pltpu.VMEM((all_keys, head_dim), f32),
                pltpu.VMEM((all_keys, head_dim), f32),
                pltpu.VMEM((rows, head_dim), f32),
            ],
            compiler_params=pltpu.CompilerParams(vmem_limit_bytes=vmem_bytes),
            cost_estimate=pl.CostEstimate(flops=4 * macs, bytes_accessed=5 * 2**20, transcendentals=tokens * width * all_keys),
            name="head_grads",
        )(*flat, segment_ids)
        query_list.append(lax.all_to_all(dq, "heads", split_axis=0, concat_axis=0, tiled=True))
        cart_list.append(lax.all_to_all(cart, "dp", split_axis=0, concat_axis=0, tiled=True))
        self_list.append(own)
    own_tokens = tokens // heads_size
    query_grads = jnp.stack(
        [part.reshape(heads_size, own_tokens, width * head_dim) for part in query_list], axis=1
    ).transpose(2, 0, 1, 3).reshape(own_tokens, heads_size * heads_local * head_dim)
    self_grads = jnp.stack(self_list, axis=2)
    cart_grads = pl.pallas_call(
        functools.partial(cart_kernel, kv_local),
        out_shape=jax.ShapeDtypeStruct((part_rows * 2 * kv_local, head_dim), f32),
        compiler_params=pltpu.CompilerParams(vmem_limit_bytes=vmem_bytes),
        cost_estimate=pl.CostEstimate(flops=2**20, bytes_accessed=2 * 2**20, transcendentals=0),
        name="cart_sum",
    )(*cart_list)
    cart_grads = cart_grads.reshape(part_rows, 2, kv_local, head_dim)
    return (cart_grads, self_grads, query_grads)


def solution(mesh):
    in_specs = (
        P(("groups", "dp"), "heads", None),
        P(("groups", "dp"), "heads", None),
        P(("groups", "dp"), "heads", None),
        P(("groups", "dp"), "heads", None),
        P("groups", "heads", None),
        P("groups", "heads", None),
        P(("groups", "dp"), None),
    )
    out_specs = (
        P(("groups", "dp"), None, "heads", None),
        P(None, ("groups", "dp"), "heads", None),
        P(("groups", "dp", "heads"), None),
    )
    return jax.shard_map(
        functools.partial(on_device, mesh.shape["dp"], mesh.shape["heads"]),
        mesh=mesh, in_specs=in_specs, out_specs=out_specs, check_vma=False,
    )
```

profile of v0, /device:TPU:0, one launch (start us, length us, event | category | flops | bytes accessed | tf_op | source)
XLA Modules:
  0.0 82.6 jit_solution(6245099525011390696)
XLA Ops:
  0.6 12.7 %head_grads.3 = (bf16[256,1024]{1,0:T(8,128)(2,1)}, bf16[4,2,256,128]{3,2,1,0:T(8,128)(2,1)}, bf16[2,256,128]{2,1,0:T(8,128)(2,1)}) custom-call(bf16[4096,128]{1,0:T(8,128)(2,1)} %bitcast.22, bf16[4096,128]{1,0:T(8,128)(2,1)} %bitcast.24, bf16[512,128]{1,0:T(8,128)(2,1)} %bitcast.30, bf16[512,128]{1,0:T(8,128)(2,1)} %bitcast.32, bf16[2048,128]{1,0:T(8,128)(2,1)} %bitcast.26, ...), custom_call_target="tpu_custom_call" | custom-call | flops 6710886400 | bytes 5242880 | tf_op jit(solution)/shard_map/head_grads/pallas_call | solution.py:150
  13.3 4.2 %all-to-all-start.3 = ((bf16[4,64,1024]{2,1,0:T(8,128)(2,1)}), bf16[4,64,1024]{2,1,0:T(8,128)(2,1)S(1)}, u32[]{:S(2)}, u32[]{:S(2)}) async-start(bf16[4,64,1024]{2,1,0:T(8,128)(2,1)} %bitcast.18), calls=%async_computation.3 | async-start | bytes 1048576 | tf_op jit(solution)/shard_map/all_to_all | solution.py:172
  17.5 12.7 %head_grads.2 = (bf16[256,1024]{1,0:T(8,128)(2,1)}, bf16[4,2,256,128]{3,2,1,0:T(8,128)(2,1)}, bf16[2,256,128]{2,1,0:T(8,128)(2,1)}) custom-call(bf16[4096,128]{1,0:T(8,128)(2,1)} %bitcast.23, bf16[4096,128]{1,0:T(8,128)(2,1)} %bitcast.25, bf16[512,128]{1,0:T(8,128)(2,1)} %bitcast.31, bf16[512,128]{1,0:T(8,128)(2,1)} %bitcast.33, bf16[2048,128]{1,0:T(8,128)(2,1)} %bitcast.27, ...), custom_call_target="tpu_custom_call" | custom-call | flops 6710886400 | bytes 5242880 | tf_op jit(solution)/shard_map/head_grads/pallas_call | solution.py:150
  30.3 0.0 all-to-all-done.3
  30.3 0.0 copy-start.1
  30.3 12.6 %all_to_all.28 = bf16[4,64,1024]{2,1,0:T(8,128)(2,1)S(1)} all-to-all(bf16[4,64,1024]{2,1,0:T(8,128)(2,1)} %bitcast.19), channel_id=1, replica_groups=mesh['groups'=2,'dp'=4,'heads'=4] {'heads'}, dimensions={0} | all-to-all | bytes 1048576 | tf_op jit(solution)/shard_map/all_to_all | solution.py:172
  42.9 0.0 copy-done.1
  42.9 19.6 %all_to_all.29.refs_1_ = bf16[4,2,256,128]{3,2,1,0:T(8,128)(2,1)} all-to-all(bf16[4,2,256,128]{3,2,1,0:T(8,128)(2,1)S(1)} %copy-done.1), channel_id=1, replica_groups=mesh['groups'=2,'dp'=4,'heads'=4] {'dp'}, dimensions={0} | all-to-all | bytes 1048576 | tf_op jit(solution)/shard_map/all_to_all | solution.py:173
  62.5 0.0 copy-start.2
  62.5 0.0 copy-start.3
  62.5 3.6 %all-to-all-start = ((bf16[4,2,256,128]{3,2,1,0:T(8,128)(2,1)}), bf16[4,2,256,128]{3,2,1,0:T(8,128)(2,1)S(1)}, u32[]{:S(2)}, u32[]{:S(2)}) async-start(bf16[4,2,256,128]{3,2,1,0:T(8,128)(2,1)} %get-tuple-element.9), calls=%async_computation | async-start | bytes 1048576 | tf_op jit(solution)/shard_map/all_to_all | solution.py:173
  66.1 0.0 copy-done.2
  66.1 0.0 copy-done.3
  66.2 1.0 %copy.11 = bf16[2,256,2,128]{3,2,1,0:T(2,128)(2,1)} copy(bf16[2,256,2,128]{3,1,0,2:T(8,128)(2,1)S(1)} %pad_maximum_fusion) | data formatting | bytes 524288
  67.2 0.1 maximum_bitcast_fusion
  67.3 1.1 %copy.10 = bf16[64,4,2,1024]{3,2,1,0:T(2,128)(2,1)S(1)} copy(bf16[64,4,2,1024]{3,0,1,2:T(8,128)(2,1)S(1)} %maximum_bitcast_fusion) | data formatting | bytes 2097152 | tf_op jit(solution)/shard_map/transpose | solution.py:178
  68.3 1.6 %reshape.43 = bf16[64,8192]{1,0:T(8,128)(2,1)} reshape(bf16[64,4,2,1024]{3,2,1,0:T(2,128)(2,1)S(1)} %copy.10) | data formatting | bytes 2097152 | tf_op jit(solution)/shard_map/reshape | solution.py:178
  70.0 9.7 %all-to-all-done.refs_0_ = bf16[4,2,256,128]{3,2,1,0:T(8,128)(2,1)S(1)} async-done(((bf16[4,2,256,128]{3,2,1,0:T(8,128)(2,1)}), bf16[4,2,256,128]{3,2,1,0:T(8,128)(2,1)S(1)}, u32[]{:S(2)}, u32[]{:S(2)}) %all-to-all-start) | async-done | bytes 524320 | tf_op jit(solution)/shard_map/all_to_all | solution.py:173
  79.6 0.0 copy-start
  79.6 0.8 copy-done
  80.4 2.1 %cart_sum.1 = f32[1024,128]{1,0:T(8,128)} custom-call(bf16[4,2,256,128]{3,2,1,0:T(8,128)(2,1)} %copy-done, bf16[4,2,256,128]{3,2,1,0:T(8,128)(2,1)} %all_to_all.29.refs_1_), custom_call_target="tpu_custom_call" | custom-call | flops 1048576 | bytes 2097152 | tf_op jit(solution)/shard_map/cart_sum/pallas_call | solution.py:180
  (1 shorter events, 0.0 us)
Async XLA Ops:
  13.3 17.0 %all-to-all-start.3 = ((bf16[4,64,1024]{2,1,0:T(8,128)(2,1)}), bf16[4,64,1024]{2,1,0:T(8,128)(2,1)S(1)}, u32[]{:S(2)}, u32[]{:S(2)}) async-start(bf16[4,64,1024]{2,1,0:T(8,128)(2,1)} %bitcast.18), calls=%async_computation.3 | async-start | bytes 1048576 | tf_op jit(solution)/shard_map/all_to_all | solution.py:172
  30.3 12.6 %copy-start.1 = (bf16[4,2,256,128]{3,2,1,0:T(8,128)(2,1)S(1)}, bf16[4,2,256,128]{3,2,1,0:T(8,128)(2,1)}, u32[]{:S(2)}) copy-start(bf16[4,2,256,128]{3,2,1,0:T(8,128)(2,1)} %get-tuple-element.10) | copy-start | bytes 1572868
  62.5 3.6 %copy-start.2 = (bf16[2,256,128]{2,1,0:T(8,128)(2,1)S(1)}, bf16[2,256,128]{2,1,0:T(8,128)(2,1)}, u32[]{:S(2)}) copy-start(bf16[2,256,128]{2,1,0:T(8,128)(2,1)} %get-tuple-element.12) | copy-start | bytes 393220
  62.5 3.6 %copy-start.3 = (bf16[2,256,128]{2,1,0:T(8,128)(2,1)S(1)}, bf16[2,256,128]{2,1,0:T(8,128)(2,1)}, u32[]{:S(2)}) copy-start(bf16[2,256,128]{2,1,0:T(8,128)(2,1)} %get-tuple-element.11) | copy-start | bytes 393220
  62.5 17.1 %all-to-all-start = ((bf16[4,2,256,128]{3,2,1,0:T(8,128)(2,1)}), bf16[4,2,256,128]{3,2,1,0:T(8,128)(2,1)S(1)}, u32[]{:S(2)}, u32[]{:S(2)}) async-start(bf16[4,2,256,128]{3,2,1,0:T(8,128)(2,1)} %get-tuple-element.9), calls=%async_computation | async-start | bytes 1048576 | tf_op jit(solution)/shard_map/all_to_all | solution.py:173
  79.6 0.8 copy-start
where the time goes:
time: 82.9 us; the launch traced here: 82.6 us
  blocking collectives  32.2 us (39%)
  Pallas kernels  27.6 us (33%)
  waiting for transfers between devices  9.69 us (12%)
  starting transfers between devices  7.81 us (9%)
  local copies, waits for them, and re-layouts  4.48 us (5%)
    pallas_call x2, Pallas kernels, on_device(): pl.pallas_call(functools.partial(head_kernel, kv_index, kv_local, width,...  25.4 us
    all_to_all x1, blocking collectives, on_device(): lax.all_to_all(cart, 'dp', split_axis=0, concat_axis=0, tiled=True)  19.6 us
    all_to_all x1, blocking collectives, on_device(): lax.all_to_all(dq, 'heads', split_axis=0, concat_axis=0, tiled=True)  12.6 us
    all_to_all x1, waiting for transfers between devices, on_device(): lax.all_to_all(cart, 'dp', split_axis=0, concat_axis=0, tiled=True)  9.69 us
    all_to_all x1, starting transfers between devices, on_device(): lax.all_to_all(dq, 'heads', split_axis=0, concat_axis=0, tiled=True)  4.21 us
    all_to_all x1, starting transfers between devices, on_device(): lax.all_to_all(cart, 'dp', split_axis=0, concat_axis=0, tiled=True)  3.6 us
    pallas_call x1, Pallas kernels, on_device(): pl.pallas_call(functools.partial(cart_kernel, kv_local), out_shape=jax.Sh...  2.11 us
    unnamed x9, local copies, waits for them, and re-layouts  1.78 us
  transfers between devices with their start and end apart: 2, of which 1 were waited for; matrix products, arithmetic and copies ran while one was open for 5% of the time, Pallas kernels for 15%

commit v1 on v0

--- a/solution.py
+++ b/solution.py
@@ -28,11 +28,15 @@
 
 
 def head_kernel(
-    kv_index, kv_local, width, block_tokens, chunk,
+    dp_size, heads_size, kv_index, kv_local, width, block_tokens, chunk,
     q_ref, g_ref, sk_ref, sv_ref, ck_ref, cv_ref, seg_ref,
-    dq_ref, cart_ref, self_ref,
-    wide_ref, keys_ref, vals_ref, keys_t_ref, s_ref, d_ref, dk_ref, dv_ref, out_ref,
+    *rest,
 ):
+    cart_outs, dq_outs = rest[:dp_size], rest[dp_size : dp_size + heads_size]
+    self_ref = rest[dp_size + heads_size]
+    (
+        wide_ref, keys_ref, vals_ref, keys_t_ref, s_ref, d_ref, dk_ref, dv_ref, out_ref, dq_ref,
+    ) = rest[dp_size + heads_size + 1 :]
     head_dim = q_ref.shape[1]
     tokens = seg_ref.shape[1]
     cart_rows = ck_ref.shape[0] // kv_local
@@ -112,25 +116,50 @@
             dq_ref[block * block_tokens : (block + 1) * block_tokens, head * head_dim : (head + 1) * head_dim] = (
                 out_ref[pl.ds(head, block_tokens, stride=width), :].astype(bf16)
             )
-    parts, _, part_rows, _ = cart_ref.shape
-    for part in range(parts):
-        span = slice(part * part_rows, (part + 1) * part_rows)
-        cart_ref[part, 0] = (dk_ref[span, :] * scale).astype(bf16)
-        cart_ref[part, 1] = dv_ref[span, :].astype(bf16)
+    part_rows = cart_rows // dp_size
+    me = lax.axis_index("dp")
+    for step, ref in enumerate(cart_outs):
+        target = lax.rem(me + step, dp_size)
+        span = pl.ds(pl.multiple_of(target * part_rows, part_rows), part_rows)
+        ref[0] = (dk_ref[span, :] * scale).astype(ref.dtype)
+        ref[1] = dv_ref[span, :].astype(ref.dtype)
+    own_tokens = tokens // heads_size
+    me = lax.axis_index("heads")
+    for step, ref in enumerate(dq_outs):
+        target = lax.rem(me + step, heads_size)
+        ref[...] = dq_ref[pl.ds(pl.multiple_of(target * own_tokens, own_tokens), own_tokens), :]
     self_ref[0] = (dk_ref[cart_rows:all_keys, :] * scale).astype(bf16)
     self_ref[1] = dv_ref[cart_rows:all_keys, :].astype(bf16)
 
 
 def cart_kernel(kv_local, *refs):
     part_refs, out_ref = refs[:-1], refs[-1]
-    count = part_refs[0].shape[0]
-    part_rows = part_refs[0].shape[2]
-    for kv_index, ref in enumerate(part_refs):
+    count = len(part_refs) // kv_local
+    part_rows = part_refs[0].shape[1]
+    for kv_index in range(kv_local):
         for kind in range(2):
-            total = ref[0, kind].astype(f32)
+            total = part_refs[kv_index * count][kind]
             for part in range(1, count):
-                total = total + ref[part, kind].astype(f32)
+                total = total + part_refs[kv_index * count + part][kind].astype(f32)
             out_ref[pl.ds(kind * kv_local + kv_index, part_rows, stride=2 * kv_local), :] = total
+
+
+def place_kernel(kv_local, *refs):
+    part_refs, out_ref = refs[:-1], refs[-1]
+    count = len(part_refs) // kv_local
+    columns = part_refs[0].shape[1]
+    me = lax.axis_index("heads")
+    for kv_index in range(kv_local):
+        for step in range(count):
+            source = lax.rem(me + count - step, count)
+            at = pl.multiple_of((source * kv_local + kv_index) * columns, columns)
+            out_ref[:, pl.ds(at, columns)] = part_refs[kv_index * count + step][...]
+
+
+def shift(values, axis, size, step):
+    if step == 0:
+        return values
+    return lax.ppermute(values, axis, [(source, (source + step) % size) for source in range(size)])
 
 
 def on_device(dp_size, heads_size, queries, out_grad, self_keys, self_values, cart_keys, cart_values, segment_ids):
@@ -143,15 +172,19 @@
     all_keys = cart_rows + tokens
     rows = block_tokens * width
     part_rows = cart_rows // dp_size
+    own_tokens = tokens // heads_size
     flat = [array.reshape(-1, head_dim) for array in (queries, out_grad, self_keys, self_values, cart_keys, cart_values)]
     macs = tokens * width * all_keys * head_dim * 5
-    query_list, cart_list, self_list = [], [], []
+    cart_list, query_list, self_list = [], [], []
     for kv_index in range(kv_local):
-        dq, cart, own = pl.pallas_call(
-            functools.partial(head_kernel, kv_index, kv_local, width, block_tokens, chunk),
+        outs = pl.pallas_call(
+            functools.partial(head_kernel, dp_size, heads_size, kv_index, kv_local, width, block_tokens, chunk),
             out_shape=(
-                jax.ShapeDtypeStruct((tokens, width * head_dim), bf16),
-                jax.ShapeDtypeStruct((dp_size, 2, part_rows, head_dim), bf16),
+                *[
+                    jax.ShapeDtypeStruct((2, part_rows, head_dim), bf16 if step else f32)
+                    for step in range(dp_size)
+                ],
+                *[jax.ShapeDtypeStruct((own_tokens, width * head_dim), bf16) for _ in range(heads_size)],
                 jax.ShapeDtypeStruct((2, tokens, head_dim), bf16),
             ),
             scratch_shapes=[
@@ -164,18 +197,22 @@
                 pltpu.VMEM((all_keys, head_dim), f32),
                 pltpu.VMEM((all_keys, head_dim), f32),
                 pltpu.VMEM((rows, head_dim), f32),
+                pltpu.VMEM((tokens, width * head_dim), bf16),
             ],
             compiler_params=pltpu.CompilerParams(vmem_limit_bytes=vmem_bytes),
             cost_estimate=pl.CostEstimate(flops=4 * macs, bytes_accessed=5 * 2**20, transcendentals=tokens * width * all_keys),
             name="head_grads",
         )(*flat, segment_ids)
-        query_list.append(lax.all_to_all(dq, "heads", split_axis=0, concat_axis=0, tiled=True))
-        cart_list.append(lax.all_to_all(cart, "dp", split_axis=0, concat_axis=0, tiled=True))
-        self_list.append(own)
-    own_tokens = tokens // heads_size
-    query_grads = jnp.stack(
-        [part.reshape(heads_size, own_tokens, width * head_dim) for part in query_list], axis=1
-    ).transpose(2, 0, 1, 3).reshape(own_tokens, heads_size * heads_local * head_dim)
+        cart_list += [shift(outs[step], "dp", dp_size, step) for step in range(dp_size)]
+        query_list += [shift(outs[dp_size + step], "heads", heads_size, step) for step in range(heads_size)]
+        self_list.append(outs[-1])
+    query_grads = pl.pallas_call(
+        functools.partial(place_kernel, kv_local),
+        out_shape=jax.ShapeDtypeStruct((own_tokens, heads_size * heads_local * head_dim), bf16),
+        compiler_params=pltpu.CompilerParams(vmem_limit_bytes=vmem_bytes),
+        cost_estimate=pl.CostEstimate(flops=2**20, bytes_accessed=2 * 2**20, transcendentals=0),
+        name="place_queries",
+    )(*query_list)
     self_grads = jnp.stack(self_list, axis=2)
     cart_grads = pl.pallas_call(
         functools.partial(cart_kernel, kv_local),

time: 82.9 us -> 57.1 us (0.69)
  blocking collectives: 32.2 us -> 0 us
  starting transfers between devices: 7.81 us -> 15.9 us
  waiting for transfers between devices: 9.69 us -> 6.39 us
  Pallas kernels: 27.6 us -> 30.5 us
  local copies, waits for them, and re-layouts: 4.48 us -> 1.79 us
    all_to_all x2 -> x0, blocking collectives: 32.2 us -> none  [the longest x1 19.6 us: on_device(): lax.all_to_all(cart, 'dp', split_axis=0, concat_axis=0, tiled=True)]
    ppermute x0 -> x12, starting transfers between devices: none -> 15.9 us  [shift(): lax.ppermute(values, axis, [(source, (source + step) % size) for source i...]
    all_to_all x2 -> x0, waiting for transfers between devices: 9.69 us -> none  [the longest x1 9.69 us: on_device(): lax.all_to_all(cart, 'dp', split_axis=0, concat_axis=0, tiled=True)]
    all_to_all x2 -> x0, starting transfers between devices: 7.81 us -> none  [the longest x1 4.21 us: on_device(): lax.all_to_all(dq, 'heads', split_axis=0, concat_axis=0, tiled=True)]
    ppermute x0 -> x12, waiting for transfers between devices: none -> 6.39 us  [shift(): lax.ppermute(values, axis, [(source, (source + step) % size) for source i...]
    pallas_call x2 -> x3, Pallas kernels: 25.4 us -> 28.2 us  [the longest x2 25.9 us: on_device(): pl.pallas_call(functools.partial(head_kernel, dp_size, heads_size, kv_ind...]
    reshape x1 -> x0, local copies, waits for them, and re-layouts: 1.61 us -> none  [on_device(): query_grads = jnp.stack([part.reshape(heads_size, own_tokens, width * hea...]
    transpose x1 -> x0, local copies, waits for them, and re-layouts: 1.08 us -> none  [on_device(): query_grads = jnp.stack([part.reshape(heads_size, own_tokens, width * hea...]
  transfers between devices with their start and end apart: 2 -> 12, of which waited for: 1 -> 2; matrix products, arithmetic and copies ran while one was open for 5% -> 3% of each run, Pallas kernels for 15% -> 27%
where the time goes in v1:
time: 57.1 us; the launch traced here: 56.2 us
  Pallas kernels  30.5 us (53%)
  starting transfers between devices  15.9 us (28%)
  waiting for transfers between devices  6.39 us (11%)
  local copies, waits for them, and re-layouts  1.79 us (3%)
  other arithmetic  0.93 us (2%)
  between operations  0.74 us (1%)
    pallas_call x2, Pallas kernels, on_device(): pl.pallas_call(functools.partial(head_kernel, dp_size, heads_size, kv_ind...  25.9 us
    ppermute x12, starting transfers between devices, shift(): lax.ppermute(values, axis, [(source, (source + step) % size) for source i...  15.9 us
    ppermute x12, waiting for transfers between devices, shift(): lax.ppermute(values, axis, [(source, (source + step) % size) for source i...  6.39 us
    pallas_call x1, Pallas kernels, on_device(): pl.pallas_call(functools.partial(place_kernel, kv_local), out_shape=jax.S...  2.33 us
    pallas_call x1, Pallas kernels, on_device(): pl.pallas_call(functools.partial(cart_kernel, kv_local), out_shape=jax.Sh...  2.24 us
    unnamed x31, local copies, waits for them, and re-layouts  1.79 us
  transfers between devices with their start and end apart: 12, of which 2 were waited for; matrix products, arithmetic and copies ran while one was open for 3% of the time, Pallas kernels for 27%

profile of v1, /device:TPU:0, one launch (start us, length us, event | category | flops | bytes accessed | tf_op | source)
XLA Modules:
  0.0 56.2 jit_solution(4256165981171374440)
XLA Ops:
  0.6 12.9 %head_grads.3 = (f32[2,256,128]{2,1,0:T(8,128)}, bf16[2,256,128]{2,1,0:T(8,128)(2,1)}, bf16[2,256,128]{2,1,0:T(8,128)(2,1)}, bf16[2,256,128]{2,1,0:T(8,128)(2,1)...) custom-call(bf16[4096,128]{1,0:T(8,128)(2,1)} %bitcast.12, ...), custom_call_target="tpu_custom_call" | custom-call | flops 6710886400 | bytes 5242880 | tf_op jit(solution)/shard_map/head_grads/pallas_call | solution.py:180
  13.5 3.0 %collective-permute-start.3 = (bf16[2,256,128]{2,1,0:T(8,128)(2,1)}, bf16[2,256,128]{2,1,0:T(8,128)(2,1)S(1)}, u32[]{:S(2)}, u32[]{:S(2)}) collective-permute-start(bf16[2,256,128]{2,1,0:T(8,128)(2,1)} %get-tuple-element.26), channel_id=1, source_target_pairs={{0,4},{4,8},{8,12},{12,0},{1,5},{5,9},{9,13},{13,1},{2,6},{6,10},{... | collective-permute-start | bytes 393224 | tf_op jit(solution)/shard_map/ppermute | solution.py:162
  16.6 2.6 %collective-permute-start.4 = (bf16[2,256,128]{2,1,0:T(8,128)(2,1)}, bf16[2,256,128]{2,1,0:T(8,128)(2,1)S(1)}, u32[]{:S(2)}, u32[]{:S(2)}) collective-permute-start(bf16[2,256,128]{2,1,0:T(8,128)(2,1)} %get-tuple-element.27), channel_id=1, source_target_pairs={{0,8},{4,12},{8,0},{12,4},{1,9},{5,13},{9,1},{13,5},{2,10},{6,14},... | collective-permute-start | bytes 393224 | tf_op jit(solution)/shard_map/ppermute | solution.py:162
  19.2 1.3 %collective-permute-start.5 = (bf16[2,256,128]{2,1,0:T(8,128)(2,1)}, bf16[2,256,128]{2,1,0:T(8,128)(2,1)S(1)}, u32[]{:S(2)}, u32[]{:S(2)}) collective-permute-start(bf16[2,256,128]{2,1,0:T(8,128)(2,1)} %get-tuple-element.28), channel_id=1, source_target_pairs={{0,12},{4,0},{8,4},{12,8},{1,13},{5,1},{9,5},{13,9},{2,14},{6,2},{... | collective-permute-start | bytes 393224 | tf_op jit(solution)/shard_map/ppermute | solution.py:162
  20.5 0.0 collective-permute-start.9
  20.5 13.0 %head_grads.2 = (f32[2,256,128]{2,1,0:T(8,128)}, bf16[2,256,128]{2,1,0:T(8,128)(2,1)}, bf16[2,256,128]{2,1,0:T(8,128)(2,1)}, bf16[2,256,128]{2,1,0:T(8,128)(2,1)...) custom-call(bf16[4096,128]{1,0:T(8,128)(2,1)} %bitcast.13, ...), custom_call_target="tpu_custom_call" | custom-call | flops 6710886400 | bytes 5242880 | tf_op jit(solution)/shard_map/head_grads/pallas_call | solution.py:180
  33.5 0.7 %collective-permute-start = (bf16[2,256,128]{2,1,0:T(8,128)(2,1)}, bf16[2,256,128]{2,1,0:T(8,128)(2,1)S(1)}, u32[]{:S(2)}, u32[]{:S(2)}) collective-permute-start(bf16[2,256,128]{2,1,0:T(8,128)(2,1)} %get-tuple-element.22), channel_id=1, source_target_pairs={{0,4},{4,8},{8,12},{12,0},{1,5},{5,9},{9,13},{13,1},{2,6},{6,10},{... | collective-permute-start | bytes 393224 | tf_op jit(solution)/shard_map/ppermute | solution.py:162
  34.2 0.0 collective-permute-done.3.refs_5_
  34.2 0.4 collective-permute-start.1
  34.6 0.0 collective-permute-done.4.refs_6_
  34.6 2.9 %collective-permute-start.2 = (bf16[2,256,128]{2,1,0:T(8,128)(2,1)}, bf16[2,256,128]{2,1,0:T(8,128)(2,1)S(1)}, u32[]{:S(2)}, u32[]{:S(2)}) collective-permute-start(bf16[2,256,128]{2,1,0:T(8,128)(2,1)} %get-tuple-element.24), channel_id=1, source_target_pairs={{0,12},{4,0},{8,4},{12,8},{1,13},{5,1},{9,5},{13,9},{2,14},{6,2},{... | collective-permute-start | bytes 393224 | tf_op jit(solution)/shard_map/ppermute | solution.py:162
  37.4 1.5 %collective-permute-start.10 = (bf16[64,1024]{1,0:T(8,128)(2,1)S(1)}, bf16[64,1024]{1,0:T(8,128)(2,1)S(1)}, u32[]{:S(2)}, u32[]{:S(2)}) collective-permute-start(bf16[64,1024]{1,0:T(8,128)(2,1)S(1)} %copy-done.14), channel_id=1, source_target_pairs={{0,2},{1,3},{2,0},{3,1},{4,6},{5,7},{6,4},{7,5},{8,10},{9,11},{10,... | collective-permute-start | bytes 393224 | tf_op jit(solution)/shard_map/ppermute | solution.py:162
  39.0 0.0 collective-permute-done.9.refs_5_
  39.0 0.9 %collective-permute-start.11 = (bf16[64,1024]{1,0:T(8,128)(2,1)S(1)}, bf16[64,1024]{1,0:T(8,128)(2,1)S(1)}, u32[]{:S(2)}, u32[]{:S(2)}) collective-permute-start(bf16[64,1024]{1,0:T(8,128)(2,1)S(1)} %copy-done.13), channel_id=1, source_target_pairs={{0,3},{1,0},{2,1},{3,2},{4,7},{5,4},{6,5},{7,6},{8,11},{9,8},{10,9... | collective-permute-start | bytes 393224 | tf_op jit(solution)/shard_map/ppermute | solution.py:162
  39.9 1.7 %collective-permute-done.refs_1_ = bf16[2,256,128]{2,1,0:T(8,128)(2,1)S(1)} collective-permute-done((bf16[2,256,128]{2,1,0:T(8,128)(2,1)}, bf16[2,256,128]{2,1,0:T(8,128)(2,1)S(1)}, u32[]{:S(2)}, u32[]{:S(2)}) %collective-permute-start) | collective-permute-done | bytes 131104 | tf_op jit(solution)/shard_map/ppermute | solution.py:162
  41.6 0.8 %collective-permute-start.6 = (bf16[64,1024]{1,0:T(8,128)(2,1)}, bf16[64,1024]{1,0:T(8,128)(2,1)S(1)}, u32[]{:S(2)}, u32[]{:S(2)}) collective-permute-start(bf16[64,1024]{1,0:T(8,128)(2,1)} %get-tuple-element.32), channel_id=1, source_target_pairs={{0,1},{1,2},{2,3},{3,0},{4,5},{5,6},{6,7},{7,4},{8,9},{9,10},{10,1... | collective-permute-start | bytes 393224 | tf_op jit(solution)/shard_map/ppermute | solution.py:162
  42.4 4.7 %collective-permute-done.1.refs_2_ = bf16[2,256,128]{2,1,0:T(8,128)(2,1)S(1)} collective-permute-done((bf16[2,256,128]{2,1,0:T(8,128)(2,1)}, bf16[2,256,128]{2,1,0:T(8,128)(2,1)S(1)}, u32[]{:S(2)}, u32[]{:S(2)}) %collective-permute-start.1) | collective-permute-done | bytes 131104 | tf_op jit(solution)/shard_map/ppermute | solution.py:162
  47.0 1.7 %collective-permute-start.7 = (bf16[64,1024]{1,0:T(8,128)(2,1)}, bf16[64,1024]{1,0:T(8,128)(2,1)S(1)}, u32[]{:S(2)}, u32[]{:S(2)}) collective-permute-start(bf16[64,1024]{1,0:T(8,128)(2,1)} %get-tuple-element.33), channel_id=1, source_target_pairs={{0,2},{1,3},{2,0},{3,1},{4,6},{5,7},{6,4},{7,5},{8,10},{9,11},{10,... | collective-permute-start | bytes 393224 | tf_op jit(solution)/shard_map/ppermute | solution.py:162
  48.7 0.0 collective-permute-done.2.refs_3_
  48.7 0.1 collective-permute-start.8
  48.8 0.9 %pad_maximum_fusion = bf16[2,256,2,128]{3,1,0,2:T(8,128)(2,1)S(1)} fusion(bf16[2,256,1,128]{3,1,0,2:T(8,128)(2,1)S(1)} %bitcast.10, bf16[2,256,1,128]{3,1,0,2:T(8,128)(2,1)} %bitcast.11), kind=kLoop, calls=%fused_computation | loop fusion | flops 131072 | bytes 524288 | tf_op jit(solution)/shard_map/stack | solution.py:216
  49.8 1.0 %copy.10 = bf16[2,256,2,128]{3,2,1,0:T(2,128)(2,1)} copy(bf16[2,256,2,128]{3,1,0,2:T(8,128)(2,1)S(1)} %pad_maximum_fusion) | data formatting | bytes 524288
  50.8 2.2 %cart_sum.1 = f32[1024,128]{1,0:T(8,128)} custom-call(f32[2,256,128]{2,1,0:T(8,128)} %get-tuple-element.21.refs_0_, bf16[2,256,128]{2,1,0:T(8,128)(2,1)} %copy-done.3, bf16[2,256,128]{2,1,0:T(8,128)(2,1)} %copy-done.4, bf16[2,256,128]{2,1,0:T(8,128)(2,1)} %copy-done.5, f32[2,256,128]{2,1,0:T(8,128)} %get-tuple-element.25.refs_4_, ...), custom_call_target="tpu_custom_call" | custom-call | flops 1048576 | bytes 2097152 | tf_op jit(solution)/shard_map/cart_sum/pallas_call | solution.py:217
  53.0 0.0 collective-permute-done.10.refs_6_
  53.0 0.0 collective-permute-done.6.refs_1_
  53.1 0.0 collective-permute-done.7.refs_2_
  53.1 0.6 %copy-done.7 = bf16[64,1024]{1,0:T(8,128)(2,1)} copy-done((bf16[64,1024]{1,0:T(8,128)(2,1)}, bf16[64,1024]{1,0:T(8,128)(2,1)S(1)}, u32[]{:S(2)}) %copy-start.7) | copy-done | bytes 131096
  53.7 0.0 copy-done.8
  53.7 0.1 copy-done.9
  53.8 0.0 copy-done.10
  53.8 0.0 copy-done.11
  53.9 2.3 %place_queries.1 = bf16[64,8192]{1,0:T(8,128)(2,1)} custom-call(bf16[64,1024]{1,0:T(8,128)(2,1)} %get-tuple-element.31.refs_0_, bf16[64,1024]{1,0:T(8,128)(2,1)} %copy-done.9, bf16[64,1024]{1,0:T(8,128)(2,1)} %copy-done.10, bf16[64,1024]{1,0:T(8,128)(2,1)} %copy-done.11, bf16[64,1024]{1,0:T(8,128)(2,1)} %get-tuple-element.35.refs_4_, ...), custom_call_target="tpu_custom_call" | custom-call | flops 1048576 | bytes 2097152 | tf_op jit(solution)/shard_map/place_queries/pallas_call | solution.py:209
  (28 shorter events, 0.1 us)
Async XLA Ops:
  13.5 20.7 %collective-permute-start.3 = (bf16[2,256,128]{2,1,0:T(8,128)(2,1)}, bf16[2,256,128]{2,1,0:T(8,128)(2,1)S(1)}, u32[]{:S(2)}, u32[]{:S(2)}) collective-permute-start(bf16[2,256,128]{2,1,0:T(8,128)(2,1)} %get-tuple-element.26), channel_id=1, source_target_pairs={{0,4},{4,8},{8,12},{12,0},{1,5},{5,9},{9,13},{13,1},{2,6},{6,10},{... | collective-permute-start | bytes 393224 | tf_op jit(solution)/shard_map/ppermute | solution.py:162
  16.6 18.0 %collective-permute-start.4 = (bf16[2,256,128]{2,1,0:T(8,128)(2,1)}, bf16[2,256,128]{2,1,0:T(8,128)(2,1)S(1)}, u32[]{:S(2)}, u32[]{:S(2)}) collective-permute-start(bf16[2,256,128]{2,1,0:T(8,128)(2,1)} %get-tuple-element.27), channel_id=1, source_target_pairs={{0,8},{4,12},{8,0},{12,4},{1,9},{5,13},{9,1},{13,5},{2,10},{6,14},... | collective-permute-start | bytes 393224 | tf_op jit(solution)/shard_map/ppermute | solution.py:162
  19.2 18.3 %collective-permute-start.5 = (bf16[2,256,128]{2,1,0:T(8,128)(2,1)}, bf16[2,256,128]{2,1,0:T(8,128)(2,1)S(1)}, u32[]{:S(2)}, u32[]{:S(2)}) collective-permute-start(bf16[2,256,128]{2,1,0:T(8,128)(2,1)} %get-tuple-element.28), channel_id=1, source_target_pairs={{0,12},{4,0},{8,4},{12,8},{1,13},{5,1},{9,5},{13,9},{2,14},{6,2},{... | collective-permute-start | bytes 393224 | tf_op jit(solution)/shard_map/ppermute | solution.py:162
  20.5 16.9 %copy-start.14 = (bf16[64,1024]{1,0:T(8,128)(2,1)S(1)}, bf16[64,1024]{1,0:T(8,128)(2,1)}, u32[]{:S(2)}) copy-start(bf16[64,1024]{1,0:T(8,128)(2,1)} %get-tuple-element.37) | copy-start | bytes 393220
  20.5 18.5 %copy-start.13 = (bf16[64,1024]{1,0:T(8,128)(2,1)S(1)}, bf16[64,1024]{1,0:T(8,128)(2,1)}, u32[]{:S(2)}) copy-start(bf16[64,1024]{1,0:T(8,128)(2,1)} %get-tuple-element.38) | copy-start | bytes 393220
  20.5 28.3 %copy-start.12 = (bf16[2,256,128]{2,1,0:T(8,128)(2,1)S(1)}, bf16[2,256,128]{2,1,0:T(8,128)(2,1)}, u32[]{:S(2)}) copy-start(bf16[2,256,128]{2,1,0:T(8,128)(2,1)} %get-tuple-element.30) | copy-start | bytes 393220
  20.5 18.5 %collective-permute-start.9 = (bf16[64,1024]{1,0:T(8,128)(2,1)}, bf16[64,1024]{1,0:T(8,128)(2,1)S(1)}, u32[]{:S(2)}, u32[]{:S(2)}) collective-permute-start(bf16[64,1024]{1,0:T(8,128)(2,1)} %get-tuple-element.36), channel_id=1, source_target_pairs={{0,1},{1,2},{2,3},{3,0},{4,5},{5,6},{6,7},{7,4},{8,9},{9,10},{10,1... | collective-permute-start | bytes 393224 | tf_op jit(solution)/shard_map/ppermute | solution.py:162
  33.5 8.1 %collective-permute-start = (bf16[2,256,128]{2,1,0:T(8,128)(2,1)}, bf16[2,256,128]{2,1,0:T(8,128)(2,1)S(1)}, u32[]{:S(2)}, u32[]{:S(2)}) collective-permute-start(bf16[2,256,128]{2,1,0:T(8,128)(2,1)} %get-tuple-element.22), channel_id=1, source_target_pairs={{0,4},{4,8},{8,12},{12,0},{1,5},{5,9},{9,13},{13,1},{2,6},{6,10},{... | collective-permute-start | bytes 393224 | tf_op jit(solution)/shard_map/ppermute | solution.py:162
  34.2 15.6 %copy-start = (bf16[2,256,128]{2,1,0:T(8,128)(2,1)}, bf16[2,256,128]{2,1,0:T(8,128)(2,1)S(1)}, u32[]{:S(2)}) copy-start(bf16[2,256,128]{2,1,0:T(8,128)(2,1)S(1)} %collective-permute-done.3.refs_5_) | copy-start | bytes 393220
  34.2 12.8 %collective-permute-start.1 = (bf16[2,256,128]{2,1,0:T(8,128)(2,1)}, bf16[2,256,128]{2,1,0:T(8,128)(2,1)S(1)}, u32[]{:S(2)}, u32[]{:S(2)}) collective-permute-start(bf16[2,256,128]{2,1,0:T(8,128)(2,1)} %get-tuple-element.23), channel_id=1, source_target_pairs={{0,8},{4,12},{8,0},{12,4},{1,9},{5,13},{9,1},{13,5},{2,10},{6,14},... | collective-permute-start | bytes 393224 | tf_op jit(solution)/shard_map/ppermute | solution.py:162
  34.6 15.2 %copy-start.1 = (bf16[2,256,128]{2,1,0:T(8,128)(2,1)}, bf16[2,256,128]{2,1,0:T(8,128)(2,1)S(1)}, u32[]{:S(2)}) copy-start(bf16[2,256,128]{2,1,0:T(8,128)(2,1)S(1)} %collective-permute-done.4.refs_6_) | copy-start | bytes 393220
  34.6 14.2 %collective-permute-start.2 = (bf16[2,256,128]{2,1,0:T(8,128)(2,1)}, bf16[2,256,128]{2,1,0:T(8,128)(2,1)S(1)}, u32[]{:S(2)}, u32[]{:S(2)}) collective-permute-start(bf16[2,256,128]{2,1,0:T(8,128)(2,1)} %get-tuple-element.24), channel_id=1, source_target_pairs={{0,12},{4,0},{8,4},{12,8},{1,13},{5,1},{9,5},{13,9},{2,14},{6,2},{... | collective-permute-start | bytes 393224 | tf_op jit(solution)/shard_map/ppermute | solution.py:162
  37.4 12.4 %copy-start.2 = (bf16[2,256,128]{2,1,0:T(8,128)(2,1)}, bf16[2,256,128]{2,1,0:T(8,128)(2,1)S(1)}, u32[]{:S(2)}) copy-start(bf16[2,256,128]{2,1,0:T(8,128)(2,1)S(1)} %collective-permute-done.5.refs_7_) | copy-start | bytes 393220
  37.4 15.6 %collective-permute-start.10 = (bf16[64,1024]{1,0:T(8,128)(2,1)S(1)}, bf16[64,1024]{1,0:T(8,128)(2,1)S(1)}, u32[]{:S(2)}, u32[]{:S(2)}) collective-permute-start(bf16[64,1024]{1,0:T(8,128)(2,1)S(1)} %copy-done.14), channel_id=1, source_target_pairs={{0,2},{1,3},{2,0},{3,1},{4,6},{5,7},{6,4},{7,5},{8,10},{9,11},{10,... | collective-permute-start | bytes 393224 | tf_op jit(solution)/shard_map/ppermute | solution.py:162
  39.0 11.8 %copy-start.6 = (bf16[64,1024]{1,0:T(8,128)(2,1)}, bf16[64,1024]{1,0:T(8,128)(2,1)S(1)}, u32[]{:S(2)}) copy-start(bf16[64,1024]{1,0:T(8,128)(2,1)S(1)} %collective-permute-done.9.refs_5_) | copy-start | bytes 393220
  39.0 14.0 %collective-permute-start.11 = (bf16[64,1024]{1,0:T(8,128)(2,1)S(1)}, bf16[64,1024]{1,0:T(8,128)(2,1)S(1)}, u32[]{:S(2)}, u32[]{:S(2)}) collective-permute-start(bf16[64,1024]{1,0:T(8,128)(2,1)S(1)} %copy-done.13), channel_id=1, source_target_pairs={{0,3},{1,0},{2,1},{3,2},{4,7},{5,4},{6,5},{7,6},{8,11},{9,8},{10,9... | collective-permute-start | bytes 393224 | tf_op jit(solution)/shard_map/ppermute | solution.py:162
  41.6 8.2 %copy-start.3 = (bf16[2,256,128]{2,1,0:T(8,128)(2,1)}, bf16[2,256,128]{2,1,0:T(8,128)(2,1)S(1)}, u32[]{:S(2)}) copy-start(bf16[2,256,128]{2,1,0:T(8,128)(2,1)S(1)} %collective-permute-done.refs_1_) | copy-start | bytes 393220
  41.6 11.5 %collective-permute-start.6 = (bf16[64,1024]{1,0:T(8,128)(2,1)}, bf16[64,1024]{1,0:T(8,128)(2,1)S(1)}, u32[]{:S(2)}, u32[]{:S(2)}) collective-permute-start(bf16[64,1024]{1,0:T(8,128)(2,1)} %get-tuple-element.32), channel_id=1, source_target_pairs={{0,1},{1,2},{2,3},{3,0},{4,5},{5,6},{6,7},{7,4},{8,9},{9,10},{10,1... | collective-permute-start | bytes 393224 | tf_op jit(solution)/shard_map/ppermute | solution.py:162
  47.0 3.7 %copy-start.4 = (bf16[2,256,128]{2,1,0:T(8,128)(2,1)}, bf16[2,256,128]{2,1,0:T(8,128)(2,1)S(1)}, u32[]{:S(2)}) copy-start(bf16[2,256,128]{2,1,0:T(8,128)(2,1)S(1)} %collective-permute-done.1.refs_2_) | copy-start | bytes 393220
  47.0 6.0 %collective-permute-start.7 = (bf16[64,1024]{1,0:T(8,128)(2,1)}, bf16[64,1024]{1,0:T(8,128)(2,1)S(1)}, u32[]{:S(2)}, u32[]{:S(2)}) collective-permute-start(bf16[64,1024]{1,0:T(8,128)(2,1)} %get-tuple-element.33), channel_id=1, source_target_pairs={{0,2},{1,3},{2,0},{3,1},{4,6},{5,7},{6,4},{7,5},{8,10},{9,11},{10,... | collective-permute-start | bytes 393224 | tf_op jit(solution)/shard_map/ppermute | solution.py:162
  48.7 2.1 %copy-start.5 = (bf16[2,256,128]{2,1,0:T(8,128)(2,1)}, bf16[2,256,128]{2,1,0:T(8,128)(2,1)S(1)}, u32[]{:S(2)}) copy-start(bf16[2,256,128]{2,1,0:T(8,128)(2,1)S(1)} %collective-permute-done.2.refs_3_) | copy-start | bytes 393220
  48.7 4.4 %collective-permute-start.8 = (bf16[64,1024]{1,0:T(8,128)(2,1)}, bf16[64,1024]{1,0:T(8,128)(2,1)S(1)}, u32[]{:S(2)}, u32[]{:S(2)}) collective-permute-start(bf16[64,1024]{1,0:T(8,128)(2,1)} %get-tuple-element.34), channel_id=1, source_target_pairs={{0,3},{1,0},{2,1},{3,2},{4,7},{5,4},{6,5},{7,6},{8,11},{9,8},{10,9... | collective-permute-start | bytes 393224 | tf_op jit(solution)/shard_map/ppermute | solution.py:162
  53.0 0.7 %copy-start.7 = (bf16[64,1024]{1,0:T(8,128)(2,1)}, bf16[64,1024]{1,0:T(8,128)(2,1)S(1)}, u32[]{:S(2)}) copy-start(bf16[64,1024]{1,0:T(8,128)(2,1)S(1)} %collective-permute-done.10.refs_6_) | copy-start | bytes 393220
  53.0 0.7 %copy-start.8 = (bf16[64,1024]{1,0:T(8,128)(2,1)}, bf16[64,1024]{1,0:T(8,128)(2,1)S(1)}, u32[]{:S(2)}) copy-start(bf16[64,1024]{1,0:T(8,128)(2,1)S(1)} %collective-permute-done.11.refs_7_) | copy-start | bytes 393220
  53.1 0.7 %copy-start.9 = (bf16[64,1024]{1,0:T(8,128)(2,1)}, bf16[64,1024]{1,0:T(8,128)(2,1)S(1)}, u32[]{:S(2)}) copy-start(bf16[64,1024]{1,0:T(8,128)(2,1)S(1)} %collective-permute-done.6.refs_1_) | copy-start | bytes 393220
  53.1 0.8 %copy-start.10 = (bf16[64,1024]{1,0:T(8,128)(2,1)}, bf16[64,1024]{1,0:T(8,128)(2,1)S(1)}, u32[]{:S(2)}) copy-start(bf16[64,1024]{1,0:T(8,128)(2,1)S(1)} %collective-permute-done.7.refs_2_) | copy-start | bytes 393220
  53.1 0.8 %copy-start.11 = (bf16[64,1024]{1,0:T(8,128)(2,1)}, bf16[64,1024]{1,0:T(8,128)(2,1)S(1)}, u32[]{:S(2)}) copy-start(bf16[64,1024]{1,0:T(8,128)(2,1)S(1)} %collective-permute-done.8.refs_3_) | copy-start | bytes 393220

commit v2 on v1

v2 whole, which is shorter than its diff:
```python
import functools
import math

import jax
import jax.numpy as jnp
from jax import lax
from jax.experimental import pallas as pl
from jax.experimental.pallas import tpu as pltpu
from jax.sharding import PartitionSpec as P

masked_score = -1e30
vmem_bytes = 56 * 1024 * 1024
f32 = jnp.float32
bf16 = jnp.bfloat16


def dot_nt(left, right):
    return lax.dot_general(left, right, (((1,), (1,)), ((), ())), preferred_element_type=f32)


def dot_nn(left, right):
    return lax.dot_general(left, right, (((1,), (0,)), ((), ())), preferred_element_type=f32)


def fold_rows(values, op):
    rows, columns = values.shape
    return op(values.reshape(rows // 8, 8, columns), axis=0)


def head_kernel(dp_size, heads_size, kv_index, kv_local, width, block_tokens, chunk, *refs):
    last = kv_index == kv_local - 1
    q_ref, g_ref, sk_ref, sv_ref, ck_ref, cv_ref, seg_ref = refs[:7]
    refs = refs[7:]
    held = kv_index if last else 0
    dq_before, self_before, refs = refs[:held], refs[held : 2 * held], refs[2 * held :]
    cart_outs, refs = refs[:dp_size], refs[dp_size:]
    dq_count = heads_size if last else 1
    dq_outs, self_ref, refs = refs[:dq_count], refs[dq_count], refs[dq_count + 1 :]
    (
        wide_ref, keys_ref, vals_ref, keys_t_ref, s_ref, w_ref, d_ref, dk_ref, dv_ref, out_ref, dq_ref,
        q_in, g_in, sk_in, sv_in, ck_in, cv_in, sems,
    ) = refs
    head_dim = q_ref.shape[1]
    tokens = seg_ref.shape[1]
    cart_rows = ck_ref.shape[0] // kv_local
    all_keys = cart_rows + tokens
    rows = block_tokens * width
    scale = head_dim ** -0.5
    scale2 = scale * math.log2(math.e)
    span = block_tokens * kv_local * width
    blocks = tokens // block_tokens

    def block_copy(source, target, block, sem):
        at = slice(block * span, (block + 1) * span)
        return pltpu.make_async_copy(source.at[at, :], target.at[at, :], sems.at[sem])

    copies = {
        name: pltpu.make_async_copy(source, target, sems.at[at])
        for at, (name, source, target) in enumerate(
            [("ck", ck_ref, ck_in), ("sk", sk_ref, sk_in), ("cv", cv_ref, cv_in), ("sv", sv_ref, sv_in)]
        )
    }
    for block in range(blocks):
        copies["q", block] = block_copy(q_ref, q_in, block, 4 + block)
        copies["g", block] = block_copy(g_ref, g_in, block, 4 + blocks + block)
    order = ["ck", "sk", ("q", 0), "cv", "sv", ("g", 0)]
    order += [(kind, block) for block in range(1, blocks) for kind in ("q", "g")]
    for name in order:
        copies[name].start()

    def pick(name, ref, dst, at):
        copies[name].wait()
        count = ref.shape[0] // kv_local
        if kv_local == 1:
            dst[at : at + count, :] = ref[...]
        else:
            wide_ref[0 : ref.shape[0], :] = ref[...].astype(f32)
            dst[at : at + count, :] = wide_ref[pl.ds(kv_index, count, stride=kv_local), :].astype(bf16)

    def rows_of(name, ref, block):
        copies[name, block].wait()
        wide = ref[block * span : (block + 1) * span, :]
        if kv_local == 1:
            return wide
        wide = wide.astype(f32).reshape(block_tokens, kv_local, width, head_dim)
        return wide[:, kv_index].reshape(rows, head_dim).astype(bf16)

    first_count = jnp.sum((seg_ref[...] == 0).astype(f32), axis=1, keepdims=True).astype(jnp.int32)

    def limit(block):
        return -(-(block + 1) * block_tokens // chunk) * chunk

    def starts_of(block):
        return range(0, cart_rows + limit(block), chunk)

    queries, grads, peaks, stats = {}, {}, {}, {}
    acc = {}

    def open_scores(block):
        queries[block] = rows_of("q", q_in, block)
        token = (lax.broadcasted_iota(jnp.int32, (1, rows), 1) + block * rows) // width
        begin = jnp.where(token >= first_count, first_count, 0)
        acc["peak"] = jnp.full((8, rows), masked_score, f32)
        acc["token"], acc["begin"] = token, begin

    def step_scores(block, start):
        score = dot_nt(keys_ref[start : start + chunk, :], queries[block])
        if start >= cart_rows:
            key_at = lax.broadcasted_iota(jnp.int32, (chunk, rows), 0) + (start - cart_rows)
            score = jnp.where((key_at >= acc["begin"]) & (key_at <= acc["token"]), score, masked_score)
        s_ref[block % 2, start : start + chunk, :] = score
        acc["peak"] = jnp.maximum(acc["peak"], fold_rows(score, jnp.max))

    def close_scores(block):
        peaks[block] = jnp.max(acc["peak"], axis=0, keepdims=True)

    def open_weights(block):
        grads[block] = rows_of("g", g_in, block)
        acc["total"] = jnp.zeros((8, rows), f32)
        acc["center"] = jnp.zeros((8, rows), f32)

    def step_weights(block, start):
        at = slice(start, start + chunk)
        weight = jnp.exp2((s_ref[block % 2, at, :] - peaks[block]) * scale2)
        dprob = dot_nt(vals_ref[at, :], grads[block])
        w_ref[block % 2, at, :] = weight
        d_ref[block % 2, at, :] = dprob
        acc["total"] = acc["total"] + fold_rows(weight, jnp.sum)
        acc["center"] = acc["center"] + fold_rows(weight * dprob, jnp.sum)

    def close_weights(block):
        share = 1.0 / jnp.sum(acc["total"], axis=0, keepdims=True)
        stats[block] = share, jnp.sum(acc["center"], axis=0, keepdims=True) * share

    def open_grads(block):
        acc["dq"] = jnp.zeros((head_dim, rows), f32)

    def step_grads(block, start):
        at = slice(start, start + chunk)
        share, center = stats[block]
        prob = w_ref[block % 2, at, :] * share
        dscore = (prob * (d_ref[block % 2, at, :] - center)).astype(bf16)
        dv = dot_nn(prob.astype(bf16), grads[block])
        dk = dot_nn(dscore, queries[block])
        if block == 0 or start >= cart_rows + limit(block - 1):
            dv_ref[at, :] = dv
            dk_ref[at, :] = dk
        else:
            dv_ref[at, :] += dv
            dk_ref[at, :] += dk
        acc["dq"] = acc["dq"] + dot_nn(keys_t_ref[:, at], dscore)

    def close_grads(block):
        out_ref[...] = (acc["dq"] * scale).T
        for head in range(width):
            dq_ref[block * block_tokens : (block + 1) * block_tokens, head * head_dim : (head + 1) * head_dim] = (
                out_ref[pl.ds(head, block_tokens, stride=width), :].astype(bf16)
            )

    pick("ck", ck_in, keys_ref, 0)
    pick("sk", sk_in, keys_ref, cart_rows)
    stages = (
        (2, open_grads, step_grads, close_grads),
        (1, open_weights, step_weights, close_weights),
        (0, open_scores, step_scores, close_scores),
    )
    for turn in range(blocks + 2):
        live = [(turn - lag, *calls) for lag, *calls in stages if 0 <= turn - lag < blocks]
        if turn == 1:
            pick("cv", cv_in, vals_ref, 0)
            pick("sv", sv_in, vals_ref, cart_rows)
            keys_t_ref[...] = keys_ref[...].astype(f32).T.astype(bf16)
        for block, begin_call, _, _ in live:
            begin_call(block)
        for start in range(0, all_keys, chunk):
            for block, _, step_call, _ in live:
                if start in starts_of(block):
                    step_call(block, start)
        for block, _, _, end_call in live:
            end_call(block)

    part_rows = cart_rows // dp_size
    me = lax.axis_index("dp")
    for step, ref in enumerate(cart_outs):
        target = lax.rem(me + step, dp_size)
        at = pl.ds(pl.multiple_of(target * part_rows, part_rows), part_rows)
        ref[0] = (dk_ref[at, :] * scale).astype(ref.dtype)
        ref[1] = dv_ref[at, :].astype(ref.dtype)
    own = dk_ref[cart_rows:all_keys, :] * scale, dv_ref[cart_rows:all_keys, :]
    if not last:
        dq_outs[0][...] = dq_ref[...]
        self_ref[0], self_ref[1] = own
        return
    own_tokens = tokens // heads_size
    columns = width * head_dim
    me = lax.axis_index("heads")
    for step, ref in enumerate(dq_outs):
        target = lax.rem(me + step, heads_size)
        at = pl.ds(pl.multiple_of(target * own_tokens, own_tokens), own_tokens)
        for index, before in enumerate((*dq_before, dq_ref)):
            ref[:, index * columns : (index + 1) * columns] = before[at, :]
    count = tokens * kv_local
    for kind in range(2):
        for index, before in enumerate(self_before):
            wide_ref[pl.ds(index, tokens, stride=kv_local), :] = before[kind]
        wide_ref[pl.ds(kv_index, tokens, stride=kv_local), :] = own[kind]
        self_ref[kind * count : (kind + 1) * count, :] = wide_ref[0:count, :].astype(bf16)


def cart_kernel(kv_local, *refs):
    part_refs, out_ref = refs[:-2], refs[-1]
    count = len(part_refs) // kv_local
    part_rows = part_refs[0].shape[1]
    for kv_index in range(kv_local):
        for kind in range(2):
            total = part_refs[kv_index * count][kind]
            for part in range(1, count):
                total = total + part_refs[kv_index * count + part][kind].astype(f32)
            out_ref[pl.ds(kind * kv_local + kv_index, part_rows, stride=2 * kv_local), :] = total


def place_kernel(*refs):
    part_refs, out_ref = refs[:-1], refs[-1]
    count = len(part_refs)
    columns = part_refs[0].shape[1]
    me = lax.axis_index("heads")
    for step, ref in enumerate(part_refs):
        source = lax.rem(me + count - step, count)
        out_ref[:, pl.ds(pl.multiple_of(source * columns, columns), columns)] = ref[...]


def shift(values, axis, size, step):
    if step == 0:
        return values
    return lax.ppermute(values, axis, [(source, (source + step) % size) for source in range(size)])


def on_device(dp_size, heads_size, queries, out_grad, self_keys, self_values, cart_keys, cart_values, segment_ids):
    tokens, heads_local, head_dim = queries.shape
    kv_local = self_keys.shape[1]
    cart_rows = cart_keys.shape[0]
    width = heads_local // kv_local
    block_tokens = 64
    chunk = 128
    all_keys = cart_rows + tokens
    rows = block_tokens * width
    part_rows = cart_rows // dp_size
    own_tokens = tokens // heads_size
    flat = [array.reshape(-1, head_dim) for array in (queries, out_grad, self_keys, self_values, cart_keys, cart_values)]
    macs = tokens * width * all_keys * head_dim * 5
    blocks = tokens // block_tokens
    columns = width * head_dim
    count = tokens * kv_local
    cart_list, query_list, self_list = [], [], []
    for kv_index in range(kv_local):
        last = kv_index == kv_local - 1
        if last:
            other_shapes = [jax.ShapeDtypeStruct((own_tokens, kv_local * columns), bf16) for _ in range(heads_size)]
            other_shapes.append(jax.ShapeDtypeStruct((2 * count, head_dim), bf16))
        else:
            other_shapes = [
                jax.ShapeDtypeStruct((tokens, columns), bf16),
                jax.ShapeDtypeStruct((2, tokens, head_dim), f32),
            ]
        before = query_list + self_list
        outs = pl.pallas_call(
            functools.partial(head_kernel, dp_size, heads_size, kv_index, kv_local, width, block_tokens, chunk),
            out_shape=(
                *[
                    jax.ShapeDtypeStruct((2, part_rows, head_dim), bf16 if step else f32)
                    for step in range(dp_size)
                ],
                *other_shapes,
            ),
            in_specs=[pl.BlockSpec(memory_space=pl.ANY)] * 6
            + [pl.BlockSpec(memory_space=pltpu.VMEM)] * (1 + (len(before) if last else 0)),
            scratch_shapes=[
                pltpu.VMEM((cart_rows * kv_local, head_dim), f32),
                pltpu.VMEM((all_keys, head_dim), bf16),
                pltpu.VMEM((all_keys, head_dim), bf16),
                pltpu.VMEM((head_dim, all_keys), bf16),
                pltpu.VMEM((2, all_keys, rows), f32),
                pltpu.VMEM((2, all_keys, rows), f32),
                pltpu.VMEM((2, all_keys, rows), f32),
                pltpu.VMEM((all_keys, head_dim), f32),
                pltpu.VMEM((all_keys, head_dim), f32),
                pltpu.VMEM((rows, head_dim), f32),
                pltpu.VMEM((tokens, columns), bf16),
                *[pltpu.VMEM(array.shape, bf16) for array in flat],
                pltpu.SemaphoreType.DMA((4 + 2 * blocks,)),
            ],
            compiler_params=pltpu.CompilerParams(vmem_limit_bytes=vmem_bytes),
            cost_estimate=pl.CostEstimate(flops=4 * macs, bytes_accessed=5 * 2**20, transcendentals=tokens * width * all_keys),
            name="head_grads",
        )(*flat, segment_ids, *(before if last else []))
        cart_list += [shift(outs[step], "dp", dp_size, step) for step in range(dp_size)]
        if last:
            query_list, self_grads = outs[dp_size:-1], outs[-1]
        else:
            query_list.append(outs[-2])
            self_list.append(outs[-1])
    query_list = [shift(part, "heads", heads_size, step) for step, part in enumerate(query_list)]
    query_grads = pl.pallas_call(
        place_kernel,
        out_shape=jax.ShapeDtypeStruct((own_tokens, heads_size * heads_local * head_dim), bf16),
        compiler_params=pltpu.CompilerParams(vmem_limit_bytes=vmem_bytes),
        cost_estimate=pl.CostEstimate(flops=2**20, bytes_accessed=2 * 2**20, transcendentals=0),
        name="place_queries",
    )(*query_list)
    cart_grads = pl.pallas_call(
        functools.partial(cart_kernel, kv_local),
        out_shape=jax.ShapeDtypeStruct((part_rows * 2 * kv_local, head_dim), f32),
        in_specs=[pl.BlockSpec(memory_space=pltpu.VMEM)] * len(cart_list) + [pl.BlockSpec(memory_space=pl.ANY)],
        compiler_params=pltpu.CompilerParams(vmem_limit_bytes=vmem_bytes),
        cost_estimate=pl.CostEstimate(flops=2**20, bytes_accessed=2 * 2**20, transcendentals=0),
        name="cart_sum",
    )(*cart_list, query_grads)
    cart_grads = cart_grads.reshape(part_rows, 2, kv_local, head_dim)
    self_grads = self_grads.reshape(2, tokens, kv_local, head_dim)
    return (cart_grads, self_grads, query_grads)


def solution(mesh):
    in_specs = (
        P(("groups", "dp"), "heads", None),
        P(("groups", "dp"), "heads", None),
        P(("groups", "dp"), "heads", None),
        P(("groups", "dp"), "heads", None),
        P("groups", "heads", None),
        P("groups", "heads", None),
        P(("groups", "dp"), None),
    )
    out_specs = (
        P(("groups", "dp"), None, "heads", None),
        P(None, ("groups", "dp"), "heads", None),
        P(("groups", "dp", "heads"), None),
    )
    return jax.shard_map(
        functools.partial(on_device, mesh.shape["dp"], mesh.shape["heads"]),
        mesh=mesh, in_specs=in_specs, out_specs=out_specs, check_vma=False,
    )
```

time: 57.1 us -> 56.9 us (level); the launches traced: 56.2 us -> 56.7 us
  waiting for transfers between devices: 6.39 us -> 9.89 us
  Pallas kernels: 30.5 us -> 28.5 us
  local copies, waits for them, and re-layouts: 1.79 us -> 0.73 us
  starting transfers between devices: 15.9 us -> 16.9 us
  other arithmetic: 0.93 us -> 0 us
    ppermute x12 -> x9, waiting for transfers between devices: 6.39 us -> 9.89 us  [shift(): lax.ppermute(values, axis, [(source, (source + step) % size) for source i...]
    pallas_call x2, Pallas kernels: 25.9 us -> 24 us  [on_device(): pl.pallas_call(functools.partial(head_kernel, dp_size, heads_size, kv_ind...]
    unnamed x31 -> x24, local copies, waits for them, and re-layouts: 1.79 us -> 0.73 us
    ppermute x12 -> x9, starting transfers between devices: 15.9 us -> 16.9 us  [shift(): lax.ppermute(values, axis, [(source, (source + step) % size) for source i...]
    another operation x1 -> x0, other arithmetic: 0.93 us -> none  [on_device(): self_grads = jnp.stack(self_list, axis=2)]
  transfers between devices with their start and end apart: 12 -> 9, of which waited for: 2 -> 3; matrix products, arithmetic and copies ran while one was open for 3% -> 0% of each run, Pallas kernels for 27% -> 4%
where the time goes in v2:
time: 56.9 us; the launch traced here: 56.7 us
  Pallas kernels  28.5 us (50%)
  starting transfers between devices  16.9 us (30%)
  waiting for transfers between devices  9.89 us (17%)
  local copies, waits for them, and re-layouts  0.73 us (1%)
  between operations  0.73 us (1%)
    pallas_call x2, Pallas kernels, on_device(): pl.pallas_call(functools.partial(head_kernel, dp_size, heads_size, kv_ind...  24 us
    ppermute x9, starting transfers between devices, shift(): lax.ppermute(values, axis, [(source, (source + step) % size) for source i...  16.9 us
    ppermute x9, waiting for transfers between devices, shift(): lax.ppermute(values, axis, [(source, (source + step) % size) for source i...  9.89 us
    pallas_call x1, Pallas kernels, on_device(): pl.pallas_call(place_kernel, out_shape=jax.ShapeDtypeStruct((own_tokens,...  2.24 us
    pallas_call x1, Pallas kernels, on_device(): pl.pallas_call(functools.partial(cart_kernel, kv_local), out_shape=jax.Sh...  2.23 us
  transfers between devices with their start and end apart: 9, of which 3 were waited for; matrix products, arithmetic and copies ran while one was open for 0% of the time, Pallas kernels for 4%

profile of v2, /device:TPU:0, one launch (start us, length us, event | category | flops | bytes accessed | tf_op | source)
XLA Modules:
  0.0 56.7 jit_solution(12743625666196963867)
XLA Ops:
  0.6 11.5 %head_grads.2 = (f32[2,256,128]{2,1,0:T(8,128)}, bf16[2,256,128]{2,1,0:T(8,128)(2,1)}, bf16[2,256,128]{2,1,0:T(8,128)(2,1)}, bf16[2,256,128]{2,1,0:T(8,128)(2,1)...) custom-call(bf16[4096,128]{1,0:T(8,128)(2,1)} %bitcast.9, bf16[4096,128]{1,0:T(8,128)(2,1)} %bitcast.11, ...), custom_call_target="tpu_custom_call" | custom-call | flops 6710886400 | bytes 5242880 | tf_op jit(solution)/shard_map/head_grads/pallas_call | solution.py:266
  12.2 0.0 copy-start.11
  12.2 0.0 copy-start.10
  12.2 0.0 copy-start.9
  12.2 12.5 %head_grads.3 = (f32[2,256,128]{2,1,0:T(8,128)}, bf16[2,256,128]{2,1,0:T(8,128)(2,1)}, bf16[2,256,128]{2,1,0:T(8,128)(2,1)}, bf16[2,256,128]{2,1,0:T(8,128)(2,1)...) custom-call(bf16[4096,128]{1,0:T(8,128)(2,1)} %bitcast.10, ...), custom_call_target="tpu_custom_call" | custom-call | flops 6710886400 | bytes 5242880 | tf_op jit(solution)/shard_map/head_grads/pallas_call | solution.py:266
  24.7 0.5 collective-permute-start.6
  25.1 2.6 %collective-permute-start.7 = (bf16[64,2048]{1,0:T(8,128)(2,1)}, bf16[64,2048]{1,0:T(8,128)(2,1)S(1)}, u32[]{:S(2)}, u32[]{:S(2)}) collective-permute-start(bf16[64,2048]{1,0:T(8,128)(2,1)} %get-tuple-element.30), channel_id=1, source_target_pairs={{0,2},{1,3},{2,0},{3,1},{4,6},{5,7},{6,4},{7,5},{8,10},{9,11},{10,... | collective-permute-start | bytes 786440 | tf_op jit(solution)/shard_map/ppermute | solution.py:235
  27.7 1.4 %collective-permute-start.8 = (bf16[64,2048]{1,0:T(8,128)(2,1)}, bf16[64,2048]{1,0:T(8,128)(2,1)S(1)}, u32[]{:S(2)}, u32[]{:S(2)}) collective-permute-start(bf16[64,2048]{1,0:T(8,128)(2,1)} %get-tuple-element.31), channel_id=1, source_target_pairs={{0,3},{1,0},{2,1},{3,2},{4,7},{5,4},{6,5},{7,6},{8,11},{9,8},{10,9... | collective-permute-start | bytes 786440 | tf_op jit(solution)/shard_map/ppermute | solution.py:235
  29.1 0.0 copy-done.11
  29.1 1.6 %collective-permute-start = (bf16[2,256,128]{2,1,0:T(8,128)(2,1)S(1)}, bf16[2,256,128]{2,1,0:T(8,128)(2,1)S(1)}, u32[]{:S(2)}, u32[]{:S(2)}) collective-permute-start(bf16[2,256,128]{2,1,0:T(8,128)(2,1)S(1)} %copy-done.11), channel_id=1, source_target_pairs={{0,4},{4,8},{8,12},{12,0},{1,5},{5,9},{9,13},{13,1},{2,6},{6,10},{... | collective-permute-start | bytes 393224 | tf_op jit(solution)/shard_map/ppermute | solution.py:235
  30.7 0.0 copy-done.10
  30.7 2.6 %collective-permute-start.1 = (bf16[2,256,128]{2,1,0:T(8,128)(2,1)S(1)}, bf16[2,256,128]{2,1,0:T(8,128)(2,1)S(1)}, u32[]{:S(2)}, u32[]{:S(2)}) collective-permute-start(bf16[2,256,128]{2,1,0:T(8,128)(2,1)S(1)} %copy-done.10), channel_id=1, source_target_pairs={{0,8},{4,12},{8,0},{12,4},{1,9},{5,13},{9,1},{13,5},{2,10},{6,14},... | collective-permute-start | bytes 393224 | tf_op jit(solution)/shard_map/ppermute | solution.py:235
  33.3 3.8 %collective-permute-done.refs_1_ = bf16[2,256,128]{2,1,0:T(8,128)(2,1)S(1)} collective-permute-done((bf16[2,256,128]{2,1,0:T(8,128)(2,1)S(1)}, bf16[2,256,128]{2,1,0:T(8,128)(2,1)S(1)}, u32[]{:S(2)}, u32[]{:S(2)}) %collective-permute-start) | collective-permute-done | bytes 131104 | tf_op jit(solution)/shard_map/ppermute | solution.py:235
  37.1 0.0 copy-done.9
  37.1 1.3 %collective-permute-start.2 = (bf16[2,256,128]{2,1,0:T(8,128)(2,1)S(1)}, bf16[2,256,128]{2,1,0:T(8,128)(2,1)S(1)}, u32[]{:S(2)}, u32[]{:S(2)}) collective-permute-start(bf16[2,256,128]{2,1,0:T(8,128)(2,1)S(1)} %copy-done.9), channel_id=1, source_target_pairs={{0,12},{4,0},{8,4},{12,8},{1,13},{5,1},{9,5},{13,9},{2,14},{6,2},{... | collective-permute-start | bytes 393224 | tf_op jit(solution)/shard_map/ppermute | solution.py:235
  38.4 0.0 collective-permute-done.6.refs_1_
  38.4 2.0 %collective-permute-start.3 = (bf16[2,256,128]{2,1,0:T(8,128)(2,1)}, bf16[2,256,128]{2,1,0:T(8,128)(2,1)S(1)}, u32[]{:S(2)}, u32[]{:S(2)}) collective-permute-start(bf16[2,256,128]{2,1,0:T(8,128)(2,1)} %get-tuple-element.25), channel_id=1, source_target_pairs={{0,4},{4,8},{8,12},{12,0},{1,5},{5,9},{9,13},{13,1},{2,6},{6,10},{... | collective-permute-start | bytes 393224 | tf_op jit(solution)/shard_map/ppermute | solution.py:235
  40.4 0.0 collective-permute-done.7.refs_2_
  40.4 4.0 %collective-permute-start.4 = (bf16[2,256,128]{2,1,0:T(8,128)(2,1)}, bf16[2,256,128]{2,1,0:T(8,128)(2,1)S(1)}, u32[]{:S(2)}, u32[]{:S(2)}) collective-permute-start(bf16[2,256,128]{2,1,0:T(8,128)(2,1)} %get-tuple-element.26), channel_id=1, source_target_pairs={{0,8},{4,12},{8,0},{12,4},{1,9},{5,13},{9,1},{13,5},{2,10},{6,14},... | collective-permute-start | bytes 393224 | tf_op jit(solution)/shard_map/ppermute | solution.py:235
  44.4 0.0 collective-permute-done.8.refs_3_
  44.4 1.0 %collective-permute-start.5 = (bf16[2,256,128]{2,1,0:T(8,128)(2,1)}, bf16[2,256,128]{2,1,0:T(8,128)(2,1)S(1)}, u32[]{:S(2)}, u32[]{:S(2)}) collective-permute-start(bf16[2,256,128]{2,1,0:T(8,128)(2,1)} %get-tuple-element.27), channel_id=1, source_target_pairs={{0,12},{4,0},{8,4},{12,8},{1,13},{5,1},{9,5},{13,9},{2,14},{6,2},{... | collective-permute-start | bytes 393224 | tf_op jit(solution)/shard_map/ppermute | solution.py:235
  45.4 0.0 copy-done.1
  45.4 2.2 %place_queries.1.refs_8_ = bf16[64,8192]{1,0:T(8,128)(2,1)} custom-call(bf16[64,2048]{1,0:T(8,128)(2,1)} %get-tuple-element.28.refs_0_, bf16[64,2048]{1,0:T(8,128)(2,1)} %copy-done, bf16[64,2048]{1,0:T(8,128)(2,1)} %copy-done.1, bf16[64,2048]{1,0:T(8,128)(2,1)} %copy-done.2), custom_call_target="tpu_custom_call" | custom-call | flops 1048576 | bytes 2097152 | tf_op jit(solution)/shard_map/place_queries/pallas_call | solution.py:303
  47.6 0.0 collective-permute-done.1.refs_2_
  47.6 0.0 collective-permute-done.2.refs_3_
  47.7 2.9 %collective-permute-done.3.refs_5_ = bf16[2,256,128]{2,1,0:T(8,128)(2,1)S(1)} collective-permute-done((bf16[2,256,128]{2,1,0:T(8,128)(2,1)}, bf16[2,256,128]{2,1,0:T(8,128)(2,1)S(1)}, u32[]{:S(2)}, u32[]{:S(2)}) %collective-permute-start.3) | collective-permute-done | bytes 131104 | tf_op jit(solution)/shard_map/ppermute | solution.py:235
  50.6 3.2 %collective-permute-done.4.refs_6_ = bf16[2,256,128]{2,1,0:T(8,128)(2,1)S(1)} collective-permute-done((bf16[2,256,128]{2,1,0:T(8,128)(2,1)}, bf16[2,256,128]{2,1,0:T(8,128)(2,1)S(1)}, u32[]{:S(2)}, u32[]{:S(2)}) %collective-permute-start.4) | collective-permute-done | bytes 131104 | tf_op jit(solution)/shard_map/ppermute | solution.py:235
  53.8 0.0 collective-permute-done.5.refs_7_
  53.8 0.0 copy-done.4
  53.8 0.6 %copy-done.7 = bf16[2,256,128]{2,1,0:T(8,128)(2,1)} copy-done((bf16[2,256,128]{2,1,0:T(8,128)(2,1)}, bf16[2,256,128]{2,1,0:T(8,128)(2,1)S(1)}, u32[]{:S(2)}) %copy-start.7) | copy-done | bytes 131096
  54.4 0.1 copy-done.8
  54.5 2.2 %cart_sum.1 = f32[1024,128]{1,0:T(8,128)} custom-call(f32[2,256,128]{2,1,0:T(8,128)} %get-tuple-element.18.refs_0_, bf16[2,256,128]{2,1,0:T(8,128)(2,1)} %copy-done.3, bf16[2,256,128]{2,1,0:T(8,128)(2,1)} %copy-done.4, bf16[2,256,128]{2,1,0:T(8,128)(2,1)} %copy-done.5, f32[2,256,128]{2,1,0:T(8,128)} %get-tuple-element.24.refs_4_, ...), custom_call_target="tpu_custom_call" | custom-call | flops 1048576 | bytes 2097152 | tf_op jit(solution)/shard_map/cart_sum/pallas_call | solution.py:310
  (14 shorter events, 0.0 us)
Async XLA Ops:
  12.2 17.0 %copy-start.11 = (bf16[2,256,128]{2,1,0:T(8,128)(2,1)S(1)}, bf16[2,256,128]{2,1,0:T(8,128)(2,1)}, u32[]{:S(2)}) copy-start(bf16[2,256,128]{2,1,0:T(8,128)(2,1)} %get-tuple-element.19) | copy-start | bytes 393220
  12.2 18.5 %copy-start.10 = (bf16[2,256,128]{2,1,0:T(8,128)(2,1)S(1)}, bf16[2,256,128]{2,1,0:T(8,128)(2,1)}, u32[]{:S(2)}) copy-start(bf16[2,256,128]{2,1,0:T(8,128)(2,1)} %get-tuple-element.20) | copy-start | bytes 393220
  12.2 24.9 %copy-start.9 = (bf16[2,256,128]{2,1,0:T(8,128)(2,1)S(1)}, bf16[2,256,128]{2,1,0:T(8,128)(2,1)}, u32[]{:S(2)}) copy-start(bf16[2,256,128]{2,1,0:T(8,128)(2,1)} %get-tuple-element.21) | copy-start | bytes 393220
  24.7 13.7 %collective-permute-start.6 = (bf16[64,2048]{1,0:T(8,128)(2,1)}, bf16[64,2048]{1,0:T(8,128)(2,1)S(1)}, u32[]{:S(2)}, u32[]{:S(2)}) collective-permute-start(bf16[64,2048]{1,0:T(8,128)(2,1)} %get-tuple-element.29), channel_id=1, source_target_pairs={{0,1},{1,2},{2,3},{3,0},{4,5},{5,6},{6,7},{7,4},{8,9},{9,10},{10,1... | collective-permute-start | bytes 786440 | tf_op jit(solution)/shard_map/ppermute | solution.py:235
  25.1 15.2 %collective-permute-start.7 = (bf16[64,2048]{1,0:T(8,128)(2,1)}, bf16[64,2048]{1,0:T(8,128)(2,1)S(1)}, u32[]{:S(2)}, u32[]{:S(2)}) collective-permute-start(bf16[64,2048]{1,0:T(8,128)(2,1)} %get-tuple-element.30), channel_id=1, source_target_pairs={{0,2},{1,3},{2,0},{3,1},{4,6},{5,7},{6,4},{7,5},{8,10},{9,11},{10,... | collective-permute-start | bytes 786440 | tf_op jit(solution)/shard_map/ppermute | solution.py:235
  27.7 16.7 %collective-permute-start.8 = (bf16[64,2048]{1,0:T(8,128)(2,1)}, bf16[64,2048]{1,0:T(8,128)(2,1)S(1)}, u32[]{:S(2)}, u32[]{:S(2)}) collective-permute-start(bf16[64,2048]{1,0:T(8,128)(2,1)} %get-tuple-element.31), channel_id=1, source_target_pairs={{0,3},{1,0},{2,1},{3,2},{4,7},{5,4},{6,5},{7,6},{8,11},{9,8},{10,9... | collective-permute-start | bytes 786440 | tf_op jit(solution)/shard_map/ppermute | solution.py:235
  29.1 8.0 %collective-permute-start = (bf16[2,256,128]{2,1,0:T(8,128)(2,1)S(1)}, bf16[2,256,128]{2,1,0:T(8,128)(2,1)S(1)}, u32[]{:S(2)}, u32[]{:S(2)}) collective-permute-start(bf16[2,256,128]{2,1,0:T(8,128)(2,1)S(1)} %copy-done.11), channel_id=1, source_target_pairs={{0,4},{4,8},{8,12},{12,0},{1,5},{5,9},{9,13},{13,1},{2,6},{6,10},{... | collective-permute-start | bytes 393224 | tf_op jit(solution)/shard_map/ppermute | solution.py:235
  30.7 16.9 %collective-permute-start.1 = (bf16[2,256,128]{2,1,0:T(8,128)(2,1)S(1)}, bf16[2,256,128]{2,1,0:T(8,128)(2,1)S(1)}, u32[]{:S(2)}, u32[]{:S(2)}) collective-permute-start(bf16[2,256,128]{2,1,0:T(8,128)(2,1)S(1)} %copy-done.10), channel_id=1, source_target_pairs={{0,8},{4,12},{8,0},{12,4},{1,9},{5,13},{9,1},{13,5},{2,10},{6,14},... | collective-permute-start | bytes 393224 | tf_op jit(solution)/shard_map/ppermute | solution.py:235
  37.1 10.6 %copy-start.3 = (bf16[2,256,128]{2,1,0:T(8,128)(2,1)}, bf16[2,256,128]{2,1,0:T(8,128)(2,1)S(1)}, u32[]{:S(2)}) copy-start(bf16[2,256,128]{2,1,0:T(8,128)(2,1)S(1)} %collective-permute-done.refs_1_) | copy-start | bytes 393220
  37.1 10.6 %collective-permute-start.2 = (bf16[2,256,128]{2,1,0:T(8,128)(2,1)S(1)}, bf16[2,256,128]{2,1,0:T(8,128)(2,1)S(1)}, u32[]{:S(2)}, u32[]{:S(2)}) collective-permute-start(bf16[2,256,128]{2,1,0:T(8,128)(2,1)S(1)} %copy-done.9), channel_id=1, source_target_pairs={{0,12},{4,0},{8,4},{12,8},{1,13},{5,1},{9,5},{13,9},{2,14},{6,2},{... | collective-permute-start | bytes 393224 | tf_op jit(solution)/shard_map/ppermute | solution.py:235
  38.4 7.0 %copy-start = (bf16[64,2048]{1,0:T(8,128)(2,1)}, bf16[64,2048]{1,0:T(8,128)(2,1)S(1)}, u32[]{:S(2)}) copy-start(bf16[64,2048]{1,0:T(8,128)(2,1)S(1)} %collective-permute-done.6.refs_1_) | copy-start | bytes 786436
  38.4 12.2 %collective-permute-start.3 = (bf16[2,256,128]{2,1,0:T(8,128)(2,1)}, bf16[2,256,128]{2,1,0:T(8,128)(2,1)S(1)}, u32[]{:S(2)}, u32[]{:S(2)}) collective-permute-start(bf16[2,256,128]{2,1,0:T(8,128)(2,1)} %get-tuple-element.25), channel_id=1, source_target_pairs={{0,4},{4,8},{8,12},{12,0},{1,5},{5,9},{9,13},{13,1},{2,6},{6,10},{... | collective-permute-start | bytes 393224 | tf_op jit(solution)/shard_map/ppermute | solution.py:235
  40.4 5.0 %copy-start.1 = (bf16[64,2048]{1,0:T(8,128)(2,1)}, bf16[64,2048]{1,0:T(8,128)(2,1)S(1)}, u32[]{:S(2)}) copy-start(bf16[64,2048]{1,0:T(8,128)(2,1)S(1)} %collective-permute-done.7.refs_2_) | copy-start | bytes 786436
  40.4 13.4 %collective-permute-start.4 = (bf16[2,256,128]{2,1,0:T(8,128)(2,1)}, bf16[2,256,128]{2,1,0:T(8,128)(2,1)S(1)}, u32[]{:S(2)}, u32[]{:S(2)}) collective-permute-start(bf16[2,256,128]{2,1,0:T(8,128)(2,1)} %get-tuple-element.26), channel_id=1, source_target_pairs={{0,8},{4,12},{8,0},{12,4},{1,9},{5,13},{9,1},{13,5},{2,10},{6,14},... | collective-permute-start | bytes 393224 | tf_op jit(solution)/shard_map/ppermute | solution.py:235
  44.4 1.0 %copy-start.2 = (bf16[64,2048]{1,0:T(8,128)(2,1)}, bf16[64,2048]{1,0:T(8,128)(2,1)S(1)}, u32[]{:S(2)}) copy-start(bf16[64,2048]{1,0:T(8,128)(2,1)S(1)} %collective-permute-done.8.refs_3_) | copy-start | bytes 786436
  44.4 9.4 %collective-permute-start.5 = (bf16[2,256,128]{2,1,0:T(8,128)(2,1)}, bf16[2,256,128]{2,1,0:T(8,128)(2,1)S(1)}, u32[]{:S(2)}, u32[]{:S(2)}) collective-permute-start(bf16[2,256,128]{2,1,0:T(8,128)(2,1)} %get-tuple-element.27), channel_id=1, source_target_pairs={{0,12},{4,0},{8,4},{12,8},{1,13},{5,1},{9,5},{13,9},{2,14},{6,2},{... | collective-permute-start | bytes 393224 | tf_op jit(solution)/shard_map/ppermute | solution.py:235
  47.6 6.2 %copy-start.4 = (bf16[2,256,128]{2,1,0:T(8,128)(2,1)}, bf16[2,256,128]{2,1,0:T(8,128)(2,1)S(1)}, u32[]{:S(2)}) copy-start(bf16[2,256,128]{2,1,0:T(8,128)(2,1)S(1)} %collective-permute-done.1.refs_2_) | copy-start | bytes 393220
  47.6 6.1 %copy-start.5 = (bf16[2,256,128]{2,1,0:T(8,128)(2,1)}, bf16[2,256,128]{2,1,0:T(8,128)(2,1)S(1)}, u32[]{:S(2)}) copy-start(bf16[2,256,128]{2,1,0:T(8,128)(2,1)S(1)} %collective-permute-done.2.refs_3_) | copy-start | bytes 393220
  50.6 3.2 %copy-start.6 = (bf16[2,256,128]{2,1,0:T(8,128)(2,1)}, bf16[2,256,128]{2,1,0:T(8,128)(2,1)S(1)}, u32[]{:S(2)}) copy-start(bf16[2,256,128]{2,1,0:T(8,128)(2,1)S(1)} %collective-permute-done.3.refs_5_) | copy-start | bytes 393220
  53.8 0.7 %copy-start.7 = (bf16[2,256,128]{2,1,0:T(8,128)(2,1)}, bf16[2,256,128]{2,1,0:T(8,128)(2,1)S(1)}, u32[]{:S(2)}) copy-start(bf16[2,256,128]{2,1,0:T(8,128)(2,1)S(1)} %collective-permute-done.4.refs_6_) | copy-start | bytes 393220
  53.8 0.7 %copy-start.8 = (bf16[2,256,128]{2,1,0:T(8,128)(2,1)}, bf16[2,256,128]{2,1,0:T(8,128)(2,1)S(1)}, u32[]{:S(2)}) copy-start(bf16[2,256,128]{2,1,0:T(8,128)(2,1)S(1)} %collective-permute-done.5.refs_7_) | copy-start | bytes 393220

commit v3 on v2

--- a/solution.py
+++ b/solution.py
@@ -22,12 +22,16 @@
     return lax.dot_general(left, right, (((1,), (0,)), ((), ())), preferred_element_type=f32)
 
 
+def dot_tn(left, right):
+    return lax.dot_general(left, right, (((0,), (0,)), ((), ())), preferred_element_type=f32)
+
+
 def fold_rows(values, op):
     rows, columns = values.shape
     return op(values.reshape(rows // 8, 8, columns), axis=0)
 
 
-def head_kernel(dp_size, heads_size, kv_index, kv_local, width, block_tokens, chunk, *refs):
+def head_kernel(dp_size, heads_size, kv_index, kv_local, width, block_tokens, chunk, fine, *refs):
     last = kv_index == kv_local - 1
     q_ref, g_ref, sk_ref, sv_ref, ck_ref, cv_ref, seg_ref = refs[:7]
     refs = refs[7:]
@@ -37,7 +41,7 @@
     dq_count = heads_size if last else 1
     dq_outs, self_ref, refs = refs[:dq_count], refs[dq_count], refs[dq_count + 1 :]
     (
-        wide_ref, keys_ref, vals_ref, keys_t_ref, s_ref, w_ref, d_ref, dk_ref, dv_ref, out_ref, dq_ref,
+        wide_ref, keys_ref, vals_ref, s_ref, w_ref, d_ref, dk_ref, dv_ref, out_ref, dq_ref,
         q_in, g_in, sk_in, sv_in, ck_in, cv_in, sems,
     ) = refs
     head_dim = q_ref.shape[1]
@@ -88,10 +92,11 @@
     first_count = jnp.sum((seg_ref[...] == 0).astype(f32), axis=1, keepdims=True).astype(jnp.int32)
 
     def limit(block):
-        return -(-(block + 1) * block_tokens // chunk) * chunk
-
-    def starts_of(block):
-        return range(0, cart_rows + limit(block), chunk)
+        return -(-(block + 1) * block_tokens // fine) * fine
+
+    def pieces(block):
+        cart = [(start, chunk) for start in range(0, cart_rows, chunk)]
+        return cart + [(cart_rows, limit(block))]
 
     queries, grads, peaks, stats = {}, {}, {}, {}
     acc = {}
@@ -103,12 +108,12 @@
         acc["peak"] = jnp.full((8, rows), masked_score, f32)
         acc["token"], acc["begin"] = token, begin
 
-    def step_scores(block, start):
-        score = dot_nt(keys_ref[start : start + chunk, :], queries[block])
+    def step_scores(block, start, size):
+        score = dot_nt(keys_ref[start : start + size, :], queries[block])
         if start >= cart_rows:
-            key_at = lax.broadcasted_iota(jnp.int32, (chunk, rows), 0) + (start - cart_rows)
+            key_at = lax.broadcasted_iota(jnp.int32, (size, rows), 0)
             score = jnp.where((key_at >= acc["begin"]) & (key_at <= acc["token"]), score, masked_score)
-        s_ref[block % 2, start : start + chunk, :] = score
+        s_ref[block % 2, start : start + size, :] = score
         acc["peak"] = jnp.maximum(acc["peak"], fold_rows(score, jnp.max))
 
     def close_scores(block):
@@ -119,8 +124,8 @@
         acc["total"] = jnp.zeros((8, rows), f32)
         acc["center"] = jnp.zeros((8, rows), f32)
 
-    def step_weights(block, start):
-        at = slice(start, start + chunk)
+    def step_weights(block, start, size):
+        at = slice(start, start + size)
         weight = jnp.exp2((s_ref[block % 2, at, :] - peaks[block]) * scale2)
         dprob = dot_nt(vals_ref[at, :], grads[block])
         w_ref[block % 2, at, :] = weight
@@ -133,25 +138,26 @@
         stats[block] = share, jnp.sum(acc["center"], axis=0, keepdims=True) * share
 
     def open_grads(block):
-        acc["dq"] = jnp.zeros((head_dim, rows), f32)
-
-    def step_grads(block, start):
-        at = slice(start, start + chunk)
+        acc["dq"] = jnp.zeros((rows, head_dim), f32)
+
+    def step_grads(block, start, size):
+        at = slice(start, start + size)
         share, center = stats[block]
         prob = w_ref[block % 2, at, :] * share
         dscore = (prob * (d_ref[block % 2, at, :] - center)).astype(bf16)
         dv = dot_nn(prob.astype(bf16), grads[block])
         dk = dot_nn(dscore, queries[block])
-        if block == 0 or start >= cart_rows + limit(block - 1):
-            dv_ref[at, :] = dv
-            dk_ref[at, :] = dk
-        else:
-            dv_ref[at, :] += dv
-            dk_ref[at, :] += dk
-        acc["dq"] = acc["dq"] + dot_nn(keys_t_ref[:, at], dscore)
+        old = size if start < cart_rows else (limit(block - 1) if block else 0)
+        old = old if block else 0
+        for ref, part in ((dv_ref, dv), (dk_ref, dk)):
+            if old:
+                ref[start : start + old, :] += part[:old]
+            if old < size:
+                ref[start + old : start + size, :] = part[old:]
+        acc["dq"] = acc["dq"] + dot_tn(dscore, keys_ref[at, :])
 
     def close_grads(block):
-        out_ref[...] = (acc["dq"] * scale).T
+        out_ref[...] = acc["dq"] * scale
         for head in range(width):
             dq_ref[block * block_tokens : (block + 1) * block_tokens, head * head_dim : (head + 1) * head_dim] = (
                 out_ref[pl.ds(head, block_tokens, stride=width), :].astype(bf16)
@@ -169,13 +175,11 @@
         if turn == 1:
             pick("cv", cv_in, vals_ref, 0)
             pick("sv", sv_in, vals_ref, cart_rows)
-            keys_t_ref[...] = keys_ref[...].astype(f32).T.astype(bf16)
         for block, begin_call, _, _ in live:
             begin_call(block)
-        for start in range(0, all_keys, chunk):
+        for index in range(len(pieces(0))):
             for block, _, step_call, _ in live:
-                if start in starts_of(block):
-                    step_call(block, start)
+                step_call(block, *pieces(block)[index])
         for block, _, _, end_call in live:
             end_call(block)
 
@@ -207,21 +211,31 @@
         self_ref[kind * count : (kind + 1) * count, :] = wide_ref[0:count, :].astype(bf16)
 
 
+def order_kernel(*refs):
+    pass
+
+
+def sum_kernel(*refs):
+    part_refs, out_ref = refs[:-1], refs[-1]
+    total = part_refs[0][...]
+    for ref in part_refs[1:]:
+        total = total + ref[...].astype(f32)
+    out_ref[...] = total
+
+
 def cart_kernel(kv_local, *refs):
-    part_refs, out_ref = refs[:-2], refs[-1]
-    count = len(part_refs) // kv_local
+    done_refs, part_refs, out_ref = refs[: kv_local - 1], refs[kv_local - 1 : -2], refs[-1]
     part_rows = part_refs[0].shape[1]
-    for kv_index in range(kv_local):
-        for kind in range(2):
-            total = part_refs[kv_index * count][kind]
-            for part in range(1, count):
-                total = total + part_refs[kv_index * count + part][kind].astype(f32)
-            out_ref[pl.ds(kind * kv_local + kv_index, part_rows, stride=2 * kv_local), :] = total
-
-
-def place_kernel(*refs):
-    part_refs, out_ref = refs[:-1], refs[-1]
-    count = len(part_refs)
+    for kind in range(2):
+        total = part_refs[0][kind]
+        for ref in part_refs[1:]:
+            total = total + ref[kind].astype(f32)
+        for kv_index, part in enumerate((*[ref[kind] for ref in done_refs], total)):
+            out_ref[pl.ds(kind * kv_local + kv_index, part_rows, stride=2 * kv_local), :] = part
+
+
+def place_kernel(count, *refs):
+    part_refs, out_ref = refs[:count], refs[-1]
     columns = part_refs[0].shape[1]
     me = lax.axis_index("heads")
     for step, ref in enumerate(part_refs):
@@ -241,7 +255,8 @@
     cart_rows = cart_keys.shape[0]
     width = heads_local // kv_local
     block_tokens = 64
-    chunk = 128
+    chunk = 512
+    fine = 128
     all_keys = cart_rows + tokens
     rows = block_tokens * width
     part_rows = cart_rows // dp_size
@@ -264,7 +279,7 @@
             ]
         before = query_list + self_list
         outs = pl.pallas_call(
-            functools.partial(head_kernel, dp_size, heads_size, kv_index, kv_local, width, block_tokens, chunk),
+            functools.partial(head_kernel, dp_size, heads_size, kv_index, kv_local, width, block_tokens, chunk, fine),
             out_shape=(
                 *[
                     jax.ShapeDtypeStruct((2, part_rows, head_dim), bf16 if step else f32)
@@ -272,13 +287,12 @@
                 ],
                 *other_shapes,
             ),
-            in_specs=[pl.BlockSpec(memory_space=pl.ANY)] * 6
+            in_specs=[pl.BlockSpec(memory_space=pltpu.HBM)] * 6
             + [pl.BlockSpec(memory_space=pltpu.VMEM)] * (1 + (len(before) if last else 0)),
             scratch_shapes=[
                 pltpu.VMEM((cart_rows * kv_local, head_dim), f32),
                 pltpu.VMEM((all_keys, head_dim), bf16),
                 pltpu.VMEM((all_keys, head_dim), bf16),
-                pltpu.VMEM((head_dim, all_keys), bf16),
                 pltpu.VMEM((2, all_keys, rows), f32),
                 pltpu.VMEM((2, all_keys, rows), f32),
                 pltpu.VMEM((2, all_keys, rows), f32),
@@ -293,28 +307,52 @@
             cost_estimate=pl.CostEstimate(flops=4 * macs, bytes_accessed=5 * 2**20, transcendentals=tokens * width * all_keys),
             name="head_grads",
         )(*flat, segment_ids, *(before if last else []))
-        cart_list += [shift(outs[step], "dp", dp_size, step) for step in range(dp_size)]
+        sends = list(outs[1:dp_size])
+        if last and cart_list:
+            anywhere = pl.BlockSpec(memory_space=pl.ANY)
+            sends = pl.pallas_call(
+                order_kernel,
+                out_shape=tuple(jax.ShapeDtypeStruct(array.shape, array.dtype) for array in sends),
+                in_specs=[anywhere] * (len(sends) + len(cart_parts) - 1),
+                out_specs=(anywhere,) * len(sends),
+                input_output_aliases={index: index for index in range(len(sends))},
+                cost_estimate=pl.CostEstimate(flops=32 * macs, bytes_accessed=0, transcendentals=0),
+                name="order_sends",
+            )(*sends, *cart_parts[1:])
+        cart_parts = [outs[0]] + [shift(array, "dp", dp_size, step + 1) for step, array in enumerate(sends)]
         if last:
             query_list, self_grads = outs[dp_size:-1], outs[-1]
         else:
             query_list.append(outs[-2])
             self_list.append(outs[-1])
+            cart_list.append(
+                pl.pallas_call(
+                    sum_kernel,
+                    out_shape=jax.ShapeDtypeStruct((2, part_rows, head_dim), f32),
+                    compiler_params=pltpu.CompilerParams(vmem_limit_bytes=vmem_bytes),
+                    cost_estimate=pl.CostEstimate(flops=2**20, bytes_accessed=2**20, transcendentals=0),
+                    name="cart_sum",
+                )(*cart_parts)
+            )
     query_list = [shift(part, "heads", heads_size, step) for step, part in enumerate(query_list)]
     query_grads = pl.pallas_call(
-        place_kernel,
+        functools.partial(place_kernel, heads_size),
         out_shape=jax.ShapeDtypeStruct((own_tokens, heads_size * heads_local * head_dim), bf16),
+        in_specs=[pl.BlockSpec(memory_space=pltpu.VMEM)] * heads_size
+        + [pl.BlockSpec(memory_space=pl.ANY)] * len(cart_list),
         compiler_params=pltpu.CompilerParams(vmem_limit_bytes=vmem_bytes),
         cost_estimate=pl.CostEstimate(flops=2**20, bytes_accessed=2 * 2**20, transcendentals=0),
         name="place_queries",
-    )(*query_list)
+    )(*query_list, *cart_list)
     cart_grads = pl.pallas_call(
         functools.partial(cart_kernel, kv_local),
         out_shape=jax.ShapeDtypeStruct((part_rows * 2 * kv_local, head_dim), f32),
-        in_specs=[pl.BlockSpec(memory_space=pltpu.VMEM)] * len(cart_list) + [pl.BlockSpec(memory_space=pl.ANY)],
+        in_specs=[pl.BlockSpec(memory_space=pltpu.VMEM)] * (len(cart_list) + dp_size)
+        + [pl.BlockSpec(memory_space=pl.ANY)],
         compiler_params=pltpu.CompilerParams(vmem_limit_bytes=vmem_bytes),
         cost_estimate=pl.CostEstimate(flops=2**20, bytes_accessed=2 * 2**20, transcendentals=0),
-        name="cart_sum",
-    )(*cart_list, query_grads)
+        name="cart_grads",
+    )(*cart_list, *cart_parts, query_grads)
     cart_grads = cart_grads.reshape(part_rows, 2, kv_local, head_dim)
     self_grads = self_grads.reshape(2, tokens, kv_local, head_dim)
     return (cart_grads, self_grads, query_grads)

time: 56.9 us -> 51.3 us (0.902); the launches traced: 56.7 us -> 50.5 us
  starting transfers between devices: 16.9 us -> 11.5 us
  waiting for transfers between devices: 9.89 us -> 6.51 us
  local copies, waits for them, and re-layouts: 0.73 us -> 2.12 us
  Pallas kernels: 28.5 us -> 29.7 us
    ppermute x9, starting transfers between devices: 16.9 us -> 11.5 us  [shift(): lax.ppermute(values, axis, [(source, (source + step) % size) for source i...]
    ppermute x9, waiting for transfers between devices: 9.89 us -> 6.51 us  [shift(): lax.ppermute(values, axis, [(source, (source + step) % size) for source i...]
    pallas_call x1 -> x3, Pallas kernels: 2.24 us -> 4.12 us  [the longest x1 2.23 us: on_device(): pl.pallas_call(functools.partial(place_kernel, heads_size), out_shape=jax...]
    unnamed x24 -> x18, local copies, waits for them, and re-layouts: 0.73 us -> 2.12 us
  transfers between devices with their start and end apart: 9 -> 9, of which waited for: 3 -> 2; matrix products, arithmetic and copies ran while one was open for 0% -> 0% of each run, Pallas kernels for 4% -> 32%
where the time goes in v3:
time: 51.3 us; the launch traced here: 50.5 us
  Pallas kernels  29.7 us (58%)
  starting transfers between devices  11.5 us (22%)
  waiting for transfers between devices  6.51 us (13%)
  local copies, waits for them, and re-layouts  2.12 us (4%)
  between operations  0.72 us (1%)
    pallas_call x2, Pallas kernels, on_device(): pl.pallas_call(functools.partial(head_kernel, dp_size, heads_size, kv_ind...  23.5 us
    ppermute x9, starting transfers between devices, shift(): lax.ppermute(values, axis, [(source, (source + step) % size) for source i...  11.5 us
    ppermute x9, waiting for transfers between devices, shift(): lax.ppermute(values, axis, [(source, (source + step) % size) for source i...  6.51 us
    pallas_call x1, Pallas kernels, on_device(): pl.pallas_call(functools.partial(place_kernel, heads_size), out_shape=jax...  2.23 us
    unnamed x18, local copies, waits for them, and re-layouts  2.12 us
    pallas_call x1, Pallas kernels, on_device(): pl.pallas_call(functools.partial(cart_kernel, kv_local), out_shape=jax.Sh...  2.04 us
    pallas_call x1, Pallas kernels, on_device(): pl.pallas_call(sum_kernel, out_shape=jax.ShapeDtypeStruct((2, part_rows,...  1.89 us
  transfers between devices with their start and end apart: 9, of which 2 were waited for; matrix products, arithmetic and copies ran while one was open for 0% of the time, Pallas kernels for 32%

profile of v3, /device:TPU:0, one launch (start us, length us, event | category | flops | bytes accessed | tf_op | source)
XLA Modules:
  0.0 50.5 jit_solution(14969295861196176509)
XLA Ops:
  0.6 11.4 %head_grads.2 = (f32[2,256,128]{2,1,0:T(8,128)}, bf16[2,256,128]{2,1,0:T(8,128)(2,1)}, bf16[2,256,128]{2,1,0:T(8,128)(2,1)}, bf16[2,256,128]{2,1,0:T(8,128)(2,1)...) custom-call(bf16[4096,128]{1,0:T(8,128)(2,1)} %bitcast.9, bf16[4096,128]{1,0:T(8,128)(2,1)} %bitcast.11, ...), custom_call_target="tpu_custom_call" | custom-call | flops 6710886400 | bytes 5242880 | tf_op jit(solution)/shard_map/head_grads/pallas_call | solution.py:281
  12.1 3.1 %collective-permute-start = (bf16[2,256,128]{2,1,0:T(8,128)(2,1)}, bf16[2,256,128]{2,1,0:T(8,128)(2,1)S(1)}, u32[]{:S(2)}, u32[]{:S(2)}) collective-permute-start(bf16[2,256,128]{2,1,0:T(8,128)(2,1)} %get-tuple-element.22), channel_id=1, source_target_pairs={{0,4},{4,8},{8,12},{12,0},{1,5},{5,9},{9,13},{13,1},{2,6},{6,10},{... | collective-permute-start | bytes 393224 | tf_op jit(solution)/shard_map/ppermute | solution.py:249
  15.1 2.6 %collective-permute-start.1 = (bf16[2,256,128]{2,1,0:T(8,128)(2,1)}, bf16[2,256,128]{2,1,0:T(8,128)(2,1)S(1)}, u32[]{:S(2)}, u32[]{:S(2)}) collective-permute-start(bf16[2,256,128]{2,1,0:T(8,128)(2,1)} %get-tuple-element.23), channel_id=1, source_target_pairs={{0,8},{4,12},{8,0},{12,4},{1,9},{5,13},{9,1},{13,5},{2,10},{6,14},... | collective-permute-start | bytes 393224 | tf_op jit(solution)/shard_map/ppermute | solution.py:249
  17.7 1.3 %collective-permute-start.2 = (bf16[2,256,128]{2,1,0:T(8,128)(2,1)}, bf16[2,256,128]{2,1,0:T(8,128)(2,1)S(1)}, u32[]{:S(2)}, u32[]{:S(2)}) collective-permute-start(bf16[2,256,128]{2,1,0:T(8,128)(2,1)} %get-tuple-element.24), channel_id=1, source_target_pairs={{0,12},{4,0},{8,4},{12,8},{1,13},{5,1},{9,5},{13,9},{2,14},{6,2},{... | collective-permute-start | bytes 393224 | tf_op jit(solution)/shard_map/ppermute | solution.py:249
  19.1 12.1 %head_grads.3 = (f32[2,256,128]{2,1,0:T(8,128)}, bf16[2,256,128]{2,1,0:T(8,128)(2,1)}, bf16[2,256,128]{2,1,0:T(8,128)(2,1)}, bf16[2,256,128]{2,1,0:T(8,128)(2,1)...) custom-call(bf16[4096,128]{1,0:T(8,128)(2,1)} %bitcast.10, ...), custom_call_target="tpu_custom_call" | custom-call | flops 6710886400 | bytes 5242880 | tf_op jit(solution)/shard_map/head_grads/pallas_call | solution.py:281
  31.2 0.1 collective-permute-start.6
  31.3 1.5 %collective-permute-start.7 = (bf16[64,2048]{1,0:T(8,128)(2,1)}, bf16[64,2048]{1,0:T(8,128)(2,1)S(1)}, u32[]{:S(2)}, u32[]{:S(2)}) collective-permute-start(bf16[64,2048]{1,0:T(8,128)(2,1)} %get-tuple-element.36), channel_id=1, source_target_pairs={{0,2},{1,3},{2,0},{3,1},{4,6},{5,7},{6,4},{7,5},{8,10},{9,11},{10,... | collective-permute-start | bytes 786440 | tf_op jit(solution)/shard_map/ppermute | solution.py:249
  32.8 0.0 collective-permute-done.refs_1_.refs_3_
  32.8 1.4 %collective-permute-start.8 = (bf16[64,2048]{1,0:T(8,128)(2,1)}, bf16[64,2048]{1,0:T(8,128)(2,1)S(1)}, u32[]{:S(2)}, u32[]{:S(2)}) collective-permute-start(bf16[64,2048]{1,0:T(8,128)(2,1)} %get-tuple-element.37), channel_id=1, source_target_pairs={{0,3},{1,0},{2,1},{3,2},{4,7},{5,4},{6,5},{7,6},{8,11},{9,8},{10,9... | collective-permute-start | bytes 786440 | tf_op jit(solution)/shard_map/ppermute | solution.py:249
  34.2 0.0 collective-permute-done.1.refs_2_.refs_4_
  34.2 0.0 collective-permute-done.2.refs_3_.refs_5_
  34.2 0.0 copy-start.5
  34.2 0.0 copy-done.3
  34.2 0.6 %copy-done.4 = bf16[2,256,128]{2,1,0:T(8,128)(2,1)} copy-done((bf16[2,256,128]{2,1,0:T(8,128)(2,1)}, bf16[2,256,128]{2,1,0:T(8,128)(2,1)S(1)}, u32[]{:S(2)}) %copy-start.4) | copy-done | bytes 131096
  34.9 0.1 copy-done.5
  34.9 0.7 %collective-permute-start.3 = (bf16[2,256,128]{2,1,0:T(8,128)(2,1)}, bf16[2,256,128]{2,1,0:T(8,128)(2,1)S(1)}, u32[]{:S(2)}, u32[]{:S(2)}) collective-permute-start(bf16[2,256,128]{2,1,0:T(8,128)(2,1)} %get-tuple-element.31), channel_id=1, source_target_pairs={{0,4},{4,8},{8,12},{12,0},{1,5},{5,9},{9,13},{13,1},{2,6},{6,10},{... | collective-permute-start | bytes 393224 | tf_op jit(solution)/shard_map/ppermute | solution.py:249
  35.6 0.3 collective-permute-start.4
  35.9 3.5 %collective-permute-done.6.refs_1_ = bf16[64,2048]{1,0:T(8,128)(2,1)S(1)} collective-permute-done((bf16[64,2048]{1,0:T(8,128)(2,1)}, bf16[64,2048]{1,0:T(8,128)(2,1)S(1)}, u32[]{:S(2)}, u32[]{:S(2)}) %collective-permute-start.6) | collective-permute-done | bytes 262176 | tf_op jit(solution)/shard_map/ppermute | solution.py:249
  39.5 0.5 collective-permute-start.5
  39.9 1.9 %cart_sum.1.refs_4_.refs_0_ = f32[2,256,128]{2,1,0:T(8,128)} custom-call(f32[2,256,128]{2,1,0:T(8,128)} %get-tuple-element.21.refs_0_, bf16[2,256,128]{2,1,0:T(8,128)(2,1)} %copy-done.3, bf16[2,256,128]{2,1,0:T(8,128)(2,1)} %copy-done.4, bf16[2,256,128]{2,1,0:T(8,128)(2,1)} %copy-done.5), custom_call_target="tpu_custom_call" | custom-call | flops 1048576 | bytes 1048576 | tf_op jit(solution)/shard_map/cart_sum/pallas_call | solution.py:329
  41.8 0.0 copy-done
  41.8 0.0 collective-permute-done.7.refs_2_
  41.8 3.0 %collective-permute-done.8.refs_3_ = bf16[64,2048]{1,0:T(8,128)(2,1)S(1)} collective-permute-done((bf16[64,2048]{1,0:T(8,128)(2,1)}, bf16[64,2048]{1,0:T(8,128)(2,1)S(1)}, u32[]{:S(2)}, u32[]{:S(2)}) %collective-permute-start.8) | collective-permute-done | bytes 262176 | tf_op jit(solution)/shard_map/ppermute | solution.py:249
  44.8 0.7 %copy-done.2 = bf16[64,2048]{1,0:T(8,128)(2,1)} copy-done((bf16[64,2048]{1,0:T(8,128)(2,1)}, bf16[64,2048]{1,0:T(8,128)(2,1)S(1)}, u32[]{:S(2)}) %copy-start.2) | copy-done | bytes 262168
  45.5 2.2 %place_queries.1.refs_5_ = bf16[64,8192]{1,0:T(8,128)(2,1)} custom-call(bf16[64,2048]{1,0:T(8,128)(2,1)} %get-tuple-element.34.refs_0_, bf16[64,2048]{1,0:T(8,128)(2,1)} %copy-done, bf16[64,2048]{1,0:T(8,128)(2,1)} %copy-done.1, bf16[64,2048]{1,0:T(8,128)(2,1)} %copy-done.2, f32[2,256,128]{2,1,0:T(8,128)} %cart_sum.1.refs_4_.refs_0_), custom_call_target="tpu_custom_call" | custom-call | flops 1048576 | bytes 2097152 | tf_op jit(solution)/shard_map/place_queries/pallas_call | solution.py:338
  47.7 0.0 collective-permute-done.3.refs_2_
  47.7 0.0 collective-permute-done.4.refs_3_
  47.8 0.0 collective-permute-done.5.refs_4_
  47.8 0.6 %copy-done.6 = bf16[2,256,128]{2,1,0:T(8,128)(2,1)} copy-done((bf16[2,256,128]{2,1,0:T(8,128)(2,1)}, bf16[2,256,128]{2,1,0:T(8,128)(2,1)S(1)}, u32[]{:S(2)}) %copy-start.6) | copy-done | bytes 131096
  48.4 0.0 copy-done.7
  48.4 0.1 copy-done.8
  48.5 2.0 %cart_grads.1 = f32[1024,128]{1,0:T(8,128)} custom-call(f32[2,256,128]{2,1,0:T(8,128)} %cart_sum.1.refs_4_.refs_0_, f32[2,256,128]{2,1,0:T(8,128)} %get-tuple-element.27.refs_1_, bf16[2,256,128]{2,1,0:T(8,128)(2,1)} %copy-done.6, bf16[2,256,128]{2,1,0:T(8,128)(2,1)} %copy-done.7, bf16[2,256,128]{2,1,0:T(8,128)(2,1)} %copy-done.8, ...), custom_call_target="tpu_custom_call" | custom-call | flops 1048576 | bytes 2097152 | tf_op jit(solution)/shard_map/cart_grads/pallas_call | solution.py:347
  (10 shorter events, 0.0 us)
Async XLA Ops:
  12.1 20.8 %collective-permute-start = (bf16[2,256,128]{2,1,0:T(8,128)(2,1)}, bf16[2,256,128]{2,1,0:T(8,128)(2,1)S(1)}, u32[]{:S(2)}, u32[]{:S(2)}) collective-permute-start(bf16[2,256,128]{2,1,0:T(8,128)(2,1)} %get-tuple-element.22), channel_id=1, source_target_pairs={{0,4},{4,8},{8,12},{12,0},{1,5},{5,9},{9,13},{13,1},{2,6},{6,10},{... | collective-permute-start | bytes 393224 | tf_op jit(solution)/shard_map/ppermute | solution.py:249
  15.1 19.1 %collective-permute-start.1 = (bf16[2,256,128]{2,1,0:T(8,128)(2,1)}, bf16[2,256,128]{2,1,0:T(8,128)(2,1)S(1)}, u32[]{:S(2)}, u32[]{:S(2)}) collective-permute-start(bf16[2,256,128]{2,1,0:T(8,128)(2,1)} %get-tuple-element.23), channel_id=1, source_target_pairs={{0,8},{4,12},{8,0},{12,4},{1,9},{5,13},{9,1},{13,5},{2,10},{6,14},... | collective-permute-start | bytes 393224 | tf_op jit(solution)/shard_map/ppermute | solution.py:249
  17.7 16.5 %collective-permute-start.2 = (bf16[2,256,128]{2,1,0:T(8,128)(2,1)}, bf16[2,256,128]{2,1,0:T(8,128)(2,1)S(1)}, u32[]{:S(2)}, u32[]{:S(2)}) collective-permute-start(bf16[2,256,128]{2,1,0:T(8,128)(2,1)} %get-tuple-element.24), channel_id=1, source_target_pairs={{0,12},{4,0},{8,4},{12,8},{1,13},{5,1},{9,5},{13,9},{2,14},{6,2},{... | collective-permute-start | bytes 393224 | tf_op jit(solution)/shard_map/ppermute | solution.py:249
  31.2 8.3 %collective-permute-start.6 = (bf16[64,2048]{1,0:T(8,128)(2,1)}, bf16[64,2048]{1,0:T(8,128)(2,1)S(1)}, u32[]{:S(2)}, u32[]{:S(2)}) collective-permute-start(bf16[64,2048]{1,0:T(8,128)(2,1)} %get-tuple-element.35), channel_id=1, source_target_pairs={{0,1},{1,2},{2,3},{3,0},{4,5},{5,6},{6,7},{7,4},{8,9},{9,10},{10,1... | collective-permute-start | bytes 786440 | tf_op jit(solution)/shard_map/ppermute | solution.py:249
  31.3 10.6 %collective-permute-start.7 = (bf16[64,2048]{1,0:T(8,128)(2,1)}, bf16[64,2048]{1,0:T(8,128)(2,1)S(1)}, u32[]{:S(2)}, u32[]{:S(2)}) collective-permute-start(bf16[64,2048]{1,0:T(8,128)(2,1)} %get-tuple-element.36), channel_id=1, source_target_pairs={{0,2},{1,3},{2,0},{3,1},{4,6},{5,7},{6,4},{7,5},{8,10},{9,11},{10,... | collective-permute-start | bytes 786440 | tf_op jit(solution)/shard_map/ppermute | solution.py:249
  32.8 1.4 %copy-start.3 = (bf16[2,256,128]{2,1,0:T(8,128)(2,1)}, bf16[2,256,128]{2,1,0:T(8,128)(2,1)S(1)}, u32[]{:S(2)}) copy-start(bf16[2,256,128]{2,1,0:T(8,128)(2,1)S(1)} %collective-permute-done.refs_1_.refs_3_) | copy-start | bytes 393220
  32.8 12.0 %collective-permute-start.8 = (bf16[64,2048]{1,0:T(8,128)(2,1)}, bf16[64,2048]{1,0:T(8,128)(2,1)S(1)}, u32[]{:S(2)}, u32[]{:S(2)}) collective-permute-start(bf16[64,2048]{1,0:T(8,128)(2,1)} %get-tuple-element.37), channel_id=1, source_target_pairs={{0,3},{1,0},{2,1},{3,2},{4,7},{5,4},{6,5},{7,6},{8,11},{9,8},{10,9... | collective-permute-start | bytes 786440 | tf_op jit(solution)/shard_map/ppermute | solution.py:249
  34.2 0.6 %copy-start.4 = (bf16[2,256,128]{2,1,0:T(8,128)(2,1)}, bf16[2,256,128]{2,1,0:T(8,128)(2,1)S(1)}, u32[]{:S(2)}) copy-start(bf16[2,256,128]{2,1,0:T(8,128)(2,1)S(1)} %collective-permute-done.1.refs_2_.refs_4_) | copy-start | bytes 393220
  34.2 0.7 %copy-start.5 = (bf16[2,256,128]{2,1,0:T(8,128)(2,1)}, bf16[2,256,128]{2,1,0:T(8,128)(2,1)S(1)}, u32[]{:S(2)}) copy-start(bf16[2,256,128]{2,1,0:T(8,128)(2,1)S(1)} %collective-permute-done.2.refs_3_.refs_5_) | copy-start | bytes 393220
  34.9 12.8 %collective-permute-start.3 = (bf16[2,256,128]{2,1,0:T(8,128)(2,1)}, bf16[2,256,128]{2,1,0:T(8,128)(2,1)S(1)}, u32[]{:S(2)}, u32[]{:S(2)}) collective-permute-start(bf16[2,256,128]{2,1,0:T(8,128)(2,1)} %get-tuple-element.31), channel_id=1, source_target_pairs={{0,4},{4,8},{8,12},{12,0},{1,5},{5,9},{9,13},{13,1},{2,6},{6,10},{... | collective-permute-start | bytes 393224 | tf_op jit(solution)/shard_map/ppermute | solution.py:249
  35.6 12.1 %collective-permute-start.4 = (bf16[2,256,128]{2,1,0:T(8,128)(2,1)}, bf16[2,256,128]{2,1,0:T(8,128)(2,1)S(1)}, u32[]{:S(2)}, u32[]{:S(2)}) collective-permute-start(bf16[2,256,128]{2,1,0:T(8,128)(2,1)} %get-tuple-element.32), channel_id=1, source_target_pairs={{0,8},{4,12},{8,0},{12,4},{1,9},{5,13},{9,1},{13,5},{2,10},{6,14},... | collective-permute-start | bytes 393224 | tf_op jit(solution)/shard_map/ppermute | solution.py:249
  39.5 2.4 %copy-start = (bf16[64,2048]{1,0:T(8,128)(2,1)}, bf16[64,2048]{1,0:T(8,128)(2,1)S(1)}, u32[]{:S(2)}) copy-start(bf16[64,2048]{1,0:T(8,128)(2,1)S(1)} %collective-permute-done.6.refs_1_) | copy-start | bytes 786436
  39.5 8.3 %collective-permute-start.5 = (bf16[2,256,128]{2,1,0:T(8,128)(2,1)}, bf16[2,256,128]{2,1,0:T(8,128)(2,1)S(1)}, u32[]{:S(2)}, u32[]{:S(2)}) collective-permute-start(bf16[2,256,128]{2,1,0:T(8,128)(2,1)} %get-tuple-element.33), channel_id=1, source_target_pairs={{0,12},{4,0},{8,4},{12,8},{1,13},{5,1},{9,5},{13,9},{2,14},{6,2},{... | collective-permute-start | bytes 393224 | tf_op jit(solution)/shard_map/ppermute | solution.py:249
  41.8 3.0 %copy-start.1 = (bf16[64,2048]{1,0:T(8,128)(2,1)}, bf16[64,2048]{1,0:T(8,128)(2,1)S(1)}, u32[]{:S(2)}) copy-start(bf16[64,2048]{1,0:T(8,128)(2,1)S(1)} %collective-permute-done.7.refs_2_) | copy-start | bytes 786436
  44.8 0.7 %copy-start.2 = (bf16[64,2048]{1,0:T(8,128)(2,1)}, bf16[64,2048]{1,0:T(8,128)(2,1)S(1)}, u32[]{:S(2)}) copy-start(bf16[64,2048]{1,0:T(8,128)(2,1)S(1)} %collective-permute-done.8.refs_3_) | copy-start | bytes 786436
  47.7 0.7 %copy-start.6 = (bf16[2,256,128]{2,1,0:T(8,128)(2,1)}, bf16[2,256,128]{2,1,0:T(8,128)(2,1)S(1)}, u32[]{:S(2)}) copy-start(bf16[2,256,128]{2,1,0:T(8,128)(2,1)S(1)} %collective-permute-done.3.refs_2_) | copy-start | bytes 393220
  47.8 0.7 %copy-start.7 = (bf16[2,256,128]{2,1,0:T(8,128)(2,1)}, bf16[2,256,128]{2,1,0:T(8,128)(2,1)S(1)}, u32[]{:S(2)}) copy-start(bf16[2,256,128]{2,1,0:T(8,128)(2,1)S(1)} %collective-permute-done.4.refs_3_) | copy-start | bytes 393220
  47.8 0.7 %copy-start.8 = (bf16[2,256,128]{2,1,0:T(8,128)(2,1)}, bf16[2,256,128]{2,1,0:T(8,128)(2,1)S(1)}, u32[]{:S(2)}) copy-start(bf16[2,256,128]{2,1,0:T(8,128)(2,1)S(1)} %collective-permute-done.5.refs_4_) | copy-start | bytes 393220

commit v4 on v3

--- a/solution.py
+++ b/solution.py
@@ -20,10 +20,6 @@
 
 def dot_nn(left, right):
     return lax.dot_general(left, right, (((1,), (0,)), ((), ())), preferred_element_type=f32)
-
-
-def dot_tn(left, right):
-    return lax.dot_general(left, right, (((0,), (0,)), ((), ())), preferred_element_type=f32)
 
 
 def fold_rows(values, op):
@@ -41,7 +37,7 @@
     dq_count = heads_size if last else 1
     dq_outs, self_ref, refs = refs[:dq_count], refs[dq_count], refs[dq_count + 1 :]
     (
-        wide_ref, keys_ref, vals_ref, s_ref, w_ref, d_ref, dk_ref, dv_ref, out_ref, dq_ref,
+        wide_ref, keys_ref, vals_ref, keys_t_ref, s_ref, w_ref, d_ref, dk_t_ref, dv_t_ref, dk_ref, dv_ref, out_ref, dq_ref,
         q_in, g_in, sk_in, sv_in, ck_in, cv_in, sems,
     ) = refs
     head_dim = q_ref.shape[1]
@@ -99,7 +95,10 @@
         return cart + [(cart_rows, limit(block))]
 
     queries, grads, peaks, stats = {}, {}, {}, {}
-    acc = {}
+    acc, turned = {}, {}
+
+    def turn_values(values):
+        return values.astype(f32).T.astype(bf16)
 
     def open_scores(block):
         queries[block] = rows_of("q", q_in, block)
@@ -138,26 +137,28 @@
         stats[block] = share, jnp.sum(acc["center"], axis=0, keepdims=True) * share
 
     def open_grads(block):
-        acc["dq"] = jnp.zeros((rows, head_dim), f32)
+        acc["dq"] = jnp.zeros((head_dim, rows), f32)
+        turned["q", block] = turn_values(queries[block])
+        turned["g", block] = turn_values(grads[block])
 
     def step_grads(block, start, size):
         at = slice(start, start + size)
         share, center = stats[block]
         prob = w_ref[block % 2, at, :] * share
         dscore = (prob * (d_ref[block % 2, at, :] - center)).astype(bf16)
-        dv = dot_nn(prob.astype(bf16), grads[block])
-        dk = dot_nn(dscore, queries[block])
+        dv = dot_nt(turned["g", block], prob.astype(bf16))
+        dk = dot_nt(turned["q", block], dscore)
         old = size if start < cart_rows else (limit(block - 1) if block else 0)
         old = old if block else 0
-        for ref, part in ((dv_ref, dv), (dk_ref, dk)):
+        for ref, part in ((dv_t_ref, dv), (dk_t_ref, dk)):
             if old:
-                ref[start : start + old, :] += part[:old]
+                ref[:, start : start + old] += part[:, :old]
             if old < size:
-                ref[start + old : start + size, :] = part[old:]
-        acc["dq"] = acc["dq"] + dot_tn(dscore, keys_ref[at, :])
+                ref[:, start + old : start + size] = part[:, old:]
+        acc["dq"] = acc["dq"] + dot_nn(keys_t_ref[:, at], dscore)
 
     def close_grads(block):
-        out_ref[...] = acc["dq"] * scale
+        out_ref[...] = (acc["dq"] * scale).T
         for head in range(width):
             dq_ref[block * block_tokens : (block + 1) * block_tokens, head * head_dim : (head + 1) * head_dim] = (
                 out_ref[pl.ds(head, block_tokens, stride=width), :].astype(bf16)
@@ -175,6 +176,7 @@
         if turn == 1:
             pick("cv", cv_in, vals_ref, 0)
             pick("sv", sv_in, vals_ref, cart_rows)
+            keys_t_ref[...] = turn_values(keys_ref[...])
         for block, begin_call, _, _ in live:
             begin_call(block)
         for index in range(len(pieces(0))):
@@ -183,6 +185,8 @@
         for block, _, _, end_call in live:
             end_call(block)
 
+    dk_ref[...] = dk_t_ref[...].T
+    dv_ref[...] = dv_t_ref[...].T
     part_rows = cart_rows // dp_size
     me = lax.axis_index("dp")
     for step, ref in enumerate(cart_outs):
@@ -293,9 +297,12 @@
                 pltpu.VMEM((cart_rows * kv_local, head_dim), f32),
                 pltpu.VMEM((all_keys, head_dim), bf16),
                 pltpu.VMEM((all_keys, head_dim), bf16),
+                pltpu.VMEM((head_dim, all_keys), bf16),
                 pltpu.VMEM((2, all_keys, rows), f32),
                 pltpu.VMEM((2, all_keys, rows), f32),
                 pltpu.VMEM((2, all_keys, rows), f32),
+                pltpu.VMEM((head_dim, all_keys), f32),
+                pltpu.VMEM((head_dim, all_keys), f32),
                 pltpu.VMEM((all_keys, head_dim), f32),
                 pltpu.VMEM((all_keys, head_dim), f32),
                 pltpu.VMEM((rows, head_dim), f32),

time: 51.3 us -> 51.2 us (level)
  no operation moved by 1% of the time
where the time goes in v4:
time: 51.2 us; the launch traced here: 50.4 us
  Pallas kernels  29.6 us (58%)
  starting transfers between devices  11.5 us (22%)
  waiting for transfers between devices  6.49 us (13%)
  local copies, waits for them, and re-layouts  2.12 us (4%)
  between operations  0.72 us (1%)
    pallas_call x2, Pallas kernels, on_device(): pl.pallas_call(functools.partial(head_kernel, dp_size, heads_size, kv_ind...  23.4 us
    ppermute x9, starting transfers between devices, shift(): lax.ppermute(values, axis, [(source, (source + step) % size) for source i...  11.5 us
    ppermute x9, waiting for transfers between devices, shift(): lax.ppermute(values, axis, [(source, (source + step) % size) for source i...  6.49 us
    pallas_call x1, Pallas kernels, on_device(): pl.pallas_call(functools.partial(place_kernel, heads_size), out_shape=jax...  2.23 us
    unnamed x18, local copies, waits for them, and re-layouts  2.12 us
    pallas_call x1, Pallas kernels, on_device(): pl.pallas_call(functools.partial(cart_kernel, kv_local), out_shape=jax.Sh...  2.04 us
    pallas_call x1, Pallas kernels, on_device(): pl.pallas_call(sum_kernel, out_shape=jax.ShapeDtypeStruct((2, part_rows,...  1.89 us
  transfers between devices with their start and end apart: 9, of which 2 were waited for; matrix products, arithmetic and copies ran while one was open for 0% of the time, Pallas kernels for 32%

profile of v4, /device:TPU:0, one launch (start us, length us, event | category | flops | bytes accessed | tf_op | source)
XLA Modules:
  0.0 50.4 jit_solution(8652781727753147260)
XLA Ops:
  0.6 11.4 %head_grads.2 = (f32[2,256,128]{2,1,0:T(8,128)}, bf16[2,256,128]{2,1,0:T(8,128)(2,1)}, bf16[2,256,128]{2,1,0:T(8,128)(2,1)}, bf16[2,256,128]{2,1,0:T(8,128)(2,1)...) custom-call(bf16[4096,128]{1,0:T(8,128)(2,1)} %bitcast.9, bf16[4096,128]{1,0:T(8,128)(2,1)} %bitcast.11, ...), custom_call_target="tpu_custom_call" | custom-call | flops 6710886400 | bytes 5242880 | tf_op jit(solution)/shard_map/head_grads/pallas_call | solution.py:285
  12.0 3.1 %collective-permute-start = (bf16[2,256,128]{2,1,0:T(8,128)(2,1)}, bf16[2,256,128]{2,1,0:T(8,128)(2,1)S(1)}, u32[]{:S(2)}, u32[]{:S(2)}) collective-permute-start(bf16[2,256,128]{2,1,0:T(8,128)(2,1)} %get-tuple-element.22), channel_id=1, source_target_pairs={{0,4},{4,8},{8,12},{12,0},{1,5},{5,9},{9,13},{13,1},{2,6},{6,10},{... | collective-permute-start | bytes 393224 | tf_op jit(solution)/shard_map/ppermute | solution.py:253
  15.1 2.6 %collective-permute-start.1 = (bf16[2,256,128]{2,1,0:T(8,128)(2,1)}, bf16[2,256,128]{2,1,0:T(8,128)(2,1)S(1)}, u32[]{:S(2)}, u32[]{:S(2)}) collective-permute-start(bf16[2,256,128]{2,1,0:T(8,128)(2,1)} %get-tuple-element.23), channel_id=1, source_target_pairs={{0,8},{4,12},{8,0},{12,4},{1,9},{5,13},{9,1},{13,5},{2,10},{6,14},... | collective-permute-start | bytes 393224 | tf_op jit(solution)/shard_map/ppermute | solution.py:253
  17.7 1.4 %collective-permute-start.2 = (bf16[2,256,128]{2,1,0:T(8,128)(2,1)}, bf16[2,256,128]{2,1,0:T(8,128)(2,1)S(1)}, u32[]{:S(2)}, u32[]{:S(2)}) collective-permute-start(bf16[2,256,128]{2,1,0:T(8,128)(2,1)} %get-tuple-element.24), channel_id=1, source_target_pairs={{0,12},{4,0},{8,4},{12,8},{1,13},{5,1},{9,5},{13,9},{2,14},{6,2},{... | collective-permute-start | bytes 393224 | tf_op jit(solution)/shard_map/ppermute | solution.py:253
  19.0 12.0 %head_grads.3 = (f32[2,256,128]{2,1,0:T(8,128)}, bf16[2,256,128]{2,1,0:T(8,128)(2,1)}, bf16[2,256,128]{2,1,0:T(8,128)(2,1)}, bf16[2,256,128]{2,1,0:T(8,128)(2,1)...) custom-call(bf16[4096,128]{1,0:T(8,128)(2,1)} %bitcast.10, ...), custom_call_target="tpu_custom_call" | custom-call | flops 6710886400 | bytes 5242880 | tf_op jit(solution)/shard_map/head_grads/pallas_call | solution.py:285
  31.1 0.1 collective-permute-start.6
  31.2 1.6 %collective-permute-start.7 = (bf16[64,2048]{1,0:T(8,128)(2,1)}, bf16[64,2048]{1,0:T(8,128)(2,1)S(1)}, u32[]{:S(2)}, u32[]{:S(2)}) collective-permute-start(bf16[64,2048]{1,0:T(8,128)(2,1)} %get-tuple-element.36), channel_id=1, source_target_pairs={{0,2},{1,3},{2,0},{3,1},{4,6},{5,7},{6,4},{7,5},{8,10},{9,11},{10,... | collective-permute-start | bytes 786440 | tf_op jit(solution)/shard_map/ppermute | solution.py:253
  32.7 0.0 collective-permute-done.refs_1_.refs_3_
  32.7 1.4 %collective-permute-start.8 = (bf16[64,2048]{1,0:T(8,128)(2,1)}, bf16[64,2048]{1,0:T(8,128)(2,1)S(1)}, u32[]{:S(2)}, u32[]{:S(2)}) collective-permute-start(bf16[64,2048]{1,0:T(8,128)(2,1)} %get-tuple-element.37), channel_id=1, source_target_pairs={{0,3},{1,0},{2,1},{3,2},{4,7},{5,4},{6,5},{7,6},{8,11},{9,8},{10,9... | collective-permute-start | bytes 786440 | tf_op jit(solution)/shard_map/ppermute | solution.py:253
  34.1 0.0 collective-permute-done.1.refs_2_.refs_4_
  34.1 0.0 collective-permute-done.2.refs_3_.refs_5_
  34.1 0.0 copy-start.5
  34.1 0.0 copy-done.3
  34.1 0.6 %copy-done.4 = bf16[2,256,128]{2,1,0:T(8,128)(2,1)} copy-done((bf16[2,256,128]{2,1,0:T(8,128)(2,1)}, bf16[2,256,128]{2,1,0:T(8,128)(2,1)S(1)}, u32[]{:S(2)}) %copy-start.4) | copy-done | bytes 131096
  34.8 0.1 copy-done.5
  34.8 0.7 %collective-permute-start.3 = (bf16[2,256,128]{2,1,0:T(8,128)(2,1)}, bf16[2,256,128]{2,1,0:T(8,128)(2,1)S(1)}, u32[]{:S(2)}, u32[]{:S(2)}) collective-permute-start(bf16[2,256,128]{2,1,0:T(8,128)(2,1)} %get-tuple-element.31), channel_id=1, source_target_pairs={{0,4},{4,8},{8,12},{12,0},{1,5},{5,9},{9,13},{13,1},{2,6},{6,10},{... | collective-permute-start | bytes 393224 | tf_op jit(solution)/shard_map/ppermute | solution.py:253
  35.5 0.4 collective-permute-start.4
  35.8 3.5 %collective-permute-done.6.refs_1_ = bf16[64,2048]{1,0:T(8,128)(2,1)S(1)} collective-permute-done((bf16[64,2048]{1,0:T(8,128)(2,1)}, bf16[64,2048]{1,0:T(8,128)(2,1)S(1)}, u32[]{:S(2)}, u32[]{:S(2)}) %collective-permute-start.6) | collective-permute-done | bytes 262176 | tf_op jit(solution)/shard_map/ppermute | solution.py:253
  39.4 0.5 collective-permute-start.5
  39.8 1.9 %cart_sum.1.refs_4_.refs_0_ = f32[2,256,128]{2,1,0:T(8,128)} custom-call(f32[2,256,128]{2,1,0:T(8,128)} %get-tuple-element.21.refs_0_, bf16[2,256,128]{2,1,0:T(8,128)(2,1)} %copy-done.3, bf16[2,256,128]{2,1,0:T(8,128)(2,1)} %copy-done.4, bf16[2,256,128]{2,1,0:T(8,128)(2,1)} %copy-done.5), custom_call_target="tpu_custom_call" | custom-call | flops 1048576 | bytes 1048576 | tf_op jit(solution)/shard_map/cart_sum/pallas_call | solution.py:336
  41.7 0.0 copy-done
  41.7 0.0 collective-permute-done.7.refs_2_
  41.7 3.0 %collective-permute-done.8.refs_3_ = bf16[64,2048]{1,0:T(8,128)(2,1)S(1)} collective-permute-done((bf16[64,2048]{1,0:T(8,128)(2,1)}, bf16[64,2048]{1,0:T(8,128)(2,1)S(1)}, u32[]{:S(2)}, u32[]{:S(2)}) %collective-permute-start.8) | collective-permute-done | bytes 262176 | tf_op jit(solution)/shard_map/ppermute | solution.py:253
  44.7 0.7 %copy-done.2 = bf16[64,2048]{1,0:T(8,128)(2,1)} copy-done((bf16[64,2048]{1,0:T(8,128)(2,1)}, bf16[64,2048]{1,0:T(8,128)(2,1)S(1)}, u32[]{:S(2)}) %copy-start.2) | copy-done | bytes 262168
  45.4 2.2 %place_queries.1.refs_5_ = bf16[64,8192]{1,0:T(8,128)(2,1)} custom-call(bf16[64,2048]{1,0:T(8,128)(2,1)} %get-tuple-element.34.refs_0_, bf16[64,2048]{1,0:T(8,128)(2,1)} %copy-done, bf16[64,2048]{1,0:T(8,128)(2,1)} %copy-done.1, bf16[64,2048]{1,0:T(8,128)(2,1)} %copy-done.2, f32[2,256,128]{2,1,0:T(8,128)} %cart_sum.1.refs_4_.refs_0_), custom_call_target="tpu_custom_call" | custom-call | flops 1048576 | bytes 2097152 | tf_op jit(solution)/shard_map/place_queries/pallas_call | solution.py:345
  47.6 0.0 collective-permute-done.3.refs_2_
  47.6 0.0 collective-permute-done.4.refs_3_
  47.6 0.0 collective-permute-done.5.refs_4_
  47.7 0.6 %copy-done.6 = bf16[2,256,128]{2,1,0:T(8,128)(2,1)} copy-done((bf16[2,256,128]{2,1,0:T(8,128)(2,1)}, bf16[2,256,128]{2,1,0:T(8,128)(2,1)S(1)}, u32[]{:S(2)}) %copy-start.6) | copy-done | bytes 131096
  48.3 0.0 copy-done.7
  48.3 0.1 copy-done.8
  48.4 2.0 %cart_grads.1 = f32[1024,128]{1,0:T(8,128)} custom-call(f32[2,256,128]{2,1,0:T(8,128)} %cart_sum.1.refs_4_.refs_0_, f32[2,256,128]{2,1,0:T(8,128)} %get-tuple-element.27.refs_1_, bf16[2,256,128]{2,1,0:T(8,128)(2,1)} %copy-done.6, bf16[2,256,128]{2,1,0:T(8,128)(2,1)} %copy-done.7, bf16[2,256,128]{2,1,0:T(8,128)(2,1)} %copy-done.8, ...), custom_call_target="tpu_custom_call" | custom-call | flops 1048576 | bytes 2097152 | tf_op jit(solution)/shard_map/cart_grads/pallas_call | solution.py:354
  (10 shorter events, 0.0 us)
Async XLA Ops:
  12.0 20.7 %collective-permute-start = (bf16[2,256,128]{2,1,0:T(8,128)(2,1)}, bf16[2,256,128]{2,1,0:T(8,128)(2,1)S(1)}, u32[]{:S(2)}, u32[]{:S(2)}) collective-permute-start(bf16[2,256,128]{2,1,0:T(8,128)(2,1)} %get-tuple-element.22), channel_id=1, source_target_pairs={{0,4},{4,8},{8,12},{12,0},{1,5},{5,9},{9,13},{13,1},{2,6},{6,10},{... | collective-permute-start | bytes 393224 | tf_op jit(solution)/shard_map/ppermute | solution.py:253
  15.1 19.0 %collective-permute-start.1 = (bf16[2,256,128]{2,1,0:T(8,128)(2,1)}, bf16[2,256,128]{2,1,0:T(8,128)(2,1)S(1)}, u32[]{:S(2)}, u32[]{:S(2)}) collective-permute-start(bf16[2,256,128]{2,1,0:T(8,128)(2,1)} %get-tuple-element.23), channel_id=1, source_target_pairs={{0,8},{4,12},{8,0},{12,4},{1,9},{5,13},{9,1},{13,5},{2,10},{6,14},... | collective-permute-start | bytes 393224 | tf_op jit(solution)/shard_map/ppermute | solution.py:253
  17.7 16.4 %collective-permute-start.2 = (bf16[2,256,128]{2,1,0:T(8,128)(2,1)}, bf16[2,256,128]{2,1,0:T(8,128)(2,1)S(1)}, u32[]{:S(2)}, u32[]{:S(2)}) collective-permute-start(bf16[2,256,128]{2,1,0:T(8,128)(2,1)} %get-tuple-element.24), channel_id=1, source_target_pairs={{0,12},{4,0},{8,4},{12,8},{1,13},{5,1},{9,5},{13,9},{2,14},{6,2},{... | collective-permute-start | bytes 393224 | tf_op jit(solution)/shard_map/ppermute | solution.py:253
  31.1 8.3 %collective-permute-start.6 = (bf16[64,2048]{1,0:T(8,128)(2,1)}, bf16[64,2048]{1,0:T(8,128)(2,1)S(1)}, u32[]{:S(2)}, u32[]{:S(2)}) collective-permute-start(bf16[64,2048]{1,0:T(8,128)(2,1)} %get-tuple-element.35), channel_id=1, source_target_pairs={{0,1},{1,2},{2,3},{3,0},{4,5},{5,6},{6,7},{7,4},{8,9},{9,10},{10,1... | collective-permute-start | bytes 786440 | tf_op jit(solution)/shard_map/ppermute | solution.py:253
  31.2 10.6 %collective-permute-start.7 = (bf16[64,2048]{1,0:T(8,128)(2,1)}, bf16[64,2048]{1,0:T(8,128)(2,1)S(1)}, u32[]{:S(2)}, u32[]{:S(2)}) collective-permute-start(bf16[64,2048]{1,0:T(8,128)(2,1)} %get-tuple-element.36), channel_id=1, source_target_pairs={{0,2},{1,3},{2,0},{3,1},{4,6},{5,7},{6,4},{7,5},{8,10},{9,11},{10,... | collective-permute-start | bytes 786440 | tf_op jit(solution)/shard_map/ppermute | solution.py:253
  32.7 1.4 %copy-start.3 = (bf16[2,256,128]{2,1,0:T(8,128)(2,1)}, bf16[2,256,128]{2,1,0:T(8,128)(2,1)S(1)}, u32[]{:S(2)}) copy-start(bf16[2,256,128]{2,1,0:T(8,128)(2,1)S(1)} %collective-permute-done.refs_1_.refs_3_) | copy-start | bytes 393220
  32.7 12.0 %collective-permute-start.8 = (bf16[64,2048]{1,0:T(8,128)(2,1)}, bf16[64,2048]{1,0:T(8,128)(2,1)S(1)}, u32[]{:S(2)}, u32[]{:S(2)}) collective-permute-start(bf16[64,2048]{1,0:T(8,128)(2,1)} %get-tuple-element.37), channel_id=1, source_target_pairs={{0,3},{1,0},{2,1},{3,2},{4,7},{5,4},{6,5},{7,6},{8,11},{9,8},{10,9... | collective-permute-start | bytes 786440 | tf_op jit(solution)/shard_map/ppermute | solution.py:253
  34.1 0.6 %copy-start.4 = (bf16[2,256,128]{2,1,0:T(8,128)(2,1)}, bf16[2,256,128]{2,1,0:T(8,128)(2,1)S(1)}, u32[]{:S(2)}) copy-start(bf16[2,256,128]{2,1,0:T(8,128)(2,1)S(1)} %collective-permute-done.1.refs_2_.refs_4_) | copy-start | bytes 393220
  34.1 0.7 %copy-start.5 = (bf16[2,256,128]{2,1,0:T(8,128)(2,1)}, bf16[2,256,128]{2,1,0:T(8,128)(2,1)S(1)}, u32[]{:S(2)}) copy-start(bf16[2,256,128]{2,1,0:T(8,128)(2,1)S(1)} %collective-permute-done.2.refs_3_.refs_5_) | copy-start | bytes 393220
  34.8 12.8 %collective-permute-start.3 = (bf16[2,256,128]{2,1,0:T(8,128)(2,1)}, bf16[2,256,128]{2,1,0:T(8,128)(2,1)S(1)}, u32[]{:S(2)}, u32[]{:S(2)}) collective-permute-start(bf16[2,256,128]{2,1,0:T(8,128)(2,1)} %get-tuple-element.31), channel_id=1, source_target_pairs={{0,4},{4,8},{8,12},{12,0},{1,5},{5,9},{9,13},{13,1},{2,6},{6,10},{... | collective-permute-start | bytes 393224 | tf_op jit(solution)/shard_map/ppermute | solution.py:253
  35.5 12.2 %collective-permute-start.4 = (bf16[2,256,128]{2,1,0:T(8,128)(2,1)}, bf16[2,256,128]{2,1,0:T(8,128)(2,1)S(1)}, u32[]{:S(2)}, u32[]{:S(2)}) collective-permute-start(bf16[2,256,128]{2,1,0:T(8,128)(2,1)} %get-tuple-element.32), channel_id=1, source_target_pairs={{0,8},{4,12},{8,0},{12,4},{1,9},{5,13},{9,1},{13,5},{2,10},{6,14},... | collective-permute-start | bytes 393224 | tf_op jit(solution)/shard_map/ppermute | solution.py:253
  39.3 2.4 %copy-start = (bf16[64,2048]{1,0:T(8,128)(2,1)}, bf16[64,2048]{1,0:T(8,128)(2,1)S(1)}, u32[]{:S(2)}) copy-start(bf16[64,2048]{1,0:T(8,128)(2,1)S(1)} %collective-permute-done.6.refs_1_) | copy-start | bytes 786436
  39.4 8.3 %collective-permute-start.5 = (bf16[2,256,128]{2,1,0:T(8,128)(2,1)}, bf16[2,256,128]{2,1,0:T(8,128)(2,1)S(1)}, u32[]{:S(2)}, u32[]{:S(2)}) collective-permute-start(bf16[2,256,128]{2,1,0:T(8,128)(2,1)} %get-tuple-element.33), channel_id=1, source_target_pairs={{0,12},{4,0},{8,4},{12,8},{1,13},{5,1},{9,5},{13,9},{2,14},{6,2},{... | collective-permute-start | bytes 393224 | tf_op jit(solution)/shard_map/ppermute | solution.py:253
  41.7 3.0 %copy-start.1 = (bf16[64,2048]{1,0:T(8,128)(2,1)}, bf16[64,2048]{1,0:T(8,128)(2,1)S(1)}, u32[]{:S(2)}) copy-start(bf16[64,2048]{1,0:T(8,128)(2,1)S(1)} %collective-permute-done.7.refs_2_) | copy-start | bytes 786436
  44.7 0.7 %copy-start.2 = (bf16[64,2048]{1,0:T(8,128)(2,1)}, bf16[64,2048]{1,0:T(8,128)(2,1)S(1)}, u32[]{:S(2)}) copy-start(bf16[64,2048]{1,0:T(8,128)(2,1)S(1)} %collective-permute-done.8.refs_3_) | copy-start | bytes 786436
  47.6 0.7 %copy-start.6 = (bf16[2,256,128]{2,1,0:T(8,128)(2,1)}, bf16[2,256,128]{2,1,0:T(8,128)(2,1)S(1)}, u32[]{:S(2)}) copy-start(bf16[2,256,128]{2,1,0:T(8,128)(2,1)S(1)} %collective-permute-done.3.refs_2_) | copy-start | bytes 393220
  47.6 0.7 %copy-start.7 = (bf16[2,256,128]{2,1,0:T(8,128)(2,1)}, bf16[2,256,128]{2,1,0:T(8,128)(2,1)S(1)}, u32[]{:S(2)}) copy-start(bf16[2,256,128]{2,1,0:T(8,128)(2,1)S(1)} %collective-permute-done.4.refs_3_) | copy-start | bytes 393220
  47.7 0.7 %copy-start.8 = (bf16[2,256,128]{2,1,0:T(8,128)(2,1)}, bf16[2,256,128]{2,1,0:T(8,128)(2,1)S(1)}, u32[]{:S(2)}) copy-start(bf16[2,256,128]{2,1,0:T(8,128)(2,1)S(1)} %collective-permute-done.5.refs_4_) | copy-start | bytes 393220

commit v5 on v3

--- a/solution.py
+++ b/solution.py
@@ -22,16 +22,12 @@
     return lax.dot_general(left, right, (((1,), (0,)), ((), ())), preferred_element_type=f32)
 
 
-def dot_tn(left, right):
-    return lax.dot_general(left, right, (((0,), (0,)), ((), ())), preferred_element_type=f32)
-
-
 def fold_rows(values, op):
     rows, columns = values.shape
     return op(values.reshape(rows // 8, 8, columns), axis=0)
 
 
-def head_kernel(dp_size, heads_size, kv_index, kv_local, width, block_tokens, chunk, fine, *refs):
+def head_kernel(dp_size, heads_size, kv_index, kv_local, width, block_tokens, chunk, fine, sub, *refs):
     last = kv_index == kv_local - 1
     q_ref, g_ref, sk_ref, sv_ref, ck_ref, cv_ref, seg_ref = refs[:7]
     refs = refs[7:]
@@ -41,7 +37,7 @@
     dq_count = heads_size if last else 1
     dq_outs, self_ref, refs = refs[:dq_count], refs[dq_count], refs[dq_count + 1 :]
     (
-        wide_ref, keys_ref, vals_ref, s_ref, w_ref, d_ref, dk_ref, dv_ref, out_ref, dq_ref,
+        wide_ref, keys_ref, vals_ref, keys_t_ref, s_ref, w_ref, d_ref, p_ref, ds_ref, dk_ref, dv_ref, out_ref, dq_ref,
         q_in, g_in, sk_in, sv_in, ck_in, cv_in, sems,
     ) = refs
     head_dim = q_ref.shape[1]
@@ -101,6 +97,9 @@
     queries, grads, peaks, stats = {}, {}, {}, {}
     acc = {}
 
+    def subs(start, size):
+        return [slice(at, at + sub) for at in range(start, start + size, sub)]
+
     def open_scores(block):
         queries[block] = rows_of("q", q_in, block)
         token = (lax.broadcasted_iota(jnp.int32, (1, rows), 1) + block * rows) // width
@@ -109,12 +108,14 @@
         acc["token"], acc["begin"] = token, begin
 
     def step_scores(block, start, size):
-        score = dot_nt(keys_ref[start : start + size, :], queries[block])
-        if start >= cart_rows:
-            key_at = lax.broadcasted_iota(jnp.int32, (size, rows), 0)
-            score = jnp.where((key_at >= acc["begin"]) & (key_at <= acc["token"]), score, masked_score)
-        s_ref[block % 2, start : start + size, :] = score
-        acc["peak"] = jnp.maximum(acc["peak"], fold_rows(score, jnp.max))
+        s_ref[block % 2, start : start + size, :] = dot_nt(keys_ref[start : start + size, :], queries[block])
+        for at in subs(start, size):
+            score = s_ref[block % 2, at, :]
+            if start >= cart_rows:
+                key_at = lax.broadcasted_iota(jnp.int32, (sub, rows), 0) + (at.start - cart_rows)
+                score = jnp.where((key_at >= acc["begin"]) & (key_at <= acc["token"]), score, masked_score)
+                s_ref[block % 2, at, :] = score
+            acc["peak"] = jnp.maximum(acc["peak"], fold_rows(score, jnp.max))
 
     def close_scores(block):
         peaks[block] = jnp.max(acc["peak"], axis=0, keepdims=True)
@@ -125,39 +126,39 @@
         acc["center"] = jnp.zeros((8, rows), f32)
 
     def step_weights(block, start, size):
-        at = slice(start, start + size)
-        weight = jnp.exp2((s_ref[block % 2, at, :] - peaks[block]) * scale2)
-        dprob = dot_nt(vals_ref[at, :], grads[block])
-        w_ref[block % 2, at, :] = weight
-        d_ref[block % 2, at, :] = dprob
-        acc["total"] = acc["total"] + fold_rows(weight, jnp.sum)
-        acc["center"] = acc["center"] + fold_rows(weight * dprob, jnp.sum)
+        d_ref[block % 2, start : start + size, :] = dot_nt(vals_ref[start : start + size, :], grads[block])
+        for at in subs(start, size):
+            weight = jnp.exp2((s_ref[block % 2, at, :] - peaks[block]) * scale2)
+            w_ref[block % 2, at, :] = weight
+            acc["total"] = acc["total"] + fold_rows(weight, jnp.sum)
+            acc["center"] = acc["center"] + fold_rows(weight * d_ref[block % 2, at, :], jnp.sum)
 
     def close_weights(block):
         share = 1.0 / jnp.sum(acc["total"], axis=0, keepdims=True)
         stats[block] = share, jnp.sum(acc["center"], axis=0, keepdims=True) * share
 
     def open_grads(block):
-        acc["dq"] = jnp.zeros((rows, head_dim), f32)
+        acc["dq"] = jnp.zeros((head_dim, rows), f32)
 
     def step_grads(block, start, size):
+        share, center = stats[block]
+        for at in subs(start, size):
+            prob = w_ref[block % 2, at, :] * share
+            p_ref[at, :] = prob.astype(bf16)
+            ds_ref[at, :] = (prob * (d_ref[block % 2, at, :] - center)).astype(bf16)
         at = slice(start, start + size)
-        share, center = stats[block]
-        prob = w_ref[block % 2, at, :] * share
-        dscore = (prob * (d_ref[block % 2, at, :] - center)).astype(bf16)
-        dv = dot_nn(prob.astype(bf16), grads[block])
-        dk = dot_nn(dscore, queries[block])
         old = size if start < cart_rows else (limit(block - 1) if block else 0)
         old = old if block else 0
-        for ref, part in ((dv_ref, dv), (dk_ref, dk)):
+        for ref, left, right in ((dv_ref, p_ref, grads[block]), (dk_ref, ds_ref, queries[block])):
+            part = dot_nn(left[at, :], right)
             if old:
                 ref[start : start + old, :] += part[:old]
             if old < size:
                 ref[start + old : start + size, :] = part[old:]
-        acc["dq"] = acc["dq"] + dot_tn(dscore, keys_ref[at, :])
+        acc["dq"] = acc["dq"] + dot_nn(keys_t_ref[:, at], ds_ref[at, :])
 
     def close_grads(block):
-        out_ref[...] = acc["dq"] * scale
+        out_ref[...] = (acc["dq"] * scale).T
         for head in range(width):
             dq_ref[block * block_tokens : (block + 1) * block_tokens, head * head_dim : (head + 1) * head_dim] = (
                 out_ref[pl.ds(head, block_tokens, stride=width), :].astype(bf16)
@@ -175,6 +176,7 @@
         if turn == 1:
             pick("cv", cv_in, vals_ref, 0)
             pick("sv", sv_in, vals_ref, cart_rows)
+            keys_t_ref[...] = keys_ref[...].astype(f32).T.astype(bf16)
         for block, begin_call, _, _ in live:
             begin_call(block)
         for index in range(len(pieces(0))):
@@ -255,8 +257,9 @@
     cart_rows = cart_keys.shape[0]
     width = heads_local // kv_local
     block_tokens = 64
-    chunk = 512
+    chunk = 256
     fine = 128
+    sub = 16
     all_keys = cart_rows + tokens
     rows = block_tokens * width
     part_rows = cart_rows // dp_size
@@ -279,7 +282,7 @@
             ]
         before = query_list + self_list
         outs = pl.pallas_call(
-            functools.partial(head_kernel, dp_size, heads_size, kv_index, kv_local, width, block_tokens, chunk, fine),
+            functools.partial(head_kernel, dp_size, heads_size, kv_index, kv_local, width, block_tokens, chunk, fine, sub),
             out_shape=(
                 *[
                     jax.ShapeDtypeStruct((2, part_rows, head_dim), bf16 if step else f32)
@@ -293,9 +296,12 @@
                 pltpu.VMEM((cart_rows * kv_local, head_dim), f32),
                 pltpu.VMEM((all_keys, head_dim), bf16),
                 pltpu.VMEM((all_keys, head_dim), bf16),
+                pltpu.VMEM((head_dim, all_keys), bf16),
                 pltpu.VMEM((2, all_keys, rows), f32),
                 pltpu.VMEM((2, all_keys, rows), f32),
                 pltpu.VMEM((2, all_keys, rows), f32),
+                pltpu.VMEM((all_keys, rows), bf16),
+                pltpu.VMEM((all_keys, rows), bf16),
                 pltpu.VMEM((all_keys, head_dim), f32),
                 pltpu.VMEM((all_keys, head_dim), f32),
                 pltpu.VMEM((rows, head_dim), f32),

time: 51.3 us -> 50.6 us (0.986)
  Pallas kernels: 29.7 us -> 28.9 us
    pallas_call x2, Pallas kernels: 23.5 us -> 22.8 us  [on_device(): pl.pallas_call(functools.partial(head_kernel, dp_size, heads_size, kv_ind...]
where the time goes in v5:
time: 50.6 us; the launch traced here: 49.8 us
  Pallas kernels  28.9 us (57%)
  starting transfers between devices  11.5 us (23%)
  waiting for transfers between devices  6.53 us (13%)
  local copies, waits for them, and re-layouts  2.12 us (4%)
  between operations  0.72 us (1%)
    pallas_call x2, Pallas kernels, on_device(): pl.pallas_call(functools.partial(head_kernel, dp_size, heads_size, kv_ind...  22.8 us
    ppermute x9, starting transfers between devices, shift(): lax.ppermute(values, axis, [(source, (source + step) % size) for source i...  11.5 us
    ppermute x9, waiting for transfers between devices, shift(): lax.ppermute(values, axis, [(source, (source + step) % size) for source i...  6.53 us
    pallas_call x1, Pallas kernels, on_device(): pl.pallas_call(functools.partial(place_kernel, heads_size), out_shape=jax...  2.23 us
    unnamed x18, local copies, waits for them, and re-layouts  2.12 us
    pallas_call x1, Pallas kernels, on_device(): pl.pallas_call(functools.partial(cart_kernel, kv_local), out_shape=jax.Sh...  2.04 us
    pallas_call x1, Pallas kernels, on_device(): pl.pallas_call(sum_kernel, out_shape=jax.ShapeDtypeStruct((2, part_rows,...  1.89 us
  transfers between devices with their start and end apart: 9, of which 2 were waited for; matrix products, arithmetic and copies ran while one was open for 0% of the time, Pallas kernels for 32%

profile of v5, /device:TPU:0, one launch (start us, length us, event | category | flops | bytes accessed | tf_op | source)
XLA Modules:
  0.0 49.8 jit_solution(17920492842518247180)
XLA Ops:
  0.6 11.0 %head_grads.2 = (f32[2,256,128]{2,1,0:T(8,128)}, bf16[2,256,128]{2,1,0:T(8,128)(2,1)}, bf16[2,256,128]{2,1,0:T(8,128)(2,1)}, bf16[2,256,128]{2,1,0:T(8,128)(2,1)...) custom-call(bf16[4096,128]{1,0:T(8,128)(2,1)} %bitcast.9, bf16[4096,128]{1,0:T(8,128)(2,1)} %bitcast.11, ...), custom_call_target="tpu_custom_call" | custom-call | flops 6710886400 | bytes 5242880 | tf_op jit(solution)/shard_map/head_grads/pallas_call | solution.py:284
  11.7 3.1 %collective-permute-start = (bf16[2,256,128]{2,1,0:T(8,128)(2,1)}, bf16[2,256,128]{2,1,0:T(8,128)(2,1)S(1)}, u32[]{:S(2)}, u32[]{:S(2)}) collective-permute-start(bf16[2,256,128]{2,1,0:T(8,128)(2,1)} %get-tuple-element.22), channel_id=1, source_target_pairs={{0,4},{4,8},{8,12},{12,0},{1,5},{5,9},{9,13},{13,1},{2,6},{6,10},{... | collective-permute-start | bytes 393224 | tf_op jit(solution)/shard_map/ppermute | solution.py:251
  14.7 2.6 %collective-permute-start.1 = (bf16[2,256,128]{2,1,0:T(8,128)(2,1)}, bf16[2,256,128]{2,1,0:T(8,128)(2,1)S(1)}, u32[]{:S(2)}, u32[]{:S(2)}) collective-permute-start(bf16[2,256,128]{2,1,0:T(8,128)(2,1)} %get-tuple-element.23), channel_id=1, source_target_pairs={{0,8},{4,12},{8,0},{12,4},{1,9},{5,13},{9,1},{13,5},{2,10},{6,14},... | collective-permute-start | bytes 393224 | tf_op jit(solution)/shard_map/ppermute | solution.py:251
  17.3 1.3 %collective-permute-start.2 = (bf16[2,256,128]{2,1,0:T(8,128)(2,1)}, bf16[2,256,128]{2,1,0:T(8,128)(2,1)S(1)}, u32[]{:S(2)}, u32[]{:S(2)}) collective-permute-start(bf16[2,256,128]{2,1,0:T(8,128)(2,1)} %get-tuple-element.24), channel_id=1, source_target_pairs={{0,12},{4,0},{8,4},{12,8},{1,13},{5,1},{9,5},{13,9},{2,14},{6,2},{... | collective-permute-start | bytes 393224 | tf_op jit(solution)/shard_map/ppermute | solution.py:251
  18.7 11.8 %head_grads.3 = (f32[2,256,128]{2,1,0:T(8,128)}, bf16[2,256,128]{2,1,0:T(8,128)(2,1)}, bf16[2,256,128]{2,1,0:T(8,128)(2,1)}, bf16[2,256,128]{2,1,0:T(8,128)(2,1)...) custom-call(bf16[4096,128]{1,0:T(8,128)(2,1)} %bitcast.10, ...), custom_call_target="tpu_custom_call" | custom-call | flops 6710886400 | bytes 5242880 | tf_op jit(solution)/shard_map/head_grads/pallas_call | solution.py:284
  30.4 0.1 collective-permute-start.6
  30.5 1.6 %collective-permute-start.7 = (bf16[64,2048]{1,0:T(8,128)(2,1)}, bf16[64,2048]{1,0:T(8,128)(2,1)S(1)}, u32[]{:S(2)}, u32[]{:S(2)}) collective-permute-start(bf16[64,2048]{1,0:T(8,128)(2,1)} %get-tuple-element.36), channel_id=1, source_target_pairs={{0,2},{1,3},{2,0},{3,1},{4,6},{5,7},{6,4},{7,5},{8,10},{9,11},{10,... | collective-permute-start | bytes 786440 | tf_op jit(solution)/shard_map/ppermute | solution.py:251
  32.0 0.0 collective-permute-done.refs_1_.refs_3_
  32.1 1.4 %collective-permute-start.8 = (bf16[64,2048]{1,0:T(8,128)(2,1)}, bf16[64,2048]{1,0:T(8,128)(2,1)S(1)}, u32[]{:S(2)}, u32[]{:S(2)}) collective-permute-start(bf16[64,2048]{1,0:T(8,128)(2,1)} %get-tuple-element.37), channel_id=1, source_target_pairs={{0,3},{1,0},{2,1},{3,2},{4,7},{5,4},{6,5},{7,6},{8,11},{9,8},{10,9... | collective-permute-start | bytes 786440 | tf_op jit(solution)/shard_map/ppermute | solution.py:251
  33.4 0.0 collective-permute-done.1.refs_2_.refs_4_
  33.4 0.0 collective-permute-done.2.refs_3_.refs_5_
  33.5 0.0 copy-start.5
  33.5 0.0 copy-done.3
  33.5 0.6 %copy-done.4 = bf16[2,256,128]{2,1,0:T(8,128)(2,1)} copy-done((bf16[2,256,128]{2,1,0:T(8,128)(2,1)}, bf16[2,256,128]{2,1,0:T(8,128)(2,1)S(1)}, u32[]{:S(2)}) %copy-start.4) | copy-done | bytes 131096
  34.1 0.1 copy-done.5
  34.2 0.7 %collective-permute-start.3 = (bf16[2,256,128]{2,1,0:T(8,128)(2,1)}, bf16[2,256,128]{2,1,0:T(8,128)(2,1)S(1)}, u32[]{:S(2)}, u32[]{:S(2)}) collective-permute-start(bf16[2,256,128]{2,1,0:T(8,128)(2,1)} %get-tuple-element.31), channel_id=1, source_target_pairs={{0,4},{4,8},{8,12},{12,0},{1,5},{5,9},{9,13},{13,1},{2,6},{6,10},{... | collective-permute-start | bytes 393224 | tf_op jit(solution)/shard_map/ppermute | solution.py:251
  34.8 0.3 collective-permute-start.4
  35.2 3.5 %collective-permute-done.6.refs_1_ = bf16[64,2048]{1,0:T(8,128)(2,1)S(1)} collective-permute-done((bf16[64,2048]{1,0:T(8,128)(2,1)}, bf16[64,2048]{1,0:T(8,128)(2,1)S(1)}, u32[]{:S(2)}, u32[]{:S(2)}) %collective-permute-start.6) | collective-permute-done | bytes 262176 | tf_op jit(solution)/shard_map/ppermute | solution.py:251
  38.7 0.5 collective-permute-start.5
  39.1 1.9 %cart_sum.1.refs_4_.refs_0_ = f32[2,256,128]{2,1,0:T(8,128)} custom-call(f32[2,256,128]{2,1,0:T(8,128)} %get-tuple-element.21.refs_0_, bf16[2,256,128]{2,1,0:T(8,128)(2,1)} %copy-done.3, bf16[2,256,128]{2,1,0:T(8,128)(2,1)} %copy-done.4, bf16[2,256,128]{2,1,0:T(8,128)(2,1)} %copy-done.5), custom_call_target="tpu_custom_call" | custom-call | flops 1048576 | bytes 1048576 | tf_op jit(solution)/shard_map/cart_sum/pallas_call | solution.py:335
  41.0 0.0 collective-permute-done.7.refs_2_
  41.0 3.0 %collective-permute-done.8.refs_3_ = bf16[64,2048]{1,0:T(8,128)(2,1)S(1)} collective-permute-done((bf16[64,2048]{1,0:T(8,128)(2,1)}, bf16[64,2048]{1,0:T(8,128)(2,1)S(1)}, u32[]{:S(2)}, u32[]{:S(2)}) %collective-permute-start.8) | collective-permute-done | bytes 262176 | tf_op jit(solution)/shard_map/ppermute | solution.py:251
  44.0 0.7 %copy-done.2 = bf16[64,2048]{1,0:T(8,128)(2,1)} copy-done((bf16[64,2048]{1,0:T(8,128)(2,1)}, bf16[64,2048]{1,0:T(8,128)(2,1)S(1)}, u32[]{:S(2)}) %copy-start.2) | copy-done | bytes 262168
  44.7 2.2 %place_queries.1.refs_5_ = bf16[64,8192]{1,0:T(8,128)(2,1)} custom-call(bf16[64,2048]{1,0:T(8,128)(2,1)} %get-tuple-element.34.refs_0_, bf16[64,2048]{1,0:T(8,128)(2,1)} %copy-done, bf16[64,2048]{1,0:T(8,128)(2,1)} %copy-done.1, bf16[64,2048]{1,0:T(8,128)(2,1)} %copy-done.2, f32[2,256,128]{2,1,0:T(8,128)} %cart_sum.1.refs_4_.refs_0_), custom_call_target="tpu_custom_call" | custom-call | flops 1048576 | bytes 2097152 | tf_op jit(solution)/shard_map/place_queries/pallas_call | solution.py:344
  47.0 0.0 collective-permute-done.3.refs_2_
  47.0 0.0 collective-permute-done.4.refs_3_
  47.0 0.0 collective-permute-done.5.refs_4_
  47.0 0.0 copy-start.8
  47.0 0.6 %copy-done.6 = bf16[2,256,128]{2,1,0:T(8,128)(2,1)} copy-done((bf16[2,256,128]{2,1,0:T(8,128)(2,1)}, bf16[2,256,128]{2,1,0:T(8,128)(2,1)S(1)}, u32[]{:S(2)}) %copy-start.6) | copy-done | bytes 131096
  47.6 0.0 copy-done.7
  47.7 0.1 copy-done.8
  47.7 2.0 %cart_grads.1 = f32[1024,128]{1,0:T(8,128)} custom-call(f32[2,256,128]{2,1,0:T(8,128)} %cart_sum.1.refs_4_.refs_0_, f32[2,256,128]{2,1,0:T(8,128)} %get-tuple-element.27.refs_1_, bf16[2,256,128]{2,1,0:T(8,128)(2,1)} %copy-done.6, bf16[2,256,128]{2,1,0:T(8,128)(2,1)} %copy-done.7, bf16[2,256,128]{2,1,0:T(8,128)(2,1)} %copy-done.8, ...), custom_call_target="tpu_custom_call" | custom-call | flops 1048576 | bytes 2097152 | tf_op jit(solution)/shard_map/cart_grads/pallas_call | solution.py:353
  (10 shorter events, 0.0 us)
Async XLA Ops:
  11.7 20.4 %collective-permute-start = (bf16[2,256,128]{2,1,0:T(8,128)(2,1)}, bf16[2,256,128]{2,1,0:T(8,128)(2,1)S(1)}, u32[]{:S(2)}, u32[]{:S(2)}) collective-permute-start(bf16[2,256,128]{2,1,0:T(8,128)(2,1)} %get-tuple-element.22), channel_id=1, source_target_pairs={{0,4},{4,8},{8,12},{12,0},{1,5},{5,9},{9,13},{13,1},{2,6},{6,10},{... | collective-permute-start | bytes 393224 | tf_op jit(solution)/shard_map/ppermute | solution.py:251
  14.7 18.7 %collective-permute-start.1 = (bf16[2,256,128]{2,1,0:T(8,128)(2,1)}, bf16[2,256,128]{2,1,0:T(8,128)(2,1)S(1)}, u32[]{:S(2)}, u32[]{:S(2)}) collective-permute-start(bf16[2,256,128]{2,1,0:T(8,128)(2,1)} %get-tuple-element.23), channel_id=1, source_target_pairs={{0,8},{4,12},{8,0},{12,4},{1,9},{5,13},{9,1},{13,5},{2,10},{6,14},... | collective-permute-start | bytes 393224 | tf_op jit(solution)/shard_map/ppermute | solution.py:251
  17.3 16.1 %collective-permute-start.2 = (bf16[2,256,128]{2,1,0:T(8,128)(2,1)}, bf16[2,256,128]{2,1,0:T(8,128)(2,1)S(1)}, u32[]{:S(2)}, u32[]{:S(2)}) collective-permute-start(bf16[2,256,128]{2,1,0:T(8,128)(2,1)} %get-tuple-element.24), channel_id=1, source_target_pairs={{0,12},{4,0},{8,4},{12,8},{1,13},{5,1},{9,5},{13,9},{2,14},{6,2},{... | collective-permute-start | bytes 393224 | tf_op jit(solution)/shard_map/ppermute | solution.py:251
  30.4 8.3 %collective-permute-start.6 = (bf16[64,2048]{1,0:T(8,128)(2,1)}, bf16[64,2048]{1,0:T(8,128)(2,1)S(1)}, u32[]{:S(2)}, u32[]{:S(2)}) collective-permute-start(bf16[64,2048]{1,0:T(8,128)(2,1)} %get-tuple-element.35), channel_id=1, source_target_pairs={{0,1},{1,2},{2,3},{3,0},{4,5},{5,6},{6,7},{7,4},{8,9},{9,10},{10,1... | collective-permute-start | bytes 786440 | tf_op jit(solution)/shard_map/ppermute | solution.py:251
  30.5 10.5 %collective-permute-start.7 = (bf16[64,2048]{1,0:T(8,128)(2,1)}, bf16[64,2048]{1,0:T(8,128)(2,1)S(1)}, u32[]{:S(2)}, u32[]{:S(2)}) collective-permute-start(bf16[64,2048]{1,0:T(8,128)(2,1)} %get-tuple-element.36), channel_id=1, source_target_pairs={{0,2},{1,3},{2,0},{3,1},{4,6},{5,7},{6,4},{7,5},{8,10},{9,11},{10,... | collective-permute-start | bytes 786440 | tf_op jit(solution)/shard_map/ppermute | solution.py:251
  32.1 1.4 %copy-start.3 = (bf16[2,256,128]{2,1,0:T(8,128)(2,1)}, bf16[2,256,128]{2,1,0:T(8,128)(2,1)S(1)}, u32[]{:S(2)}) copy-start(bf16[2,256,128]{2,1,0:T(8,128)(2,1)S(1)} %collective-permute-done.refs_1_.refs_3_) | copy-start | bytes 393220
  32.1 12.0 %collective-permute-start.8 = (bf16[64,2048]{1,0:T(8,128)(2,1)}, bf16[64,2048]{1,0:T(8,128)(2,1)S(1)}, u32[]{:S(2)}, u32[]{:S(2)}) collective-permute-start(bf16[64,2048]{1,0:T(8,128)(2,1)} %get-tuple-element.37), channel_id=1, source_target_pairs={{0,3},{1,0},{2,1},{3,2},{4,7},{5,4},{6,5},{7,6},{8,11},{9,8},{10,9... | collective-permute-start | bytes 786440 | tf_op jit(solution)/shard_map/ppermute | solution.py:251
  33.4 0.6 %copy-start.4 = (bf16[2,256,128]{2,1,0:T(8,128)(2,1)}, bf16[2,256,128]{2,1,0:T(8,128)(2,1)S(1)}, u32[]{:S(2)}) copy-start(bf16[2,256,128]{2,1,0:T(8,128)(2,1)S(1)} %collective-permute-done.1.refs_2_.refs_4_) | copy-start | bytes 393220
  33.5 0.7 %copy-start.5 = (bf16[2,256,128]{2,1,0:T(8,128)(2,1)}, bf16[2,256,128]{2,1,0:T(8,128)(2,1)S(1)}, u32[]{:S(2)}) copy-start(bf16[2,256,128]{2,1,0:T(8,128)(2,1)S(1)} %collective-permute-done.2.refs_3_.refs_5_) | copy-start | bytes 393220
  34.2 12.8 %collective-permute-start.3 = (bf16[2,256,128]{2,1,0:T(8,128)(2,1)}, bf16[2,256,128]{2,1,0:T(8,128)(2,1)S(1)}, u32[]{:S(2)}, u32[]{:S(2)}) collective-permute-start(bf16[2,256,128]{2,1,0:T(8,128)(2,1)} %get-tuple-element.31), channel_id=1, source_target_pairs={{0,4},{4,8},{8,12},{12,0},{1,5},{5,9},{9,13},{13,1},{2,6},{6,10},{... | collective-permute-start | bytes 393224 | tf_op jit(solution)/shard_map/ppermute | solution.py:251
  34.8 12.2 %collective-permute-start.4 = (bf16[2,256,128]{2,1,0:T(8,128)(2,1)}, bf16[2,256,128]{2,1,0:T(8,128)(2,1)S(1)}, u32[]{:S(2)}, u32[]{:S(2)}) collective-permute-start(bf16[2,256,128]{2,1,0:T(8,128)(2,1)} %get-tuple-element.32), channel_id=1, source_target_pairs={{0,8},{4,12},{8,0},{12,4},{1,9},{5,13},{9,1},{13,5},{2,10},{6,14},... | collective-permute-start | bytes 393224 | tf_op jit(solution)/shard_map/ppermute | solution.py:251
  38.7 2.3 %copy-start = (bf16[64,2048]{1,0:T(8,128)(2,1)}, bf16[64,2048]{1,0:T(8,128)(2,1)S(1)}, u32[]{:S(2)}) copy-start(bf16[64,2048]{1,0:T(8,128)(2,1)S(1)} %collective-permute-done.6.refs_1_) | copy-start | bytes 786436
  38.7 8.3 %collective-permute-start.5 = (bf16[2,256,128]{2,1,0:T(8,128)(2,1)}, bf16[2,256,128]{2,1,0:T(8,128)(2,1)S(1)}, u32[]{:S(2)}, u32[]{:S(2)}) collective-permute-start(bf16[2,256,128]{2,1,0:T(8,128)(2,1)} %get-tuple-element.33), channel_id=1, source_target_pairs={{0,12},{4,0},{8,4},{12,8},{1,13},{5,1},{9,5},{13,9},{2,14},{6,2},{... | collective-permute-start | bytes 393224 | tf_op jit(solution)/shard_map/ppermute | solution.py:251
  41.0 3.0 %copy-start.1 = (bf16[64,2048]{1,0:T(8,128)(2,1)}, bf16[64,2048]{1,0:T(8,128)(2,1)S(1)}, u32[]{:S(2)}) copy-start(bf16[64,2048]{1,0:T(8,128)(2,1)S(1)} %collective-permute-done.7.refs_2_) | copy-start | bytes 786436
  44.0 0.7 %copy-start.2 = (bf16[64,2048]{1,0:T(8,128)(2,1)}, bf16[64,2048]{1,0:T(8,128)(2,1)S(1)}, u32[]{:S(2)}) copy-start(bf16[64,2048]{1,0:T(8,128)(2,1)S(1)} %collective-permute-done.8.refs_3_) | copy-start | bytes 786436
  47.0 0.7 %copy-start.6 = (bf16[2,256,128]{2,1,0:T(8,128)(2,1)}, bf16[2,256,128]{2,1,0:T(8,128)(2,1)S(1)}, u32[]{:S(2)}) copy-start(bf16[2,256,128]{2,1,0:T(8,128)(2,1)S(1)} %collective-permute-done.3.refs_2_) | copy-start | bytes 393220
  47.0 0.7 %copy-start.7 = (bf16[2,256,128]{2,1,0:T(8,128)(2,1)}, bf16[2,256,128]{2,1,0:T(8,128)(2,1)S(1)}, u32[]{:S(2)}) copy-start(bf16[2,256,128]{2,1,0:T(8,128)(2,1)S(1)} %collective-permute-done.4.refs_3_) | copy-start | bytes 393220
  47.0 0.7 %copy-start.8 = (bf16[2,256,128]{2,1,0:T(8,128)(2,1)}, bf16[2,256,128]{2,1,0:T(8,128)(2,1)S(1)}, u32[]{:S(2)}) copy-start(bf16[2,256,128]{2,1,0:T(8,128)(2,1)S(1)} %collective-permute-done.5.refs_4_) | copy-start | bytes 393220

commit v6 on v5

--- a/solution.py
+++ b/solution.py
@@ -27,7 +27,7 @@
     return op(values.reshape(rows // 8, 8, columns), axis=0)
 
 
-def head_kernel(dp_size, heads_size, kv_index, kv_local, width, block_tokens, chunk, fine, sub, *refs):
+def head_kernel(dp_size, heads_size, kv_index, kv_local, width, block_tokens, chunk, sub, *refs):
     last = kv_index == kv_local - 1
     q_ref, g_ref, sk_ref, sv_ref, ck_ref, cv_ref, seg_ref = refs[:7]
     refs = refs[7:]
@@ -37,8 +37,8 @@
     dq_count = heads_size if last else 1
     dq_outs, self_ref, refs = refs[:dq_count], refs[dq_count], refs[dq_count + 1 :]
     (
-        wide_ref, keys_ref, vals_ref, keys_t_ref, s_ref, w_ref, d_ref, p_ref, ds_ref, dk_ref, dv_ref, out_ref, dq_ref,
-        q_in, g_in, sk_in, sv_in, ck_in, cv_in, sems,
+        wide_ref, keys_ref, vals_ref, keys_t_ref, s_even, s_odd, w_even, w_odd, d_even, d_odd, p_ref, ds_ref, dk_ref, dv_ref, out_ref, dq_ref,
+        q_rows, g_rows, q_in, g_in, sk_in, sv_in, ck_in, cv_in, sems,
     ) = refs
     head_dim = q_ref.shape[1]
     tokens = seg_ref.shape[1]
@@ -77,113 +77,104 @@
             wide_ref[0 : ref.shape[0], :] = ref[...].astype(f32)
             dst[at : at + count, :] = wide_ref[pl.ds(kv_index, count, stride=kv_local), :].astype(bf16)
 
-    def rows_of(name, ref, block):
-        copies[name, block].wait()
+    def fill_rows(ref, dst, block):
         wide = ref[block * span : (block + 1) * span, :]
-        if kv_local == 1:
-            return wide
-        wide = wide.astype(f32).reshape(block_tokens, kv_local, width, head_dim)
-        return wide[:, kv_index].reshape(rows, head_dim).astype(bf16)
+        if kv_local > 1:
+            wide = wide.astype(f32).reshape(block_tokens, kv_local, width, head_dim)
+            wide = wide[:, kv_index].reshape(rows, head_dim).astype(bf16)
+        dst[block] = wide
 
     first_count = jnp.sum((seg_ref[...] == 0).astype(f32), axis=1, keepdims=True).astype(jnp.int32)
 
-    def limit(block):
-        return -(-(block + 1) * block_tokens // fine) * fine
-
-    def pieces(block):
-        cart = [(start, chunk) for start in range(0, cart_rows, chunk)]
-        return cart + [(cart_rows, limit(block))]
-
-    queries, grads, peaks, stats = {}, {}, {}, {}
-    acc = {}
-
-    def subs(start, size):
-        return [slice(at, at + sub) for at in range(start, start + size, sub)]
-
-    def open_scores(block):
-        queries[block] = rows_of("q", q_in, block)
-        token = (lax.broadcasted_iota(jnp.int32, (1, rows), 1) + block * rows) // width
-        begin = jnp.where(token >= first_count, first_count, 0)
-        acc["peak"] = jnp.full((8, rows), masked_score, f32)
-        acc["token"], acc["begin"] = token, begin
-
-    def step_scores(block, start, size):
-        s_ref[block % 2, start : start + size, :] = dot_nt(keys_ref[start : start + size, :], queries[block])
-        for at in subs(start, size):
-            score = s_ref[block % 2, at, :]
-            if start >= cart_rows:
-                key_at = lax.broadcasted_iota(jnp.int32, (sub, rows), 0) + (at.start - cart_rows)
-                score = jnp.where((key_at >= acc["begin"]) & (key_at <= acc["token"]), score, masked_score)
-                s_ref[block % 2, at, :] = score
-            acc["peak"] = jnp.maximum(acc["peak"], fold_rows(score, jnp.max))
-
-    def close_scores(block):
-        peaks[block] = jnp.max(acc["peak"], axis=0, keepdims=True)
-
-    def open_weights(block):
-        grads[block] = rows_of("g", g_in, block)
-        acc["total"] = jnp.zeros((8, rows), f32)
-        acc["center"] = jnp.zeros((8, rows), f32)
-
-    def step_weights(block, start, size):
-        d_ref[block % 2, start : start + size, :] = dot_nt(vals_ref[start : start + size, :], grads[block])
-        for at in subs(start, size):
-            weight = jnp.exp2((s_ref[block % 2, at, :] - peaks[block]) * scale2)
-            w_ref[block % 2, at, :] = weight
-            acc["total"] = acc["total"] + fold_rows(weight, jnp.sum)
-            acc["center"] = acc["center"] + fold_rows(weight * d_ref[block % 2, at, :], jnp.sum)
-
-    def close_weights(block):
-        share = 1.0 / jnp.sum(acc["total"], axis=0, keepdims=True)
-        stats[block] = share, jnp.sum(acc["center"], axis=0, keepdims=True) * share
-
-    def open_grads(block):
-        acc["dq"] = jnp.zeros((head_dim, rows), f32)
-
-    def step_grads(block, start, size):
-        share, center = stats[block]
-        for at in subs(start, size):
-            prob = w_ref[block % 2, at, :] * share
-            p_ref[at, :] = prob.astype(bf16)
-            ds_ref[at, :] = (prob * (d_ref[block % 2, at, :] - center)).astype(bf16)
-        at = slice(start, start + size)
-        old = size if start < cart_rows else (limit(block - 1) if block else 0)
-        old = old if block else 0
-        for ref, left, right in ((dv_ref, p_ref, grads[block]), (dk_ref, ds_ref, queries[block])):
-            part = dot_nn(left[at, :], right)
-            if old:
-                ref[start : start + old, :] += part[:old]
-            if old < size:
-                ref[start + old : start + size, :] = part[old:]
-        acc["dq"] = acc["dq"] + dot_nn(keys_t_ref[:, at], ds_ref[at, :])
-
-    def close_grads(block):
-        out_ref[...] = (acc["dq"] * scale).T
-        for head in range(width):
-            dq_ref[block * block_tokens : (block + 1) * block_tokens, head * head_dim : (head + 1) * head_dim] = (
-                out_ref[pl.ds(head, block_tokens, stride=width), :].astype(bf16)
-            )
-
+    s_refs, w_refs, d_refs = (s_even, s_odd), (w_even, w_odd), (d_even, d_odd)
+
+    def chunk_step(turn, live, carry, start, size, own):
+        peak, peak8, total8, center8, share, center = carry
+        scoring, weighing, grading = live
+        whole = pl.ds(start, size)
+        if grading:
+            block, slot = turn - 2, (turn - 2) % 2
+            for at in range(0, size, sub):
+                here = pl.ds(start + at, sub)
+                prob = w_refs[slot][here, :] * share
+                p_ref[here, :] = prob.astype(bf16)
+                ds_ref[here, :] = (prob * (d_refs[slot][here, :] - center)).astype(bf16)
+        if scoring:
+            s_refs[turn % 2][whole, :] = dot_nt(keys_ref[whole, :], q_rows[turn])
+        if weighing:
+            d_refs[(turn - 1) % 2][whole, :] = dot_nt(vals_ref[whole, :], g_rows[turn - 1])
+        if grading:
+            dv_ref[whole, :] += dot_nn(p_ref[whole, :], g_rows[block])
+            dk_ref[whole, :] += dot_nn(ds_ref[whole, :], q_rows[block])
+        if weighing:
+            slot = (turn - 1) % 2
+            for at in range(0, size, sub):
+                here = pl.ds(start + at, sub)
+                weight = jnp.exp2((s_refs[slot][here, :] - peak) * scale2)
+                w_refs[slot][here, :] = weight
+                total8 = total8 + fold_rows(weight, jnp.sum)
+                center8 = center8 + fold_rows(weight * d_refs[slot][here, :], jnp.sum)
+        if scoring:
+            slot = turn % 2
+            if own:
+                token = (lax.broadcasted_iota(jnp.int32, (1, rows), 1) + turn * rows) // width
+                begin = jnp.where(token >= first_count, first_count, 0)
+            for at in range(0, size, sub):
+                here = pl.ds(start + at, sub)
+                score = s_refs[slot][here, :]
+                if own:
+                    key_at = lax.broadcasted_iota(jnp.int32, (sub, rows), 0) + at
+                    score = jnp.where((key_at >= begin) & (key_at <= token), score, masked_score)
+                    s_refs[slot][here, :] = score
+                peak8 = jnp.maximum(peak8, fold_rows(score, jnp.max))
+        return peak, peak8, total8, center8, share, center
+
+    def run_turn(turn, live, peak, share, center):
+        if live[0]:
+            fill_rows(q_in, q_rows, turn)
+        if live[1]:
+            fill_rows(g_in, g_rows, turn - 1)
+        carry = (
+            peak, jnp.full((8, rows), masked_score, f32), jnp.zeros((8, rows), f32), jnp.zeros((8, rows), f32),
+            share, center,
+        )
+
+        def step(index, carry):
+            return chunk_step(turn, live, carry, pl.multiple_of(index * chunk, chunk), chunk, False)
+
+        carry = lax.fori_loop(0, cart_rows // chunk, step, carry)
+        carry = chunk_step(turn, live, carry, cart_rows, tokens, True)
+        _, peak8, total8, center8, _, _ = carry
+        if live[2]:
+            out_ref[...] = (dot_nn(keys_t_ref[...], ds_ref[...]) * scale).T
+            at = slice((turn - 2) * block_tokens, (turn - 1) * block_tokens)
+            for head in range(width):
+                dq_ref[at, head * head_dim : (head + 1) * head_dim] = (
+                    out_ref[pl.ds(head, block_tokens, stride=width), :].astype(bf16)
+                )
+        peak = jnp.max(peak8, axis=0, keepdims=True)
+        if live[1]:
+            share = 1.0 / jnp.sum(total8, axis=0, keepdims=True)
+            center = jnp.sum(center8, axis=0, keepdims=True) * share
+        return peak, share, center
+
+    dk_ref[...] = jnp.zeros_like(dk_ref)
+    dv_ref[...] = jnp.zeros_like(dv_ref)
     pick("ck", ck_in, keys_ref, 0)
     pick("sk", sk_in, keys_ref, cart_rows)
-    stages = (
-        (2, open_grads, step_grads, close_grads),
-        (1, open_weights, step_weights, close_weights),
-        (0, open_scores, step_scores, close_scores),
-    )
-    for turn in range(blocks + 2):
-        live = [(turn - lag, *calls) for lag, *calls in stages if 0 <= turn - lag < blocks]
-        if turn == 1:
-            pick("cv", cv_in, vals_ref, 0)
-            pick("sv", sv_in, vals_ref, cart_rows)
-            keys_t_ref[...] = keys_ref[...].astype(f32).T.astype(bf16)
-        for block, begin_call, _, _ in live:
-            begin_call(block)
-        for index in range(len(pieces(0))):
-            for block, _, step_call, _ in live:
-                step_call(block, *pieces(block)[index])
-        for block, _, _, end_call in live:
-            end_call(block)
+    copies["q", 0].wait()
+    empty = jnp.zeros((1, rows), f32)
+    state = run_turn(0, (True, False, False), empty, empty, empty)
+    pick("cv", cv_in, vals_ref, 0)
+    pick("sv", sv_in, vals_ref, cart_rows)
+    keys_t_ref[...] = keys_ref[...].astype(f32).T.astype(bf16)
+    for turn in range(1, blocks + 2):
+        live = turn < blocks, turn <= blocks, turn > 1
+        if live[0]:
+            copies["q", turn].wait()
+        if live[1]:
+            copies["g", turn - 1].wait()
+        state = run_turn(turn, live, *state)
 
     part_rows = cart_rows // dp_size
     me = lax.axis_index("dp")
@@ -258,7 +249,6 @@
     width = heads_local // kv_local
     block_tokens = 64
     chunk = 256
-    fine = 128
     sub = 16
     all_keys = cart_rows + tokens
     rows = block_tokens * width
@@ -282,7 +272,7 @@
             ]
         before = query_list + self_list
         outs = pl.pallas_call(
-            functools.partial(head_kernel, dp_size, heads_size, kv_index, kv_local, width, block_tokens, chunk, fine, sub),
+            functools.partial(head_kernel, dp_size, heads_size, kv_index, kv_local, width, block_tokens, chunk, sub),
             out_shape=(
                 *[
                     jax.ShapeDtypeStruct((2, part_rows, head_dim), bf16 if step else f32)
@@ -297,15 +287,15 @@
                 pltpu.VMEM((all_keys, head_dim), bf16),
                 pltpu.VMEM((all_keys, head_dim), bf16),
                 pltpu.VMEM((head_dim, all_keys), bf16),
-                pltpu.VMEM((2, all_keys, rows), f32),
-                pltpu.VMEM((2, all_keys, rows), f32),
-                pltpu.VMEM((2, all_keys, rows), f32),
+                *[pltpu.VMEM((all_keys, rows), f32) for _ in range(6)],
                 pltpu.VMEM((all_keys, rows), bf16),
                 pltpu.VMEM((all_keys, rows), bf16),
                 pltpu.VMEM((all_keys, head_dim), f32),
                 pltpu.VMEM((all_keys, head_dim), f32),
                 pltpu.VMEM((rows, head_dim), f32),
                 pltpu.VMEM((tokens, columns), bf16),
+                pltpu.VMEM((blocks, rows, head_dim), bf16),
+                pltpu.VMEM((blocks, rows, head_dim), bf16),
                 *[pltpu.VMEM(array.shape, bf16) for array in flat],
                 pltpu.SemaphoreType.DMA((4 + 2 * blocks,)),
             ],

time: 50.6 us -> 62.1 us (1.23)
  Pallas kernels: 28.9 us -> 40.5 us
    pallas_call x2, Pallas kernels: 22.8 us -> 34.3 us  [on_device(): pl.pallas_call(functools.partial(head_kernel, dp_size, heads_size, kv_ind...]
  transfers between devices with their start and end apart: 9 -> 9, of which waited for: 2 -> 2; matrix products, arithmetic and copies ran while one was open for 0% -> 0% of each run, Pallas kernels for 32% -> 35%
where the time goes in v6:
time: 62.1 us; the launch traced here: 61.3 us
  Pallas kernels  40.5 us (65%)
  starting transfers between devices  11.5 us (19%)
  waiting for transfers between devices  6.55 us (11%)
  local copies, waits for them, and re-layouts  2.12 us (3%)
  between operations  0.72 us (1%)
    pallas_call x2, Pallas kernels, on_device(): pl.pallas_call(functools.partial(head_kernel, dp_size, heads_size, kv_ind...  34.3 us
    ppermute x9, starting transfers between devices, shift(): lax.ppermute(values, axis, [(source, (source + step) % size) for source i...  11.5 us
    ppermute x9, waiting for transfers between devices, shift(): lax.ppermute(values, axis, [(source, (source + step) % size) for source i...  6.55 us
    pallas_call x1, Pallas kernels, on_device(): pl.pallas_call(functools.partial(place_kernel, heads_size), out_shape=jax...  2.23 us
    unnamed x18, local copies, waits for them, and re-layouts  2.12 us
    pallas_call x1, Pallas kernels, on_device(): pl.pallas_call(functools.partial(cart_kernel, kv_local), out_shape=jax.Sh...  2.04 us
    pallas_call x1, Pallas kernels, on_device(): pl.pallas_call(sum_kernel, out_shape=jax.ShapeDtypeStruct((2, part_rows,...  1.89 us
  transfers between devices with their start and end apart: 9, of which 2 were waited for; matrix products, arithmetic and copies ran while one was open for 0% of the time, Pallas kernels for 35%

profile of v6, /device:TPU:0, one launch (start us, length us, event | category | flops | bytes accessed | tf_op | source)
XLA Modules:
  0.0 61.3 jit_solution(3692279293480455990)
XLA Ops:
  0.6 16.8 %head_grads.2 = (f32[2,256,128]{2,1,0:T(8,128)}, bf16[2,256,128]{2,1,0:T(8,128)(2,1)}, bf16[2,256,128]{2,1,0:T(8,128)(2,1)}, bf16[2,256,128]{2,1,0:T(8,128)(2,1)...) custom-call(bf16[4096,128]{1,0:T(8,128)(2,1)} %bitcast.9, bf16[4096,128]{1,0:T(8,128)(2,1)} %bitcast.11, ...), custom_call_target="tpu_custom_call" | custom-call | flops 6710886400 | bytes 5242880 | tf_op jit(solution)/shard_map/head_grads/pallas_call | solution.py:274
  17.4 3.1 %collective-permute-start = (bf16[2,256,128]{2,1,0:T(8,128)(2,1)}, bf16[2,256,128]{2,1,0:T(8,128)(2,1)S(1)}, u32[]{:S(2)}, u32[]{:S(2)}) collective-permute-start(bf16[2,256,128]{2,1,0:T(8,128)(2,1)} %get-tuple-element.22), channel_id=1, source_target_pairs={{0,4},{4,8},{8,12},{12,0},{1,5},{5,9},{9,13},{13,1},{2,6},{6,10},{... | collective-permute-start | bytes 393224 | tf_op jit(solution)/shard_map/ppermute | solution.py:242
  20.5 2.6 %collective-permute-start.1 = (bf16[2,256,128]{2,1,0:T(8,128)(2,1)}, bf16[2,256,128]{2,1,0:T(8,128)(2,1)S(1)}, u32[]{:S(2)}, u32[]{:S(2)}) collective-permute-start(bf16[2,256,128]{2,1,0:T(8,128)(2,1)} %get-tuple-element.23), channel_id=1, source_target_pairs={{0,8},{4,12},{8,0},{12,4},{1,9},{5,13},{9,1},{13,5},{2,10},{6,14},... | collective-permute-start | bytes 393224 | tf_op jit(solution)/shard_map/ppermute | solution.py:242
  23.1 1.4 %collective-permute-start.2 = (bf16[2,256,128]{2,1,0:T(8,128)(2,1)}, bf16[2,256,128]{2,1,0:T(8,128)(2,1)S(1)}, u32[]{:S(2)}, u32[]{:S(2)}) collective-permute-start(bf16[2,256,128]{2,1,0:T(8,128)(2,1)} %get-tuple-element.24), channel_id=1, source_target_pairs={{0,12},{4,0},{8,4},{12,8},{1,13},{5,1},{9,5},{13,9},{2,14},{6,2},{... | collective-permute-start | bytes 393224 | tf_op jit(solution)/shard_map/ppermute | solution.py:242
  24.5 17.5 %head_grads.3 = (f32[2,256,128]{2,1,0:T(8,128)}, bf16[2,256,128]{2,1,0:T(8,128)(2,1)}, bf16[2,256,128]{2,1,0:T(8,128)(2,1)}, bf16[2,256,128]{2,1,0:T(8,128)(2,1)...) custom-call(bf16[4096,128]{1,0:T(8,128)(2,1)} %bitcast.10, ...), custom_call_target="tpu_custom_call" | custom-call | flops 6710886400 | bytes 5242880 | tf_op jit(solution)/shard_map/head_grads/pallas_call | solution.py:274
  42.0 0.1 collective-permute-start.6
  42.0 1.6 %collective-permute-start.7 = (bf16[64,2048]{1,0:T(8,128)(2,1)}, bf16[64,2048]{1,0:T(8,128)(2,1)S(1)}, u32[]{:S(2)}, u32[]{:S(2)}) collective-permute-start(bf16[64,2048]{1,0:T(8,128)(2,1)} %get-tuple-element.36), channel_id=1, source_target_pairs={{0,2},{1,3},{2,0},{3,1},{4,6},{5,7},{6,4},{7,5},{8,10},{9,11},{10,... | collective-permute-start | bytes 786440 | tf_op jit(solution)/shard_map/ppermute | solution.py:242
  43.6 0.0 collective-permute-done.refs_1_.refs_3_
  43.6 1.4 %collective-permute-start.8 = (bf16[64,2048]{1,0:T(8,128)(2,1)}, bf16[64,2048]{1,0:T(8,128)(2,1)S(1)}, u32[]{:S(2)}, u32[]{:S(2)}) collective-permute-start(bf16[64,2048]{1,0:T(8,128)(2,1)} %get-tuple-element.37), channel_id=1, source_target_pairs={{0,3},{1,0},{2,1},{3,2},{4,7},{5,4},{6,5},{7,6},{8,11},{9,8},{10,9... | collective-permute-start | bytes 786440 | tf_op jit(solution)/shard_map/ppermute | solution.py:242
  45.0 0.0 collective-permute-done.1.refs_2_.refs_4_
  45.0 0.0 collective-permute-done.2.refs_3_.refs_5_
  45.0 0.0 copy-start.5
  45.0 0.6 %copy-done.4 = bf16[2,256,128]{2,1,0:T(8,128)(2,1)} copy-done((bf16[2,256,128]{2,1,0:T(8,128)(2,1)}, bf16[2,256,128]{2,1,0:T(8,128)(2,1)S(1)}, u32[]{:S(2)}) %copy-start.4) | copy-done | bytes 131096
  45.6 0.1 copy-done.5
  45.7 0.7 %collective-permute-start.3 = (bf16[2,256,128]{2,1,0:T(8,128)(2,1)}, bf16[2,256,128]{2,1,0:T(8,128)(2,1)S(1)}, u32[]{:S(2)}, u32[]{:S(2)}) collective-permute-start(bf16[2,256,128]{2,1,0:T(8,128)(2,1)} %get-tuple-element.31), channel_id=1, source_target_pairs={{0,4},{4,8},{8,12},{12,0},{1,5},{5,9},{9,13},{13,1},{2,6},{6,10},{... | collective-permute-start | bytes 393224 | tf_op jit(solution)/shard_map/ppermute | solution.py:242
  46.4 0.3 collective-permute-start.4
  46.7 3.5 %collective-permute-done.6.refs_1_ = bf16[64,2048]{1,0:T(8,128)(2,1)S(1)} collective-permute-done((bf16[64,2048]{1,0:T(8,128)(2,1)}, bf16[64,2048]{1,0:T(8,128)(2,1)S(1)}, u32[]{:S(2)}, u32[]{:S(2)}) %collective-permute-start.6) | collective-permute-done | bytes 262176 | tf_op jit(solution)/shard_map/ppermute | solution.py:242
  50.2 0.4 collective-permute-start.5
  50.7 1.9 %cart_sum.1.refs_4_.refs_0_ = f32[2,256,128]{2,1,0:T(8,128)} custom-call(f32[2,256,128]{2,1,0:T(8,128)} %get-tuple-element.21.refs_0_, bf16[2,256,128]{2,1,0:T(8,128)(2,1)} %copy-done.3, bf16[2,256,128]{2,1,0:T(8,128)(2,1)} %copy-done.4, bf16[2,256,128]{2,1,0:T(8,128)(2,1)} %copy-done.5), custom_call_target="tpu_custom_call" | custom-call | flops 1048576 | bytes 1048576 | tf_op jit(solution)/shard_map/cart_sum/pallas_call | solution.py:325
  52.6 0.0 collective-permute-done.7.refs_2_
  52.6 3.0 %collective-permute-done.8.refs_3_ = bf16[64,2048]{1,0:T(8,128)(2,1)S(1)} collective-permute-done((bf16[64,2048]{1,0:T(8,128)(2,1)}, bf16[64,2048]{1,0:T(8,128)(2,1)S(1)}, u32[]{:S(2)}, u32[]{:S(2)}) %collective-permute-start.8) | collective-permute-done | bytes 262176 | tf_op jit(solution)/shard_map/ppermute | solution.py:242
  55.6 0.0 copy-done.1
  55.6 0.7 %copy-done.2 = bf16[64,2048]{1,0:T(8,128)(2,1)} copy-done((bf16[64,2048]{1,0:T(8,128)(2,1)}, bf16[64,2048]{1,0:T(8,128)(2,1)S(1)}, u32[]{:S(2)}) %copy-start.2) | copy-done | bytes 262168
  56.3 2.2 %place_queries.1.refs_5_ = bf16[64,8192]{1,0:T(8,128)(2,1)} custom-call(bf16[64,2048]{1,0:T(8,128)(2,1)} %get-tuple-element.34.refs_0_, bf16[64,2048]{1,0:T(8,128)(2,1)} %copy-done, bf16[64,2048]{1,0:T(8,128)(2,1)} %copy-done.1, bf16[64,2048]{1,0:T(8,128)(2,1)} %copy-done.2, f32[2,256,128]{2,1,0:T(8,128)} %cart_sum.1.refs_4_.refs_0_), custom_call_target="tpu_custom_call" | custom-call | flops 1048576 | bytes 2097152 | tf_op jit(solution)/shard_map/place_queries/pallas_call | solution.py:334
  58.5 0.0 collective-permute-done.3.refs_2_
  58.5 0.0 collective-permute-done.4.refs_3_
  58.5 0.0 copy-start.7
  58.5 0.0 collective-permute-done.5.refs_4_
  58.6 0.6 %copy-done.6 = bf16[2,256,128]{2,1,0:T(8,128)(2,1)} copy-done((bf16[2,256,128]{2,1,0:T(8,128)(2,1)}, bf16[2,256,128]{2,1,0:T(8,128)(2,1)S(1)}, u32[]{:S(2)}) %copy-start.6) | copy-done | bytes 131096
  59.2 0.0 copy-done.7
  59.2 0.1 copy-done.8
  59.3 2.0 %cart_grads.1 = f32[1024,128]{1,0:T(8,128)} custom-call(f32[2,256,128]{2,1,0:T(8,128)} %cart_sum.1.refs_4_.refs_0_, f32[2,256,128]{2,1,0:T(8,128)} %get-tuple-element.27.refs_1_, bf16[2,256,128]{2,1,0:T(8,128)(2,1)} %copy-done.6, bf16[2,256,128]{2,1,0:T(8,128)(2,1)} %copy-done.7, bf16[2,256,128]{2,1,0:T(8,128)(2,1)} %copy-done.8, ...), custom_call_target="tpu_custom_call" | custom-call | flops 1048576 | bytes 2097152 | tf_op jit(solution)/shard_map/cart_grads/pallas_call | solution.py:343
  (10 shorter events, 0.0 us)
Async XLA Ops:
  17.4 26.2 %collective-permute-start = (bf16[2,256,128]{2,1,0:T(8,128)(2,1)}, bf16[2,256,128]{2,1,0:T(8,128)(2,1)S(1)}, u32[]{:S(2)}, u32[]{:S(2)}) collective-permute-start(bf16[2,256,128]{2,1,0:T(8,128)(2,1)} %get-tuple-element.22), channel_id=1, source_target_pairs={{0,4},{4,8},{8,12},{12,0},{1,5},{5,9},{9,13},{13,1},{2,6},{6,10},{... | collective-permute-start | bytes 393224 | tf_op jit(solution)/shard_map/ppermute | solution.py:242
  20.5 24.5 %collective-permute-start.1 = (bf16[2,256,128]{2,1,0:T(8,128)(2,1)}, bf16[2,256,128]{2,1,0:T(8,128)(2,1)S(1)}, u32[]{:S(2)}, u32[]{:S(2)}) collective-permute-start(bf16[2,256,128]{2,1,0:T(8,128)(2,1)} %get-tuple-element.23), channel_id=1, source_target_pairs={{0,8},{4,12},{8,0},{12,4},{1,9},{5,13},{9,1},{13,5},{2,10},{6,14},... | collective-permute-start | bytes 393224 | tf_op jit(solution)/shard_map/ppermute | solution.py:242
  23.1 21.9 %collective-permute-start.2 = (bf16[2,256,128]{2,1,0:T(8,128)(2,1)}, bf16[2,256,128]{2,1,0:T(8,128)(2,1)S(1)}, u32[]{:S(2)}, u32[]{:S(2)}) collective-permute-start(bf16[2,256,128]{2,1,0:T(8,128)(2,1)} %get-tuple-element.24), channel_id=1, source_target_pairs={{0,12},{4,0},{8,4},{12,8},{1,13},{5,1},{9,5},{13,9},{2,14},{6,2},{... | collective-permute-start | bytes 393224 | tf_op jit(solution)/shard_map/ppermute | solution.py:242
  42.0 8.3 %collective-permute-start.6 = (bf16[64,2048]{1,0:T(8,128)(2,1)}, bf16[64,2048]{1,0:T(8,128)(2,1)S(1)}, u32[]{:S(2)}, u32[]{:S(2)}) collective-permute-start(bf16[64,2048]{1,0:T(8,128)(2,1)} %get-tuple-element.35), channel_id=1, source_target_pairs={{0,1},{1,2},{2,3},{3,0},{4,5},{5,6},{6,7},{7,4},{8,9},{9,10},{10,1... | collective-permute-start | bytes 786440 | tf_op jit(solution)/shard_map/ppermute | solution.py:242
  42.0 10.5 %collective-permute-start.7 = (bf16[64,2048]{1,0:T(8,128)(2,1)}, bf16[64,2048]{1,0:T(8,128)(2,1)S(1)}, u32[]{:S(2)}, u32[]{:S(2)}) collective-permute-start(bf16[64,2048]{1,0:T(8,128)(2,1)} %get-tuple-element.36), channel_id=1, source_target_pairs={{0,2},{1,3},{2,0},{3,1},{4,6},{5,7},{6,4},{7,5},{8,10},{9,11},{10,... | collective-permute-start | bytes 786440 | tf_op jit(solution)/shard_map/ppermute | solution.py:242
  43.6 1.4 %copy-start.3 = (bf16[2,256,128]{2,1,0:T(8,128)(2,1)}, bf16[2,256,128]{2,1,0:T(8,128)(2,1)S(1)}, u32[]{:S(2)}) copy-start(bf16[2,256,128]{2,1,0:T(8,128)(2,1)S(1)} %collective-permute-done.refs_1_.refs_3_) | copy-start | bytes 393220
  43.6 12.0 %collective-permute-start.8 = (bf16[64,2048]{1,0:T(8,128)(2,1)}, bf16[64,2048]{1,0:T(8,128)(2,1)S(1)}, u32[]{:S(2)}, u32[]{:S(2)}) collective-permute-start(bf16[64,2048]{1,0:T(8,128)(2,1)} %get-tuple-element.37), channel_id=1, source_target_pairs={{0,3},{1,0},{2,1},{3,2},{4,7},{5,4},{6,5},{7,6},{8,11},{9,8},{10,9... | collective-permute-start | bytes 786440 | tf_op jit(solution)/shard_map/ppermute | solution.py:242
  45.0 0.6 %copy-start.4 = (bf16[2,256,128]{2,1,0:T(8,128)(2,1)}, bf16[2,256,128]{2,1,0:T(8,128)(2,1)S(1)}, u32[]{:S(2)}) copy-start(bf16[2,256,128]{2,1,0:T(8,128)(2,1)S(1)} %collective-permute-done.1.refs_2_.refs_4_) | copy-start | bytes 393220
  45.0 0.7 %copy-start.5 = (bf16[2,256,128]{2,1,0:T(8,128)(2,1)}, bf16[2,256,128]{2,1,0:T(8,128)(2,1)S(1)}, u32[]{:S(2)}) copy-start(bf16[2,256,128]{2,1,0:T(8,128)(2,1)S(1)} %collective-permute-done.2.refs_3_.refs_5_) | copy-start | bytes 393220
  45.7 12.8 %collective-permute-start.3 = (bf16[2,256,128]{2,1,0:T(8,128)(2,1)}, bf16[2,256,128]{2,1,0:T(8,128)(2,1)S(1)}, u32[]{:S(2)}, u32[]{:S(2)}) collective-permute-start(bf16[2,256,128]{2,1,0:T(8,128)(2,1)} %get-tuple-element.31), channel_id=1, source_target_pairs={{0,4},{4,8},{8,12},{12,0},{1,5},{5,9},{9,13},{13,1},{2,6},{6,10},{... | collective-permute-start | bytes 393224 | tf_op jit(solution)/shard_map/ppermute | solution.py:242
  46.4 12.2 %collective-permute-start.4 = (bf16[2,256,128]{2,1,0:T(8,128)(2,1)}, bf16[2,256,128]{2,1,0:T(8,128)(2,1)S(1)}, u32[]{:S(2)}, u32[]{:S(2)}) collective-permute-start(bf16[2,256,128]{2,1,0:T(8,128)(2,1)} %get-tuple-element.32), channel_id=1, source_target_pairs={{0,8},{4,12},{8,0},{12,4},{1,9},{5,13},{9,1},{13,5},{2,10},{6,14},... | collective-permute-start | bytes 393224 | tf_op jit(solution)/shard_map/ppermute | solution.py:242
  50.2 2.3 %copy-start = (bf16[64,2048]{1,0:T(8,128)(2,1)}, bf16[64,2048]{1,0:T(8,128)(2,1)S(1)}, u32[]{:S(2)}) copy-start(bf16[64,2048]{1,0:T(8,128)(2,1)S(1)} %collective-permute-done.6.refs_1_) | copy-start | bytes 786436
  50.2 8.3 %collective-permute-start.5 = (bf16[2,256,128]{2,1,0:T(8,128)(2,1)}, bf16[2,256,128]{2,1,0:T(8,128)(2,1)S(1)}, u32[]{:S(2)}, u32[]{:S(2)}) collective-permute-start(bf16[2,256,128]{2,1,0:T(8,128)(2,1)} %get-tuple-element.33), channel_id=1, source_target_pairs={{0,12},{4,0},{8,4},{12,8},{1,13},{5,1},{9,5},{13,9},{2,14},{6,2},{... | collective-permute-start | bytes 393224 | tf_op jit(solution)/shard_map/ppermute | solution.py:242
  52.6 3.0 %copy-start.1 = (bf16[64,2048]{1,0:T(8,128)(2,1)}, bf16[64,2048]{1,0:T(8,128)(2,1)S(1)}, u32[]{:S(2)}) copy-start(bf16[64,2048]{1,0:T(8,128)(2,1)S(1)} %collective-permute-done.7.refs_2_) | copy-start | bytes 786436
  55.6 0.7 %copy-start.2 = (bf16[64,2048]{1,0:T(8,128)(2,1)}, bf16[64,2048]{1,0:T(8,128)(2,1)S(1)}, u32[]{:S(2)}) copy-start(bf16[64,2048]{1,0:T(8,128)(2,1)S(1)} %collective-permute-done.8.refs_3_) | copy-start | bytes 786436
  58.5 0.7 %copy-start.6 = (bf16[2,256,128]{2,1,0:T(8,128)(2,1)}, bf16[2,256,128]{2,1,0:T(8,128)(2,1)S(1)}, u32[]{:S(2)}) copy-start(bf16[2,256,128]{2,1,0:T(8,128)(2,1)S(1)} %collective-permute-done.3.refs_2_) | copy-start | bytes 393220
  58.5 0.7 %copy-start.7 = (bf16[2,256,128]{2,1,0:T(8,128)(2,1)}, bf16[2,256,128]{2,1,0:T(8,128)(2,1)S(1)}, u32[]{:S(2)}) copy-start(bf16[2,256,128]{2,1,0:T(8,128)(2,1)S(1)} %collective-permute-done.4.refs_3_) | copy-start | bytes 393220
  58.5 0.7 %copy-start.8 = (bf16[2,256,128]{2,1,0:T(8,128)(2,1)}, bf16[2,256,128]{2,1,0:T(8,128)(2,1)S(1)}, u32[]{:S(2)}) copy-start(bf16[2,256,128]{2,1,0:T(8,128)(2,1)S(1)} %collective-permute-done.5.refs_4_) | copy-start | bytes 393220

commit v7 on v5

--- a/solution.py
+++ b/solution.py
@@ -10,6 +10,7 @@
 
 masked_score = -1e30
 vmem_bytes = 56 * 1024 * 1024
+small_vmem_bytes = 8 * 1024 * 1024
 f32 = jnp.float32
 bf16 = jnp.bfloat16
 
@@ -188,7 +189,7 @@
     part_rows = cart_rows // dp_size
     me = lax.axis_index("dp")
     for step, ref in enumerate(cart_outs):
-        target = lax.rem(me + step, dp_size)
+        target = target_of(me, step, dp_size)
         at = pl.ds(pl.multiple_of(target * part_rows, part_rows), part_rows)
         ref[0] = (dk_ref[at, :] * scale).astype(ref.dtype)
         ref[1] = dv_ref[at, :].astype(ref.dtype)
@@ -201,7 +202,7 @@
     columns = width * head_dim
     me = lax.axis_index("heads")
     for step, ref in enumerate(dq_outs):
-        target = lax.rem(me + step, heads_size)
+        target = target_of(me, step, heads_size)
         at = pl.ds(pl.multiple_of(target * own_tokens, own_tokens), own_tokens)
         for index, before in enumerate((*dq_before, dq_ref)):
             ref[:, index * columns : (index + 1) * columns] = before[at, :]
@@ -213,10 +214,6 @@
         self_ref[kind * count : (kind + 1) * count, :] = wide_ref[0:count, :].astype(bf16)
 
 
-def order_kernel(*refs):
-    pass
-
-
 def sum_kernel(*refs):
     part_refs, out_ref = refs[:-1], refs[-1]
     total = part_refs[0][...]
@@ -226,7 +223,7 @@
 
 
 def cart_kernel(kv_local, *refs):
-    done_refs, part_refs, out_ref = refs[: kv_local - 1], refs[kv_local - 1 : -2], refs[-1]
+    done_refs, part_refs, out_ref = refs[: kv_local - 1], refs[kv_local - 1 : -1], refs[-1]
     part_rows = part_refs[0].shape[1]
     for kind in range(2):
         total = part_refs[0][kind]
@@ -237,18 +234,36 @@
 
 
 def place_kernel(count, *refs):
-    part_refs, out_ref = refs[:count], refs[-1]
+    part_refs, out_ref, sems = refs[:count], *refs[-2:]
     columns = part_refs[0].shape[1]
     me = lax.axis_index("heads")
+    copies = []
     for step, ref in enumerate(part_refs):
-        source = lax.rem(me + count - step, count)
-        out_ref[:, pl.ds(pl.multiple_of(source * columns, columns), columns)] = ref[...]
+        source = source_of(me, step, count)
+        at = pl.ds(pl.multiple_of(source * columns, columns), columns)
+        copies.append(pltpu.make_async_copy(ref, out_ref.at[:, at], sems.at[step]))
+    for copy in copies:
+        copy.start()
+    for copy in copies:
+        copy.wait()
+
+
+def paired(size):
+    return size & (size - 1) == 0
+
+
+def target_of(me, step, size):
+    return me ^ step if paired(size) else (me + step) % size
+
+
+def source_of(me, step, size):
+    return me ^ step if paired(size) else (me + size - step) % size
 
 
 def shift(values, axis, size, step):
     if step == 0:
         return values
-    return lax.ppermute(values, axis, [(source, (source + step) % size) for source in range(size)])
+    return lax.ppermute(values, axis, [(source, target_of(source, step, size)) for source in range(size)])
 
 
 def on_device(dp_size, heads_size, queries, out_grad, self_keys, self_values, cart_keys, cart_values, segment_ids):
@@ -270,6 +285,7 @@
     columns = width * head_dim
     count = tokens * kv_local
     cart_list, query_list, self_list = [], [], []
+    anywhere = pl.BlockSpec(memory_space=pl.ANY)
     for kv_index in range(kv_local):
         last = kv_index == kv_local - 1
         if last:
@@ -314,20 +330,14 @@
             name="head_grads",
         )(*flat, segment_ids, *(before if last else []))
         sends = list(outs[1:dp_size])
+        if last:
+            sends += outs[dp_size + 1 : -1]
         if last and cart_list:
-            anywhere = pl.BlockSpec(memory_space=pl.ANY)
-            sends = pl.pallas_call(
-                order_kernel,
-                out_shape=tuple(jax.ShapeDtypeStruct(array.shape, array.dtype) for array in sends),
-                in_specs=[anywhere] * (len(sends) + len(cart_parts) - 1),
-                out_specs=(anywhere,) * len(sends),
-                input_output_aliases={index: index for index in range(len(sends))},
-                cost_estimate=pl.CostEstimate(flops=32 * macs, bytes_accessed=0, transcendentals=0),
-                name="order_sends",
-            )(*sends, *cart_parts[1:])
-        cart_parts = [outs[0]] + [shift(array, "dp", dp_size, step + 1) for step, array in enumerate(sends)]
+            received = cart_parts[1:]
+            sends, received = lax.optimization_barrier((sends, received))
+        cart_parts = [outs[0]] + [shift(array, "dp", dp_size, step + 1) for step, array in enumerate(sends[: dp_size - 1])]
         if last:
-            query_list, self_grads = outs[dp_size:-1], outs[-1]
+            query_list, self_grads = [outs[dp_size], *sends[dp_size - 1 :]], outs[-1]
         else:
             query_list.append(outs[-2])
             self_list.append(outs[-1])
@@ -335,7 +345,7 @@
                 pl.pallas_call(
                     sum_kernel,
                     out_shape=jax.ShapeDtypeStruct((2, part_rows, head_dim), f32),
-                    compiler_params=pltpu.CompilerParams(vmem_limit_bytes=vmem_bytes),
+                    compiler_params=pltpu.CompilerParams(vmem_limit_bytes=small_vmem_bytes),
                     cost_estimate=pl.CostEstimate(flops=2**20, bytes_accessed=2**20, transcendentals=0),
                     name="cart_sum",
                 )(*cart_parts)
@@ -344,21 +354,21 @@
     query_grads = pl.pallas_call(
         functools.partial(place_kernel, heads_size),
         out_shape=jax.ShapeDtypeStruct((own_tokens, heads_size * heads_local * head_dim), bf16),
-        in_specs=[pl.BlockSpec(memory_space=pltpu.VMEM)] * heads_size
-        + [pl.BlockSpec(memory_space=pl.ANY)] * len(cart_list),
-        compiler_params=pltpu.CompilerParams(vmem_limit_bytes=vmem_bytes),
+        in_specs=[anywhere] * heads_size,
+        out_specs=anywhere,
+        scratch_shapes=[pltpu.SemaphoreType.DMA((heads_size,))],
+        compiler_params=pltpu.CompilerParams(vmem_limit_bytes=small_vmem_bytes),
         cost_estimate=pl.CostEstimate(flops=2**20, bytes_accessed=2 * 2**20, transcendentals=0),
         name="place_queries",
-    )(*query_list, *cart_list)
+    )(*query_list)
+    query_grads, cart_list, cart_parts = lax.optimization_barrier((query_grads, cart_list, cart_parts))
     cart_grads = pl.pallas_call(
         functools.partial(cart_kernel, kv_local),
         out_shape=jax.ShapeDtypeStruct((part_rows * 2 * kv_local, head_dim), f32),
-        in_specs=[pl.BlockSpec(memory_space=pltpu.VMEM)] * (len(cart_list) + dp_size)
-        + [pl.BlockSpec(memory_space=pl.ANY)],
-        compiler_params=pltpu.CompilerParams(vmem_limit_bytes=vmem_bytes),
+        compiler_params=pltpu.CompilerParams(vmem_limit_bytes=small_vmem_bytes),
         cost_estimate=pl.CostEstimate(flops=2**20, bytes_accessed=2 * 2**20, transcendentals=0),
         name="cart_grads",
-    )(*cart_list, *cart_parts, query_grads)
+    )(*cart_list, *cart_parts)
     cart_grads = cart_grads.reshape(part_rows, 2, kv_local, head_dim)
     self_grads = self_grads.reshape(2, tokens, kv_local, head_dim)
     return (cart_grads, self_grads, query_grads)

time: 50.6 us -> 46.9 us (0.927); the launches traced: 49.8 us -> 46.7 us
  Pallas kernels: 28.9 us -> 24.9 us
  waiting for transfers between devices: 6.53 us -> 9.08 us
  local copies, waits for them, and re-layouts: 2.12 us -> 0.01 us
    ppermute x9, waiting for transfers between devices: 6.53 us -> 9.08 us  [shift(): lax.ppermute(values, axis, [(source, target_of(source, step, size)) for s...]
    unnamed x18 -> x6, local copies, waits for them, and re-layouts: 2.12 us -> 0.01 us
    pallas_call x1, Pallas kernels: 1.89 us -> 0.06 us  [on_device(): pl.pallas_call(sum_kernel, out_shape=jax.ShapeDtypeStruct((2, part_rows,...]
    pallas_call x1, Pallas kernels: 2.23 us -> 0.99 us  [on_device(): pl.pallas_call(functools.partial(place_kernel, heads_size), out_shape=jax...]
    pallas_call x1, Pallas kernels: 2.04 us -> 0.87 us  [on_device(): pl.pallas_call(functools.partial(cart_kernel, kv_local), out_shape=jax.Sh...]
    ppermute x9, starting transfers between devices: 11.5 us -> 12 us  [shift(): lax.ppermute(values, axis, [(source, target_of(source, step, size)) for s...]
  transfers between devices with their start and end apart: 9 -> 9, of which waited for: 2 -> 3; matrix products, arithmetic and copies ran while one was open for 0% -> 0% of each run, Pallas kernels for 32% -> 28%
where the time goes in v7:
time: 46.9 us; the launch traced here: 46.7 us
  Pallas kernels  24.9 us (53%)
  starting transfers between devices  12 us (26%)
  waiting for transfers between devices  9.08 us (19%)
  between operations  0.72 us (2%)
    pallas_call x2, Pallas kernels, on_device(): pl.pallas_call(functools.partial(head_kernel, dp_size, heads_size, kv_ind...  22.9 us
    ppermute x9, starting transfers between devices, shift(): lax.ppermute(values, axis, [(source, target_of(source, step, size)) for s...  12 us
    ppermute x9, waiting for transfers between devices, shift(): lax.ppermute(values, axis, [(source, target_of(source, step, size)) for s...  9.08 us
    pallas_call x1, Pallas kernels, on_device(): pl.pallas_call(functools.partial(place_kernel, heads_size), out_shape=jax...  0.99 us
  transfers between devices with their start and end apart: 9, of which 3 were waited for; matrix products, arithmetic and copies ran while one was open for 0% of the time, Pallas kernels for 28%

profile of v7, /device:TPU:0, one launch (start us, length us, event | category | flops | bytes accessed | tf_op | source)
XLA Modules:
  0.0 46.7 jit_solution(14272259078647549995)
XLA Ops:
  0.6 11.0 %head_grads.2 = (f32[2,256,128]{2,1,0:T(8,128)}, bf16[2,256,128]{2,1,0:T(8,128)(2,1)}, bf16[2,256,128]{2,1,0:T(8,128)(2,1)}, bf16[2,256,128]{2,1,0:T(8,128)(2,1)...) custom-call(bf16[4096,128]{1,0:T(8,128)(2,1)} %bitcast.9, bf16[4096,128]{1,0:T(8,128)(2,1)} %bitcast.11, ...), custom_call_target="tpu_custom_call" | custom-call | flops 6710886400 | bytes 5242880 | tf_op jit(solution)/shard_map/head_grads/pallas_call | solution.py:300
  11.7 3.1 %collective-permute-start = (bf16[2,256,128]{2,1,0:T(8,128)(2,1)}, bf16[2,256,128]{2,1,0:T(8,128)(2,1)S(1)}, u32[]{:S(2)}, u32[]{:S(2)}) collective-permute-start(bf16[2,256,128]{2,1,0:T(8,128)(2,1)} %get-tuple-element.39), channel_id=1, source_target_pairs={{0,4},{4,0},{8,12},{12,8},{1,5},{5,1},{9,13},{13,9},{2,6},{6,2},{1... | collective-permute-start | bytes 393224 | tf_op jit(solution)/shard_map/ppermute | solution.py:266
  14.7 2.6 %collective-permute-start.1 = (bf16[2,256,128]{2,1,0:T(8,128)(2,1)}, bf16[2,256,128]{2,1,0:T(8,128)(2,1)S(1)}, u32[]{:S(2)}, u32[]{:S(2)}) collective-permute-start(bf16[2,256,128]{2,1,0:T(8,128)(2,1)} %get-tuple-element.40), channel_id=1, source_target_pairs={{0,8},{4,12},{8,0},{12,4},{1,9},{5,13},{9,1},{13,5},{2,10},{6,14},... | collective-permute-start | bytes 393224 | tf_op jit(solution)/shard_map/ppermute | solution.py:266
  17.3 0.0 collective-permute-start.2
  17.3 0.0 copy-start
  17.3 11.9 %head_grads.3 = (f32[2,256,128]{2,1,0:T(8,128)}, bf16[2,256,128]{2,1,0:T(8,128)(2,1)}, bf16[2,256,128]{2,1,0:T(8,128)(2,1)}, bf16[2,256,128]{2,1,0:T(8,128)(2,1)...) custom-call(bf16[4096,128]{1,0:T(8,128)(2,1)} %bitcast.10, ...), custom_call_target="tpu_custom_call" | custom-call | flops 6710886400 | bytes 5242880 | tf_op jit(solution)/shard_map/head_grads/pallas_call | solution.py:300
  29.3 0.0 collective-permute-done.refs_1_
  29.3 0.0 collective-permute-done.1.refs_2_
  29.3 0.0 collective-permute-done.2.refs_3_
  29.3 0.1 collective-permute-start.3
  29.4 1.8 %collective-permute-start.4 = (bf16[64,2048]{1,0:T(8,128)(2,1)}, bf16[64,2048]{1,0:T(8,128)(2,1)S(1)}, u32[]{:S(2)}, u32[]{:S(2)}) collective-permute-start(bf16[64,2048]{1,0:T(8,128)(2,1)} %get-tuple-element.43), channel_id=1, source_target_pairs={{0,2},{1,3},{2,0},{3,1},{4,6},{5,7},{6,4},{7,5},{8,10},{9,11},{10,... | collective-permute-start | bytes 786440 | tf_op jit(solution)/shard_map/ppermute | solution.py:266
  31.2 0.1 collective-permute-start.5
  31.3 0.9 %collective-permute-start.6 = (bf16[2,256,128]{2,1,0:T(8,128)(2,1)}, bf16[2,256,128]{2,1,0:T(8,128)(2,1)S(1)}, u32[]{:S(2)}, u32[]{:S(2)}) collective-permute-start(bf16[2,256,128]{2,1,0:T(8,128)(2,1)} %get-tuple-element.47), channel_id=1, source_target_pairs={{0,4},{4,0},{8,12},{12,8},{1,5},{5,1},{9,13},{13,9},{2,6},{6,2},{1... | collective-permute-start | bytes 393224 | tf_op jit(solution)/shard_map/ppermute | solution.py:266
  32.2 3.5 %collective-permute-start.7 = (bf16[2,256,128]{2,1,0:T(8,128)(2,1)}, bf16[2,256,128]{2,1,0:T(8,128)(2,1)S(1)}, u32[]{:S(2)}, u32[]{:S(2)}) collective-permute-start(bf16[2,256,128]{2,1,0:T(8,128)(2,1)} %get-tuple-element.48), channel_id=1, source_target_pairs={{0,8},{4,12},{8,0},{12,4},{1,9},{5,13},{9,1},{13,5},{2,10},{6,14},... | collective-permute-start | bytes 393224 | tf_op jit(solution)/shard_map/ppermute | solution.py:266
  35.6 0.0 collective-permute-done.3.refs_1_
  35.6 0.0 collective-permute-start.8
  35.7 0.0 copy-done
  35.7 0.0 copy-start.2
  35.7 0.1 cart_sum.1.refs_0_
  35.7 3.0 %collective-permute-done.4.refs_2_ = bf16[64,2048]{1,0:T(8,128)(2,1)S(1)} collective-permute-done((bf16[64,2048]{1,0:T(8,128)(2,1)}, bf16[64,2048]{1,0:T(8,128)(2,1)S(1)}, u32[]{:S(2)}, u32[]{:S(2)}) %collective-permute-start.4) | collective-permute-done | bytes 262176 | tf_op jit(solution)/shard_map/ppermute | solution.py:266
  38.8 4.7 %collective-permute-done.5.refs_3_ = bf16[64,2048]{1,0:T(8,128)(2,1)S(1)} collective-permute-done((bf16[64,2048]{1,0:T(8,128)(2,1)}, bf16[64,2048]{1,0:T(8,128)(2,1)S(1)}, u32[]{:S(2)}, u32[]{:S(2)}) %collective-permute-start.5) | collective-permute-done | bytes 262176 | tf_op jit(solution)/shard_map/ppermute | solution.py:266
  43.5 0.0 copy-done.2
  43.5 0.0 copy-start.1
  43.5 1.0 %place_queries.1 = bf16[64,8192]{1,0:T(8,128)(2,1)} custom-call(bf16[64,2048]{1,0:T(8,128)(2,1)S(1)} %copy-done.2, bf16[64,2048]{1,0:T(8,128)(2,1)S(1)} %collective-permute-done.3.refs_1_, bf16[64,2048]{1,0:T(8,128)(2,1)S(1)} %collective-permute-done.4.refs_2_, bf16[64,2048]{1,0:T(8,128)(2,1)S(1)} %collective-permute-done.5.refs_3_), custom_call_target="tpu_custom_call" | custom-call | flops 1048576 | bytes 2097152 | tf_op jit(solution)/shard_map/place_queries/pallas_call | solution.py:354
  44.5 0.0 collective-permute-done.6.refs_2_
  44.5 1.3 %collective-permute-done.7.refs_3_ = bf16[2,256,128]{2,1,0:T(8,128)(2,1)S(1)} collective-permute-done((bf16[2,256,128]{2,1,0:T(8,128)(2,1)}, bf16[2,256,128]{2,1,0:T(8,128)(2,1)S(1)}, u32[]{:S(2)}, u32[]{:S(2)}) %collective-permute-start.7) | collective-permute-done | bytes 131104 | tf_op jit(solution)/shard_map/ppermute | solution.py:266
  45.8 0.0 collective-permute-done.8.refs_4_
  45.8 0.0 copy-done.1
  45.8 0.9 %cart_grads.1 = f32[1024,128]{1,0:T(8,128)} custom-call(f32[2,256,128]{2,1,0:T(8,128)S(1)} %cart_sum.1.refs_0_, f32[2,256,128]{2,1,0:T(8,128)S(1)} %copy-done.1, bf16[2,256,128]{2,1,0:T(8,128)(2,1)S(1)} %collective-permute-done.6.refs_2_, bf16[2,256,128]{2,1,0:T(8,128)(2,1)S(1)} %collective-permute-done.7.refs_3_, ...), custom_call_target="tpu_custom_call" | custom-call | flops 1048576 | bytes 2097152 | tf_op jit(solution)/shard_map/cart_grads/pallas_call | solution.py:365
Async XLA Ops:
  11.7 17.6 %collective-permute-start = (bf16[2,256,128]{2,1,0:T(8,128)(2,1)}, bf16[2,256,128]{2,1,0:T(8,128)(2,1)S(1)}, u32[]{:S(2)}, u32[]{:S(2)}) collective-permute-start(bf16[2,256,128]{2,1,0:T(8,128)(2,1)} %get-tuple-element.39), channel_id=1, source_target_pairs={{0,4},{4,0},{8,12},{12,8},{1,5},{5,1},{9,13},{13,9},{2,6},{6,2},{1... | collective-permute-start | bytes 393224 | tf_op jit(solution)/shard_map/ppermute | solution.py:266
  14.7 14.5 %collective-permute-start.1 = (bf16[2,256,128]{2,1,0:T(8,128)(2,1)}, bf16[2,256,128]{2,1,0:T(8,128)(2,1)S(1)}, u32[]{:S(2)}, u32[]{:S(2)}) collective-permute-start(bf16[2,256,128]{2,1,0:T(8,128)(2,1)} %get-tuple-element.40), channel_id=1, source_target_pairs={{0,8},{4,12},{8,0},{12,4},{1,9},{5,13},{9,1},{13,5},{2,10},{6,14},... | collective-permute-start | bytes 393224 | tf_op jit(solution)/shard_map/ppermute | solution.py:266
  17.3 12.0 %collective-permute-start.2 = (bf16[2,256,128]{2,1,0:T(8,128)(2,1)}, bf16[2,256,128]{2,1,0:T(8,128)(2,1)S(1)}, u32[]{:S(2)}, u32[]{:S(2)}) collective-permute-start(bf16[2,256,128]{2,1,0:T(8,128)(2,1)} %get-tuple-element.41), channel_id=1, source_target_pairs={{0,12},{4,8},{8,4},{12,0},{1,13},{5,9},{9,5},{13,1},{2,14},{6,10},... | collective-permute-start | bytes 393224 | tf_op jit(solution)/shard_map/ppermute | solution.py:266
  17.3 18.3 %copy-start = (f32[2,256,128]{2,1,0:T(8,128)S(1)}, f32[2,256,128]{2,1,0:T(8,128)}, u32[]{:S(2)}) copy-start(f32[2,256,128]{2,1,0:T(8,128)} %get-tuple-element.45.refs_0_) | copy-start | bytes 786436
  29.3 6.3 %collective-permute-start.3 = (bf16[64,2048]{1,0:T(8,128)(2,1)}, bf16[64,2048]{1,0:T(8,128)(2,1)S(1)}, u32[]{:S(2)}, u32[]{:S(2)}) collective-permute-start(bf16[64,2048]{1,0:T(8,128)(2,1)} %get-tuple-element.42), channel_id=1, source_target_pairs={{0,1},{1,0},{2,3},{3,2},{4,5},{5,4},{6,7},{7,6},{8,9},{9,8},{10,11... | collective-permute-start | bytes 786440 | tf_op jit(solution)/shard_map/ppermute | solution.py:266
  29.4 9.4 %collective-permute-start.4 = (bf16[64,2048]{1,0:T(8,128)(2,1)}, bf16[64,2048]{1,0:T(8,128)(2,1)S(1)}, u32[]{:S(2)}, u32[]{:S(2)}) collective-permute-start(bf16[64,2048]{1,0:T(8,128)(2,1)} %get-tuple-element.43), channel_id=1, source_target_pairs={{0,2},{1,3},{2,0},{3,1},{4,6},{5,7},{6,4},{7,5},{8,10},{9,11},{10,... | collective-permute-start | bytes 786440 | tf_op jit(solution)/shard_map/ppermute | solution.py:266
  31.2 12.3 %collective-permute-start.5 = (bf16[64,2048]{1,0:T(8,128)(2,1)}, bf16[64,2048]{1,0:T(8,128)(2,1)S(1)}, u32[]{:S(2)}, u32[]{:S(2)}) collective-permute-start(bf16[64,2048]{1,0:T(8,128)(2,1)} %get-tuple-element.44), channel_id=1, source_target_pairs={{0,3},{1,2},{2,1},{3,0},{4,7},{5,6},{6,5},{7,4},{8,11},{9,10},{10,... | collective-permute-start | bytes 786440 | tf_op jit(solution)/shard_map/ppermute | solution.py:266
  31.3 13.2 %collective-permute-start.6 = (bf16[2,256,128]{2,1,0:T(8,128)(2,1)}, bf16[2,256,128]{2,1,0:T(8,128)(2,1)S(1)}, u32[]{:S(2)}, u32[]{:S(2)}) collective-permute-start(bf16[2,256,128]{2,1,0:T(8,128)(2,1)} %get-tuple-element.47), channel_id=1, source_target_pairs={{0,4},{4,0},{8,12},{12,8},{1,5},{5,1},{9,13},{13,9},{2,6},{6,2},{1... | collective-permute-start | bytes 393224 | tf_op jit(solution)/shard_map/ppermute | solution.py:266
  32.2 13.7 %collective-permute-start.7 = (bf16[2,256,128]{2,1,0:T(8,128)(2,1)}, bf16[2,256,128]{2,1,0:T(8,128)(2,1)S(1)}, u32[]{:S(2)}, u32[]{:S(2)}) collective-permute-start(bf16[2,256,128]{2,1,0:T(8,128)(2,1)} %get-tuple-element.48), channel_id=1, source_target_pairs={{0,8},{4,12},{8,0},{12,4},{1,9},{5,13},{9,1},{13,5},{2,10},{6,14},... | collective-permute-start | bytes 393224 | tf_op jit(solution)/shard_map/ppermute | solution.py:266
  35.6 10.2 %collective-permute-start.8 = (bf16[2,256,128]{2,1,0:T(8,128)(2,1)}, bf16[2,256,128]{2,1,0:T(8,128)(2,1)S(1)}, u32[]{:S(2)}, u32[]{:S(2)}) collective-permute-start(bf16[2,256,128]{2,1,0:T(8,128)(2,1)} %get-tuple-element.49), channel_id=1, source_target_pairs={{0,12},{4,8},{8,4},{12,0},{1,13},{5,9},{9,5},{13,1},{2,14},{6,10},... | collective-permute-start | bytes 393224 | tf_op jit(solution)/shard_map/ppermute | solution.py:266
  35.7 7.8 %copy-start.2 = (bf16[64,2048]{1,0:T(8,128)(2,1)S(1)}, bf16[64,2048]{1,0:T(8,128)(2,1)}, u32[]{:S(2)}) copy-start(bf16[64,2048]{1,0:T(8,128)(2,1)} %get-tuple-element.32.refs_0_) | copy-start | bytes 786436
  43.5 2.3 %copy-start.1 = (f32[2,256,128]{2,1,0:T(8,128)S(1)}, f32[2,256,128]{2,1,0:T(8,128)}, u32[]{:S(2)}) copy-start(f32[2,256,128]{2,1,0:T(8,128)} %get-tuple-element.51.refs_1_) | copy-start | bytes 786436

commit v8 on v7

--- a/solution.py
+++ b/solution.py
@@ -11,6 +11,7 @@
 masked_score = -1e30
 vmem_bytes = 56 * 1024 * 1024
 small_vmem_bytes = 8 * 1024 * 1024
+kept_steps = 2
 f32 = jnp.float32
 bf16 = jnp.bfloat16
 
@@ -33,10 +34,11 @@
     q_ref, g_ref, sk_ref, sv_ref, ck_ref, cv_ref, seg_ref = refs[:7]
     refs = refs[7:]
     held = kv_index if last else 0
-    dq_before, self_before, refs = refs[:held], refs[held : 2 * held], refs[2 * held :]
+    kept = min(kept_steps, heads_size)
+    dq_before, refs = refs[: held * kept], refs[held * kept :]
+    self_before, refs = refs[:held], refs[held:]
     cart_outs, refs = refs[:dp_size], refs[dp_size:]
-    dq_count = heads_size if last else 1
-    dq_outs, self_ref, refs = refs[:dq_count], refs[dq_count], refs[dq_count + 1 :]
+    dq_outs, self_ref, refs = refs[:heads_size], refs[heads_size], refs[heads_size + 1 :]
     (
         wide_ref, keys_ref, vals_ref, keys_t_ref, s_ref, w_ref, d_ref, p_ref, ds_ref, dk_ref, dv_ref, out_ref, dq_ref,
         q_in, g_in, sk_in, sv_in, ck_in, cv_in, sems,
@@ -98,6 +100,9 @@
     queries, grads, peaks, stats = {}, {}, {}, {}
     acc = {}
 
+    def spread(values):
+        return jnp.concatenate([values] * (sub // 8), axis=0)
+
     def subs(start, size):
         return [slice(at, at + sub) for at in range(start, start + size, sub)]
 
@@ -119,7 +124,7 @@
             acc["peak"] = jnp.maximum(acc["peak"], fold_rows(score, jnp.max))
 
     def close_scores(block):
-        peaks[block] = jnp.max(acc["peak"], axis=0, keepdims=True)
+        peaks[block] = jnp.broadcast_to(jnp.max(acc["peak"], axis=0, keepdims=True), (8, rows))
 
     def open_weights(block):
         grads[block] = rows_of("g", g_in, block)
@@ -129,14 +134,15 @@
     def step_weights(block, start, size):
         d_ref[block % 2, start : start + size, :] = dot_nt(vals_ref[start : start + size, :], grads[block])
         for at in subs(start, size):
-            weight = jnp.exp2((s_ref[block % 2, at, :] - peaks[block]) * scale2)
+            weight = jnp.exp2((s_ref[block % 2, at, :] - spread(peaks[block])) * scale2)
             w_ref[block % 2, at, :] = weight
             acc["total"] = acc["total"] + fold_rows(weight, jnp.sum)
             acc["center"] = acc["center"] + fold_rows(weight * d_ref[block % 2, at, :], jnp.sum)
 
     def close_weights(block):
         share = 1.0 / jnp.sum(acc["total"], axis=0, keepdims=True)
-        stats[block] = share, jnp.sum(acc["center"], axis=0, keepdims=True) * share
+        center = jnp.sum(acc["center"], axis=0, keepdims=True) * share
+        stats[block] = jnp.broadcast_to(share, (8, rows)), jnp.broadcast_to(center, (8, rows))
 
     def open_grads(block):
         acc["dq"] = jnp.zeros((head_dim, rows), f32)
@@ -144,9 +150,9 @@
     def step_grads(block, start, size):
         share, center = stats[block]
         for at in subs(start, size):
-            prob = w_ref[block % 2, at, :] * share
+            prob = w_ref[block % 2, at, :] * spread(share)
             p_ref[at, :] = prob.astype(bf16)
-            ds_ref[at, :] = (prob * (d_ref[block % 2, at, :] - center)).astype(bf16)
+            ds_ref[at, :] = (prob * (d_ref[block % 2, at, :] - spread(center))).astype(bf16)
         at = slice(start, start + size)
         old = size if start < cart_rows else (limit(block - 1) if block else 0)
         old = old if block else 0
@@ -194,18 +200,21 @@
         ref[0] = (dk_ref[at, :] * scale).astype(ref.dtype)
         ref[1] = dv_ref[at, :].astype(ref.dtype)
     own = dk_ref[cart_rows:all_keys, :] * scale, dv_ref[cart_rows:all_keys, :]
-    if not last:
-        dq_outs[0][...] = dq_ref[...]
-        self_ref[0], self_ref[1] = own
-        return
     own_tokens = tokens // heads_size
     columns = width * head_dim
     me = lax.axis_index("heads")
     for step, ref in enumerate(dq_outs):
         target = target_of(me, step, heads_size)
         at = pl.ds(pl.multiple_of(target * own_tokens, own_tokens), own_tokens)
-        for index, before in enumerate((*dq_before, dq_ref)):
-            ref[:, index * columns : (index + 1) * columns] = before[at, :]
+        if last and step < kept:
+            for index in range(held):
+                ref[:, index * columns : (index + 1) * columns] = dq_before[index * kept + step][...]
+            ref[:, held * columns :] = dq_ref[at, :]
+        else:
+            ref[...] = dq_ref[at, :]
+    if not last:
+        self_ref[0], self_ref[1] = own
+        return
     count = tokens * kv_local
     for kind in range(2):
         for index, before in enumerate(self_before):
@@ -233,15 +242,18 @@
             out_ref[pl.ds(kind * kv_local + kv_index, part_rows, stride=2 * kv_local), :] = part
 
 
-def place_kernel(count, *refs):
-    part_refs, out_ref, sems = refs[:count], *refs[-2:]
-    columns = part_refs[0].shape[1]
+def place_kernel(heads_size, kv_local, *refs):
+    part_refs, out_ref, sems = refs[:-2], refs[-2], refs[-1]
+    kept = min(kept_steps, heads_size)
+    columns = out_ref.shape[1] // (heads_size * kv_local)
     me = lax.axis_index("heads")
+    places = [(step, 0) for step in range(kept)]
+    places += [(step, kv_index) for kv_index in range(kv_local) for step in range(kept, heads_size)]
     copies = []
-    for step, ref in enumerate(part_refs):
-        source = source_of(me, step, count)
-        at = pl.ds(pl.multiple_of(source * columns, columns), columns)
-        copies.append(pltpu.make_async_copy(ref, out_ref.at[:, at], sems.at[step]))
+    for index, ((step, kv_index), ref) in enumerate(zip(places, part_refs)):
+        source = source_of(me, step, heads_size)
+        at = pl.multiple_of((source * kv_local + kv_index) * columns, columns)
+        copies.append(pltpu.make_async_copy(ref, out_ref.at[:, pl.ds(at, ref.shape[1])], sems.at[index]))
     for copy in copies:
         copy.start()
     for copy in copies:
@@ -284,19 +296,17 @@
     blocks = tokens // block_tokens
     columns = width * head_dim
     count = tokens * kv_local
-    cart_list, query_list, self_list = [], [], []
+    kept = min(kept_steps, heads_size)
     anywhere = pl.BlockSpec(memory_space=pl.ANY)
+    cart_list, kept_list, far_list, self_list, received = [], [], [], [], []
     for kv_index in range(kv_local):
         last = kv_index == kv_local - 1
-        if last:
-            other_shapes = [jax.ShapeDtypeStruct((own_tokens, kv_local * columns), bf16) for _ in range(heads_size)]
-            other_shapes.append(jax.ShapeDtypeStruct((2 * count, head_dim), bf16))
-        else:
-            other_shapes = [
-                jax.ShapeDtypeStruct((tokens, columns), bf16),
-                jax.ShapeDtypeStruct((2, tokens, head_dim), f32),
-            ]
-        before = query_list + self_list
+        near = jax.ShapeDtypeStruct((own_tokens, kv_local * columns if last else columns), bf16)
+        far = jax.ShapeDtypeStruct((own_tokens, columns), bf16)
+        own_shape = (2 * count, head_dim) if last else (2, tokens, head_dim)
+        other_shapes = [near] * kept + [far] * (heads_size - kept)
+        other_shapes.append(jax.ShapeDtypeStruct(own_shape, bf16 if last else f32))
+        before = kept_list + self_list
         outs = pl.pallas_call(
             functools.partial(head_kernel, dp_size, heads_size, kv_index, kv_local, width, block_tokens, chunk, fine, sub),
             out_shape=(
@@ -329,39 +339,38 @@
             cost_estimate=pl.CostEstimate(flops=4 * macs, bytes_accessed=5 * 2**20, transcendentals=tokens * width * all_keys),
             name="head_grads",
         )(*flat, segment_ids, *(before if last else []))
-        sends = list(outs[1:dp_size])
+        cart_sends, near, far = outs[1:dp_size], outs[dp_size : dp_size + kept], outs[dp_size + kept : -1]
         if last:
-            sends += outs[dp_size + 1 : -1]
-        if last and cart_list:
-            received = cart_parts[1:]
-            sends, received = lax.optimization_barrier((sends, received))
-        cart_parts = [outs[0]] + [shift(array, "dp", dp_size, step + 1) for step, array in enumerate(sends[: dp_size - 1])]
-        if last:
-            query_list, self_grads = [outs[dp_size], *sends[dp_size - 1 :]], outs[-1]
+            cart_sends, near, far, received = lax.optimization_barrier((cart_sends, near, far, received))
         else:
-            query_list.append(outs[-2])
+            kept_list += near
             self_list.append(outs[-1])
-            cart_list.append(
-                pl.pallas_call(
-                    sum_kernel,
-                    out_shape=jax.ShapeDtypeStruct((2, part_rows, head_dim), f32),
-                    compiler_params=pltpu.CompilerParams(vmem_limit_bytes=small_vmem_bytes),
-                    cost_estimate=pl.CostEstimate(flops=2**20, bytes_accessed=2**20, transcendentals=0),
-                    name="cart_sum",
-                )(*cart_parts)
-            )
-    query_list = [shift(part, "heads", heads_size, step) for step, part in enumerate(query_list)]
+        cart_parts = [outs[0], *[shift(part, "dp", dp_size, step + 1) for step, part in enumerate(cart_sends)]]
+        far_parts = [shift(part, "heads", heads_size, kept + step) for step, part in enumerate(far)]
+        if not last:
+            received.append((cart_parts, far_parts))
+    for early_cart, early_far in received:
+        cart_list.append(
+            pl.pallas_call(
+                sum_kernel,
+                out_shape=jax.ShapeDtypeStruct((2, part_rows, head_dim), f32),
+                compiler_params=pltpu.CompilerParams(vmem_limit_bytes=small_vmem_bytes),
+                cost_estimate=pl.CostEstimate(flops=2**20, bytes_accessed=2**20, transcendentals=0),
+                name="cart_sum",
+            )(*early_cart)
+        )
+        far_list += early_far
+    query_list = [shift(part, "heads", heads_size, step) for step, part in enumerate(near)] + far_list + far_parts
     query_grads = pl.pallas_call(
-        functools.partial(place_kernel, heads_size),
+        functools.partial(place_kernel, heads_size, kv_local),
         out_shape=jax.ShapeDtypeStruct((own_tokens, heads_size * heads_local * head_dim), bf16),
-        in_specs=[anywhere] * heads_size,
+        in_specs=[anywhere] * len(query_list),
         out_specs=anywhere,
-        scratch_shapes=[pltpu.SemaphoreType.DMA((heads_size,))],
+        scratch_shapes=[pltpu.SemaphoreType.DMA((len(query_list),))],
         compiler_params=pltpu.CompilerParams(vmem_limit_bytes=small_vmem_bytes),
         cost_estimate=pl.CostEstimate(flops=2**20, bytes_accessed=2 * 2**20, transcendentals=0),
         name="place_queries",
     )(*query_list)
-    query_grads, cart_list, cart_parts = lax.optimization_barrier((query_grads, cart_list, cart_parts))
     cart_grads = pl.pallas_call(
         functools.partial(cart_kernel, kv_local),
         out_shape=jax.ShapeDtypeStruct((part_rows * 2 * kv_local, head_dim), f32),
@@ -370,7 +379,7 @@
         name="cart_grads",
     )(*cart_list, *cart_parts)
     cart_grads = cart_grads.reshape(part_rows, 2, kv_local, head_dim)
-    self_grads = self_grads.reshape(2, tokens, kv_local, head_dim)
+    self_grads = outs[-1].reshape(2, tokens, kv_local, head_dim)
     return (cart_grads, self_grads, query_grads)
 
 

time: 46.9 us -> 48 us (1.023)
  starting transfers between devices: 12 us -> 13.7 us
  waiting for transfers between devices: 9.08 us -> 8.37 us
    ppermute x9 -> x11, starting transfers between devices: 12 us -> 13.7 us  [shift(): lax.ppermute(values, axis, [(source, target_of(source, step, size)) for s...]
    ppermute x9 -> x11, waiting for transfers between devices: 9.08 us -> 8.37 us  [shift(): lax.ppermute(values, axis, [(source, target_of(source, step, size)) for s...]
  transfers between devices with their start and end apart: 9 -> 11, of which waited for: 3 -> 2; matrix products, arithmetic and copies ran while one was open for 0% -> 0% of each run, Pallas kernels for 28% -> 27%
where the time goes in v8:
time: 48 us; the launch traced here: 47.8 us
  Pallas kernels  24.7 us (51%)
  starting transfers between devices  13.7 us (29%)
  waiting for transfers between devices  8.37 us (17%)
  between operations  0.88 us (2%)
    pallas_call x2, Pallas kernels, on_device(): pl.pallas_call(functools.partial(head_kernel, dp_size, heads_size, kv_ind...  22.8 us
    ppermute x11, starting transfers between devices, shift(): lax.ppermute(values, axis, [(source, target_of(source, step, size)) for s...  13.7 us
    ppermute x11, waiting for transfers between devices, shift(): lax.ppermute(values, axis, [(source, target_of(source, step, size)) for s...  8.37 us
    pallas_call x1, Pallas kernels, on_device(): pl.pallas_call(functools.partial(place_kernel, heads_size, kv_local), out...  1.01 us
  transfers between devices with their start and end apart: 11, of which 2 were waited for; matrix products, arithmetic and copies ran while one was open for 0% of the time, Pallas kernels for 27%

profile of v8, /device:TPU:0, one launch (start us, length us, event | category | flops | bytes accessed | tf_op | source)
XLA Modules:
  0.0 47.8 jit_solution(10590654194086436748)
XLA Ops:
  0.6 11.1 %head_grads.2 = (f32[2,256,128]{2,1,0:T(8,128)}, bf16[2,256,128]{2,1,0:T(8,128)(2,1)}, bf16[2,256,128]{2,1,0:T(8,128)(2,1)}, bf16[2,256,128]{2,1,0:T(8,128)(2,1)...) custom-call(bf16[4096,128]{1,0:T(8,128)(2,1)} %bitcast.9, ...), custom_call_target="tpu_custom_call" | custom-call | flops 6710886400 | bytes 5242880 | tf_op jit(solution)/shard_map/head_grads/pallas_call | solution.py:310
  11.7 3.1 %collective-permute-start = (bf16[2,256,128]{2,1,0:T(8,128)(2,1)}, bf16[2,256,128]{2,1,0:T(8,128)(2,1)S(1)}, u32[]{:S(2)}, u32[]{:S(2)}) collective-permute-start(bf16[2,256,128]{2,1,0:T(8,128)(2,1)} %get-tuple-element.45), channel_id=1, source_target_pairs={{0,4},{4,0},{8,12},{12,8},{1,5},{5,1},{9,13},{13,9},{2,6},{6,2},{1... | collective-permute-start | bytes 393224 | tf_op jit(solution)/shard_map/ppermute | solution.py:278
  14.8 2.6 %collective-permute-start.1 = (bf16[2,256,128]{2,1,0:T(8,128)(2,1)}, bf16[2,256,128]{2,1,0:T(8,128)(2,1)S(1)}, u32[]{:S(2)}, u32[]{:S(2)}) collective-permute-start(bf16[2,256,128]{2,1,0:T(8,128)(2,1)} %get-tuple-element.46), channel_id=1, source_target_pairs={{0,8},{4,12},{8,0},{12,4},{1,9},{5,13},{9,1},{13,5},{2,10},{6,14},... | collective-permute-start | bytes 393224 | tf_op jit(solution)/shard_map/ppermute | solution.py:278
  17.4 0.0 collective-permute-start.2
  17.4 1.7 %collective-permute-start.3 = (bf16[64,1024]{1,0:T(8,128)(2,1)}, bf16[64,1024]{1,0:T(8,128)(2,1)S(1)}, u32[]{:S(2)}, u32[]{:S(2)}) collective-permute-start(bf16[64,1024]{1,0:T(8,128)(2,1)} %get-tuple-element.48), channel_id=1, source_target_pairs={{0,2},{1,3},{2,0},{3,1},{4,6},{5,7},{6,4},{7,5},{8,10},{9,11},{10,... | collective-permute-start | bytes 393224 | tf_op jit(solution)/shard_map/ppermute | solution.py:278
  19.1 0.0 collective-permute-start.4
  19.1 0.0 copy-start
  19.1 11.7 %head_grads.3 = (f32[2,256,128]{2,1,0:T(8,128)}, bf16[2,256,128]{2,1,0:T(8,128)(2,1)}, bf16[2,256,128]{2,1,0:T(8,128)(2,1)}, bf16[2,256,128]{2,1,0:T(8,128)(2,1)...) custom-call(bf16[4096,128]{1,0:T(8,128)(2,1)} %bitcast.10, ...), custom_call_target="tpu_custom_call" | custom-call | flops 6710886400 | bytes 5242880 | tf_op jit(solution)/shard_map/head_grads/pallas_call | solution.py:310
  30.9 0.0 collective-permute-done.refs_1_
  30.9 0.0 collective-permute-done.1.refs_2_
  30.9 0.0 collective-permute-done.2.refs_3_
  30.9 0.0 collective-permute-done.3.refs_2_
  30.9 0.0 collective-permute-done.4.refs_3_
  30.9 0.0 copy-start.1
  30.9 0.8 %collective-permute-start.5 = (bf16[2,256,128]{2,1,0:T(8,128)(2,1)}, bf16[2,256,128]{2,1,0:T(8,128)(2,1)S(1)}, u32[]{:S(2)}, u32[]{:S(2)}) collective-permute-start(bf16[2,256,128]{2,1,0:T(8,128)(2,1)} %get-tuple-element.55), channel_id=1, source_target_pairs={{0,4},{4,0},{8,12},{12,8},{1,5},{5,1},{9,13},{13,9},{2,6},{6,2},{1... | collective-permute-start | bytes 393224 | tf_op jit(solution)/shard_map/ppermute | solution.py:278
  31.7 0.3 collective-permute-start.8
  32.0 3.5 %collective-permute-start.6 = (bf16[2,256,128]{2,1,0:T(8,128)(2,1)}, bf16[2,256,128]{2,1,0:T(8,128)(2,1)S(1)}, u32[]{:S(2)}, u32[]{:S(2)}) collective-permute-start(bf16[2,256,128]{2,1,0:T(8,128)(2,1)} %get-tuple-element.56), channel_id=1, source_target_pairs={{0,8},{4,12},{8,0},{12,4},{1,9},{5,13},{9,1},{13,5},{2,10},{6,14},... | collective-permute-start | bytes 393224 | tf_op jit(solution)/shard_map/ppermute | solution.py:278
  35.5 0.0 collective-permute-start.7
  35.5 1.7 %collective-permute-start.9 = (bf16[64,1024]{1,0:T(8,128)(2,1)}, bf16[64,1024]{1,0:T(8,128)(2,1)S(1)}, u32[]{:S(2)}, u32[]{:S(2)}) collective-permute-start(bf16[64,1024]{1,0:T(8,128)(2,1)} %get-tuple-element.63), channel_id=1, source_target_pairs={{0,2},{1,3},{2,0},{3,1},{4,6},{5,7},{6,4},{7,5},{8,10},{9,11},{10,... | collective-permute-start | bytes 393224 | tf_op jit(solution)/shard_map/ppermute | solution.py:278
  37.2 2.2 %collective-permute-done.5.refs_2_ = bf16[2,256,128]{2,1,0:T(8,128)(2,1)S(1)} collective-permute-done((bf16[2,256,128]{2,1,0:T(8,128)(2,1)}, bf16[2,256,128]{2,1,0:T(8,128)(2,1)S(1)}, u32[]{:S(2)}, u32[]{:S(2)}) %collective-permute-start.5) | collective-permute-done | bytes 131104 | tf_op jit(solution)/shard_map/ppermute | solution.py:278
  39.4 0.0 collective-permute-start.10
  39.4 0.0 copy-done
  39.4 0.1 cart_sum.1.refs_0_
  39.5 6.2 %collective-permute-done.6.refs_3_ = bf16[2,256,128]{2,1,0:T(8,128)(2,1)S(1)} collective-permute-done((bf16[2,256,128]{2,1,0:T(8,128)(2,1)}, bf16[2,256,128]{2,1,0:T(8,128)(2,1)S(1)}, u32[]{:S(2)}, u32[]{:S(2)}) %collective-permute-start.6) | collective-permute-done | bytes 131104 | tf_op jit(solution)/shard_map/ppermute | solution.py:278
  45.7 0.0 collective-permute-done.7.refs_4_
  45.7 0.0 copy-done.1
  45.7 0.9 %cart_grads.1 = f32[1024,128]{1,0:T(8,128)} custom-call(f32[2,256,128]{2,1,0:T(8,128)S(1)} %cart_sum.1.refs_0_, f32[2,256,128]{2,1,0:T(8,128)S(1)} %copy-done.1, bf16[2,256,128]{2,1,0:T(8,128)(2,1)S(1)} %collective-permute-done.5.refs_2_, bf16[2,256,128]{2,1,0:T(8,128)(2,1)S(1)} %collective-permute-done.6.refs_3_, ...), custom_call_target="tpu_custom_call" | custom-call | flops 1048576 | bytes 2097152 | tf_op jit(solution)/shard_map/cart_grads/pallas_call | solution.py:374
  46.5 0.0 collective-permute-done.9.refs_4_
  46.6 0.0 collective-permute-done.10.refs_5_
  46.6 0.0 collective-permute-done.8.refs_1_
  46.6 0.1 copy-done.2
  46.6 1.0 %place_queries.1 = bf16[64,8192]{1,0:T(8,128)(2,1)} custom-call(bf16[64,2048]{1,0:T(8,128)(2,1)S(1)} %copy-done.2, bf16[64,2048]{1,0:T(8,128)(2,1)S(1)} %collective-permute-done.8.refs_1_, bf16[64,1024]{1,0:T(8,128)(2,1)S(1)} %collective-permute-done.3.refs_2_, bf16[64,1024]{1,0:T(8,128)(2,1)S(1)} %collective-permute-done.4.refs_3_, ...), custom_call_target="tpu_custom_call" | custom-call | flops 1048576 | bytes 2097152 | tf_op jit(solution)/shard_map/place_queries/pallas_call | solution.py:364
  (1 shorter events, 0.0 us)
Async XLA Ops:
  11.7 19.2 %collective-permute-start = (bf16[2,256,128]{2,1,0:T(8,128)(2,1)}, bf16[2,256,128]{2,1,0:T(8,128)(2,1)S(1)}, u32[]{:S(2)}, u32[]{:S(2)}) collective-permute-start(bf16[2,256,128]{2,1,0:T(8,128)(2,1)} %get-tuple-element.45), channel_id=1, source_target_pairs={{0,4},{4,0},{8,12},{12,8},{1,5},{5,1},{9,13},{13,9},{2,6},{6,2},{1... | collective-permute-start | bytes 393224 | tf_op jit(solution)/shard_map/ppermute | solution.py:278
  14.8 16.1 %collective-permute-start.1 = (bf16[2,256,128]{2,1,0:T(8,128)(2,1)}, bf16[2,256,128]{2,1,0:T(8,128)(2,1)S(1)}, u32[]{:S(2)}, u32[]{:S(2)}) collective-permute-start(bf16[2,256,128]{2,1,0:T(8,128)(2,1)} %get-tuple-element.46), channel_id=1, source_target_pairs={{0,8},{4,12},{8,0},{12,4},{1,9},{5,13},{9,1},{13,5},{2,10},{6,14},... | collective-permute-start | bytes 393224 | tf_op jit(solution)/shard_map/ppermute | solution.py:278
  17.4 13.5 %collective-permute-start.2 = (bf16[2,256,128]{2,1,0:T(8,128)(2,1)}, bf16[2,256,128]{2,1,0:T(8,128)(2,1)S(1)}, u32[]{:S(2)}, u32[]{:S(2)}) collective-permute-start(bf16[2,256,128]{2,1,0:T(8,128)(2,1)} %get-tuple-element.47), channel_id=1, source_target_pairs={{0,12},{4,8},{8,4},{12,0},{1,13},{5,9},{9,5},{13,1},{2,14},{6,10},... | collective-permute-start | bytes 393224 | tf_op jit(solution)/shard_map/ppermute | solution.py:278
  17.4 13.5 %collective-permute-start.3 = (bf16[64,1024]{1,0:T(8,128)(2,1)}, bf16[64,1024]{1,0:T(8,128)(2,1)S(1)}, u32[]{:S(2)}, u32[]{:S(2)}) collective-permute-start(bf16[64,1024]{1,0:T(8,128)(2,1)} %get-tuple-element.48), channel_id=1, source_target_pairs={{0,2},{1,3},{2,0},{3,1},{4,6},{5,7},{6,4},{7,5},{8,10},{9,11},{10,... | collective-permute-start | bytes 393224 | tf_op jit(solution)/shard_map/ppermute | solution.py:278
  19.1 11.8 %collective-permute-start.4 = (bf16[64,1024]{1,0:T(8,128)(2,1)}, bf16[64,1024]{1,0:T(8,128)(2,1)S(1)}, u32[]{:S(2)}, u32[]{:S(2)}) collective-permute-start(bf16[64,1024]{1,0:T(8,128)(2,1)} %get-tuple-element.49), channel_id=1, source_target_pairs={{0,3},{1,2},{2,1},{3,0},{4,7},{5,6},{6,5},{7,4},{8,11},{9,10},{10,... | collective-permute-start | bytes 393224 | tf_op jit(solution)/shard_map/ppermute | solution.py:278
  19.1 20.3 %copy-start = (f32[2,256,128]{2,1,0:T(8,128)S(1)}, f32[2,256,128]{2,1,0:T(8,128)}, u32[]{:S(2)}) copy-start(f32[2,256,128]{2,1,0:T(8,128)} %get-tuple-element.50.refs_0_) | copy-start | bytes 786436
  30.9 14.8 %copy-start.1 = (f32[2,256,128]{2,1,0:T(8,128)S(1)}, f32[2,256,128]{2,1,0:T(8,128)}, u32[]{:S(2)}) copy-start(f32[2,256,128]{2,1,0:T(8,128)} %get-tuple-element.54.refs_1_) | copy-start | bytes 786436
  30.9 8.5 %collective-permute-start.5 = (bf16[2,256,128]{2,1,0:T(8,128)(2,1)}, bf16[2,256,128]{2,1,0:T(8,128)(2,1)S(1)}, u32[]{:S(2)}, u32[]{:S(2)}) collective-permute-start(bf16[2,256,128]{2,1,0:T(8,128)(2,1)} %get-tuple-element.55), channel_id=1, source_target_pairs={{0,4},{4,0},{8,12},{12,8},{1,5},{5,1},{9,13},{13,9},{2,6},{6,2},{1... | collective-permute-start | bytes 393224 | tf_op jit(solution)/shard_map/ppermute | solution.py:278
  31.7 14.9 %collective-permute-start.8 = (bf16[64,2048]{1,0:T(8,128)(2,1)}, bf16[64,2048]{1,0:T(8,128)(2,1)S(1)}, u32[]{:S(2)}, u32[]{:S(2)}) collective-permute-start(bf16[64,2048]{1,0:T(8,128)(2,1)} %get-tuple-element.60), channel_id=1, source_target_pairs={{0,1},{1,0},{2,3},{3,2},{4,5},{5,4},{6,7},{7,6},{8,9},{9,8},{10,11... | collective-permute-start | bytes 786440 | tf_op jit(solution)/shard_map/ppermute | solution.py:278
  32.0 13.6 %collective-permute-start.6 = (bf16[2,256,128]{2,1,0:T(8,128)(2,1)}, bf16[2,256,128]{2,1,0:T(8,128)(2,1)S(1)}, u32[]{:S(2)}, u32[]{:S(2)}) collective-permute-start(bf16[2,256,128]{2,1,0:T(8,128)(2,1)} %get-tuple-element.56), channel_id=1, source_target_pairs={{0,8},{4,12},{8,0},{12,4},{1,9},{5,13},{9,1},{13,5},{2,10},{6,14},... | collective-permute-start | bytes 393224 | tf_op jit(solution)/shard_map/ppermute | solution.py:278
  35.5 10.2 %collective-permute-start.7 = (bf16[2,256,128]{2,1,0:T(8,128)(2,1)}, bf16[2,256,128]{2,1,0:T(8,128)(2,1)S(1)}, u32[]{:S(2)}, u32[]{:S(2)}) collective-permute-start(bf16[2,256,128]{2,1,0:T(8,128)(2,1)} %get-tuple-element.57), channel_id=1, source_target_pairs={{0,12},{4,8},{8,4},{12,0},{1,13},{5,9},{9,5},{13,1},{2,14},{6,10},... | collective-permute-start | bytes 393224 | tf_op jit(solution)/shard_map/ppermute | solution.py:278
  35.5 11.0 %collective-permute-start.9 = (bf16[64,1024]{1,0:T(8,128)(2,1)}, bf16[64,1024]{1,0:T(8,128)(2,1)S(1)}, u32[]{:S(2)}, u32[]{:S(2)}) collective-permute-start(bf16[64,1024]{1,0:T(8,128)(2,1)} %get-tuple-element.63), channel_id=1, source_target_pairs={{0,2},{1,3},{2,0},{3,1},{4,6},{5,7},{6,4},{7,5},{8,10},{9,11},{10,... | collective-permute-start | bytes 393224 | tf_op jit(solution)/shard_map/ppermute | solution.py:278
  39.4 7.1 %collective-permute-start.10 = (bf16[64,1024]{1,0:T(8,128)(2,1)}, bf16[64,1024]{1,0:T(8,128)(2,1)S(1)}, u32[]{:S(2)}, u32[]{:S(2)}) collective-permute-start(bf16[64,1024]{1,0:T(8,128)(2,1)} %get-tuple-element.64), channel_id=1, source_target_pairs={{0,3},{1,2},{2,1},{3,0},{4,7},{5,6},{6,5},{7,4},{8,11},{9,10},{10,... | collective-permute-start | bytes 393224 | tf_op jit(solution)/shard_map/ppermute | solution.py:278
  45.7 1.0 %copy-start.2 = (bf16[64,2048]{1,0:T(8,128)(2,1)S(1)}, bf16[64,2048]{1,0:T(8,128)(2,1)}, u32[]{:S(2)}) copy-start(bf16[64,2048]{1,0:T(8,128)(2,1)} %get-tuple-element.59.refs_0_) | copy-start | bytes 786436

commit v9 on v8

--- a/solution.py
+++ b/solution.py
@@ -11,7 +11,7 @@
 masked_score = -1e30
 vmem_bytes = 56 * 1024 * 1024
 small_vmem_bytes = 8 * 1024 * 1024
-kept_steps = 2
+early_steps = (2,)
 f32 = jnp.float32
 bf16 = jnp.bfloat16
 
@@ -34,7 +34,8 @@
     q_ref, g_ref, sk_ref, sv_ref, ck_ref, cv_ref, seg_ref = refs[:7]
     refs = refs[7:]
     held = kv_index if last else 0
-    kept = min(kept_steps, heads_size)
+    near_steps, far_steps = split_steps(heads_size)
+    kept = len(near_steps)
     dq_before, refs = refs[: held * kept], refs[held * kept :]
     self_before, refs = refs[:held], refs[held:]
     cart_outs, refs = refs[:dp_size], refs[dp_size:]
@@ -195,7 +196,7 @@
     part_rows = cart_rows // dp_size
     me = lax.axis_index("dp")
     for step, ref in enumerate(cart_outs):
-        target = target_of(me, step, dp_size)
+        target = target_of(me, step, "dp", dp_size)
         at = pl.ds(pl.multiple_of(target * part_rows, part_rows), part_rows)
         ref[0] = (dk_ref[at, :] * scale).astype(ref.dtype)
         ref[1] = dv_ref[at, :].astype(ref.dtype)
@@ -203,12 +204,12 @@
     own_tokens = tokens // heads_size
     columns = width * head_dim
     me = lax.axis_index("heads")
-    for step, ref in enumerate(dq_outs):
-        target = target_of(me, step, heads_size)
+    for place, (step, ref) in enumerate(zip(near_steps + far_steps, dq_outs)):
+        target = target_of(me, step, "heads", heads_size)
         at = pl.ds(pl.multiple_of(target * own_tokens, own_tokens), own_tokens)
-        if last and step < kept:
+        if last and place < kept:
             for index in range(held):
-                ref[:, index * columns : (index + 1) * columns] = dq_before[index * kept + step][...]
+                ref[:, index * columns : (index + 1) * columns] = dq_before[index * kept + place][...]
             ref[:, held * columns :] = dq_ref[at, :]
         else:
             ref[...] = dq_ref[at, :]
@@ -244,14 +245,14 @@
 
 def place_kernel(heads_size, kv_local, *refs):
     part_refs, out_ref, sems = refs[:-2], refs[-2], refs[-1]
-    kept = min(kept_steps, heads_size)
+    near_steps, far_steps = split_steps(heads_size)
     columns = out_ref.shape[1] // (heads_size * kv_local)
     me = lax.axis_index("heads")
-    places = [(step, 0) for step in range(kept)]
-    places += [(step, kv_index) for kv_index in range(kv_local) for step in range(kept, heads_size)]
+    places = [(step, 0) for step in near_steps]
+    places += [(step, kv_index) for kv_index in range(kv_local) for step in far_steps]
     copies = []
     for index, ((step, kv_index), ref) in enumerate(zip(places, part_refs)):
-        source = source_of(me, step, heads_size)
+        source = source_of(me, step, "heads", heads_size)
         at = pl.multiple_of((source * kv_local + kv_index) * columns, columns)
         copies.append(pltpu.make_async_copy(ref, out_ref.at[:, pl.ds(at, ref.shape[1])], sems.at[index]))
     for copy in copies:
@@ -260,22 +261,27 @@
         copy.wait()
 
 
-def paired(size):
-    return size & (size - 1) == 0
-
-
-def target_of(me, step, size):
-    return me ^ step if paired(size) else (me + step) % size
-
-
-def source_of(me, step, size):
-    return me ^ step if paired(size) else (me + size - step) % size
+def paired(axis, size):
+    return axis == "heads" and size & (size - 1) == 0
+
+
+def target_of(me, step, axis, size):
+    return me ^ step if paired(axis, size) else (me + step) % size
+
+
+def source_of(me, step, axis, size):
+    return me ^ step if paired(axis, size) else (me + size - step) % size
 
 
 def shift(values, axis, size, step):
     if step == 0:
         return values
-    return lax.ppermute(values, axis, [(source, target_of(source, step, size)) for source in range(size)])
+    return lax.ppermute(values, axis, [(source, target_of(source, step, axis, size)) for source in range(size)])
+
+
+def split_steps(heads_size):
+    early = [step for step in range(heads_size) if step in early_steps]
+    return [step for step in range(heads_size) if step not in early], early
 
 
 def on_device(dp_size, heads_size, queries, out_grad, self_keys, self_values, cart_keys, cart_values, segment_ids):
@@ -296,7 +302,8 @@
     blocks = tokens // block_tokens
     columns = width * head_dim
     count = tokens * kv_local
-    kept = min(kept_steps, heads_size)
+    near_steps, far_steps = split_steps(heads_size)
+    kept = len(near_steps)
     anywhere = pl.BlockSpec(memory_space=pl.ANY)
     cart_list, kept_list, far_list, self_list, received = [], [], [], [], []
     for kv_index in range(kv_local):
@@ -346,7 +353,7 @@
             kept_list += near
             self_list.append(outs[-1])
         cart_parts = [outs[0], *[shift(part, "dp", dp_size, step + 1) for step, part in enumerate(cart_sends)]]
-        far_parts = [shift(part, "heads", heads_size, kept + step) for step, part in enumerate(far)]
+        far_parts = [shift(part, "heads", heads_size, step) for step, part in zip(far_steps, far)]
         if not last:
             received.append((cart_parts, far_parts))
     for early_cart, early_far in received:
@@ -360,7 +367,7 @@
             )(*early_cart)
         )
         far_list += early_far
-    query_list = [shift(part, "heads", heads_size, step) for step, part in enumerate(near)] + far_list + far_parts
+    query_list = [shift(part, "heads", heads_size, step) for step, part in zip(near_steps, near)] + far_list + far_parts
     query_grads = pl.pallas_call(
         functools.partial(place_kernel, heads_size, kv_local),
         out_shape=jax.ShapeDtypeStruct((own_tokens, heads_size * heads_local * head_dim), bf16),

time: 48 us -> 47.1 us (0.981)
  starting transfers between devices: 13.7 us -> 13 us
    ppermute x11 -> x10, starting transfers between devices: 13.7 us -> 13 us  [shift(): lax.ppermute(values, axis, [(source, target_of(source, step, axis, size))...]
    ppermute x11 -> x10, waiting for transfers between devices: 8.37 us -> 8.32 us  [shift(): lax.ppermute(values, axis, [(source, target_of(source, step, axis, size))...]
  transfers between devices with their start and end apart: 11 -> 10, of which waited for: 2 -> 3; matrix products, arithmetic and copies ran while one was open for 0% -> 0% of each run, Pallas kernels for 27% -> 27%
where the time goes in v9:
time: 47.1 us; the launch traced here: 47 us
  Pallas kernels  24.7 us (52%)
  starting transfers between devices  13 us (28%)
  waiting for transfers between devices  8.32 us (18%)
  between operations  0.87 us (2%)
    pallas_call x2, Pallas kernels, on_device(): pl.pallas_call(functools.partial(head_kernel, dp_size, heads_size, kv_ind...  22.8 us
    ppermute x10, starting transfers between devices, shift(): lax.ppermute(values, axis, [(source, target_of(source, step, axis, size))...  13 us
    ppermute x10, waiting for transfers between devices, shift(): lax.ppermute(values, axis, [(source, target_of(source, step, axis, size))...  8.32 us
    pallas_call x1, Pallas kernels, on_device(): pl.pallas_call(functools.partial(place_kernel, heads_size, kv_local), out...  1.01 us
  transfers between devices with their start and end apart: 10, of which 3 were waited for; matrix products, arithmetic and copies ran while one was open for 0% of the time, Pallas kernels for 27%

profile of v9, /device:TPU:0, one launch (start us, length us, event | category | flops | bytes accessed | tf_op | source)
XLA Modules:
  0.0 47.0 jit_solution(9029368414531527518)
XLA Ops:
  0.6 11.1 %head_grads.2 = (f32[2,256,128]{2,1,0:T(8,128)}, bf16[2,256,128]{2,1,0:T(8,128)(2,1)}, bf16[2,256,128]{2,1,0:T(8,128)(2,1)}, bf16[2,256,128]{2,1,0:T(8,128)(2,1)...) custom-call(bf16[4096,128]{1,0:T(8,128)(2,1)} %bitcast.9, ...), custom_call_target="tpu_custom_call" | custom-call | flops 6710886400 | bytes 5242880 | tf_op jit(solution)/shard_map/head_grads/pallas_call | solution.py:317
  11.7 3.1 %collective-permute-start = (bf16[2,256,128]{2,1,0:T(8,128)(2,1)}, bf16[2,256,128]{2,1,0:T(8,128)(2,1)S(1)}, u32[]{:S(2)}, u32[]{:S(2)}) collective-permute-start(bf16[2,256,128]{2,1,0:T(8,128)(2,1)} %get-tuple-element.45), channel_id=1, source_target_pairs={{0,4},{4,8},{8,12},{12,0},{1,5},{5,9},{9,13},{13,1},{2,6},{6,10},{... | collective-permute-start | bytes 393224 | tf_op jit(solution)/shard_map/ppermute | solution.py:279
  14.8 2.6 %collective-permute-start.1 = (bf16[2,256,128]{2,1,0:T(8,128)(2,1)}, bf16[2,256,128]{2,1,0:T(8,128)(2,1)S(1)}, u32[]{:S(2)}, u32[]{:S(2)}) collective-permute-start(bf16[2,256,128]{2,1,0:T(8,128)(2,1)} %get-tuple-element.46), channel_id=1, source_target_pairs={{0,8},{4,12},{8,0},{12,4},{1,9},{5,13},{9,1},{13,5},{2,10},{6,14},... | collective-permute-start | bytes 393224 | tf_op jit(solution)/shard_map/ppermute | solution.py:279
  17.4 1.3 %collective-permute-start.2 = (bf16[2,256,128]{2,1,0:T(8,128)(2,1)}, bf16[2,256,128]{2,1,0:T(8,128)(2,1)S(1)}, u32[]{:S(2)}, u32[]{:S(2)}) collective-permute-start(bf16[2,256,128]{2,1,0:T(8,128)(2,1)} %get-tuple-element.47), channel_id=1, source_target_pairs={{0,12},{4,0},{8,4},{12,8},{1,13},{5,1},{9,5},{13,9},{2,14},{6,2},{... | collective-permute-start | bytes 393224 | tf_op jit(solution)/shard_map/ppermute | solution.py:279
  18.7 1.5 %collective-permute-start.3 = (bf16[64,1024]{1,0:T(8,128)(2,1)}, bf16[64,1024]{1,0:T(8,128)(2,1)S(1)}, u32[]{:S(2)}, u32[]{:S(2)}) collective-permute-start(bf16[64,1024]{1,0:T(8,128)(2,1)} %get-tuple-element.48), channel_id=1, source_target_pairs={{0,2},{1,3},{2,0},{3,1},{4,6},{5,7},{6,4},{7,5},{8,10},{9,11},{10,... | collective-permute-start | bytes 393224 | tf_op jit(solution)/shard_map/ppermute | solution.py:279
  20.2 0.0 copy-start
  20.2 11.7 %head_grads.3 = (f32[2,256,128]{2,1,0:T(8,128)}, bf16[2,256,128]{2,1,0:T(8,128)(2,1)}, bf16[2,256,128]{2,1,0:T(8,128)(2,1)}, bf16[2,256,128]{2,1,0:T(8,128)(2,1)...) custom-call(bf16[4096,128]{1,0:T(8,128)(2,1)} %bitcast.10, ...), custom_call_target="tpu_custom_call" | custom-call | flops 6710886400 | bytes 5242880 | tf_op jit(solution)/shard_map/head_grads/pallas_call | solution.py:317
  32.0 0.0 collective-permute-done.refs_1_
  32.0 0.0 collective-permute-done.1.refs_2_
  32.0 0.0 collective-permute-done.2.refs_3_
  32.0 0.0 collective-permute-done.3.refs_3_
  32.0 0.0 copy-start.1
  32.0 0.7 %collective-permute-start.4 = (bf16[2,256,128]{2,1,0:T(8,128)(2,1)}, bf16[2,256,128]{2,1,0:T(8,128)(2,1)S(1)}, u32[]{:S(2)}, u32[]{:S(2)}) collective-permute-start(bf16[2,256,128]{2,1,0:T(8,128)(2,1)} %get-tuple-element.54), channel_id=1, source_target_pairs={{0,4},{4,8},{8,12},{12,0},{1,5},{5,9},{9,13},{13,1},{2,6},{6,10},{... | collective-permute-start | bytes 393224 | tf_op jit(solution)/shard_map/ppermute | solution.py:279
  32.7 0.0 collective-permute-start.7
  32.7 0.7 %collective-permute-start.8 = (bf16[64,2048]{1,0:T(8,128)(2,1)}, bf16[64,2048]{1,0:T(8,128)(2,1)S(1)}, u32[]{:S(2)}, u32[]{:S(2)}) collective-permute-start(bf16[64,2048]{1,0:T(8,128)(2,1)} %get-tuple-element.60), channel_id=1, source_target_pairs={{0,3},{1,2},{2,1},{3,0},{4,7},{5,6},{6,5},{7,4},{8,11},{9,10},{10,... | collective-permute-start | bytes 786440 | tf_op jit(solution)/shard_map/ppermute | solution.py:279
  33.4 0.3 collective-permute-start.5
  33.7 2.8 %collective-permute-start.6 = (bf16[2,256,128]{2,1,0:T(8,128)(2,1)}, bf16[2,256,128]{2,1,0:T(8,128)(2,1)S(1)}, u32[]{:S(2)}, u32[]{:S(2)}) collective-permute-start(bf16[2,256,128]{2,1,0:T(8,128)(2,1)} %get-tuple-element.56), channel_id=1, source_target_pairs={{0,12},{4,0},{8,4},{12,8},{1,13},{5,1},{9,5},{13,9},{2,14},{6,2},{... | collective-permute-start | bytes 393224 | tf_op jit(solution)/shard_map/ppermute | solution.py:279
  36.5 4.1 %collective-permute-done.4.refs_2_ = bf16[2,256,128]{2,1,0:T(8,128)(2,1)S(1)} collective-permute-done((bf16[2,256,128]{2,1,0:T(8,128)(2,1)}, bf16[2,256,128]{2,1,0:T(8,128)(2,1)S(1)}, u32[]{:S(2)}, u32[]{:S(2)}) %collective-permute-start.4) | collective-permute-done | bytes 131104 | tf_op jit(solution)/shard_map/ppermute | solution.py:279
  40.6 0.0 collective-permute-start.9
  40.6 0.0 copy-done
  40.6 0.1 cart_sum.1.refs_0_
  40.7 4.0 %collective-permute-done.5.refs_3_ = bf16[2,256,128]{2,1,0:T(8,128)(2,1)S(1)} collective-permute-done((bf16[2,256,128]{2,1,0:T(8,128)(2,1)}, bf16[2,256,128]{2,1,0:T(8,128)(2,1)S(1)}, u32[]{:S(2)}, u32[]{:S(2)}) %collective-permute-start.5) | collective-permute-done | bytes 131104 | tf_op jit(solution)/shard_map/ppermute | solution.py:279
  44.7 0.0 collective-permute-done.6.refs_4_
  44.7 0.0 copy-done.1
  44.7 0.0 copy-start.2
  44.7 0.9 %cart_grads.1 = f32[1024,128]{1,0:T(8,128)} custom-call(f32[2,256,128]{2,1,0:T(8,128)S(1)} %cart_sum.1.refs_0_, f32[2,256,128]{2,1,0:T(8,128)S(1)} %copy-done.1, bf16[2,256,128]{2,1,0:T(8,128)(2,1)S(1)} %collective-permute-done.4.refs_2_, bf16[2,256,128]{2,1,0:T(8,128)(2,1)S(1)} %collective-permute-done.5.refs_3_, ...), custom_call_target="tpu_custom_call" | custom-call | flops 1048576 | bytes 2097152 | tf_op jit(solution)/shard_map/cart_grads/pallas_call | solution.py:381
  45.6 0.2 collective-permute-done.9.refs_4_
  45.8 0.0 collective-permute-done.7.refs_1_
  45.8 0.0 collective-permute-done.8.refs_2_
  45.8 0.0 copy-done.2
  45.8 1.0 %place_queries.1 = bf16[64,8192]{1,0:T(8,128)(2,1)} custom-call(bf16[64,2048]{1,0:T(8,128)(2,1)S(1)} %copy-done.2, bf16[64,2048]{1,0:T(8,128)(2,1)S(1)} %collective-permute-done.7.refs_1_, bf16[64,2048]{1,0:T(8,128)(2,1)S(1)} %collective-permute-done.8.refs_2_, bf16[64,1024]{1,0:T(8,128)(2,1)S(1)} %collective-permute-done.3.refs_3_, ...), custom_call_target="tpu_custom_call" | custom-call | flops 1048576 | bytes 2097152 | tf_op jit(solution)/shard_map/place_queries/pallas_call | solution.py:371
Async XLA Ops:
  11.7 20.2 %collective-permute-start = (bf16[2,256,128]{2,1,0:T(8,128)(2,1)}, bf16[2,256,128]{2,1,0:T(8,128)(2,1)S(1)}, u32[]{:S(2)}, u32[]{:S(2)}) collective-permute-start(bf16[2,256,128]{2,1,0:T(8,128)(2,1)} %get-tuple-element.45), channel_id=1, source_target_pairs={{0,4},{4,8},{8,12},{12,0},{1,5},{5,9},{9,13},{13,1},{2,6},{6,10},{... | collective-permute-start | bytes 393224 | tf_op jit(solution)/shard_map/ppermute | solution.py:279
  14.8 17.2 %collective-permute-start.1 = (bf16[2,256,128]{2,1,0:T(8,128)(2,1)}, bf16[2,256,128]{2,1,0:T(8,128)(2,1)S(1)}, u32[]{:S(2)}, u32[]{:S(2)}) collective-permute-start(bf16[2,256,128]{2,1,0:T(8,128)(2,1)} %get-tuple-element.46), channel_id=1, source_target_pairs={{0,8},{4,12},{8,0},{12,4},{1,9},{5,13},{9,1},{13,5},{2,10},{6,14},... | collective-permute-start | bytes 393224 | tf_op jit(solution)/shard_map/ppermute | solution.py:279
  17.4 14.6 %collective-permute-start.2 = (bf16[2,256,128]{2,1,0:T(8,128)(2,1)}, bf16[2,256,128]{2,1,0:T(8,128)(2,1)S(1)}, u32[]{:S(2)}, u32[]{:S(2)}) collective-permute-start(bf16[2,256,128]{2,1,0:T(8,128)(2,1)} %get-tuple-element.47), channel_id=1, source_target_pairs={{0,12},{4,0},{8,4},{12,8},{1,13},{5,1},{9,5},{13,9},{2,14},{6,2},{... | collective-permute-start | bytes 393224 | tf_op jit(solution)/shard_map/ppermute | solution.py:279
  18.7 13.3 %collective-permute-start.3 = (bf16[64,1024]{1,0:T(8,128)(2,1)}, bf16[64,1024]{1,0:T(8,128)(2,1)S(1)}, u32[]{:S(2)}, u32[]{:S(2)}) collective-permute-start(bf16[64,1024]{1,0:T(8,128)(2,1)} %get-tuple-element.48), channel_id=1, source_target_pairs={{0,2},{1,3},{2,0},{3,1},{4,6},{5,7},{6,4},{7,5},{8,10},{9,11},{10,... | collective-permute-start | bytes 393224 | tf_op jit(solution)/shard_map/ppermute | solution.py:279
  20.2 20.4 %copy-start = (f32[2,256,128]{2,1,0:T(8,128)S(1)}, f32[2,256,128]{2,1,0:T(8,128)}, u32[]{:S(2)}) copy-start(f32[2,256,128]{2,1,0:T(8,128)} %get-tuple-element.49.refs_0_) | copy-start | bytes 786436
  32.0 12.7 %copy-start.1 = (f32[2,256,128]{2,1,0:T(8,128)S(1)}, f32[2,256,128]{2,1,0:T(8,128)}, u32[]{:S(2)}) copy-start(f32[2,256,128]{2,1,0:T(8,128)} %get-tuple-element.53.refs_1_) | copy-start | bytes 786436
  32.0 8.6 %collective-permute-start.4 = (bf16[2,256,128]{2,1,0:T(8,128)(2,1)}, bf16[2,256,128]{2,1,0:T(8,128)(2,1)S(1)}, u32[]{:S(2)}, u32[]{:S(2)}) collective-permute-start(bf16[2,256,128]{2,1,0:T(8,128)(2,1)} %get-tuple-element.54), channel_id=1, source_target_pairs={{0,4},{4,8},{8,12},{12,0},{1,5},{5,9},{9,13},{13,1},{2,6},{6,10},{... | collective-permute-start | bytes 393224 | tf_op jit(solution)/shard_map/ppermute | solution.py:279
  32.7 13.1 %collective-permute-start.7 = (bf16[64,2048]{1,0:T(8,128)(2,1)}, bf16[64,2048]{1,0:T(8,128)(2,1)S(1)}, u32[]{:S(2)}, u32[]{:S(2)}) collective-permute-start(bf16[64,2048]{1,0:T(8,128)(2,1)} %get-tuple-element.59), channel_id=1, source_target_pairs={{0,1},{1,0},{2,3},{3,2},{4,5},{5,4},{6,7},{7,6},{8,9},{9,8},{10,11... | collective-permute-start | bytes 786440 | tf_op jit(solution)/shard_map/ppermute | solution.py:279
  32.7 13.1 %collective-permute-start.8 = (bf16[64,2048]{1,0:T(8,128)(2,1)}, bf16[64,2048]{1,0:T(8,128)(2,1)S(1)}, u32[]{:S(2)}, u32[]{:S(2)}) collective-permute-start(bf16[64,2048]{1,0:T(8,128)(2,1)} %get-tuple-element.60), channel_id=1, source_target_pairs={{0,3},{1,2},{2,1},{3,0},{4,7},{5,6},{6,5},{7,4},{8,11},{9,10},{10,... | collective-permute-start | bytes 786440 | tf_op jit(solution)/shard_map/ppermute | solution.py:279
  33.4 11.3 %collective-permute-start.5 = (bf16[2,256,128]{2,1,0:T(8,128)(2,1)}, bf16[2,256,128]{2,1,0:T(8,128)(2,1)S(1)}, u32[]{:S(2)}, u32[]{:S(2)}) collective-permute-start(bf16[2,256,128]{2,1,0:T(8,128)(2,1)} %get-tuple-element.55), channel_id=1, source_target_pairs={{0,8},{4,12},{8,0},{12,4},{1,9},{5,13},{9,1},{13,5},{2,10},{6,14},... | collective-permute-start | bytes 393224 | tf_op jit(solution)/shard_map/ppermute | solution.py:279
  33.7 11.0 %collective-permute-start.6 = (bf16[2,256,128]{2,1,0:T(8,128)(2,1)}, bf16[2,256,128]{2,1,0:T(8,128)(2,1)S(1)}, u32[]{:S(2)}, u32[]{:S(2)}) collective-permute-start(bf16[2,256,128]{2,1,0:T(8,128)(2,1)} %get-tuple-element.56), channel_id=1, source_target_pairs={{0,12},{4,0},{8,4},{12,8},{1,13},{5,1},{9,5},{13,9},{2,14},{6,2},{... | collective-permute-start | bytes 393224 | tf_op jit(solution)/shard_map/ppermute | solution.py:279
  40.6 5.2 %collective-permute-start.9 = (bf16[64,1024]{1,0:T(8,128)(2,1)}, bf16[64,1024]{1,0:T(8,128)(2,1)S(1)}, u32[]{:S(2)}, u32[]{:S(2)}) collective-permute-start(bf16[64,1024]{1,0:T(8,128)(2,1)} %get-tuple-element.62), channel_id=1, source_target_pairs={{0,2},{1,3},{2,0},{3,1},{4,6},{5,7},{6,4},{7,5},{8,10},{9,11},{10,... | collective-permute-start | bytes 393224 | tf_op jit(solution)/shard_map/ppermute | solution.py:279
  44.7 1.1 %copy-start.2 = (bf16[64,2048]{1,0:T(8,128)(2,1)S(1)}, bf16[64,2048]{1,0:T(8,128)(2,1)}, u32[]{:S(2)}) copy-start(bf16[64,2048]{1,0:T(8,128)(2,1)} %get-tuple-element.58.refs_0_) | copy-start | bytes 786436

commit v10 on v9

--- a/solution.py
+++ b/solution.py
@@ -146,27 +146,29 @@
         stats[block] = jnp.broadcast_to(share, (8, rows)), jnp.broadcast_to(center, (8, rows))
 
     def open_grads(block):
-        acc["dq"] = jnp.zeros((head_dim, rows), f32)
+        pass
 
     def step_grads(block, start, size):
+        slot = block % 2
         share, center = stats[block]
         for at in subs(start, size):
-            prob = w_ref[block % 2, at, :] * spread(share)
-            p_ref[at, :] = prob.astype(bf16)
-            ds_ref[at, :] = (prob * (d_ref[block % 2, at, :] - spread(center))).astype(bf16)
+            prob = w_ref[slot, at, :] * spread(share)
+            p_ref[slot, at, :] = prob.astype(bf16)
+            ds_ref[slot, at, :] = (prob * (d_ref[slot, at, :] - spread(center))).astype(bf16)
         at = slice(start, start + size)
         old = size if start < cart_rows else (limit(block - 1) if block else 0)
         old = old if block else 0
         for ref, left, right in ((dv_ref, p_ref, grads[block]), (dk_ref, ds_ref, queries[block])):
-            part = dot_nn(left[at, :], right)
+            part = dot_nn(left[slot, at, :], right)
             if old:
                 ref[start : start + old, :] += part[:old]
             if old < size:
                 ref[start + old : start + size, :] = part[old:]
-        acc["dq"] = acc["dq"] + dot_nn(keys_t_ref[:, at], ds_ref[at, :])
 
     def close_grads(block):
-        out_ref[...] = (acc["dq"] * scale).T
+        seen = cart_rows + limit(block)
+        dq_t = dot_nn(keys_t_ref[:, 0:seen], ds_ref[block % 2, 0:seen, :])
+        out_ref[...] = (dq_t * scale).T
         for head in range(width):
             dq_ref[block * block_tokens : (block + 1) * block_tokens, head * head_dim : (head + 1) * head_dim] = (
                 out_ref[pl.ds(head, block_tokens, stride=width), :].astype(bf16)
@@ -290,7 +292,7 @@
     cart_rows = cart_keys.shape[0]
     width = heads_local // kv_local
     block_tokens = 64
-    chunk = 256
+    chunk = 512
     fine = 128
     sub = 16
     all_keys = cart_rows + tokens
@@ -333,8 +335,8 @@
                 pltpu.VMEM((2, all_keys, rows), f32),
                 pltpu.VMEM((2, all_keys, rows), f32),
                 pltpu.VMEM((2, all_keys, rows), f32),
-                pltpu.VMEM((all_keys, rows), bf16),
-                pltpu.VMEM((all_keys, rows), bf16),
+                pltpu.VMEM((2, all_keys, rows), bf16),
+                pltpu.VMEM((2, all_keys, rows), bf16),
                 pltpu.VMEM((all_keys, head_dim), f32),
                 pltpu.VMEM((all_keys, head_dim), f32),
                 pltpu.VMEM((rows, head_dim), f32),

time: 47.1 us -> 46.9 us (level)
  no operation moved by 1% of the time
where the time goes in v10:
time: 46.9 us; the launch traced here: 46.8 us
  Pallas kernels  24.5 us (52%)
  starting transfers between devices  13 us (28%)
  waiting for transfers between devices  8.33 us (18%)
  between operations  0.87 us (2%)
    pallas_call x2, Pallas kernels, on_device(): pl.pallas_call(functools.partial(head_kernel, dp_size, heads_size, kv_ind...  22.6 us
    ppermute x10, starting transfers between devices, shift(): lax.ppermute(values, axis, [(source, target_of(source, step, axis, size))...  13 us
    ppermute x10, waiting for transfers between devices, shift(): lax.ppermute(values, axis, [(source, target_of(source, step, axis, size))...  8.33 us
    pallas_call x1, Pallas kernels, on_device(): pl.pallas_call(functools.partial(place_kernel, heads_size, kv_local), out...  1.01 us
  transfers between devices with their start and end apart: 10, of which 3 were waited for; matrix products, arithmetic and copies ran while one was open for 0% of the time, Pallas kernels for 27%

profile of v10, /device:TPU:0, one launch (start us, length us, event | category | flops | bytes accessed | tf_op | source)
XLA Modules:
  0.0 46.8 jit_solution(1748993272905885579)
XLA Ops:
  0.6 11.0 %head_grads.2 = (f32[2,256,128]{2,1,0:T(8,128)}, bf16[2,256,128]{2,1,0:T(8,128)(2,1)}, bf16[2,256,128]{2,1,0:T(8,128)(2,1)}, bf16[2,256,128]{2,1,0:T(8,128)(2,1)...) custom-call(bf16[4096,128]{1,0:T(8,128)(2,1)} %bitcast.9, ...), custom_call_target="tpu_custom_call" | custom-call | flops 6710886400 | bytes 5242880 | tf_op jit(solution)/shard_map/head_grads/pallas_call | solution.py:319
  11.6 3.1 %collective-permute-start = (bf16[2,256,128]{2,1,0:T(8,128)(2,1)}, bf16[2,256,128]{2,1,0:T(8,128)(2,1)S(1)}, u32[]{:S(2)}, u32[]{:S(2)}) collective-permute-start(bf16[2,256,128]{2,1,0:T(8,128)(2,1)} %get-tuple-element.45), channel_id=1, source_target_pairs={{0,4},{4,8},{8,12},{12,0},{1,5},{5,9},{9,13},{13,1},{2,6},{6,10},{... | collective-permute-start | bytes 393224 | tf_op jit(solution)/shard_map/ppermute | solution.py:281
  14.7 2.6 %collective-permute-start.1 = (bf16[2,256,128]{2,1,0:T(8,128)(2,1)}, bf16[2,256,128]{2,1,0:T(8,128)(2,1)S(1)}, u32[]{:S(2)}, u32[]{:S(2)}) collective-permute-start(bf16[2,256,128]{2,1,0:T(8,128)(2,1)} %get-tuple-element.46), channel_id=1, source_target_pairs={{0,8},{4,12},{8,0},{12,4},{1,9},{5,13},{9,1},{13,5},{2,10},{6,14},... | collective-permute-start | bytes 393224 | tf_op jit(solution)/shard_map/ppermute | solution.py:281
  17.3 1.3 %collective-permute-start.2 = (bf16[2,256,128]{2,1,0:T(8,128)(2,1)}, bf16[2,256,128]{2,1,0:T(8,128)(2,1)S(1)}, u32[]{:S(2)}, u32[]{:S(2)}) collective-permute-start(bf16[2,256,128]{2,1,0:T(8,128)(2,1)} %get-tuple-element.47), channel_id=1, source_target_pairs={{0,12},{4,0},{8,4},{12,8},{1,13},{5,1},{9,5},{13,9},{2,14},{6,2},{... | collective-permute-start | bytes 393224 | tf_op jit(solution)/shard_map/ppermute | solution.py:281
  18.6 1.5 %collective-permute-start.3 = (bf16[64,1024]{1,0:T(8,128)(2,1)}, bf16[64,1024]{1,0:T(8,128)(2,1)S(1)}, u32[]{:S(2)}, u32[]{:S(2)}) collective-permute-start(bf16[64,1024]{1,0:T(8,128)(2,1)} %get-tuple-element.48), channel_id=1, source_target_pairs={{0,2},{1,3},{2,0},{3,1},{4,6},{5,7},{6,4},{7,5},{8,10},{9,11},{10,... | collective-permute-start | bytes 393224 | tf_op jit(solution)/shard_map/ppermute | solution.py:281
  20.1 0.0 copy-start
  20.1 11.6 %head_grads.3 = (f32[2,256,128]{2,1,0:T(8,128)}, bf16[2,256,128]{2,1,0:T(8,128)(2,1)}, bf16[2,256,128]{2,1,0:T(8,128)(2,1)}, bf16[2,256,128]{2,1,0:T(8,128)(2,1)...) custom-call(bf16[4096,128]{1,0:T(8,128)(2,1)} %bitcast.10, ...), custom_call_target="tpu_custom_call" | custom-call | flops 6710886400 | bytes 5242880 | tf_op jit(solution)/shard_map/head_grads/pallas_call | solution.py:319
  31.8 0.0 collective-permute-done.refs_1_
  31.8 0.0 collective-permute-done.1.refs_2_
  31.8 0.0 collective-permute-done.2.refs_3_
  31.8 0.0 collective-permute-done.3.refs_3_
  31.8 0.0 copy-start.1
  31.8 0.7 %collective-permute-start.4 = (bf16[2,256,128]{2,1,0:T(8,128)(2,1)}, bf16[2,256,128]{2,1,0:T(8,128)(2,1)S(1)}, u32[]{:S(2)}, u32[]{:S(2)}) collective-permute-start(bf16[2,256,128]{2,1,0:T(8,128)(2,1)} %get-tuple-element.54), channel_id=1, source_target_pairs={{0,4},{4,8},{8,12},{12,0},{1,5},{5,9},{9,13},{13,1},{2,6},{6,10},{... | collective-permute-start | bytes 393224 | tf_op jit(solution)/shard_map/ppermute | solution.py:281
  32.5 0.0 collective-permute-start.7
  32.5 0.6 %collective-permute-start.8 = (bf16[64,2048]{1,0:T(8,128)(2,1)}, bf16[64,2048]{1,0:T(8,128)(2,1)S(1)}, u32[]{:S(2)}, u32[]{:S(2)}) collective-permute-start(bf16[64,2048]{1,0:T(8,128)(2,1)} %get-tuple-element.60), channel_id=1, source_target_pairs={{0,3},{1,2},{2,1},{3,0},{4,7},{5,6},{6,5},{7,4},{8,11},{9,10},{10,... | collective-permute-start | bytes 786440 | tf_op jit(solution)/shard_map/ppermute | solution.py:281
  33.2 0.4 collective-permute-start.5
  33.5 2.8 %collective-permute-start.6 = (bf16[2,256,128]{2,1,0:T(8,128)(2,1)}, bf16[2,256,128]{2,1,0:T(8,128)(2,1)S(1)}, u32[]{:S(2)}, u32[]{:S(2)}) collective-permute-start(bf16[2,256,128]{2,1,0:T(8,128)(2,1)} %get-tuple-element.56), channel_id=1, source_target_pairs={{0,12},{4,0},{8,4},{12,8},{1,13},{5,1},{9,5},{13,9},{2,14},{6,2},{... | collective-permute-start | bytes 393224 | tf_op jit(solution)/shard_map/ppermute | solution.py:281
  36.3 4.1 %collective-permute-done.4.refs_2_ = bf16[2,256,128]{2,1,0:T(8,128)(2,1)S(1)} collective-permute-done((bf16[2,256,128]{2,1,0:T(8,128)(2,1)}, bf16[2,256,128]{2,1,0:T(8,128)(2,1)S(1)}, u32[]{:S(2)}, u32[]{:S(2)}) %collective-permute-start.4) | collective-permute-done | bytes 131104 | tf_op jit(solution)/shard_map/ppermute | solution.py:281
  40.4 0.0 collective-permute-start.9
  40.4 0.0 copy-done
  40.4 0.1 cart_sum.1.refs_0_
  40.5 4.0 %collective-permute-done.5.refs_3_ = bf16[2,256,128]{2,1,0:T(8,128)(2,1)S(1)} collective-permute-done((bf16[2,256,128]{2,1,0:T(8,128)(2,1)}, bf16[2,256,128]{2,1,0:T(8,128)(2,1)S(1)}, u32[]{:S(2)}, u32[]{:S(2)}) %collective-permute-start.5) | collective-permute-done | bytes 131104 | tf_op jit(solution)/shard_map/ppermute | solution.py:281
  44.5 0.0 collective-permute-done.6.refs_4_
  44.5 0.0 copy-done.1
  44.5 0.0 copy-start.2
  44.5 0.9 %cart_grads.1 = f32[1024,128]{1,0:T(8,128)} custom-call(f32[2,256,128]{2,1,0:T(8,128)S(1)} %cart_sum.1.refs_0_, f32[2,256,128]{2,1,0:T(8,128)S(1)} %copy-done.1, bf16[2,256,128]{2,1,0:T(8,128)(2,1)S(1)} %collective-permute-done.4.refs_2_, bf16[2,256,128]{2,1,0:T(8,128)(2,1)S(1)} %collective-permute-done.5.refs_3_, ...), custom_call_target="tpu_custom_call" | custom-call | flops 1048576 | bytes 2097152 | tf_op jit(solution)/shard_map/cart_grads/pallas_call | solution.py:383
  45.4 0.2 collective-permute-done.9.refs_4_
  45.6 0.0 collective-permute-done.7.refs_1_
  45.6 0.0 collective-permute-done.8.refs_2_
  45.6 0.0 copy-done.2
  45.6 1.0 %place_queries.1 = bf16[64,8192]{1,0:T(8,128)(2,1)} custom-call(bf16[64,2048]{1,0:T(8,128)(2,1)S(1)} %copy-done.2, bf16[64,2048]{1,0:T(8,128)(2,1)S(1)} %collective-permute-done.7.refs_1_, bf16[64,2048]{1,0:T(8,128)(2,1)S(1)} %collective-permute-done.8.refs_2_, bf16[64,1024]{1,0:T(8,128)(2,1)S(1)} %collective-permute-done.3.refs_3_, ...), custom_call_target="tpu_custom_call" | custom-call | flops 1048576 | bytes 2097152 | tf_op jit(solution)/shard_map/place_queries/pallas_call | solution.py:373
Async XLA Ops:
  11.6 20.2 %collective-permute-start = (bf16[2,256,128]{2,1,0:T(8,128)(2,1)}, bf16[2,256,128]{2,1,0:T(8,128)(2,1)S(1)}, u32[]{:S(2)}, u32[]{:S(2)}) collective-permute-start(bf16[2,256,128]{2,1,0:T(8,128)(2,1)} %get-tuple-element.45), channel_id=1, source_target_pairs={{0,4},{4,8},{8,12},{12,0},{1,5},{5,9},{9,13},{13,1},{2,6},{6,10},{... | collective-permute-start | bytes 393224 | tf_op jit(solution)/shard_map/ppermute | solution.py:281
  14.7 17.1 %collective-permute-start.1 = (bf16[2,256,128]{2,1,0:T(8,128)(2,1)}, bf16[2,256,128]{2,1,0:T(8,128)(2,1)S(1)}, u32[]{:S(2)}, u32[]{:S(2)}) collective-permute-start(bf16[2,256,128]{2,1,0:T(8,128)(2,1)} %get-tuple-element.46), channel_id=1, source_target_pairs={{0,8},{4,12},{8,0},{12,4},{1,9},{5,13},{9,1},{13,5},{2,10},{6,14},... | collective-permute-start | bytes 393224 | tf_op jit(solution)/shard_map/ppermute | solution.py:281
  17.3 14.5 %collective-permute-start.2 = (bf16[2,256,128]{2,1,0:T(8,128)(2,1)}, bf16[2,256,128]{2,1,0:T(8,128)(2,1)S(1)}, u32[]{:S(2)}, u32[]{:S(2)}) collective-permute-start(bf16[2,256,128]{2,1,0:T(8,128)(2,1)} %get-tuple-element.47), channel_id=1, source_target_pairs={{0,12},{4,0},{8,4},{12,8},{1,13},{5,1},{9,5},{13,9},{2,14},{6,2},{... | collective-permute-start | bytes 393224 | tf_op jit(solution)/shard_map/ppermute | solution.py:281
  18.6 13.2 %collective-permute-start.3 = (bf16[64,1024]{1,0:T(8,128)(2,1)}, bf16[64,1024]{1,0:T(8,128)(2,1)S(1)}, u32[]{:S(2)}, u32[]{:S(2)}) collective-permute-start(bf16[64,1024]{1,0:T(8,128)(2,1)} %get-tuple-element.48), channel_id=1, source_target_pairs={{0,2},{1,3},{2,0},{3,1},{4,6},{5,7},{6,4},{7,5},{8,10},{9,11},{10,... | collective-permute-start | bytes 393224 | tf_op jit(solution)/shard_map/ppermute | solution.py:281
  20.1 20.3 %copy-start = (f32[2,256,128]{2,1,0:T(8,128)S(1)}, f32[2,256,128]{2,1,0:T(8,128)}, u32[]{:S(2)}) copy-start(f32[2,256,128]{2,1,0:T(8,128)} %get-tuple-element.49.refs_0_) | copy-start | bytes 786436
  31.8 12.7 %copy-start.1 = (f32[2,256,128]{2,1,0:T(8,128)S(1)}, f32[2,256,128]{2,1,0:T(8,128)}, u32[]{:S(2)}) copy-start(f32[2,256,128]{2,1,0:T(8,128)} %get-tuple-element.53.refs_1_) | copy-start | bytes 786436
  31.8 8.6 %collective-permute-start.4 = (bf16[2,256,128]{2,1,0:T(8,128)(2,1)}, bf16[2,256,128]{2,1,0:T(8,128)(2,1)S(1)}, u32[]{:S(2)}, u32[]{:S(2)}) collective-permute-start(bf16[2,256,128]{2,1,0:T(8,128)(2,1)} %get-tuple-element.54), channel_id=1, source_target_pairs={{0,4},{4,8},{8,12},{12,0},{1,5},{5,9},{9,13},{13,1},{2,6},{6,10},{... | collective-permute-start | bytes 393224 | tf_op jit(solution)/shard_map/ppermute | solution.py:281
  32.5 13.1 %collective-permute-start.7 = (bf16[64,2048]{1,0:T(8,128)(2,1)}, bf16[64,2048]{1,0:T(8,128)(2,1)S(1)}, u32[]{:S(2)}, u32[]{:S(2)}) collective-permute-start(bf16[64,2048]{1,0:T(8,128)(2,1)} %get-tuple-element.59), channel_id=1, source_target_pairs={{0,1},{1,0},{2,3},{3,2},{4,5},{5,4},{6,7},{7,6},{8,9},{9,8},{10,11... | collective-permute-start | bytes 786440 | tf_op jit(solution)/shard_map/ppermute | solution.py:281
  32.5 13.1 %collective-permute-start.8 = (bf16[64,2048]{1,0:T(8,128)(2,1)}, bf16[64,2048]{1,0:T(8,128)(2,1)S(1)}, u32[]{:S(2)}, u32[]{:S(2)}) collective-permute-start(bf16[64,2048]{1,0:T(8,128)(2,1)} %get-tuple-element.60), channel_id=1, source_target_pairs={{0,3},{1,2},{2,1},{3,0},{4,7},{5,6},{6,5},{7,4},{8,11},{9,10},{10,... | collective-permute-start | bytes 786440 | tf_op jit(solution)/shard_map/ppermute | solution.py:281
  33.2 11.3 %collective-permute-start.5 = (bf16[2,256,128]{2,1,0:T(8,128)(2,1)}, bf16[2,256,128]{2,1,0:T(8,128)(2,1)S(1)}, u32[]{:S(2)}, u32[]{:S(2)}) collective-permute-start(bf16[2,256,128]{2,1,0:T(8,128)(2,1)} %get-tuple-element.55), channel_id=1, source_target_pairs={{0,8},{4,12},{8,0},{12,4},{1,9},{5,13},{9,1},{13,5},{2,10},{6,14},... | collective-permute-start | bytes 393224 | tf_op jit(solution)/shard_map/ppermute | solution.py:281
  33.5 11.0 %collective-permute-start.6 = (bf16[2,256,128]{2,1,0:T(8,128)(2,1)}, bf16[2,256,128]{2,1,0:T(8,128)(2,1)S(1)}, u32[]{:S(2)}, u32[]{:S(2)}) collective-permute-start(bf16[2,256,128]{2,1,0:T(8,128)(2,1)} %get-tuple-element.56), channel_id=1, source_target_pairs={{0,12},{4,0},{8,4},{12,8},{1,13},{5,1},{9,5},{13,9},{2,14},{6,2},{... | collective-permute-start | bytes 393224 | tf_op jit(solution)/shard_map/ppermute | solution.py:281
  40.4 5.2 %collective-permute-start.9 = (bf16[64,1024]{1,0:T(8,128)(2,1)}, bf16[64,1024]{1,0:T(8,128)(2,1)S(1)}, u32[]{:S(2)}, u32[]{:S(2)}) collective-permute-start(bf16[64,1024]{1,0:T(8,128)(2,1)} %get-tuple-element.62), channel_id=1, source_target_pairs={{0,2},{1,3},{2,0},{3,1},{4,6},{5,7},{6,4},{7,5},{8,10},{9,11},{10,... | collective-permute-start | bytes 393224 | tf_op jit(solution)/shard_map/ppermute | solution.py:281
  44.5 1.1 %copy-start.2 = (bf16[64,2048]{1,0:T(8,128)(2,1)S(1)}, bf16[64,2048]{1,0:T(8,128)(2,1)}, u32[]{:S(2)}) copy-start(bf16[64,2048]{1,0:T(8,128)(2,1)} %get-tuple-element.58.refs_0_) | copy-start | bytes 786436

commit v11 on v10

--- a/solution.py
+++ b/solution.py
@@ -38,7 +38,7 @@
     kept = len(near_steps)
     dq_before, refs = refs[: held * kept], refs[held * kept :]
     self_before, refs = refs[:held], refs[held:]
-    cart_outs, refs = refs[:dp_size], refs[dp_size:]
+    (keep_ref, send_ref), refs = refs[:2], refs[2:]
     dq_outs, self_ref, refs = refs[:heads_size], refs[heads_size], refs[heads_size + 1 :]
     (
         wide_ref, keys_ref, vals_ref, keys_t_ref, s_ref, w_ref, d_ref, p_ref, ds_ref, dk_ref, dv_ref, out_ref, dq_ref,
@@ -197,17 +197,17 @@
 
     part_rows = cart_rows // dp_size
     me = lax.axis_index("dp")
-    for step, ref in enumerate(cart_outs):
-        target = target_of(me, step, "dp", dp_size)
-        at = pl.ds(pl.multiple_of(target * part_rows, part_rows), part_rows)
-        ref[0] = (dk_ref[at, :] * scale).astype(ref.dtype)
-        ref[1] = dv_ref[at, :].astype(ref.dtype)
+    for step in range(dp_size):
+        at = pl.ds(pl.multiple_of((me ^ step) * part_rows, part_rows), part_rows)
+        ref = send_ref if step % 2 else keep_ref
+        ref[step // 2, 0] = (dk_ref[at, :] * scale).astype(ref.dtype)
+        ref[step // 2, 1] = dv_ref[at, :].astype(ref.dtype)
     own = dk_ref[cart_rows:all_keys, :] * scale, dv_ref[cart_rows:all_keys, :]
     own_tokens = tokens // heads_size
     columns = width * head_dim
     me = lax.axis_index("heads")
     for place, (step, ref) in enumerate(zip(near_steps + far_steps, dq_outs)):
-        target = target_of(me, step, "heads", heads_size)
+        target = me ^ step
         at = pl.ds(pl.multiple_of(target * own_tokens, own_tokens), own_tokens)
         if last and place < kept:
             for index in range(held):
@@ -226,23 +226,20 @@
         self_ref[kind * count : (kind + 1) * count, :] = wide_ref[0:count, :].astype(bf16)
 
 
-def sum_kernel(*refs):
-    part_refs, out_ref = refs[:-1], refs[-1]
-    total = part_refs[0][...]
-    for ref in part_refs[1:]:
-        total = total + ref[...].astype(f32)
-    out_ref[...] = total
+def fold_kernel(part_ref, got_ref, keep_ref, send_ref):
+    for index in range(part_ref.shape[0]):
+        total = part_ref[index] + got_ref[index].astype(f32)
+        ref = send_ref if index % 2 else keep_ref
+        ref[index // 2] = total.astype(ref.dtype)
 
 
 def cart_kernel(kv_local, *refs):
-    done_refs, part_refs, out_ref = refs[: kv_local - 1], refs[kv_local - 1 : -1], refs[-1]
-    part_rows = part_refs[0].shape[1]
-    for kind in range(2):
-        total = part_refs[0][kind]
-        for ref in part_refs[1:]:
-            total = total + ref[kind].astype(f32)
-        for kv_index, part in enumerate((*[ref[kind] for ref in done_refs], total)):
-            out_ref[pl.ds(kind * kv_local + kv_index, part_rows, stride=2 * kv_local), :] = part
+    part_refs, got_refs, out_ref = refs[:kv_local], refs[kv_local:-1], refs[-1]
+    part_rows = part_refs[0].shape[2]
+    for kv_index in range(kv_local):
+        for kind in range(2):
+            total = part_refs[kv_index][0, kind] + got_refs[kv_index][0, kind].astype(f32)
+            out_ref[pl.ds(kind * kv_local + kv_index, part_rows, stride=2 * kv_local), :] = total
 
 
 def place_kernel(heads_size, kv_local, *refs):
@@ -254,7 +251,7 @@
     places += [(step, kv_index) for kv_index in range(kv_local) for step in far_steps]
     copies = []
     for index, ((step, kv_index), ref) in enumerate(zip(places, part_refs)):
-        source = source_of(me, step, "heads", heads_size)
+        source = me ^ step
         at = pl.multiple_of((source * kv_local + kv_index) * columns, columns)
         copies.append(pltpu.make_async_copy(ref, out_ref.at[:, pl.ds(at, ref.shape[1])], sems.at[index]))
     for copy in copies:
@@ -263,22 +260,24 @@
         copy.wait()
 
 
-def paired(axis, size):
-    return axis == "heads" and size & (size - 1) == 0
-
-
-def target_of(me, step, axis, size):
-    return me ^ step if paired(axis, size) else (me + step) % size
-
-
-def source_of(me, step, axis, size):
-    return me ^ step if paired(axis, size) else (me + size - step) % size
-
-
-def shift(values, axis, size, step):
+def swap(values, axis, size, step):
     if step == 0:
         return values
-    return lax.ppermute(values, axis, [(source, target_of(source, step, axis, size)) for source in range(size)])
+    return lax.ppermute(values, axis, [(source, source ^ step) for source in range(size)])
+
+
+def fold(part, got):
+    half = part.shape[0] // 2
+    return pl.pallas_call(
+        fold_kernel,
+        out_shape=(
+            jax.ShapeDtypeStruct((half, *part.shape[1:]), f32),
+            jax.ShapeDtypeStruct((half, *part.shape[1:]), bf16),
+        ),
+        compiler_params=pltpu.CompilerParams(vmem_limit_bytes=small_vmem_bytes),
+        cost_estimate=pl.CostEstimate(flops=2**20, bytes_accessed=2**20, transcendentals=0),
+        name="cart_fold",
+    )(part, got)
 
 
 def split_steps(heads_size):
@@ -319,10 +318,8 @@
         outs = pl.pallas_call(
             functools.partial(head_kernel, dp_size, heads_size, kv_index, kv_local, width, block_tokens, chunk, fine, sub),
             out_shape=(
-                *[
-                    jax.ShapeDtypeStruct((2, part_rows, head_dim), bf16 if step else f32)
-                    for step in range(dp_size)
-                ],
+                jax.ShapeDtypeStruct((dp_size // 2, 2, part_rows, head_dim), f32),
+                jax.ShapeDtypeStruct((dp_size // 2, 2, part_rows, head_dim), bf16),
                 *other_shapes,
             ),
             in_specs=[pl.BlockSpec(memory_space=pltpu.HBM)] * 6
@@ -348,28 +345,25 @@
             cost_estimate=pl.CostEstimate(flops=4 * macs, bytes_accessed=5 * 2**20, transcendentals=tokens * width * all_keys),
             name="head_grads",
         )(*flat, segment_ids, *(before if last else []))
-        cart_sends, near, far = outs[1:dp_size], outs[dp_size : dp_size + kept], outs[dp_size + kept : -1]
+        part, send, near, far = outs[0], outs[1], outs[2 : 2 + kept], outs[2 + kept : -1]
         if last:
-            cart_sends, near, far, received = lax.optimization_barrier((cart_sends, near, far, received))
+            part, send, near, far, received = lax.optimization_barrier((part, send, near, far, received))
         else:
             kept_list += near
             self_list.append(outs[-1])
-        cart_parts = [outs[0], *[shift(part, "dp", dp_size, step + 1) for step, part in enumerate(cart_sends)]]
-        far_parts = [shift(part, "heads", heads_size, step) for step, part in zip(far_steps, far)]
+        received.append((part, swap(send, "dp", dp_size, 1)))
+        far_parts = [swap(block, "heads", heads_size, step) for step, block in zip(far_steps, far)]
         if not last:
-            received.append((cart_parts, far_parts))
-    for early_cart, early_far in received:
-        cart_list.append(
-            pl.pallas_call(
-                sum_kernel,
-                out_shape=jax.ShapeDtypeStruct((2, part_rows, head_dim), f32),
-                compiler_params=pltpu.CompilerParams(vmem_limit_bytes=small_vmem_bytes),
-                cost_estimate=pl.CostEstimate(flops=2**20, bytes_accessed=2**20, transcendentals=0),
-                name="cart_sum",
-            )(*early_cart)
-        )
-        far_list += early_far
-    query_list = [shift(part, "heads", heads_size, step) for step, part in zip(near_steps, near)] + far_list + far_parts
+            received[-1] += tuple(far_parts)
+    far_list = [block for _, _, *blocks_far in received for block in blocks_far]
+    for part, got, *_ in received:
+        step = 2
+        while step < dp_size:
+            part, send = fold(part, got)
+            got = swap(send, "dp", dp_size, step)
+            step *= 2
+        cart_list.append((part, got))
+    query_list = [swap(block, "heads", heads_size, step) for step, block in zip(near_steps, near)] + far_list + far_parts
     query_grads = pl.pallas_call(
         functools.partial(place_kernel, heads_size, kv_local),
         out_shape=jax.ShapeDtypeStruct((own_tokens, heads_size * heads_local * head_dim), bf16),
@@ -386,7 +380,7 @@
         compiler_params=pltpu.CompilerParams(vmem_limit_bytes=small_vmem_bytes),
         cost_estimate=pl.CostEstimate(flops=2**20, bytes_accessed=2 * 2**20, transcendentals=0),
         name="cart_grads",
-    )(*cart_list, *cart_parts)
+    )(*[part for part, _ in cart_list], *[got for _, got in cart_list])
     cart_grads = cart_grads.reshape(part_rows, 2, kv_local, head_dim)
     self_grads = outs[-1].reshape(2, tokens, kv_local, head_dim)
     return (cart_grads, self_grads, query_grads)

time: 46.9 us -> 47 us (level)
  starting transfers between devices: 13 us -> 10.7 us
  waiting for transfers between devices: 8.33 us -> 10.5 us
    ppermute x10 -> x8, starting transfers between devices: 13 us -> 10.7 us  [swap(): lax.ppermute(values, axis, [(source, source ^ step) for source in range(s...]
    ppermute x10 -> x8, waiting for transfers between devices: 8.33 us -> 10.5 us  [swap(): lax.ppermute(values, axis, [(source, source ^ step) for source in range(s...]
  transfers between devices with their start and end apart: 10 -> 8, of which waited for: 3 -> 2; matrix products, arithmetic and copies ran while one was open for 0% -> 0% of each run, Pallas kernels for 27% -> 28%
where the time goes in v11:
time: 47 us; the launch traced here: 46.8 us
  Pallas kernels  24.9 us (53%)
  starting transfers between devices  10.7 us (23%)
  waiting for transfers between devices  10.5 us (22%)
  between operations  0.72 us (2%)
    pallas_call x2, Pallas kernels, on_device(): pl.pallas_call(functools.partial(head_kernel, dp_size, heads_size, kv_ind...  22.9 us
    ppermute x8, starting transfers between devices, swap(): lax.ppermute(values, axis, [(source, source ^ step) for source in range(s...  10.7 us
    ppermute x8, waiting for transfers between devices, swap(): lax.ppermute(values, axis, [(source, source ^ step) for source in range(s...  10.5 us
    pallas_call x1, Pallas kernels, on_device(): pl.pallas_call(functools.partial(place_kernel, heads_size, kv_local), out...  1.01 us
  transfers between devices with their start and end apart: 8, of which 2 were waited for; matrix products, arithmetic and copies ran while one was open for 0% of the time, Pallas kernels for 28%

profile of v11, /device:TPU:0, one launch (start us, length us, event | category | flops | bytes accessed | tf_op | source)
XLA Modules:
  0.0 46.8 jit_solution(9510788112958630783)
XLA Ops:
  0.6 11.0 %head_grads.2 = (f32[2,2,256,128]{3,2,1,0:T(8,128)}, bf16[2,2,256,128]{3,2,1,0:T(8,128)(2,1)}, bf16[64,1024]{1,0:T(8,128)(2,1)}, bf16[64,1024]{1,0:T(8,128)(2,1)...) custom-call(bf16[4096,128]{1,0:T(8,128)(2,1)} %bitcast.9, ...), custom_call_target="tpu_custom_call" | custom-call | flops 6710886400 | bytes 5242880 | tf_op jit(solution)/shard_map/head_grads/pallas_call | solution.py:318
  11.7 3.0 %collective-permute-start.1 = (bf16[64,1024]{1,0:T(8,128)(2,1)}, bf16[64,1024]{1,0:T(8,128)(2,1)S(1)}, u32[]{:S(2)}, u32[]{:S(2)}) collective-permute-start(bf16[64,1024]{1,0:T(8,128)(2,1)} %get-tuple-element.42), channel_id=1, source_target_pairs={{0,2},{1,3},{2,0},{3,1},{4,6},{5,7},{6,4},{7,5},{8,10},{9,11},{10,... | collective-permute-start | bytes 393224 | tf_op jit(solution)/shard_map/ppermute | solution.py:266
  14.7 1.6 %collective-permute-start = (bf16[2,2,256,128]{3,2,1,0:T(8,128)(2,1)}, bf16[2,2,256,128]{3,2,1,0:T(8,128)(2,1)S(1)}, u32[]{:S(2)}, u32[]{:S(2)}) collective-permute-start(bf16[2,2,256,128]{3,2,1,0:T(8,128)(2,1)} %get-tuple-element.41), channel_id=1, source_target_pairs={{0,4},{4,0},{8,12},{12,8},{1,5},{5,1},{9,13},{13,9},{2,6},{6,2},{1... | collective-permute-start | bytes 786440 | tf_op jit(solution)/shard_map/ppermute | solution.py:266
  16.3 0.0 copy-start.1
  16.3 11.9 %head_grads.3 = (f32[2,2,256,128]{3,2,1,0:T(8,128)}, bf16[2,2,256,128]{3,2,1,0:T(8,128)(2,1)}, bf16[64,2048]{1,0:T(8,128)(2,1)}, bf16[64,2048]{1,0:T(8,128)(2,1)...) custom-call(bf16[4096,128]{1,0:T(8,128)(2,1)} %bitcast.10, ...), custom_call_target="tpu_custom_call" | custom-call | flops 6710886400 | bytes 5242880 | tf_op jit(solution)/shard_map/head_grads/pallas_call | solution.py:318
  28.2 0.0 copy-start
  28.2 0.0 collective-permute-done.1.refs_3_
  28.2 0.0 collective-permute-done.got_ref
  28.2 0.5 %collective-permute-start.2 = (bf16[2,2,256,128]{3,2,1,0:T(8,128)(2,1)}, bf16[2,2,256,128]{3,2,1,0:T(8,128)(2,1)S(1)}, u32[]{:S(2)}, u32[]{:S(2)}) collective-permute-start(bf16[2,2,256,128]{3,2,1,0:T(8,128)(2,1)} %get-tuple-element.47), channel_id=1, source_target_pairs={{0,4},{4,0},{8,12},{12,8},{1,5},{5,1},{9,13},{13,9},{2,6},{6,2},{1... | collective-permute-start | bytes 786440 | tf_op jit(solution)/shard_map/ppermute | solution.py:266
  28.7 0.0 collective-permute-start.5
  28.7 0.3 collective-permute-start.6
  29.0 1.8 %collective-permute-start.7 = (bf16[64,1024]{1,0:T(8,128)(2,1)}, bf16[64,1024]{1,0:T(8,128)(2,1)S(1)}, u32[]{:S(2)}, u32[]{:S(2)}) collective-permute-start(bf16[64,1024]{1,0:T(8,128)(2,1)} %get-tuple-element.56), channel_id=1, source_target_pairs={{0,2},{1,3},{2,0},{3,1},{4,6},{5,7},{6,4},{7,5},{8,10},{9,11},{10,... | collective-permute-start | bytes 393224 | tf_op jit(solution)/shard_map/ppermute | solution.py:266
  30.8 0.0 copy-done.1
  30.9 0.0 copy-start.2
  30.9 2.7 %collective-permute-start.3 = (bf16[1,2,256,128]{3,2,1,0:T(8,128)(2,1)S(1)}, bf16[1,2,256,128]{3,2,1,0:T(8,128)(2,1)S(1)}, u32[]{:S(2)}, u32[]{:S(2)}) collective-permute-start(bf16[1,2,256,128]{3,2,1,0:T(8,128)(2,1)S(1)} %get-tuple-element.49), channel_id=1, source_target_pairs={{0,8},{4,12},{8,0},{12,4},{1,9},{5,13},{9,1},{13,5},{2,10},{6,14},... | collective-permute-start | bytes 393224 | tf_op jit(solution)/shard_map/ppermute | solution.py:266
  33.6 6.0 %collective-permute-done.2.got_ref = bf16[2,2,256,128]{3,2,1,0:T(8,128)(2,1)S(1)} collective-permute-done((bf16[2,2,256,128]{3,2,1,0:T(8,128)(2,1)}, bf16[2,2,256,128]{3,2,1,0:T(8,128)(2,1)S(1)}, u32[]{:S(2)}, u32[]{:S(2)}) %collective-permute-start.2) | collective-permute-done | bytes 262176 | tf_op jit(solution)/shard_map/ppermute | solution.py:266
  39.6 0.0 copy-done
  39.6 0.8 %collective-permute-start.4 = (bf16[1,2,256,128]{3,2,1,0:T(8,128)(2,1)S(1)}, bf16[1,2,256,128]{3,2,1,0:T(8,128)(2,1)S(1)}, u32[]{:S(2)}, u32[]{:S(2)}) collective-permute-start(bf16[1,2,256,128]{3,2,1,0:T(8,128)(2,1)S(1)} %get-tuple-element.50), channel_id=1, source_target_pairs={{0,8},{4,12},{8,0},{12,4},{1,9},{5,13},{9,1},{13,5},{2,10},{6,14},... | collective-permute-start | bytes 393224 | tf_op jit(solution)/shard_map/ppermute | solution.py:266
  40.4 0.0 collective-permute-done.7.refs_4_
  40.4 0.0 collective-permute-done.5.refs_1_
  40.4 0.0 collective-permute-done.6.refs_2_
  40.4 0.0 copy-done.2
  40.4 1.0 %place_queries.1 = bf16[64,8192]{1,0:T(8,128)(2,1)} custom-call(bf16[64,2048]{1,0:T(8,128)(2,1)S(1)} %copy-done.2, bf16[64,2048]{1,0:T(8,128)(2,1)S(1)} %collective-permute-done.5.refs_1_, bf16[64,2048]{1,0:T(8,128)(2,1)S(1)} %collective-permute-done.6.refs_2_, bf16[64,1024]{1,0:T(8,128)(2,1)S(1)} %collective-permute-done.1.refs_3_, ...), custom_call_target="tpu_custom_call" | custom-call | flops 1048576 | bytes 2097152 | tf_op jit(solution)/shard_map/place_queries/pallas_call | solution.py:367
  41.5 0.0 collective-permute-done.3.refs_2_
  41.5 4.5 %collective-permute-done.4.refs_3_ = bf16[1,2,256,128]{3,2,1,0:T(8,128)(2,1)S(1)} collective-permute-done((bf16[1,2,256,128]{3,2,1,0:T(8,128)(2,1)S(1)}, bf16[1,2,256,128]{3,2,1,0:T(8,128)(2,1)S(1)}, u32[]{:S(2)}, u32[]{:S(2)}) %collective-permute-start.4) | collective-permute-done | bytes 131104 | tf_op jit(solution)/shard_map/ppermute | solution.py:266
  45.9 0.9 %cart_grads.1 = f32[1024,128]{1,0:T(8,128)} custom-call(f32[1,2,256,128]{3,2,1,0:T(8,128)S(1)} %get-tuple-element.45.refs_0_, f32[1,2,256,128]{3,2,1,0:T(8,128)S(1)} %get-tuple-element.48.refs_1_, bf16[1,2,256,128]{3,2,1,0:T(8,128)(2,1)S(1)} %collective-permute-done.3.refs_2_, bf16[1,2,256,128]{3,2,1,0:T(8,128)(2,1)S(1)} %collective-permute-done.4.refs_3_), custom_call_target="tpu_custom_call" | custom-call | flops 1048576 | bytes 2097152 | tf_op jit(solution)/shard_map/cart_grads/pallas_call | solution.py:377
  (2 shorter events, 0.1 us)
Async XLA Ops:
  11.7 16.5 %collective-permute-start.1 = (bf16[64,1024]{1,0:T(8,128)(2,1)}, bf16[64,1024]{1,0:T(8,128)(2,1)S(1)}, u32[]{:S(2)}, u32[]{:S(2)}) collective-permute-start(bf16[64,1024]{1,0:T(8,128)(2,1)} %get-tuple-element.42), channel_id=1, source_target_pairs={{0,2},{1,3},{2,0},{3,1},{4,6},{5,7},{6,4},{7,5},{8,10},{9,11},{10,... | collective-permute-start | bytes 393224 | tf_op jit(solution)/shard_map/ppermute | solution.py:266
  14.7 13.5 %collective-permute-start = (bf16[2,2,256,128]{3,2,1,0:T(8,128)(2,1)}, bf16[2,2,256,128]{3,2,1,0:T(8,128)(2,1)S(1)}, u32[]{:S(2)}, u32[]{:S(2)}) collective-permute-start(bf16[2,2,256,128]{3,2,1,0:T(8,128)(2,1)} %get-tuple-element.41), channel_id=1, source_target_pairs={{0,4},{4,0},{8,12},{12,8},{1,5},{5,1},{9,13},{13,9},{2,6},{6,2},{1... | collective-permute-start | bytes 786440 | tf_op jit(solution)/shard_map/ppermute | solution.py:266
  16.3 14.6 %copy-start.1 = (f32[2,2,256,128]{3,2,1,0:T(8,128)S(1)}, f32[2,2,256,128]{3,2,1,0:T(8,128)}, u32[]{:S(2)}) copy-start(f32[2,2,256,128]{3,2,1,0:T(8,128)} %get-tuple-element.43.part_ref) | copy-start | bytes 1572868
  28.2 11.4 %copy-start = (f32[2,2,256,128]{3,2,1,0:T(8,128)S(1)}, f32[2,2,256,128]{3,2,1,0:T(8,128)}, u32[]{:S(2)}) copy-start(f32[2,2,256,128]{3,2,1,0:T(8,128)} %get-tuple-element.46.part_ref) | copy-start | bytes 1572868
  28.2 11.4 %collective-permute-start.2 = (bf16[2,2,256,128]{3,2,1,0:T(8,128)(2,1)}, bf16[2,2,256,128]{3,2,1,0:T(8,128)(2,1)S(1)}, u32[]{:S(2)}, u32[]{:S(2)}) collective-permute-start(bf16[2,2,256,128]{3,2,1,0:T(8,128)(2,1)} %get-tuple-element.47), channel_id=1, source_target_pairs={{0,4},{4,0},{8,12},{12,8},{1,5},{5,1},{9,13},{13,9},{2,6},{6,2},{1... | collective-permute-start | bytes 786440 | tf_op jit(solution)/shard_map/ppermute | solution.py:266
  28.7 11.7 %collective-permute-start.5 = (bf16[64,2048]{1,0:T(8,128)(2,1)}, bf16[64,2048]{1,0:T(8,128)(2,1)S(1)}, u32[]{:S(2)}, u32[]{:S(2)}) collective-permute-start(bf16[64,2048]{1,0:T(8,128)(2,1)} %get-tuple-element.53), channel_id=1, source_target_pairs={{0,1},{1,0},{2,3},{3,2},{4,5},{5,4},{6,7},{7,6},{8,9},{9,8},{10,11... | collective-permute-start | bytes 786440 | tf_op jit(solution)/shard_map/ppermute | solution.py:266
  28.7 11.7 %collective-permute-start.6 = (bf16[64,2048]{1,0:T(8,128)(2,1)}, bf16[64,2048]{1,0:T(8,128)(2,1)S(1)}, u32[]{:S(2)}, u32[]{:S(2)}) collective-permute-start(bf16[64,2048]{1,0:T(8,128)(2,1)} %get-tuple-element.54), channel_id=1, source_target_pairs={{0,3},{1,2},{2,1},{3,0},{4,7},{5,6},{6,5},{7,4},{8,11},{9,10},{10,... | collective-permute-start | bytes 786440 | tf_op jit(solution)/shard_map/ppermute | solution.py:266
  29.0 11.4 %collective-permute-start.7 = (bf16[64,1024]{1,0:T(8,128)(2,1)}, bf16[64,1024]{1,0:T(8,128)(2,1)S(1)}, u32[]{:S(2)}, u32[]{:S(2)}) collective-permute-start(bf16[64,1024]{1,0:T(8,128)(2,1)} %get-tuple-element.56), channel_id=1, source_target_pairs={{0,2},{1,3},{2,0},{3,1},{4,6},{5,7},{6,4},{7,5},{8,10},{9,11},{10,... | collective-permute-start | bytes 393224 | tf_op jit(solution)/shard_map/ppermute | solution.py:266
  30.9 9.5 %copy-start.2 = (bf16[64,2048]{1,0:T(8,128)(2,1)S(1)}, bf16[64,2048]{1,0:T(8,128)(2,1)}, u32[]{:S(2)}) copy-start(bf16[64,2048]{1,0:T(8,128)(2,1)} %get-tuple-element.52.refs_0_) | copy-start | bytes 786436
  30.9 10.6 %collective-permute-start.3 = (bf16[1,2,256,128]{3,2,1,0:T(8,128)(2,1)S(1)}, bf16[1,2,256,128]{3,2,1,0:T(8,128)(2,1)S(1)}, u32[]{:S(2)}, u32[]{:S(2)}) collective-permute-start(bf16[1,2,256,128]{3,2,1,0:T(8,128)(2,1)S(1)} %get-tuple-element.49), channel_id=1, source_target_pairs={{0,8},{4,12},{8,0},{12,4},{1,9},{5,13},{9,1},{13,5},{2,10},{6,14},... | collective-permute-start | bytes 393224 | tf_op jit(solution)/shard_map/ppermute | solution.py:266
  39.6 6.3 %collective-permute-start.4 = (bf16[1,2,256,128]{3,2,1,0:T(8,128)(2,1)S(1)}, bf16[1,2,256,128]{3,2,1,0:T(8,128)(2,1)S(1)}, u32[]{:S(2)}, u32[]{:S(2)}) collective-permute-start(bf16[1,2,256,128]{3,2,1,0:T(8,128)(2,1)S(1)} %get-tuple-element.50), channel_id=1, source_target_pairs={{0,8},{4,12},{8,0},{12,4},{1,9},{5,13},{9,1},{13,5},{2,10},{6,14},... | collective-permute-start | bytes 393224 | tf_op jit(solution)/shard_map/ppermute | solution.py:266

commit v12 on v11

--- a/solution.py
+++ b/solution.py
@@ -11,7 +11,7 @@
 masked_score = -1e30
 vmem_bytes = 56 * 1024 * 1024
 small_vmem_bytes = 8 * 1024 * 1024
-early_steps = (2,)
+early_steps = ()
 f32 = jnp.float32
 bf16 = jnp.bfloat16
 
@@ -197,11 +197,12 @@
 
     part_rows = cart_rows // dp_size
     me = lax.axis_index("dp")
-    for step in range(dp_size):
-        at = pl.ds(pl.multiple_of((me ^ step) * part_rows, part_rows), part_rows)
-        ref = send_ref if step % 2 else keep_ref
-        ref[step // 2, 0] = (dk_ref[at, :] * scale).astype(ref.dtype)
-        ref[step // 2, 1] = dv_ref[at, :].astype(ref.dtype)
+    half = dp_size // 2
+    for index, share in enumerate(share_order(dp_size, last)):
+        at = pl.ds(pl.multiple_of((me ^ share) * part_rows, part_rows), part_rows)
+        ref = send_ref if index >= half else keep_ref
+        ref[index % half, 0] = (dk_ref[at, :] * scale).astype(ref.dtype)
+        ref[index % half, 1] = dv_ref[at, :].astype(ref.dtype)
     own = dk_ref[cart_rows:all_keys, :] * scale, dv_ref[cart_rows:all_keys, :]
     own_tokens = tokens // heads_size
     columns = width * head_dim
@@ -227,10 +228,11 @@
 
 
 def fold_kernel(part_ref, got_ref, keep_ref, send_ref):
-    for index in range(part_ref.shape[0]):
+    half = keep_ref.shape[0]
+    for index in range(2 * half):
         total = part_ref[index] + got_ref[index].astype(f32)
-        ref = send_ref if index % 2 else keep_ref
-        ref[index // 2] = total.astype(ref.dtype)
+        ref = send_ref if index >= half else keep_ref
+        ref[index % half] = total.astype(ref.dtype)
 
 
 def cart_kernel(kv_local, *refs):
@@ -282,7 +284,20 @@
 
 def split_steps(heads_size):
     early = [step for step in range(heads_size) if step in early_steps]
-    return [step for step in range(heads_size) if step not in early], early
+    late = [0, *range(2, heads_size), 1]
+    return [step for step in late if step < heads_size and step not in early], early
+
+
+def swap_order(dp_size, last):
+    bits = [1 << bit for bit in range(dp_size.bit_length() - 1)]
+    return bits if last else bits[::-1]
+
+
+def share_order(dp_size, last):
+    shares = [0]
+    for bit in reversed(swap_order(dp_size, last)):
+        shares = shares + [share ^ bit for share in shares]
+    return shares
 
 
 def on_device(dp_size, heads_size, queries, out_grad, self_keys, self_values, cart_keys, cart_values, segment_ids):
@@ -306,7 +321,7 @@
     near_steps, far_steps = split_steps(heads_size)
     kept = len(near_steps)
     anywhere = pl.BlockSpec(memory_space=pl.ANY)
-    cart_list, kept_list, far_list, self_list, received = [], [], [], [], []
+    kept_list, self_list, received = [], [], []
     for kv_index in range(kv_local):
         last = kv_index == kv_local - 1
         near = jax.ShapeDtypeStruct((own_tokens, kv_local * columns if last else columns), bf16)
@@ -351,18 +366,21 @@
         else:
             kept_list += near
             self_list.append(outs[-1])
-        received.append((part, swap(send, "dp", dp_size, 1)))
+        received.append((part, swap(send, "dp", dp_size, swap_order(dp_size, last)[0])))
         far_parts = [swap(block, "heads", heads_size, step) for step, block in zip(far_steps, far)]
         if not last:
             received[-1] += tuple(far_parts)
     far_list = [block for _, _, *blocks_far in received for block in blocks_far]
-    for part, got, *_ in received:
-        step = 2
-        while step < dp_size:
-            part, send = fold(part, got)
-            got = swap(send, "dp", dp_size, step)
-            step *= 2
-        cart_list.append((part, got))
+    state = [(part, got) for part, got, *_ in received]
+    for level in range(1, dp_size.bit_length() - 1):
+        state = [fold(part, got) for part, got in state]
+        kept_parts, sends = zip(*state)
+        sends = lax.optimization_barrier(sends)
+        state = [
+            (part, swap(send, "dp", dp_size, swap_order(dp_size, index == kv_local - 1)[level]))
+            for index, (part, send) in reversed(list(enumerate(zip(kept_parts, sends))))
+        ][::-1]
+    cart_list = state
     query_list = [swap(block, "heads", heads_size, step) for step, block in zip(near_steps, near)] + far_list + far_parts
     query_grads = pl.pallas_call(
         functools.partial(place_kernel, heads_size, kv_local),

time: 47 us -> 47.1 us (level)
  starting transfers between devices: 10.7 us -> 12.5 us
  waiting for transfers between devices: 10.5 us -> 8.8 us
    ppermute x8 -> x7, starting transfers between devices: 10.7 us -> 12.5 us  [swap(): lax.ppermute(values, axis, [(source, source ^ step) for source in range(s...]
    ppermute x8 -> x7, waiting for transfers between devices: 10.5 us -> 8.8 us  [swap(): lax.ppermute(values, axis, [(source, source ^ step) for source in range(s...]
  transfers between devices with their start and end apart: 8 -> 7, of which waited for: 2 -> 4; matrix products, arithmetic and copies ran while one was open for 0% -> 0% of each run, Pallas kernels for 28% -> 28%
where the time goes in v12:
time: 47.1 us; the launch traced here: 46.9 us
  Pallas kernels  25 us (53%)
  starting transfers between devices  12.5 us (27%)
  waiting for transfers between devices  8.8 us (19%)
  between operations  0.69 us (1%)
    pallas_call x2, Pallas kernels, on_device(): pl.pallas_call(functools.partial(head_kernel, dp_size, heads_size, kv_ind...  23 us
    ppermute x7, starting transfers between devices, swap(): lax.ppermute(values, axis, [(source, source ^ step) for source in range(s...  12.5 us
    ppermute x7, waiting for transfers between devices, swap(): lax.ppermute(values, axis, [(source, source ^ step) for source in range(s...  8.8 us
    pallas_call x1, Pallas kernels, on_device(): pl.pallas_call(functools.partial(place_kernel, heads_size, kv_local), out...  1 us
  transfers between devices with their start and end apart: 7, of which 4 were waited for; matrix products, arithmetic and copies ran while one was open for 0% of the time, Pallas kernels for 28%

profile of v12, /device:TPU:0, one launch (start us, length us, event | category | flops | bytes accessed | tf_op | source)
XLA Modules:
  0.0 46.9 jit_solution(5873312668914625573)
XLA Ops:
  0.6 11.0 %head_grads.2 = (f32[2,2,256,128]{3,2,1,0:T(8,128)}, bf16[2,2,256,128]{3,2,1,0:T(8,128)(2,1)}, bf16[64,1024]{1,0:T(8,128)(2,1)}, bf16[64,1024]{1,0:T(8,128)(2,1)...) custom-call(bf16[4096,128]{1,0:T(8,128)(2,1)} %bitcast.9, ...), custom_call_target="tpu_custom_call" | custom-call | flops 6710886400 | bytes 5242880 | tf_op jit(solution)/shard_map/head_grads/pallas_call | solution.py:333
  11.7 4.1 %collective-permute-start = (bf16[2,2,256,128]{3,2,1,0:T(8,128)(2,1)}, bf16[2,2,256,128]{3,2,1,0:T(8,128)(2,1)S(1)}, u32[]{:S(2)}, u32[]{:S(2)}) collective-permute-start(bf16[2,2,256,128]{3,2,1,0:T(8,128)(2,1)} %get-tuple-element.43), channel_id=1, source_target_pairs={{0,8},{4,12},{8,0},{12,4},{1,9},{5,13},{9,1},{13,5},{2,10},{6,14},... | collective-permute-start | bytes 786440 | tf_op jit(solution)/shard_map/ppermute | solution.py:268
  15.8 0.0 copy-start.1
  15.8 12.0 %head_grads.3 = (f32[2,2,256,128]{3,2,1,0:T(8,128)}, bf16[2,2,256,128]{3,2,1,0:T(8,128)(2,1)}, bf16[64,2048]{1,0:T(8,128)(2,1)}, bf16[64,2048]{1,0:T(8,128)(2,1)...) custom-call(bf16[4096,128]{1,0:T(8,128)(2,1)} %bitcast.10, ...), custom_call_target="tpu_custom_call" | custom-call | flops 6710886400 | bytes 5242880 | tf_op jit(solution)/shard_map/head_grads/pallas_call | solution.py:333
  27.8 0.0 copy-start
  27.8 0.1 collective-permute-done.got_ref
  27.9 1.5 %collective-permute-start.1 = (bf16[2,2,256,128]{3,2,1,0:T(8,128)(2,1)}, bf16[2,2,256,128]{3,2,1,0:T(8,128)(2,1)S(1)}, u32[]{:S(2)}, u32[]{:S(2)}) collective-permute-start(bf16[2,2,256,128]{3,2,1,0:T(8,128)(2,1)} %get-tuple-element.48), channel_id=1, source_target_pairs={{0,4},{4,0},{8,12},{12,8},{1,5},{5,1},{9,13},{13,9},{2,6},{6,2},{1... | collective-permute-start | bytes 786440 | tf_op jit(solution)/shard_map/ppermute | solution.py:268
  29.4 1.5 %collective-permute-start.4 = (bf16[64,2048]{1,0:T(8,128)(2,1)}, bf16[64,2048]{1,0:T(8,128)(2,1)S(1)}, u32[]{:S(2)}, u32[]{:S(2)}) collective-permute-start(bf16[64,2048]{1,0:T(8,128)(2,1)} %get-tuple-element.56), channel_id=1, source_target_pairs={{0,2},{1,3},{2,0},{3,1},{4,6},{5,7},{6,4},{7,5},{8,10},{9,11},{10,... | collective-permute-start | bytes 786440 | tf_op jit(solution)/shard_map/ppermute | solution.py:268
  30.9 0.0 collective-permute-start.5
  30.9 0.6 %collective-permute-start.6 = (bf16[64,2048]{1,0:T(8,128)(2,1)}, bf16[64,2048]{1,0:T(8,128)(2,1)S(1)}, u32[]{:S(2)}, u32[]{:S(2)}) collective-permute-start(bf16[64,2048]{1,0:T(8,128)(2,1)} %get-tuple-element.58), channel_id=1, source_target_pairs={{0,1},{1,0},{2,3},{3,2},{4,5},{5,4},{6,7},{7,6},{8,9},{9,8},{10,11... | collective-permute-start | bytes 786440 | tf_op jit(solution)/shard_map/ppermute | solution.py:268
  31.6 0.0 copy-done.1
  31.6 0.0 copy-start.2
  31.6 4.2 %collective-permute-done.1.got_ref = bf16[2,2,256,128]{3,2,1,0:T(8,128)(2,1)S(1)} collective-permute-done((bf16[2,2,256,128]{3,2,1,0:T(8,128)(2,1)}, bf16[2,2,256,128]{3,2,1,0:T(8,128)(2,1)S(1)}, u32[]{:S(2)}, u32[]{:S(2)}) %collective-permute-start.1) | collective-permute-done | bytes 262176 | tf_op jit(solution)/shard_map/ppermute | solution.py:268
  35.8 0.0 copy-done
  35.9 1.6 %collective-permute-start.2 = (bf16[1,2,256,128]{3,2,1,0:T(8,128)(2,1)S(1)}, bf16[1,2,256,128]{3,2,1,0:T(8,128)(2,1)S(1)}, u32[]{:S(2)}, u32[]{:S(2)}) collective-permute-start(bf16[1,2,256,128]{3,2,1,0:T(8,128)(2,1)S(1)} %get-tuple-element.52), channel_id=1, source_target_pairs={{0,4},{4,0},{8,12},{12,8},{1,5},{5,1},{9,13},{13,9},{2,6},{6,2},{1... | collective-permute-start | bytes 393224 | tf_op jit(solution)/shard_map/ppermute | solution.py:268
  37.5 3.0 %collective-permute-start.3 = (bf16[1,2,256,128]{3,2,1,0:T(8,128)(2,1)S(1)}, bf16[1,2,256,128]{3,2,1,0:T(8,128)(2,1)S(1)}, u32[]{:S(2)}, u32[]{:S(2)}) collective-permute-start(bf16[1,2,256,128]{3,2,1,0:T(8,128)(2,1)S(1)} %get-tuple-element.53), channel_id=1, source_target_pairs={{0,8},{4,12},{8,0},{12,4},{1,9},{5,13},{9,1},{13,5},{2,10},{6,14},... | collective-permute-start | bytes 393224 | tf_op jit(solution)/shard_map/ppermute | solution.py:268
  40.6 0.0 collective-permute-done.4.refs_1_
  40.6 1.3 %collective-permute-done.5.refs_2_ = bf16[64,2048]{1,0:T(8,128)(2,1)S(1)} collective-permute-done((bf16[64,2048]{1,0:T(8,128)(2,1)}, bf16[64,2048]{1,0:T(8,128)(2,1)S(1)}, u32[]{:S(2)}, u32[]{:S(2)}) %collective-permute-start.5) | collective-permute-done | bytes 262176 | tf_op jit(solution)/shard_map/ppermute | solution.py:268
  41.9 0.0 collective-permute-done.6.refs_3_
  41.9 0.0 copy-done.2
  41.9 1.0 %place_queries.1 = bf16[64,8192]{1,0:T(8,128)(2,1)} custom-call(bf16[64,2048]{1,0:T(8,128)(2,1)S(1)} %copy-done.2, bf16[64,2048]{1,0:T(8,128)(2,1)S(1)} %collective-permute-done.4.refs_1_, bf16[64,2048]{1,0:T(8,128)(2,1)S(1)} %collective-permute-done.5.refs_2_, bf16[64,2048]{1,0:T(8,128)(2,1)S(1)} %collective-permute-done.6.refs_3_), custom_call_target="tpu_custom_call" | custom-call | flops 1048576 | bytes 2097152 | tf_op jit(solution)/shard_map/place_queries/pallas_call | solution.py:385
  42.9 0.0 collective-permute-done.2.refs_2_
  42.9 3.2 %collective-permute-done.3.refs_3_ = bf16[1,2,256,128]{3,2,1,0:T(8,128)(2,1)S(1)} collective-permute-done((bf16[1,2,256,128]{3,2,1,0:T(8,128)(2,1)S(1)}, bf16[1,2,256,128]{3,2,1,0:T(8,128)(2,1)S(1)}, u32[]{:S(2)}, u32[]{:S(2)}) %collective-permute-start.3) | collective-permute-done | bytes 131104 | tf_op jit(solution)/shard_map/ppermute | solution.py:268
  46.1 0.9 %cart_grads.1 = f32[1024,128]{1,0:T(8,128)} custom-call(f32[1,2,256,128]{3,2,1,0:T(8,128)S(1)} %get-tuple-element.46.refs_0_, f32[1,2,256,128]{3,2,1,0:T(8,128)S(1)} %get-tuple-element.49.refs_1_, bf16[1,2,256,128]{3,2,1,0:T(8,128)(2,1)S(1)} %collective-permute-done.2.refs_2_, bf16[1,2,256,128]{3,2,1,0:T(8,128)(2,1)S(1)} %collective-permute-done.3.refs_3_), custom_call_target="tpu_custom_call" | custom-call | flops 1048576 | bytes 2097152 | tf_op jit(solution)/shard_map/cart_grads/pallas_call | solution.py:395
  (2 shorter events, 0.1 us)
Async XLA Ops:
  11.7 16.2 %collective-permute-start = (bf16[2,2,256,128]{3,2,1,0:T(8,128)(2,1)}, bf16[2,2,256,128]{3,2,1,0:T(8,128)(2,1)S(1)}, u32[]{:S(2)}, u32[]{:S(2)}) collective-permute-start(bf16[2,2,256,128]{3,2,1,0:T(8,128)(2,1)} %get-tuple-element.43), channel_id=1, source_target_pairs={{0,8},{4,12},{8,0},{12,4},{1,9},{5,13},{9,1},{13,5},{2,10},{6,14},... | collective-permute-start | bytes 786440 | tf_op jit(solution)/shard_map/ppermute | solution.py:268
  15.8 15.8 %copy-start.1 = (f32[2,2,256,128]{3,2,1,0:T(8,128)S(1)}, f32[2,2,256,128]{3,2,1,0:T(8,128)}, u32[]{:S(2)}) copy-start(f32[2,2,256,128]{3,2,1,0:T(8,128)} %get-tuple-element.44.part_ref) | copy-start | bytes 1572868
  27.8 8.1 %copy-start = (f32[2,2,256,128]{3,2,1,0:T(8,128)S(1)}, f32[2,2,256,128]{3,2,1,0:T(8,128)}, u32[]{:S(2)}) copy-start(f32[2,2,256,128]{3,2,1,0:T(8,128)} %get-tuple-element.47.part_ref) | copy-start | bytes 1572868
  27.9 7.9 %collective-permute-start.1 = (bf16[2,2,256,128]{3,2,1,0:T(8,128)(2,1)}, bf16[2,2,256,128]{3,2,1,0:T(8,128)(2,1)S(1)}, u32[]{:S(2)}, u32[]{:S(2)}) collective-permute-start(bf16[2,2,256,128]{3,2,1,0:T(8,128)(2,1)} %get-tuple-element.48), channel_id=1, source_target_pairs={{0,4},{4,0},{8,12},{12,8},{1,5},{5,1},{9,13},{13,9},{2,6},{6,2},{1... | collective-permute-start | bytes 786440 | tf_op jit(solution)/shard_map/ppermute | solution.py:268
  29.4 11.1 %collective-permute-start.4 = (bf16[64,2048]{1,0:T(8,128)(2,1)}, bf16[64,2048]{1,0:T(8,128)(2,1)S(1)}, u32[]{:S(2)}, u32[]{:S(2)}) collective-permute-start(bf16[64,2048]{1,0:T(8,128)(2,1)} %get-tuple-element.56), channel_id=1, source_target_pairs={{0,2},{1,3},{2,0},{3,1},{4,6},{5,7},{6,4},{7,5},{8,10},{9,11},{10,... | collective-permute-start | bytes 786440 | tf_op jit(solution)/shard_map/ppermute | solution.py:268
  30.9 10.9 %collective-permute-start.5 = (bf16[64,2048]{1,0:T(8,128)(2,1)}, bf16[64,2048]{1,0:T(8,128)(2,1)S(1)}, u32[]{:S(2)}, u32[]{:S(2)}) collective-permute-start(bf16[64,2048]{1,0:T(8,128)(2,1)} %get-tuple-element.57), channel_id=1, source_target_pairs={{0,3},{1,2},{2,1},{3,0},{4,7},{5,6},{6,5},{7,4},{8,11},{9,10},{10,... | collective-permute-start | bytes 786440 | tf_op jit(solution)/shard_map/ppermute | solution.py:268
  30.9 10.9 %collective-permute-start.6 = (bf16[64,2048]{1,0:T(8,128)(2,1)}, bf16[64,2048]{1,0:T(8,128)(2,1)S(1)}, u32[]{:S(2)}, u32[]{:S(2)}) collective-permute-start(bf16[64,2048]{1,0:T(8,128)(2,1)} %get-tuple-element.58), channel_id=1, source_target_pairs={{0,1},{1,0},{2,3},{3,2},{4,5},{5,4},{6,7},{7,6},{8,9},{9,8},{10,11... | collective-permute-start | bytes 786440 | tf_op jit(solution)/shard_map/ppermute | solution.py:268
  31.6 10.2 %copy-start.2 = (bf16[64,2048]{1,0:T(8,128)(2,1)S(1)}, bf16[64,2048]{1,0:T(8,128)(2,1)}, u32[]{:S(2)}) copy-start(bf16[64,2048]{1,0:T(8,128)(2,1)} %get-tuple-element.55.refs_0_) | copy-start | bytes 786436
  35.9 7.0 %collective-permute-start.2 = (bf16[1,2,256,128]{3,2,1,0:T(8,128)(2,1)S(1)}, bf16[1,2,256,128]{3,2,1,0:T(8,128)(2,1)S(1)}, u32[]{:S(2)}, u32[]{:S(2)}) collective-permute-start(bf16[1,2,256,128]{3,2,1,0:T(8,128)(2,1)S(1)} %get-tuple-element.52), channel_id=1, source_target_pairs={{0,4},{4,0},{8,12},{12,8},{1,5},{5,1},{9,13},{13,9},{2,6},{6,2},{1... | collective-permute-start | bytes 393224 | tf_op jit(solution)/shard_map/ppermute | solution.py:268
  37.5 8.5 %collective-permute-start.3 = (bf16[1,2,256,128]{3,2,1,0:T(8,128)(2,1)S(1)}, bf16[1,2,256,128]{3,2,1,0:T(8,128)(2,1)S(1)}, u32[]{:S(2)}, u32[]{:S(2)}) collective-permute-start(bf16[1,2,256,128]{3,2,1,0:T(8,128)(2,1)S(1)} %get-tuple-element.53), channel_id=1, source_target_pairs={{0,8},{4,12},{8,0},{12,4},{1,9},{5,13},{9,1},{13,5},{2,10},{6,14},... | collective-permute-start | bytes 393224 | tf_op jit(solution)/shard_map/ppermute | solution.py:268

commit v13 on v11

--- a/solution.py
+++ b/solution.py
@@ -9,7 +9,7 @@
 from jax.sharding import PartitionSpec as P
 
 masked_score = -1e30
-vmem_bytes = 56 * 1024 * 1024
+vmem_bytes = 46 * 1024 * 1024
 small_vmem_bytes = 8 * 1024 * 1024
 early_steps = (2,)
 f32 = jnp.float32
@@ -42,7 +42,7 @@
     dq_outs, self_ref, refs = refs[:heads_size], refs[heads_size], refs[heads_size + 1 :]
     (
         wide_ref, keys_ref, vals_ref, keys_t_ref, s_ref, w_ref, d_ref, p_ref, ds_ref, dk_ref, dv_ref, out_ref, dq_ref,
-        q_in, g_in, sk_in, sv_in, ck_in, cv_in, sems,
+        q_in, g_in, sk_in, sv_in, ck_in, cv_in, seg_in, sems,
     ) = refs
     head_dim = q_ref.shape[1]
     tokens = seg_ref.shape[1]
@@ -67,7 +67,8 @@
     for block in range(blocks):
         copies["q", block] = block_copy(q_ref, q_in, block, 4 + block)
         copies["g", block] = block_copy(g_ref, g_in, block, 4 + blocks + block)
-    order = ["ck", "sk", ("q", 0), "cv", "sv", ("g", 0)]
+    copies["seg"] = pltpu.make_async_copy(seg_ref, seg_in, sems.at[4 + 2 * blocks])
+    order = ["ck", "sk", ("q", 0), "seg", "cv", "sv", ("g", 0)]
     order += [(kind, block) for block in range(1, blocks) for kind in ("q", "g")]
     for name in order:
         copies[name].start()
@@ -89,7 +90,8 @@
         wide = wide.astype(f32).reshape(block_tokens, kv_local, width, head_dim)
         return wide[:, kv_index].reshape(rows, head_dim).astype(bf16)
 
-    first_count = jnp.sum((seg_ref[...] == 0).astype(f32), axis=1, keepdims=True).astype(jnp.int32)
+    copies["seg"].wait()
+    first_count = jnp.sum((seg_in[...] == 0).astype(f32), axis=1, keepdims=True).astype(jnp.int32)
 
     def limit(block):
         return -(-(block + 1) * block_tokens // fine) * fine
@@ -298,7 +300,8 @@
     rows = block_tokens * width
     part_rows = cart_rows // dp_size
     own_tokens = tokens // heads_size
-    flat = [array.reshape(-1, head_dim) for array in (queries, out_grad, self_keys, self_values, cart_keys, cart_values)]
+    flat = [pltpu.with_memory_space_constraint(array.reshape(-1, head_dim), pltpu.HBM) for array in (queries, out_grad, self_keys, self_values, cart_keys, cart_values)]
+    segments = pltpu.with_memory_space_constraint(segment_ids, pltpu.HBM)
     macs = tokens * width * all_keys * head_dim * 5
     blocks = tokens // block_tokens
     columns = width * head_dim
@@ -322,8 +325,8 @@
                 jax.ShapeDtypeStruct((dp_size // 2, 2, part_rows, head_dim), bf16),
                 *other_shapes,
             ),
-            in_specs=[pl.BlockSpec(memory_space=pltpu.HBM)] * 6
-            + [pl.BlockSpec(memory_space=pltpu.VMEM)] * (1 + (len(before) if last else 0)),
+            in_specs=[pl.BlockSpec(memory_space=pltpu.HBM)] * 7
+            + [pl.BlockSpec(memory_space=pltpu.VMEM)] * (len(before) if last else 0),
             scratch_shapes=[
                 pltpu.VMEM((cart_rows * kv_local, head_dim), f32),
                 pltpu.VMEM((all_keys, head_dim), bf16),
@@ -339,12 +342,13 @@
                 pltpu.VMEM((rows, head_dim), f32),
                 pltpu.VMEM((tokens, columns), bf16),
                 *[pltpu.VMEM(array.shape, bf16) for array in flat],
-                pltpu.SemaphoreType.DMA((4 + 2 * blocks,)),
+                pltpu.VMEM(segment_ids.shape, jnp.int32),
+                pltpu.SemaphoreType.DMA((5 + 2 * blocks,)),
             ],
             compiler_params=pltpu.CompilerParams(vmem_limit_bytes=vmem_bytes),
             cost_estimate=pl.CostEstimate(flops=4 * macs, bytes_accessed=5 * 2**20, transcendentals=tokens * width * all_keys),
             name="head_grads",
-        )(*flat, segment_ids, *(before if last else []))
+        )(*flat, segments, *(before if last else []))
         part, send, near, far = outs[0], outs[1], outs[2 : 2 + kept], outs[2 + kept : -1]
         if last:
             part, send, near, far, received = lax.optimization_barrier((part, send, near, far, received))

time: 47 us -> 43 us (0.915)
  Pallas kernels: 24.9 us -> 21.4 us
  waiting for transfers between devices: 10.5 us -> 9.74 us
    pallas_call x2, Pallas kernels: 22.9 us -> 19.4 us  [on_device(): pl.pallas_call(functools.partial(head_kernel, dp_size, heads_size, kv_ind...]
    ppermute x8, waiting for transfers between devices: 10.5 us -> 9.74 us  [swap(): lax.ppermute(values, axis, [(source, source ^ step) for source in range(s...]
  transfers between devices with their start and end apart: 8 -> 8, of which waited for: 2 -> 2; matrix products, arithmetic and copies ran while one was open for 0% -> 0% of each run, Pallas kernels for 28% -> 26%
where the time goes in v13:
time: 43 us; the launch traced here: 42.8 us
  Pallas kernels  21.4 us (50%)
  starting transfers between devices  11 us (26%)
  waiting for transfers between devices  9.74 us (23%)
  between operations  0.69 us (2%)
    pallas_call x2, Pallas kernels, on_device(): pl.pallas_call(functools.partial(head_kernel, dp_size, heads_size, kv_ind...  19.4 us
    ppermute x8, starting transfers between devices, swap(): lax.ppermute(values, axis, [(source, source ^ step) for source in range(s...  11 us
    ppermute x8, waiting for transfers between devices, swap(): lax.ppermute(values, axis, [(source, source ^ step) for source in range(s...  9.74 us
    pallas_call x1, Pallas kernels, on_device(): pl.pallas_call(functools.partial(place_kernel, heads_size, kv_local), out...  1.01 us
    pallas_call x1, Pallas kernels, on_device(): pl.pallas_call(functools.partial(cart_kernel, kv_local), out_shape=jax.Sh...  0.87 us
  transfers between devices with their start and end apart: 8, of which 2 were waited for; matrix products, arithmetic and copies ran while one was open for 0% of the time, Pallas kernels for 26%

profile of v13, /device:TPU:0, one launch (start us, length us, event | category | flops | bytes accessed | tf_op | source)
XLA Modules:
  0.0 42.8 jit_solution(17249521344868493509)
XLA Ops:
  0.6 9.4 %head_grads.2 = (f32[2,2,256,128]{3,2,1,0:T(8,128)S(1)}, bf16[2,2,256,128]{3,2,1,0:T(8,128)(2,1)S(1)}, bf16[64,1024]{1,0:T(8,128)(2,1)S(1)}, bf16[64,1024]{1,0:T...) custom-call(bf16[4096,128]{1,0:T(8,128)(2,1)} %bitcast.9, ...), custom_call_target="tpu_custom_call" | custom-call | flops 6710886400 | bytes 5242880 | tf_op jit(solution)/shard_map/head_grads/pallas_call | solution.py:321
  10.0 3.0 %collective-permute-start.1 = (bf16[64,1024]{1,0:T(8,128)(2,1)S(1)}, bf16[64,1024]{1,0:T(8,128)(2,1)S(1)}, u32[]{:S(2)}, u32[]{:S(2)}) collective-permute-start(bf16[64,1024]{1,0:T(8,128)(2,1)S(1)} %get-tuple-element.42), channel_id=1, source_target_pairs={{0,2},{1,3},{2,0},{3,1},{4,6},{5,7},{6,4},{7,5},{8,10},{9,11},{10,... | collective-permute-start | bytes 393224 | tf_op jit(solution)/shard_map/ppermute | solution.py:268
  13.0 1.6 %collective-permute-start = (bf16[2,2,256,128]{3,2,1,0:T(8,128)(2,1)S(1)}, bf16[2,2,256,128]{3,2,1,0:T(8,128)(2,1)S(1)}, u32[]{:S(2)}, u32[]{:S(2)}) collective-permute-start(bf16[2,2,256,128]{3,2,1,0:T(8,128)(2,1)S(1)} %get-tuple-element.41), channel_id=1, source_target_pairs={{0,4},{4,0},{8,12},{12,8},{1,5},{5,1},{9,13},{13,9},{2,6},{6,2},{1... | collective-permute-start | bytes 786440 | tf_op jit(solution)/shard_map/ppermute | solution.py:268
  14.6 10.0 %head_grads.3 = (f32[2,2,256,128]{3,2,1,0:T(8,128)S(1)}, bf16[2,2,256,128]{3,2,1,0:T(8,128)(2,1)S(1)}, bf16[64,2048]{1,0:T(8,128)(2,1)S(1)}, bf16[64,2048]{1,0:T...) custom-call(bf16[4096,128]{1,0:T(8,128)(2,1)} %bitcast.10, ...), custom_call_target="tpu_custom_call" | custom-call | flops 6710886400 | bytes 5242880 | tf_op jit(solution)/shard_map/head_grads/pallas_call | solution.py:321
  24.6 0.0 collective-permute-done.1.refs_3_
  24.7 0.0 collective-permute-done.got_ref
  24.7 0.5 %collective-permute-start.2 = (bf16[2,2,256,128]{3,2,1,0:T(8,128)(2,1)S(1)}, bf16[2,2,256,128]{3,2,1,0:T(8,128)(2,1)S(1)}, u32[]{:S(2)}, u32[]{:S(2)}) collective-permute-start(bf16[2,2,256,128]{3,2,1,0:T(8,128)(2,1)S(1)} %get-tuple-element.47), channel_id=1, source_target_pairs={{0,4},{4,0},{8,12},{12,8},{1,5},{5,1},{9,13},{13,9},{2,6},{6,2},{1... | collective-permute-start | bytes 786440 | tf_op jit(solution)/shard_map/ppermute | solution.py:268
  25.2 0.0 collective-permute-start.5
  25.2 0.3 collective-permute-start.6
  25.5 1.9 %collective-permute-start.7 = (bf16[64,1024]{1,0:T(8,128)(2,1)S(1)}, bf16[64,1024]{1,0:T(8,128)(2,1)S(1)}, u32[]{:S(2)}, u32[]{:S(2)}) collective-permute-start(bf16[64,1024]{1,0:T(8,128)(2,1)S(1)} %get-tuple-element.56), channel_id=1, source_target_pairs={{0,2},{1,3},{2,0},{3,1},{4,6},{5,7},{6,4},{7,5},{8,10},{9,11},{10,... | collective-permute-start | bytes 393224 | tf_op jit(solution)/shard_map/ppermute | solution.py:268
  27.4 2.7 %collective-permute-start.3 = (bf16[1,2,256,128]{3,2,1,0:T(8,128)(2,1)S(1)}, bf16[1,2,256,128]{3,2,1,0:T(8,128)(2,1)S(1)}, u32[]{:S(2)}, u32[]{:S(2)}) collective-permute-start(bf16[1,2,256,128]{3,2,1,0:T(8,128)(2,1)S(1)} %get-tuple-element.49), channel_id=1, source_target_pairs={{0,8},{4,12},{8,0},{12,4},{1,9},{5,13},{9,1},{13,5},{2,10},{6,14},... | collective-permute-start | bytes 393224 | tf_op jit(solution)/shard_map/ppermute | solution.py:268
  30.0 5.5 %collective-permute-done.2.got_ref = bf16[2,2,256,128]{3,2,1,0:T(8,128)(2,1)S(1)} collective-permute-done((bf16[2,2,256,128]{3,2,1,0:T(8,128)(2,1)S(1)}, bf16[2,2,256,128]{3,2,1,0:T(8,128)(2,1)S(1)}, u32[]{:S(2)}, u32[]{:S(2)}) %collective-permute-start.2) | collective-permute-done | bytes 262176 | tf_op jit(solution)/shard_map/ppermute | solution.py:268
  35.6 1.1 %collective-permute-start.4 = (bf16[1,2,256,128]{3,2,1,0:T(8,128)(2,1)S(1)}, bf16[1,2,256,128]{3,2,1,0:T(8,128)(2,1)S(1)}, u32[]{:S(2)}, u32[]{:S(2)}) collective-permute-start(bf16[1,2,256,128]{3,2,1,0:T(8,128)(2,1)S(1)} %get-tuple-element.50), channel_id=1, source_target_pairs={{0,8},{4,12},{8,0},{12,4},{1,9},{5,13},{9,1},{13,5},{2,10},{6,14},... | collective-permute-start | bytes 393224 | tf_op jit(solution)/shard_map/ppermute | solution.py:268
  36.7 0.0 collective-permute-done.7.refs_4_
  36.7 0.0 collective-permute-done.5.refs_1_
  36.7 0.0 collective-permute-done.6.refs_2_
  36.7 1.0 %place_queries.1 = bf16[64,8192]{1,0:T(8,128)(2,1)} custom-call(bf16[64,2048]{1,0:T(8,128)(2,1)S(1)} %get-tuple-element.52.refs_0_, bf16[64,2048]{1,0:T(8,128)(2,1)S(1)} %collective-permute-done.5.refs_1_, bf16[64,2048]{1,0:T(8,128)(2,1)S(1)} %collective-permute-done.6.refs_2_, bf16[64,1024]{1,0:T(8,128)(2,1)S(1)} %collective-permute-done.1.refs_3_, ...), custom_call_target="tpu_custom_call" | custom-call | flops 1048576 | bytes 2097152 | tf_op jit(solution)/shard_map/place_queries/pallas_call | solution.py:371
  37.7 0.0 collective-permute-done.3.refs_2_
  37.7 4.2 %collective-permute-done.4.refs_3_ = bf16[1,2,256,128]{3,2,1,0:T(8,128)(2,1)S(1)} collective-permute-done((bf16[1,2,256,128]{3,2,1,0:T(8,128)(2,1)S(1)}, bf16[1,2,256,128]{3,2,1,0:T(8,128)(2,1)S(1)}, u32[]{:S(2)}, u32[]{:S(2)}) %collective-permute-start.4) | collective-permute-done | bytes 131104 | tf_op jit(solution)/shard_map/ppermute | solution.py:268
  41.9 0.9 %cart_grads.1 = f32[1024,128]{1,0:T(8,128)} custom-call(f32[1,2,256,128]{3,2,1,0:T(8,128)S(1)} %get-tuple-element.45.refs_0_, f32[1,2,256,128]{3,2,1,0:T(8,128)S(1)} %get-tuple-element.48.refs_1_, bf16[1,2,256,128]{3,2,1,0:T(8,128)(2,1)S(1)} %collective-permute-done.3.refs_2_, bf16[1,2,256,128]{3,2,1,0:T(8,128)(2,1)S(1)} %collective-permute-done.4.refs_3_), custom_call_target="tpu_custom_call" | custom-call | flops 1048576 | bytes 2097152 | tf_op jit(solution)/shard_map/cart_grads/pallas_call | solution.py:381
  (2 shorter events, 0.1 us)
Async XLA Ops:
  10.0 14.6 %collective-permute-start.1 = (bf16[64,1024]{1,0:T(8,128)(2,1)S(1)}, bf16[64,1024]{1,0:T(8,128)(2,1)S(1)}, u32[]{:S(2)}, u32[]{:S(2)}) collective-permute-start(bf16[64,1024]{1,0:T(8,128)(2,1)S(1)} %get-tuple-element.42), channel_id=1, source_target_pairs={{0,2},{1,3},{2,0},{3,1},{4,6},{5,7},{6,4},{7,5},{8,10},{9,11},{10,... | collective-permute-start | bytes 393224 | tf_op jit(solution)/shard_map/ppermute | solution.py:268
  13.0 11.6 %collective-permute-start = (bf16[2,2,256,128]{3,2,1,0:T(8,128)(2,1)S(1)}, bf16[2,2,256,128]{3,2,1,0:T(8,128)(2,1)S(1)}, u32[]{:S(2)}, u32[]{:S(2)}) collective-permute-start(bf16[2,2,256,128]{3,2,1,0:T(8,128)(2,1)S(1)} %get-tuple-element.41), channel_id=1, source_target_pairs={{0,4},{4,0},{8,12},{12,8},{1,5},{5,1},{9,13},{13,9},{2,6},{6,2},{1... | collective-permute-start | bytes 786440 | tf_op jit(solution)/shard_map/ppermute | solution.py:268
  24.7 10.9 %collective-permute-start.2 = (bf16[2,2,256,128]{3,2,1,0:T(8,128)(2,1)S(1)}, bf16[2,2,256,128]{3,2,1,0:T(8,128)(2,1)S(1)}, u32[]{:S(2)}, u32[]{:S(2)}) collective-permute-start(bf16[2,2,256,128]{3,2,1,0:T(8,128)(2,1)S(1)} %get-tuple-element.47), channel_id=1, source_target_pairs={{0,4},{4,0},{8,12},{12,8},{1,5},{5,1},{9,13},{13,9},{2,6},{6,2},{1... | collective-permute-start | bytes 786440 | tf_op jit(solution)/shard_map/ppermute | solution.py:268
  25.2 11.5 %collective-permute-start.5 = (bf16[64,2048]{1,0:T(8,128)(2,1)S(1)}, bf16[64,2048]{1,0:T(8,128)(2,1)S(1)}, u32[]{:S(2)}, u32[]{:S(2)}) collective-permute-start(bf16[64,2048]{1,0:T(8,128)(2,1)S(1)} %get-tuple-element.53), channel_id=1, source_target_pairs={{0,1},{1,0},{2,3},{3,2},{4,5},{5,4},{6,7},{7,6},{8,9},{9,8},{10,11... | collective-permute-start | bytes 786440 | tf_op jit(solution)/shard_map/ppermute | solution.py:268
  25.2 11.5 %collective-permute-start.6 = (bf16[64,2048]{1,0:T(8,128)(2,1)S(1)}, bf16[64,2048]{1,0:T(8,128)(2,1)S(1)}, u32[]{:S(2)}, u32[]{:S(2)}) collective-permute-start(bf16[64,2048]{1,0:T(8,128)(2,1)S(1)} %get-tuple-element.54), channel_id=1, source_target_pairs={{0,3},{1,2},{2,1},{3,0},{4,7},{5,6},{6,5},{7,4},{8,11},{9,10},{10,... | collective-permute-start | bytes 786440 | tf_op jit(solution)/shard_map/ppermute | solution.py:268
  25.5 11.2 %collective-permute-start.7 = (bf16[64,1024]{1,0:T(8,128)(2,1)S(1)}, bf16[64,1024]{1,0:T(8,128)(2,1)S(1)}, u32[]{:S(2)}, u32[]{:S(2)}) collective-permute-start(bf16[64,1024]{1,0:T(8,128)(2,1)S(1)} %get-tuple-element.56), channel_id=1, source_target_pairs={{0,2},{1,3},{2,0},{3,1},{4,6},{5,7},{6,4},{7,5},{8,10},{9,11},{10,... | collective-permute-start | bytes 393224 | tf_op jit(solution)/shard_map/ppermute | solution.py:268
  27.4 10.3 %collective-permute-start.3 = (bf16[1,2,256,128]{3,2,1,0:T(8,128)(2,1)S(1)}, bf16[1,2,256,128]{3,2,1,0:T(8,128)(2,1)S(1)}, u32[]{:S(2)}, u32[]{:S(2)}) collective-permute-start(bf16[1,2,256,128]{3,2,1,0:T(8,128)(2,1)S(1)} %get-tuple-element.49), channel_id=1, source_target_pairs={{0,8},{4,12},{8,0},{12,4},{1,9},{5,13},{9,1},{13,5},{2,10},{6,14},... | collective-permute-start | bytes 393224 | tf_op jit(solution)/shard_map/ppermute | solution.py:268
  35.6 6.4 %collective-permute-start.4 = (bf16[1,2,256,128]{3,2,1,0:T(8,128)(2,1)S(1)}, bf16[1,2,256,128]{3,2,1,0:T(8,128)(2,1)S(1)}, u32[]{:S(2)}, u32[]{:S(2)}) collective-permute-start(bf16[1,2,256,128]{3,2,1,0:T(8,128)(2,1)S(1)} %get-tuple-element.50), channel_id=1, source_target_pairs={{0,8},{4,12},{8,0},{12,4},{1,9},{5,13},{9,1},{13,5},{2,10},{6,14},... | collective-permute-start | bytes 393224 | tf_op jit(solution)/shard_map/ppermute | solution.py:268

commit v14 on v13

--- a/solution.py
+++ b/solution.py
@@ -31,8 +31,11 @@
 
 def head_kernel(dp_size, heads_size, kv_index, kv_local, width, block_tokens, chunk, fine, sub, *refs):
     last = kv_index == kv_local - 1
-    q_ref, g_ref, sk_ref, sv_ref, ck_ref, cv_ref, seg_ref = refs[:7]
-    refs = refs[7:]
+    first = kv_index == 0
+    if first:
+        (q_ref, g_ref, sk_ref, sv_ref, ck_ref, cv_ref, seg_ref), refs = refs[:7], refs[7:]
+    else:
+        (keys_ref, vals_ref, keys_t_ref, q_rows, g_rows, seg_in), refs = refs[:6], refs[6:]
     held = kv_index if last else 0
     near_steps, far_steps = split_steps(heads_size)
     kept = len(near_steps)
@@ -40,38 +43,45 @@
     self_before, refs = refs[:held], refs[held:]
     (keep_ref, send_ref), refs = refs[:2], refs[2:]
     dq_outs, self_ref, refs = refs[:heads_size], refs[heads_size], refs[heads_size + 1 :]
-    (
-        wide_ref, keys_ref, vals_ref, keys_t_ref, s_ref, w_ref, d_ref, p_ref, ds_ref, dk_ref, dv_ref, out_ref, dq_ref,
-        q_in, g_in, sk_in, sv_in, ck_in, cv_in, seg_in, sems,
-    ) = refs
-    head_dim = q_ref.shape[1]
-    tokens = seg_ref.shape[1]
-    cart_rows = ck_ref.shape[0] // kv_local
-    all_keys = cart_rows + tokens
+    if first:
+        others = range(1, kv_local)
+        next_refs = {other: refs[5 * other - 5 : 5 * other] for other in others}
+        refs = refs[5 * len(others) :]
+        if kv_local > 1:
+            seg_out, refs = refs[0], refs[1:]
+        (
+            keys_ref, vals_ref, keys_t_ref, q_in, g_in, sk_in, sv_in, ck_in, cv_in, seg_in, sems,
+        ), refs = refs[:11], refs[11:]
+    wide_ref, s_ref, w_ref, d_ref, p_ref, ds_ref, dk_ref, dv_ref, out_ref, dq_ref = refs
+    all_keys, head_dim = keys_ref.shape
+    tokens = seg_in.shape[1]
+    cart_rows = all_keys - tokens
     rows = block_tokens * width
     scale = head_dim ** -0.5
     scale2 = scale * math.log2(math.e)
     span = block_tokens * kv_local * width
     blocks = tokens // block_tokens
 
-    def block_copy(source, target, block, sem):
-        at = slice(block * span, (block + 1) * span)
-        return pltpu.make_async_copy(source.at[at, :], target.at[at, :], sems.at[sem])
-
-    copies = {
-        name: pltpu.make_async_copy(source, target, sems.at[at])
-        for at, (name, source, target) in enumerate(
-            [("ck", ck_ref, ck_in), ("sk", sk_ref, sk_in), ("cv", cv_ref, cv_in), ("sv", sv_ref, sv_in)]
-        )
-    }
-    for block in range(blocks):
-        copies["q", block] = block_copy(q_ref, q_in, block, 4 + block)
-        copies["g", block] = block_copy(g_ref, g_in, block, 4 + blocks + block)
-    copies["seg"] = pltpu.make_async_copy(seg_ref, seg_in, sems.at[4 + 2 * blocks])
-    order = ["ck", "sk", ("q", 0), "seg", "cv", "sv", ("g", 0)]
-    order += [(kind, block) for block in range(1, blocks) for kind in ("q", "g")]
-    for name in order:
-        copies[name].start()
+    if first:
+
+        def block_copy(source, target, block, sem):
+            at = slice(block * span, (block + 1) * span)
+            return pltpu.make_async_copy(source.at[at, :], target.at[at, :], sems.at[sem])
+
+        copies = {
+            name: pltpu.make_async_copy(source, target, sems.at[at])
+            for at, (name, source, target) in enumerate(
+                [("ck", ck_ref, ck_in), ("sk", sk_ref, sk_in), ("cv", cv_ref, cv_in), ("sv", sv_ref, sv_in)]
+            )
+        }
+        for block in range(blocks):
+            copies["q", block] = block_copy(q_ref, q_in, block, 4 + block)
+            copies["g", block] = block_copy(g_ref, g_in, block, 4 + blocks + block)
+        copies["seg"] = pltpu.make_async_copy(seg_ref, seg_in, sems.at[4 + 2 * blocks])
+        order = ["ck", "sk", ("q", 0), "seg", "cv", "sv", ("g", 0)]
+        order += [(kind, block) for block in range(1, blocks) for kind in ("q", "g")]
+        for name in order:
+            copies[name].start()
 
     def pick(name, ref, dst, at):
         copies[name].wait()
@@ -80,17 +90,28 @@
             dst[at : at + count, :] = ref[...]
         else:
             wide_ref[0 : ref.shape[0], :] = ref[...].astype(f32)
-            dst[at : at + count, :] = wide_ref[pl.ds(kv_index, count, stride=kv_local), :].astype(bf16)
-
-    def rows_of(name, ref, block):
+            dst[at : at + count, :] = wide_ref[pl.ds(0, count, stride=kv_local), :].astype(bf16)
+            for other in others:
+                next_ref = next_refs[other][0 if dst is keys_ref else 1]
+                next_ref[at : at + count, :] = wide_ref[pl.ds(other, count, stride=kv_local), :].astype(bf16)
+
+    def rows_of(name, block):
+        at = slice(block * rows, (block + 1) * rows)
+        if not first:
+            return (q_rows if name == "q" else g_rows)[at, :]
         copies[name, block].wait()
-        wide = ref[block * span : (block + 1) * span, :]
+        wide = (q_in if name == "q" else g_in)[block * span : (block + 1) * span, :]
         if kv_local == 1:
             return wide
         wide = wide.astype(f32).reshape(block_tokens, kv_local, width, head_dim)
-        return wide[:, kv_index].reshape(rows, head_dim).astype(bf16)
-
-    copies["seg"].wait()
+        for other in others:
+            next_refs[other][3 if name == "q" else 4][at, :] = wide[:, other].reshape(rows, head_dim).astype(bf16)
+        return wide[:, 0].reshape(rows, head_dim).astype(bf16)
+
+    if first:
+        copies["seg"].wait()
+        if kv_local > 1:
+            seg_out[...] = seg_in[...]
     first_count = jnp.sum((seg_in[...] == 0).astype(f32), axis=1, keepdims=True).astype(jnp.int32)
 
     def limit(block):
@@ -110,7 +131,7 @@
         return [slice(at, at + sub) for at in range(start, start + size, sub)]
 
     def open_scores(block):
-        queries[block] = rows_of("q", q_in, block)
+        queries[block] = rows_of("q", block)
         token = (lax.broadcasted_iota(jnp.int32, (1, rows), 1) + block * rows) // width
         begin = jnp.where(token >= first_count, first_count, 0)
         acc["peak"] = jnp.full((8, rows), masked_score, f32)
@@ -130,7 +151,7 @@
         peaks[block] = jnp.broadcast_to(jnp.max(acc["peak"], axis=0, keepdims=True), (8, rows))
 
     def open_weights(block):
-        grads[block] = rows_of("g", g_in, block)
+        grads[block] = rows_of("g", block)
         acc["total"] = jnp.zeros((8, rows), f32)
         acc["center"] = jnp.zeros((8, rows), f32)
 
@@ -176,8 +197,9 @@
                 out_ref[pl.ds(head, block_tokens, stride=width), :].astype(bf16)
             )
 
-    pick("ck", ck_in, keys_ref, 0)
-    pick("sk", sk_in, keys_ref, cart_rows)
+    if first:
+        pick("ck", ck_in, keys_ref, 0)
+        pick("sk", sk_in, keys_ref, cart_rows)
     stages = (
         (2, open_grads, step_grads, close_grads),
         (1, open_weights, step_weights, close_weights),
@@ -185,10 +207,12 @@
     )
     for turn in range(blocks + 2):
         live = [(turn - lag, *calls) for lag, *calls in stages if 0 <= turn - lag < blocks]
-        if turn == 1:
+        if turn == 1 and first:
             pick("cv", cv_in, vals_ref, 0)
             pick("sv", sv_in, vals_ref, cart_rows)
             keys_t_ref[...] = keys_ref[...].astype(f32).T.astype(bf16)
+            for other in others:
+                next_refs[other][2][...] = next_refs[other][0][...].astype(f32).T.astype(bf16)
         for block, begin_call, _, _ in live:
             begin_call(block)
         for index in range(len(pieces(0))):
@@ -317,21 +341,39 @@
         own_shape = (2 * count, head_dim) if last else (2, tokens, head_dim)
         other_shapes = [near] * kept + [far] * (heads_size - kept)
         other_shapes.append(jax.ShapeDtypeStruct(own_shape, bf16 if last else f32))
-        before = kept_list + self_list
+        next_shapes, first_scratch = [], []
+        if kv_index == 0:
+            key_like = jax.ShapeDtypeStruct((all_keys, head_dim), bf16)
+            turned = jax.ShapeDtypeStruct((head_dim, all_keys), bf16)
+            row_like = jax.ShapeDtypeStruct((tokens * width, head_dim), bf16)
+            next_shapes = [key_like, key_like, turned, row_like, row_like] * (kv_local - 1)
+            if kv_local > 1:
+                next_shapes.append(jax.ShapeDtypeStruct(segment_ids.shape, jnp.int32))
+            inputs = [*flat, segments]
+            first_scratch = [
+                pltpu.VMEM((all_keys, head_dim), bf16),
+                pltpu.VMEM((all_keys, head_dim), bf16),
+                pltpu.VMEM((head_dim, all_keys), bf16),
+                *[pltpu.VMEM(array.shape, bf16) for array in flat],
+                pltpu.VMEM(segment_ids.shape, jnp.int32),
+                pltpu.SemaphoreType.DMA((5 + 2 * blocks,)),
+            ]
+        else:
+            inputs = [*prepared[5 * kv_index - 5 : 5 * kv_index], prepared[-1]]
+        before = kept_list + self_list if last else []
         outs = pl.pallas_call(
             functools.partial(head_kernel, dp_size, heads_size, kv_index, kv_local, width, block_tokens, chunk, fine, sub),
             out_shape=(
                 jax.ShapeDtypeStruct((dp_size // 2, 2, part_rows, head_dim), f32),
                 jax.ShapeDtypeStruct((dp_size // 2, 2, part_rows, head_dim), bf16),
                 *other_shapes,
+                *next_shapes,
             ),
-            in_specs=[pl.BlockSpec(memory_space=pltpu.HBM)] * 7
-            + [pl.BlockSpec(memory_space=pltpu.VMEM)] * (len(before) if last else 0),
+            in_specs=[pl.BlockSpec(memory_space=pltpu.VMEM if kv_index else pltpu.HBM)] * len(inputs)
+            + [pl.BlockSpec(memory_space=pltpu.VMEM)] * len(before),
             scratch_shapes=[
+                *first_scratch,
                 pltpu.VMEM((cart_rows * kv_local, head_dim), f32),
-                pltpu.VMEM((all_keys, head_dim), bf16),
-                pltpu.VMEM((all_keys, head_dim), bf16),
-                pltpu.VMEM((head_dim, all_keys), bf16),
                 pltpu.VMEM((2, all_keys, rows), f32),
                 pltpu.VMEM((2, all_keys, rows), f32),
                 pltpu.VMEM((2, all_keys, rows), f32),
@@ -341,14 +383,14 @@
                 pltpu.VMEM((all_keys, head_dim), f32),
                 pltpu.VMEM((rows, head_dim), f32),
                 pltpu.VMEM((tokens, columns), bf16),
-                *[pltpu.VMEM(array.shape, bf16) for array in flat],
-                pltpu.VMEM(segment_ids.shape, jnp.int32),
-                pltpu.SemaphoreType.DMA((5 + 2 * blocks,)),
             ],
             compiler_params=pltpu.CompilerParams(vmem_limit_bytes=vmem_bytes),
             cost_estimate=pl.CostEstimate(flops=4 * macs, bytes_accessed=5 * 2**20, transcendentals=tokens * width * all_keys),
             name="head_grads",
-        )(*flat, segments, *(before if last else []))
+        )(*inputs, *before)
+        if kv_index == 0:
+            prepared = outs[len(outs) - len(next_shapes) :]
+        outs = outs[: len(outs) - len(next_shapes)]
         part, send, near, far = outs[0], outs[1], outs[2 : 2 + kept], outs[2 + kept : -1]
         if last:
             part, send, near, far, received = lax.optimization_barrier((part, send, near, far, received))

time: 43 us -> 42.2 us (0.981)
  Pallas kernels: 21.4 us -> 20.7 us
    pallas_call x2, Pallas kernels: 19.4 us -> 18.7 us  [on_device(): pl.pallas_call(functools.partial(head_kernel, dp_size, heads_size, kv_ind...]
  transfers between devices with their start and end apart: 8 -> 8, of which waited for: 2 -> 2; matrix products, arithmetic and copies ran while one was open for 0% -> 0% of each run, Pallas kernels for 26% -> 24%
where the time goes in v14:
time: 42.2 us; the launch traced here: 42 us
  Pallas kernels  20.7 us (49%)
  starting transfers between devices  10.9 us (26%)
  waiting for transfers between devices  9.73 us (23%)
  between operations  0.67 us (2%)
    pallas_call x2, Pallas kernels, on_device(): pl.pallas_call(functools.partial(head_kernel, dp_size, heads_size, kv_ind...  18.7 us
    ppermute x8, starting transfers between devices, swap(): lax.ppermute(values, axis, [(source, source ^ step) for source in range(s...  10.9 us
    ppermute x8, waiting for transfers between devices, swap(): lax.ppermute(values, axis, [(source, source ^ step) for source in range(s...  9.73 us
    pallas_call x1, Pallas kernels, on_device(): pl.pallas_call(functools.partial(place_kernel, heads_size, kv_local), out...  1.01 us
    pallas_call x1, Pallas kernels, on_device(): pl.pallas_call(functools.partial(cart_kernel, kv_local), out_shape=jax.Sh...  0.87 us
  transfers between devices with their start and end apart: 8, of which 2 were waited for; matrix products, arithmetic and copies ran while one was open for 0% of the time, Pallas kernels for 24%

profile of v14, /device:TPU:0, one launch (start us, length us, event | category | flops | bytes accessed | tf_op | source)
XLA Modules:
  0.0 42.0 jit_solution(8990888700667635339)
XLA Ops:
  0.6 9.7 %head_grads.2 = (f32[2,2,256,128]{3,2,1,0:T(8,128)S(1)}, bf16[2,2,256,128]{3,2,1,0:T(8,128)(2,1)S(1)}, bf16[64,1024]{1,0:T(8,128)(2,1)S(1)}, bf16[64,1024]{1,0:T...) custom-call(bf16[4096,128]{1,0:T(8,128)(2,1)} %bitcast.9, ...), custom_call_target="tpu_custom_call" | custom-call | flops 6710886400 | bytes 5242880 | tf_op jit(solution)/shard_map/head_grads/pallas_call | solution.py:364
  10.3 3.0 %collective-permute-start.1 = (bf16[64,1024]{1,0:T(8,128)(2,1)S(1)}, bf16[64,1024]{1,0:T(8,128)(2,1)S(1)}, u32[]{:S(2)}, u32[]{:S(2)}) collective-permute-start(bf16[64,1024]{1,0:T(8,128)(2,1)S(1)} %get-tuple-element.54), channel_id=1, source_target_pairs={{0,2},{1,3},{2,0},{3,1},{4,6},{5,7},{6,4},{7,5},{8,10},{9,11},{10,... | collective-permute-start | bytes 393224 | tf_op jit(solution)/shard_map/ppermute | solution.py:292
  13.3 1.6 %collective-permute-start = (bf16[2,2,256,128]{3,2,1,0:T(8,128)(2,1)S(1)}, bf16[2,2,256,128]{3,2,1,0:T(8,128)(2,1)S(1)}, u32[]{:S(2)}, u32[]{:S(2)}) collective-permute-start(bf16[2,2,256,128]{3,2,1,0:T(8,128)(2,1)S(1)} %get-tuple-element.53), channel_id=1, source_target_pairs={{0,4},{4,0},{8,12},{12,8},{1,5},{5,1},{9,13},{13,9},{2,6},{6,2},{1... | collective-permute-start | bytes 786440 | tf_op jit(solution)/shard_map/ppermute | solution.py:292
  14.9 9.1 %head_grads.3 = (f32[2,2,256,128]{3,2,1,0:T(8,128)S(1)}, bf16[2,2,256,128]{3,2,1,0:T(8,128)(2,1)S(1)}, bf16[64,2048]{1,0:T(8,128)(2,1)S(1)}, bf16[64,2048]{1,0:T...) custom-call(bf16[1280,128]{1,0:T(8,128)(2,1)S(1)} %get-tuple-element.36.refs, ...), custom_call_target="tpu_custom_call" | custom-call | flops 6710886400 | bytes 5242880 | tf_op jit(solution)/shard_map/head_grads/pallas_call | solution.py:364
  24.0 0.0 collective-permute-done.1.refs_3_
  24.0 0.0 collective-permute-done.got_ref
  24.0 0.4 %collective-permute-start.2 = (bf16[2,2,256,128]{3,2,1,0:T(8,128)(2,1)S(1)}, bf16[2,2,256,128]{3,2,1,0:T(8,128)(2,1)S(1)}, u32[]{:S(2)}, u32[]{:S(2)}) collective-permute-start(bf16[2,2,256,128]{3,2,1,0:T(8,128)(2,1)S(1)} %get-tuple-element.59), channel_id=1, source_target_pairs={{0,4},{4,0},{8,12},{12,8},{1,5},{5,1},{9,13},{13,9},{2,6},{6,2},{1... | collective-permute-start | bytes 786440 | tf_op jit(solution)/shard_map/ppermute | solution.py:292
  24.4 0.0 collective-permute-start.5
  24.4 0.3 collective-permute-start.6
  24.7 1.8 %collective-permute-start.7 = (bf16[64,1024]{1,0:T(8,128)(2,1)S(1)}, bf16[64,1024]{1,0:T(8,128)(2,1)S(1)}, u32[]{:S(2)}, u32[]{:S(2)}) collective-permute-start(bf16[64,1024]{1,0:T(8,128)(2,1)S(1)} %get-tuple-element.68), channel_id=1, source_target_pairs={{0,2},{1,3},{2,0},{3,1},{4,6},{5,7},{6,4},{7,5},{8,10},{9,11},{10,... | collective-permute-start | bytes 393224 | tf_op jit(solution)/shard_map/ppermute | solution.py:292
  26.6 2.7 %collective-permute-start.3 = (bf16[1,2,256,128]{3,2,1,0:T(8,128)(2,1)S(1)}, bf16[1,2,256,128]{3,2,1,0:T(8,128)(2,1)S(1)}, u32[]{:S(2)}, u32[]{:S(2)}) collective-permute-start(bf16[1,2,256,128]{3,2,1,0:T(8,128)(2,1)S(1)} %get-tuple-element.61), channel_id=1, source_target_pairs={{0,8},{4,12},{8,0},{12,4},{1,9},{5,13},{9,1},{13,5},{2,10},{6,14},... | collective-permute-start | bytes 393224 | tf_op jit(solution)/shard_map/ppermute | solution.py:292
  29.3 5.5 %collective-permute-done.2.got_ref = bf16[2,2,256,128]{3,2,1,0:T(8,128)(2,1)S(1)} collective-permute-done((bf16[2,2,256,128]{3,2,1,0:T(8,128)(2,1)S(1)}, bf16[2,2,256,128]{3,2,1,0:T(8,128)(2,1)S(1)}, u32[]{:S(2)}, u32[]{:S(2)}) %collective-permute-start.2) | collective-permute-done | bytes 262176 | tf_op jit(solution)/shard_map/ppermute | solution.py:292
  34.8 0.1 cart_fold.3
  34.9 1.0 %collective-permute-start.4 = (bf16[1,2,256,128]{3,2,1,0:T(8,128)(2,1)S(1)}, bf16[1,2,256,128]{3,2,1,0:T(8,128)(2,1)S(1)}, u32[]{:S(2)}, u32[]{:S(2)}) collective-permute-start(bf16[1,2,256,128]{3,2,1,0:T(8,128)(2,1)S(1)} %get-tuple-element.62), channel_id=1, source_target_pairs={{0,8},{4,12},{8,0},{12,4},{1,9},{5,13},{9,1},{13,5},{2,10},{6,14},... | collective-permute-start | bytes 393224 | tf_op jit(solution)/shard_map/ppermute | solution.py:292
  35.9 0.0 collective-permute-done.7.refs_4_
  35.9 0.0 collective-permute-done.5.refs_1_
  35.9 0.0 collective-permute-done.6.refs_2_
  35.9 1.0 %place_queries.1 = bf16[64,8192]{1,0:T(8,128)(2,1)} custom-call(bf16[64,2048]{1,0:T(8,128)(2,1)S(1)} %get-tuple-element.64.refs_0_, bf16[64,2048]{1,0:T(8,128)(2,1)S(1)} %collective-permute-done.5.refs_1_, bf16[64,2048]{1,0:T(8,128)(2,1)S(1)} %collective-permute-done.6.refs_2_, bf16[64,1024]{1,0:T(8,128)(2,1)S(1)} %collective-permute-done.1.refs_3_, ...), custom_call_target="tpu_custom_call" | custom-call | flops 1048576 | bytes 2097152 | tf_op jit(solution)/shard_map/place_queries/pallas_call | solution.py:413
  37.0 0.0 collective-permute-done.3.refs_2_
  37.0 4.2 %collective-permute-done.4.refs_3_ = bf16[1,2,256,128]{3,2,1,0:T(8,128)(2,1)S(1)} collective-permute-done((bf16[1,2,256,128]{3,2,1,0:T(8,128)(2,1)S(1)}, bf16[1,2,256,128]{3,2,1,0:T(8,128)(2,1)S(1)}, u32[]{:S(2)}, u32[]{:S(2)}) %collective-permute-start.4) | collective-permute-done | bytes 131104 | tf_op jit(solution)/shard_map/ppermute | solution.py:292
  41.2 0.9 %cart_grads.1 = f32[1024,128]{1,0:T(8,128)} custom-call(f32[1,2,256,128]{3,2,1,0:T(8,128)S(1)} %get-tuple-element.57.refs_0_, f32[1,2,256,128]{3,2,1,0:T(8,128)S(1)} %get-tuple-element.60.refs_1_, bf16[1,2,256,128]{3,2,1,0:T(8,128)(2,1)S(1)} %collective-permute-done.3.refs_2_, bf16[1,2,256,128]{3,2,1,0:T(8,128)(2,1)S(1)} %collective-permute-done.4.refs_3_), custom_call_target="tpu_custom_call" | custom-call | flops 1048576 | bytes 2097152 | tf_op jit(solution)/shard_map/cart_grads/pallas_call | solution.py:423
  (1 shorter events, 0.0 us)
Async XLA Ops:
  10.3 13.7 %collective-permute-start.1 = (bf16[64,1024]{1,0:T(8,128)(2,1)S(1)}, bf16[64,1024]{1,0:T(8,128)(2,1)S(1)}, u32[]{:S(2)}, u32[]{:S(2)}) collective-permute-start(bf16[64,1024]{1,0:T(8,128)(2,1)S(1)} %get-tuple-element.54), channel_id=1, source_target_pairs={{0,2},{1,3},{2,0},{3,1},{4,6},{5,7},{6,4},{7,5},{8,10},{9,11},{10,... | collective-permute-start | bytes 393224 | tf_op jit(solution)/shard_map/ppermute | solution.py:292
  13.3 10.7 %collective-permute-start = (bf16[2,2,256,128]{3,2,1,0:T(8,128)(2,1)S(1)}, bf16[2,2,256,128]{3,2,1,0:T(8,128)(2,1)S(1)}, u32[]{:S(2)}, u32[]{:S(2)}) collective-permute-start(bf16[2,2,256,128]{3,2,1,0:T(8,128)(2,1)S(1)} %get-tuple-element.53), channel_id=1, source_target_pairs={{0,4},{4,0},{8,12},{12,8},{1,5},{5,1},{9,13},{13,9},{2,6},{6,2},{1... | collective-permute-start | bytes 786440 | tf_op jit(solution)/shard_map/ppermute | solution.py:292
  24.0 10.9 %collective-permute-start.2 = (bf16[2,2,256,128]{3,2,1,0:T(8,128)(2,1)S(1)}, bf16[2,2,256,128]{3,2,1,0:T(8,128)(2,1)S(1)}, u32[]{:S(2)}, u32[]{:S(2)}) collective-permute-start(bf16[2,2,256,128]{3,2,1,0:T(8,128)(2,1)S(1)} %get-tuple-element.59), channel_id=1, source_target_pairs={{0,4},{4,0},{8,12},{12,8},{1,5},{5,1},{9,13},{13,9},{2,6},{6,2},{1... | collective-permute-start | bytes 786440 | tf_op jit(solution)/shard_map/ppermute | solution.py:292
  24.4 11.5 %collective-permute-start.5 = (bf16[64,2048]{1,0:T(8,128)(2,1)S(1)}, bf16[64,2048]{1,0:T(8,128)(2,1)S(1)}, u32[]{:S(2)}, u32[]{:S(2)}) collective-permute-start(bf16[64,2048]{1,0:T(8,128)(2,1)S(1)} %get-tuple-element.65), channel_id=1, source_target_pairs={{0,1},{1,0},{2,3},{3,2},{4,5},{5,4},{6,7},{7,6},{8,9},{9,8},{10,11... | collective-permute-start | bytes 786440 | tf_op jit(solution)/shard_map/ppermute | solution.py:292
  24.4 11.5 %collective-permute-start.6 = (bf16[64,2048]{1,0:T(8,128)(2,1)S(1)}, bf16[64,2048]{1,0:T(8,128)(2,1)S(1)}, u32[]{:S(2)}, u32[]{:S(2)}) collective-permute-start(bf16[64,2048]{1,0:T(8,128)(2,1)S(1)} %get-tuple-element.66), channel_id=1, source_target_pairs={{0,3},{1,2},{2,1},{3,0},{4,7},{5,6},{6,5},{7,4},{8,11},{9,10},{10,... | collective-permute-start | bytes 786440 | tf_op jit(solution)/shard_map/ppermute | solution.py:292
  24.7 11.2 %collective-permute-start.7 = (bf16[64,1024]{1,0:T(8,128)(2,1)S(1)}, bf16[64,1024]{1,0:T(8,128)(2,1)S(1)}, u32[]{:S(2)}, u32[]{:S(2)}) collective-permute-start(bf16[64,1024]{1,0:T(8,128)(2,1)S(1)} %get-tuple-element.68), channel_id=1, source_target_pairs={{0,2},{1,3},{2,0},{3,1},{4,6},{5,7},{6,4},{7,5},{8,10},{9,11},{10,... | collective-permute-start | bytes 393224 | tf_op jit(solution)/shard_map/ppermute | solution.py:292
  26.6 10.4 %collective-permute-start.3 = (bf16[1,2,256,128]{3,2,1,0:T(8,128)(2,1)S(1)}, bf16[1,2,256,128]{3,2,1,0:T(8,128)(2,1)S(1)}, u32[]{:S(2)}, u32[]{:S(2)}) collective-permute-start(bf16[1,2,256,128]{3,2,1,0:T(8,128)(2,1)S(1)} %get-tuple-element.61), channel_id=1, source_target_pairs={{0,8},{4,12},{8,0},{12,4},{1,9},{5,13},{9,1},{13,5},{2,10},{6,14},... | collective-permute-start | bytes 393224 | tf_op jit(solution)/shard_map/ppermute | solution.py:292
  34.9 6.3 %collective-permute-start.4 = (bf16[1,2,256,128]{3,2,1,0:T(8,128)(2,1)S(1)}, bf16[1,2,256,128]{3,2,1,0:T(8,128)(2,1)S(1)}, u32[]{:S(2)}, u32[]{:S(2)}) collective-permute-start(bf16[1,2,256,128]{3,2,1,0:T(8,128)(2,1)S(1)} %get-tuple-element.62), channel_id=1, source_target_pairs={{0,8},{4,12},{8,0},{12,4},{1,9},{5,13},{9,1},{13,5},{2,10},{6,14},... | collective-permute-start | bytes 393224 | tf_op jit(solution)/shard_map/ppermute | solution.py:292

commit v15 on v14

--- a/solution.py
+++ b/solution.py
@@ -11,7 +11,7 @@
 masked_score = -1e30
 vmem_bytes = 46 * 1024 * 1024
 small_vmem_bytes = 8 * 1024 * 1024
-early_steps = (2,)
+early_steps = ()
 f32 = jnp.float32
 bf16 = jnp.bfloat16
 
@@ -223,11 +223,12 @@
 
     part_rows = cart_rows // dp_size
     me = lax.axis_index("dp")
-    for step in range(dp_size):
-        at = pl.ds(pl.multiple_of((me ^ step) * part_rows, part_rows), part_rows)
-        ref = send_ref if step % 2 else keep_ref
-        ref[step // 2, 0] = (dk_ref[at, :] * scale).astype(ref.dtype)
-        ref[step // 2, 1] = dv_ref[at, :].astype(ref.dtype)
+    half = dp_size // 2
+    for index, share in enumerate(share_order(dp_size, last)):
+        at = pl.ds(pl.multiple_of((me ^ share) * part_rows, part_rows), part_rows)
+        ref = send_ref if index >= half else keep_ref
+        ref[index % half, 0] = (dk_ref[at, :] * scale).astype(ref.dtype)
+        ref[index % half, 1] = dv_ref[at, :].astype(ref.dtype)
     own = dk_ref[cart_rows:all_keys, :] * scale, dv_ref[cart_rows:all_keys, :]
     own_tokens = tokens // heads_size
     columns = width * head_dim
@@ -253,10 +254,11 @@
 
 
 def fold_kernel(part_ref, got_ref, keep_ref, send_ref):
-    for index in range(part_ref.shape[0]):
+    half = keep_ref.shape[0]
+    for index in range(2 * half):
         total = part_ref[index] + got_ref[index].astype(f32)
-        ref = send_ref if index % 2 else keep_ref
-        ref[index // 2] = total.astype(ref.dtype)
+        ref = send_ref if index >= half else keep_ref
+        ref[index % half] = total.astype(ref.dtype)
 
 
 def cart_kernel(kv_local, *refs):
@@ -308,7 +310,20 @@
 
 def split_steps(heads_size):
     early = [step for step in range(heads_size) if step in early_steps]
-    return [step for step in range(heads_size) if step not in early], early
+    late = [0, *range(2, heads_size), 1]
+    return [step for step in late if step < heads_size and step not in early], early
+
+
+def swap_order(dp_size, last):
+    bits = [1 << bit for bit in range(dp_size.bit_length() - 1)]
+    return bits if last else bits[::-1]
+
+
+def share_order(dp_size, last):
+    shares = [0]
+    for bit in reversed(swap_order(dp_size, last)):
+        shares = shares + [share ^ bit for share in shares]
+    return shares
 
 
 def on_device(dp_size, heads_size, queries, out_grad, self_keys, self_values, cart_keys, cart_values, segment_ids):
@@ -393,21 +408,21 @@
         outs = outs[: len(outs) - len(next_shapes)]
         part, send, near, far = outs[0], outs[1], outs[2 : 2 + kept], outs[2 + kept : -1]
         if last:
-            part, send, near, far, received = lax.optimization_barrier((part, send, near, far, received))
+            held_back, received = lax.optimization_barrier((near[-1], received))
+            near = [*near[:-1], held_back]
         else:
             kept_list += near
             self_list.append(outs[-1])
-        received.append((part, swap(send, "dp", dp_size, 1)))
+        received.append((part, swap(send, "dp", dp_size, swap_order(dp_size, last)[0])))
         far_parts = [swap(block, "heads", heads_size, step) for step, block in zip(far_steps, far)]
         if not last:
             received[-1] += tuple(far_parts)
     far_list = [block for _, _, *blocks_far in received for block in blocks_far]
-    for part, got, *_ in received:
-        step = 2
-        while step < dp_size:
+    cart_list = []
+    for index, (part, got, *_) in enumerate(received):
+        for step in swap_order(dp_size, index == kv_local - 1)[1:]:
             part, send = fold(part, got)
             got = swap(send, "dp", dp_size, step)
-            step *= 2
         cart_list.append((part, got))
     query_list = [swap(block, "heads", heads_size, step) for step, block in zip(near_steps, near)] + far_list + far_parts
     query_grads = pl.pallas_call(

time: 42.2 us -> 43.2 us (1.024)
  starting transfers between devices: 10.9 us -> 12.1 us
    ppermute x8 -> x7, starting transfers between devices: 10.9 us -> 12.1 us  [swap(): lax.ppermute(values, axis, [(source, source ^ step) for source in range(s...]
    ppermute x8 -> x7, waiting for transfers between devices: 9.73 us -> 9.52 us  [swap(): lax.ppermute(values, axis, [(source, source ^ step) for source in range(s...]
  transfers between devices with their start and end apart: 8 -> 7, of which waited for: 2 -> 3; matrix products, arithmetic and copies ran while one was open for 0% -> 0% of each run, Pallas kernels for 24% -> 23%
where the time goes in v15:
time: 43.2 us; the launch traced here: 43.1 us
  Pallas kernels  20.7 us (48%)
  starting transfers between devices  12.1 us (28%)
  waiting for transfers between devices  9.52 us (22%)
  between operations  0.82 us (2%)
    pallas_call x2, Pallas kernels, on_device(): pl.pallas_call(functools.partial(head_kernel, dp_size, heads_size, kv_ind...  18.7 us
    ppermute x7, starting transfers between devices, swap(): lax.ppermute(values, axis, [(source, source ^ step) for source in range(s...  12.1 us
    ppermute x7, waiting for transfers between devices, swap(): lax.ppermute(values, axis, [(source, source ^ step) for source in range(s...  9.52 us
    pallas_call x1, Pallas kernels, on_device(): pl.pallas_call(functools.partial(place_kernel, heads_size, kv_local), out...  1 us
    pallas_call x1, Pallas kernels, on_device(): pl.pallas_call(functools.partial(cart_kernel, kv_local), out_shape=jax.Sh...  0.87 us
  transfers between devices with their start and end apart: 7, of which 3 were waited for; matrix products, arithmetic and copies ran while one was open for 0% of the time, Pallas kernels for 23%

profile of v15, /device:TPU:0, one launch (start us, length us, event | category | flops | bytes accessed | tf_op | source)
XLA Modules:
  0.0 43.1 jit_solution(11864255756863006399)
XLA Ops:
  0.6 9.6 %head_grads.2 = (f32[2,2,256,128]{3,2,1,0:T(8,128)S(1)}, bf16[2,2,256,128]{3,2,1,0:T(8,128)(2,1)S(1)}, bf16[64,1024]{1,0:T(8,128)(2,1)S(1)}, bf16[64,1024]{1,0:T...) custom-call(bf16[4096,128]{1,0:T(8,128)(2,1)} %bitcast.9, ...), custom_call_target="tpu_custom_call" | custom-call | flops 6710886400 | bytes 5242880 | tf_op jit(solution)/shard_map/head_grads/pallas_call | solution.py:379
  10.3 4.1 %collective-permute-start = (bf16[2,2,256,128]{3,2,1,0:T(8,128)(2,1)S(1)}, bf16[2,2,256,128]{3,2,1,0:T(8,128)(2,1)S(1)}, u32[]{:S(2)}, u32[]{:S(2)}) collective-permute-start(bf16[2,2,256,128]{3,2,1,0:T(8,128)(2,1)S(1)} %get-tuple-element.43), channel_id=1, source_target_pairs={{0,8},{4,12},{8,0},{12,4},{1,9},{5,13},{9,1},{13,5},{2,10},{6,14},... | collective-permute-start | bytes 786440 | tf_op jit(solution)/shard_map/ppermute | solution.py:294
  14.4 9.1 %head_grads.3 = (f32[2,2,256,128]{3,2,1,0:T(8,128)S(1)}, bf16[2,2,256,128]{3,2,1,0:T(8,128)(2,1)S(1)}, bf16[64,2048]{1,0:T(8,128)(2,1)S(1)}, bf16[64,2048]{1,0:T...) custom-call(bf16[1280,128]{1,0:T(8,128)(2,1)S(1)} %get-tuple-element.30.refs, ...), custom_call_target="tpu_custom_call" | custom-call | flops 6710886400 | bytes 5242880 | tf_op jit(solution)/shard_map/head_grads/pallas_call | solution.py:379
  23.5 1.6 %collective-permute-start.1 = (bf16[2,2,256,128]{3,2,1,0:T(8,128)(2,1)S(1)}, bf16[2,2,256,128]{3,2,1,0:T(8,128)(2,1)S(1)}, u32[]{:S(2)}, u32[]{:S(2)}) collective-permute-start(bf16[2,2,256,128]{3,2,1,0:T(8,128)(2,1)S(1)} %get-tuple-element.48), channel_id=1, source_target_pairs={{0,4},{4,0},{8,12},{12,8},{1,5},{5,1},{9,13},{13,9},{2,6},{6,2},{1... | collective-permute-start | bytes 786440 | tf_op jit(solution)/shard_map/ppermute | solution.py:294
  25.0 1.5 %collective-permute-start.4 = (bf16[64,2048]{1,0:T(8,128)(2,1)S(1)}, bf16[64,2048]{1,0:T(8,128)(2,1)S(1)}, u32[]{:S(2)}, u32[]{:S(2)}) collective-permute-start(bf16[64,2048]{1,0:T(8,128)(2,1)S(1)} %get-tuple-element.54), channel_id=1, source_target_pairs={{0,2},{1,3},{2,0},{3,1},{4,6},{5,7},{6,4},{7,5},{8,10},{9,11},{10,... | collective-permute-start | bytes 786440 | tf_op jit(solution)/shard_map/ppermute | solution.py:294
  26.5 0.0 collective-permute-start.5
  26.5 0.0 collective-permute-done.got_ref
  26.5 0.7 %collective-permute-start.6 = (bf16[64,2048]{1,0:T(8,128)(2,1)S(1)}, bf16[64,2048]{1,0:T(8,128)(2,1)S(1)}, u32[]{:S(2)}, u32[]{:S(2)}) collective-permute-start(bf16[64,2048]{1,0:T(8,128)(2,1)S(1)} %get-tuple-element.56), channel_id=1, source_target_pairs={{0,1},{1,0},{2,3},{3,2},{4,5},{5,4},{6,7},{7,6},{8,9},{9,8},{10,11... | collective-permute-start | bytes 786440 | tf_op jit(solution)/shard_map/ppermute | solution.py:294
  27.2 4.7 %collective-permute-done.1.got_ref = bf16[2,2,256,128]{3,2,1,0:T(8,128)(2,1)S(1)} collective-permute-done((bf16[2,2,256,128]{3,2,1,0:T(8,128)(2,1)S(1)}, bf16[2,2,256,128]{3,2,1,0:T(8,128)(2,1)S(1)}, u32[]{:S(2)}, u32[]{:S(2)}) %collective-permute-start.1) | collective-permute-done | bytes 262176 | tf_op jit(solution)/shard_map/ppermute | solution.py:294
  31.9 0.1 cart_fold.3
  32.0 1.7 %collective-permute-start.3 = (bf16[1,2,256,128]{3,2,1,0:T(8,128)(2,1)S(1)}, bf16[1,2,256,128]{3,2,1,0:T(8,128)(2,1)S(1)}, u32[]{:S(2)}, u32[]{:S(2)}) collective-permute-start(bf16[1,2,256,128]{3,2,1,0:T(8,128)(2,1)S(1)} %get-tuple-element.51), channel_id=1, source_target_pairs={{0,8},{4,12},{8,0},{12,4},{1,9},{5,13},{9,1},{13,5},{2,10},{6,14},... | collective-permute-start | bytes 393224 | tf_op jit(solution)/shard_map/ppermute | solution.py:294
  33.7 2.5 %collective-permute-start.2 = (bf16[1,2,256,128]{3,2,1,0:T(8,128)(2,1)S(1)}, bf16[1,2,256,128]{3,2,1,0:T(8,128)(2,1)S(1)}, u32[]{:S(2)}, u32[]{:S(2)}) collective-permute-start(bf16[1,2,256,128]{3,2,1,0:T(8,128)(2,1)S(1)} %get-tuple-element.50), channel_id=1, source_target_pairs={{0,4},{4,0},{8,12},{12,8},{1,5},{5,1},{9,13},{13,9},{2,6},{6,2},{1... | collective-permute-start | bytes 393224 | tf_op jit(solution)/shard_map/ppermute | solution.py:294
  36.3 4.5 %collective-permute-done.3.refs_3_ = bf16[1,2,256,128]{3,2,1,0:T(8,128)(2,1)S(1)} collective-permute-done((bf16[1,2,256,128]{3,2,1,0:T(8,128)(2,1)S(1)}, bf16[1,2,256,128]{3,2,1,0:T(8,128)(2,1)S(1)}, u32[]{:S(2)}, u32[]{:S(2)}) %collective-permute-start.3) | collective-permute-done | bytes 131104 | tf_op jit(solution)/shard_map/ppermute | solution.py:294
  40.8 0.3 collective-permute-done.2.refs_2_
  41.0 0.9 %cart_grads.1 = f32[1024,128]{1,0:T(8,128)} custom-call(f32[1,2,256,128]{3,2,1,0:T(8,128)S(1)} %get-tuple-element.46.refs_0_, f32[1,2,256,128]{3,2,1,0:T(8,128)S(1)} %get-tuple-element.49.refs_1_, bf16[1,2,256,128]{3,2,1,0:T(8,128)(2,1)S(1)} %collective-permute-done.2.refs_2_, bf16[1,2,256,128]{3,2,1,0:T(8,128)(2,1)S(1)} %collective-permute-done.3.refs_3_), custom_call_target="tpu_custom_call" | custom-call | flops 1048576 | bytes 2097152 | tf_op jit(solution)/shard_map/cart_grads/pallas_call | solution.py:438
  41.9 0.0 collective-permute-done.4.refs_1_
  41.9 0.0 collective-permute-done.5.refs_2_
  41.9 0.0 collective-permute-done.6.refs_3_
  41.9 1.0 %place_queries.1 = bf16[64,8192]{1,0:T(8,128)(2,1)} custom-call(bf16[64,2048]{1,0:T(8,128)(2,1)S(1)} %get-tuple-element.53.refs_0_, bf16[64,2048]{1,0:T(8,128)(2,1)S(1)} %collective-permute-done.4.refs_1_, bf16[64,2048]{1,0:T(8,128)(2,1)S(1)} %collective-permute-done.5.refs_2_, bf16[64,2048]{1,0:T(8,128)(2,1)S(1)} %collective-permute-done.6.refs_3_), custom_call_target="tpu_custom_call" | custom-call | flops 1048576 | bytes 2097152 | tf_op jit(solution)/shard_map/place_queries/pallas_call | solution.py:428
  (1 shorter events, 0.0 us)
Async XLA Ops:
  10.3 16.3 %collective-permute-start = (bf16[2,2,256,128]{3,2,1,0:T(8,128)(2,1)S(1)}, bf16[2,2,256,128]{3,2,1,0:T(8,128)(2,1)S(1)}, u32[]{:S(2)}, u32[]{:S(2)}) collective-permute-start(bf16[2,2,256,128]{3,2,1,0:T(8,128)(2,1)S(1)} %get-tuple-element.43), channel_id=1, source_target_pairs={{0,8},{4,12},{8,0},{12,4},{1,9},{5,13},{9,1},{13,5},{2,10},{6,14},... | collective-permute-start | bytes 786440 | tf_op jit(solution)/shard_map/ppermute | solution.py:294
  23.5 8.5 %collective-permute-start.1 = (bf16[2,2,256,128]{3,2,1,0:T(8,128)(2,1)S(1)}, bf16[2,2,256,128]{3,2,1,0:T(8,128)(2,1)S(1)}, u32[]{:S(2)}, u32[]{:S(2)}) collective-permute-start(bf16[2,2,256,128]{3,2,1,0:T(8,128)(2,1)S(1)} %get-tuple-element.48), channel_id=1, source_target_pairs={{0,4},{4,0},{8,12},{12,8},{1,5},{5,1},{9,13},{13,9},{2,6},{6,2},{1... | collective-permute-start | bytes 786440 | tf_op jit(solution)/shard_map/ppermute | solution.py:294
  25.0 16.9 %collective-permute-start.4 = (bf16[64,2048]{1,0:T(8,128)(2,1)S(1)}, bf16[64,2048]{1,0:T(8,128)(2,1)S(1)}, u32[]{:S(2)}, u32[]{:S(2)}) collective-permute-start(bf16[64,2048]{1,0:T(8,128)(2,1)S(1)} %get-tuple-element.54), channel_id=1, source_target_pairs={{0,2},{1,3},{2,0},{3,1},{4,6},{5,7},{6,4},{7,5},{8,10},{9,11},{10,... | collective-permute-start | bytes 786440 | tf_op jit(solution)/shard_map/ppermute | solution.py:294
  26.5 15.4 %collective-permute-start.5 = (bf16[64,2048]{1,0:T(8,128)(2,1)S(1)}, bf16[64,2048]{1,0:T(8,128)(2,1)S(1)}, u32[]{:S(2)}, u32[]{:S(2)}) collective-permute-start(bf16[64,2048]{1,0:T(8,128)(2,1)S(1)} %get-tuple-element.55), channel_id=1, source_target_pairs={{0,3},{1,2},{2,1},{3,0},{4,7},{5,6},{6,5},{7,4},{8,11},{9,10},{10,... | collective-permute-start | bytes 786440 | tf_op jit(solution)/shard_map/ppermute | solution.py:294
  26.5 15.4 %collective-permute-start.6 = (bf16[64,2048]{1,0:T(8,128)(2,1)S(1)}, bf16[64,2048]{1,0:T(8,128)(2,1)S(1)}, u32[]{:S(2)}, u32[]{:S(2)}) collective-permute-start(bf16[64,2048]{1,0:T(8,128)(2,1)S(1)} %get-tuple-element.56), channel_id=1, source_target_pairs={{0,1},{1,0},{2,3},{3,2},{4,5},{5,4},{6,7},{7,6},{8,9},{9,8},{10,11... | collective-permute-start | bytes 786440 | tf_op jit(solution)/shard_map/ppermute | solution.py:294
  32.0 8.8 %collective-permute-start.3 = (bf16[1,2,256,128]{3,2,1,0:T(8,128)(2,1)S(1)}, bf16[1,2,256,128]{3,2,1,0:T(8,128)(2,1)S(1)}, u32[]{:S(2)}, u32[]{:S(2)}) collective-permute-start(bf16[1,2,256,128]{3,2,1,0:T(8,128)(2,1)S(1)} %get-tuple-element.51), channel_id=1, source_target_pairs={{0,8},{4,12},{8,0},{12,4},{1,9},{5,13},{9,1},{13,5},{2,10},{6,14},... | collective-permute-start | bytes 393224 | tf_op jit(solution)/shard_map/ppermute | solution.py:294
  33.7 7.3 %collective-permute-start.2 = (bf16[1,2,256,128]{3,2,1,0:T(8,128)(2,1)S(1)}, bf16[1,2,256,128]{3,2,1,0:T(8,128)(2,1)S(1)}, u32[]{:S(2)}, u32[]{:S(2)}) collective-permute-start(bf16[1,2,256,128]{3,2,1,0:T(8,128)(2,1)S(1)} %get-tuple-element.50), channel_id=1, source_target_pairs={{0,4},{4,0},{8,12},{12,8},{1,5},{5,1},{9,13},{13,9},{2,6},{6,2},{1... | collective-permute-start | bytes 393224 | tf_op jit(solution)/shard_map/ppermute | solution.py:294

commit v16 on v14

--- a/solution.py
+++ b/solution.py
@@ -11,7 +11,7 @@
 masked_score = -1e30
 vmem_bytes = 46 * 1024 * 1024
 small_vmem_bytes = 8 * 1024 * 1024
-early_steps = (2,)
+early_steps = ()
 f32 = jnp.float32
 bf16 = jnp.bfloat16
 
@@ -308,7 +308,8 @@
 
 def split_steps(heads_size):
     early = [step for step in range(heads_size) if step in early_steps]
-    return [step for step in range(heads_size) if step not in early], early
+    late = [0, *range(2, heads_size), 1]
+    return [step for step in late if step < heads_size and step not in early], early
 
 
 def on_device(dp_size, heads_size, queries, out_grad, self_keys, self_values, cart_keys, cart_values, segment_ids):

time: 42.2 us -> 41.7 us (0.988)
  starting transfers between devices: 10.9 us -> 9.68 us
  waiting for transfers between devices: 9.73 us -> 10.5 us
    ppermute x8 -> x7, starting transfers between devices: 10.9 us -> 9.68 us  [swap(): lax.ppermute(values, axis, [(source, source ^ step) for source in range(s...]
    ppermute x8 -> x7, waiting for transfers between devices: 9.73 us -> 10.5 us  [swap(): lax.ppermute(values, axis, [(source, source ^ step) for source in range(s...]
  transfers between devices with their start and end apart: 8 -> 7, of which waited for: 2 -> 3; matrix products, arithmetic and copies ran while one was open for 0% -> 0% of each run, Pallas kernels for 24% -> 25%
where the time goes in v16:
time: 41.7 us; the launch traced here: 41.5 us
  Pallas kernels  20.7 us (50%)
  waiting for transfers between devices  10.5 us (25%)
  starting transfers between devices  9.68 us (23%)
  between operations  0.67 us (2%)
    pallas_call x2, Pallas kernels, on_device(): pl.pallas_call(functools.partial(head_kernel, dp_size, heads_size, kv_ind...  18.7 us
    ppermute x7, waiting for transfers between devices, swap(): lax.ppermute(values, axis, [(source, source ^ step) for source in range(s...  10.5 us
    ppermute x7, starting transfers between devices, swap(): lax.ppermute(values, axis, [(source, source ^ step) for source in range(s...  9.68 us
    pallas_call x1, Pallas kernels, on_device(): pl.pallas_call(functools.partial(place_kernel, heads_size, kv_local), out...  0.99 us
    pallas_call x1, Pallas kernels, on_device(): pl.pallas_call(functools.partial(cart_kernel, kv_local), out_shape=jax.Sh...  0.87 us
  transfers between devices with their start and end apart: 7, of which 3 were waited for; matrix products, arithmetic and copies ran while one was open for 0% of the time, Pallas kernels for 25%

profile of v16, /device:TPU:0, one launch (start us, length us, event | category | flops | bytes accessed | tf_op | source)
XLA Modules:
  0.0 41.5 jit_solution(4713433102369830605)
XLA Ops:
  0.6 9.7 %head_grads.2 = (f32[2,2,256,128]{3,2,1,0:T(8,128)S(1)}, bf16[2,2,256,128]{3,2,1,0:T(8,128)(2,1)S(1)}, bf16[64,1024]{1,0:T(8,128)(2,1)S(1)}, bf16[64,1024]{1,0:T...) custom-call(bf16[4096,128]{1,0:T(8,128)(2,1)} %bitcast.9, ...), custom_call_target="tpu_custom_call" | custom-call | flops 6710886400 | bytes 5242880 | tf_op jit(solution)/shard_map/head_grads/pallas_call | solution.py:365
  10.3 3.1 %collective-permute-start = (bf16[2,2,256,128]{3,2,1,0:T(8,128)(2,1)S(1)}, bf16[2,2,256,128]{3,2,1,0:T(8,128)(2,1)S(1)}, u32[]{:S(2)}, u32[]{:S(2)}) collective-permute-start(bf16[2,2,256,128]{3,2,1,0:T(8,128)(2,1)S(1)} %get-tuple-element.53), channel_id=1, source_target_pairs={{0,4},{4,0},{8,12},{12,8},{1,5},{5,1},{9,13},{13,9},{2,6},{6,2},{1... | collective-permute-start | bytes 786440 | tf_op jit(solution)/shard_map/ppermute | solution.py:292
  13.4 9.1 %head_grads.3 = (f32[2,2,256,128]{3,2,1,0:T(8,128)S(1)}, bf16[2,2,256,128]{3,2,1,0:T(8,128)(2,1)S(1)}, bf16[64,2048]{1,0:T(8,128)(2,1)S(1)}, bf16[64,2048]{1,0:T...) custom-call(bf16[1280,128]{1,0:T(8,128)(2,1)S(1)} %get-tuple-element.35.refs, ...), custom_call_target="tpu_custom_call" | custom-call | flops 6710886400 | bytes 5242880 | tf_op jit(solution)/shard_map/head_grads/pallas_call | solution.py:365
  22.5 0.0 collective-permute-done.got_ref
  22.5 0.0 collective-permute-start.1
  22.5 1.9 %collective-permute-start.4 = (bf16[64,2048]{1,0:T(8,128)(2,1)S(1)}, bf16[64,2048]{1,0:T(8,128)(2,1)S(1)}, u32[]{:S(2)}, u32[]{:S(2)}) collective-permute-start(bf16[64,2048]{1,0:T(8,128)(2,1)S(1)} %get-tuple-element.64), channel_id=1, source_target_pairs={{0,2},{1,3},{2,0},{3,1},{4,6},{5,7},{6,4},{7,5},{8,10},{9,11},{10,... | collective-permute-start | bytes 786440 | tf_op jit(solution)/shard_map/ppermute | solution.py:292
  24.4 0.0 collective-permute-start.5
  24.4 0.2 collective-permute-start.6
  24.7 3.1 %collective-permute-start.2 = (bf16[1,2,256,128]{3,2,1,0:T(8,128)(2,1)S(1)}, bf16[1,2,256,128]{3,2,1,0:T(8,128)(2,1)S(1)}, u32[]{:S(2)}, u32[]{:S(2)}) collective-permute-start(bf16[1,2,256,128]{3,2,1,0:T(8,128)(2,1)S(1)} %get-tuple-element.60), channel_id=1, source_target_pairs={{0,8},{4,12},{8,0},{12,4},{1,9},{5,13},{9,1},{13,5},{2,10},{6,14},... | collective-permute-start | bytes 393224 | tf_op jit(solution)/shard_map/ppermute | solution.py:292
  27.8 5.3 %collective-permute-done.1.got_ref = bf16[2,2,256,128]{3,2,1,0:T(8,128)(2,1)S(1)} collective-permute-done((bf16[2,2,256,128]{3,2,1,0:T(8,128)(2,1)S(1)}, bf16[2,2,256,128]{3,2,1,0:T(8,128)(2,1)S(1)}, u32[]{:S(2)}, u32[]{:S(2)}) %collective-permute-start.1) | collective-permute-done | bytes 262176 | tf_op jit(solution)/shard_map/ppermute | solution.py:292
  33.0 0.1 cart_fold.3
  33.1 1.3 %collective-permute-start.3 = (bf16[1,2,256,128]{3,2,1,0:T(8,128)(2,1)S(1)}, bf16[1,2,256,128]{3,2,1,0:T(8,128)(2,1)S(1)}, u32[]{:S(2)}, u32[]{:S(2)}) collective-permute-start(bf16[1,2,256,128]{3,2,1,0:T(8,128)(2,1)S(1)} %get-tuple-element.61), channel_id=1, source_target_pairs={{0,8},{4,12},{8,0},{12,4},{1,9},{5,13},{9,1},{13,5},{2,10},{6,14},... | collective-permute-start | bytes 393224 | tf_op jit(solution)/shard_map/ppermute | solution.py:292
  34.4 0.0 collective-permute-done.4.refs_1_
  34.4 0.6 %collective-permute-done.5.refs_2_ = bf16[64,2048]{1,0:T(8,128)(2,1)S(1)} collective-permute-done((bf16[64,2048]{1,0:T(8,128)(2,1)S(1)}, bf16[64,2048]{1,0:T(8,128)(2,1)S(1)}, u32[]{:S(2)}, u32[]{:S(2)}) %collective-permute-start.5) | collective-permute-done | bytes 262176 | tf_op jit(solution)/shard_map/ppermute | solution.py:292
  35.0 0.0 collective-permute-done.6.refs_3_
  35.0 1.0 %place_queries.1 = bf16[64,8192]{1,0:T(8,128)(2,1)} custom-call(bf16[64,2048]{1,0:T(8,128)(2,1)S(1)} %get-tuple-element.63.refs_0_, bf16[64,2048]{1,0:T(8,128)(2,1)S(1)} %collective-permute-done.4.refs_1_, bf16[64,2048]{1,0:T(8,128)(2,1)S(1)} %collective-permute-done.5.refs_2_, bf16[64,2048]{1,0:T(8,128)(2,1)S(1)} %collective-permute-done.6.refs_3_), custom_call_target="tpu_custom_call" | custom-call | flops 1048576 | bytes 2097152 | tf_op jit(solution)/shard_map/place_queries/pallas_call | solution.py:414
  36.0 0.0 collective-permute-done.2.refs_2_
  36.1 4.6 %collective-permute-done.3.refs_3_ = bf16[1,2,256,128]{3,2,1,0:T(8,128)(2,1)S(1)} collective-permute-done((bf16[1,2,256,128]{3,2,1,0:T(8,128)(2,1)S(1)}, bf16[1,2,256,128]{3,2,1,0:T(8,128)(2,1)S(1)}, u32[]{:S(2)}, u32[]{:S(2)}) %collective-permute-start.3) | collective-permute-done | bytes 131104 | tf_op jit(solution)/shard_map/ppermute | solution.py:292
  40.7 0.9 %cart_grads.1 = f32[1024,128]{1,0:T(8,128)} custom-call(f32[1,2,256,128]{3,2,1,0:T(8,128)S(1)} %get-tuple-element.56.refs_0_, f32[1,2,256,128]{3,2,1,0:T(8,128)S(1)} %get-tuple-element.59.refs_1_, bf16[1,2,256,128]{3,2,1,0:T(8,128)(2,1)S(1)} %collective-permute-done.2.refs_2_, bf16[1,2,256,128]{3,2,1,0:T(8,128)(2,1)S(1)} %collective-permute-done.3.refs_3_), custom_call_target="tpu_custom_call" | custom-call | flops 1048576 | bytes 2097152 | tf_op jit(solution)/shard_map/cart_grads/pallas_call | solution.py:424
  (1 shorter events, 0.0 us)
Async XLA Ops:
  10.3 12.2 %collective-permute-start = (bf16[2,2,256,128]{3,2,1,0:T(8,128)(2,1)S(1)}, bf16[2,2,256,128]{3,2,1,0:T(8,128)(2,1)S(1)}, u32[]{:S(2)}, u32[]{:S(2)}) collective-permute-start(bf16[2,2,256,128]{3,2,1,0:T(8,128)(2,1)S(1)} %get-tuple-element.53), channel_id=1, source_target_pairs={{0,4},{4,0},{8,12},{12,8},{1,5},{5,1},{9,13},{13,9},{2,6},{6,2},{1... | collective-permute-start | bytes 786440 | tf_op jit(solution)/shard_map/ppermute | solution.py:292
  22.5 10.6 %collective-permute-start.1 = (bf16[2,2,256,128]{3,2,1,0:T(8,128)(2,1)S(1)}, bf16[2,2,256,128]{3,2,1,0:T(8,128)(2,1)S(1)}, u32[]{:S(2)}, u32[]{:S(2)}) collective-permute-start(bf16[2,2,256,128]{3,2,1,0:T(8,128)(2,1)S(1)} %get-tuple-element.58), channel_id=1, source_target_pairs={{0,4},{4,0},{8,12},{12,8},{1,5},{5,1},{9,13},{13,9},{2,6},{6,2},{1... | collective-permute-start | bytes 786440 | tf_op jit(solution)/shard_map/ppermute | solution.py:292
  22.5 11.9 %collective-permute-start.4 = (bf16[64,2048]{1,0:T(8,128)(2,1)S(1)}, bf16[64,2048]{1,0:T(8,128)(2,1)S(1)}, u32[]{:S(2)}, u32[]{:S(2)}) collective-permute-start(bf16[64,2048]{1,0:T(8,128)(2,1)S(1)} %get-tuple-element.64), channel_id=1, source_target_pairs={{0,2},{1,3},{2,0},{3,1},{4,6},{5,7},{6,4},{7,5},{8,10},{9,11},{10,... | collective-permute-start | bytes 786440 | tf_op jit(solution)/shard_map/ppermute | solution.py:292
  24.4 10.7 %collective-permute-start.5 = (bf16[64,2048]{1,0:T(8,128)(2,1)S(1)}, bf16[64,2048]{1,0:T(8,128)(2,1)S(1)}, u32[]{:S(2)}, u32[]{:S(2)}) collective-permute-start(bf16[64,2048]{1,0:T(8,128)(2,1)S(1)} %get-tuple-element.65), channel_id=1, source_target_pairs={{0,3},{1,2},{2,1},{3,0},{4,7},{5,6},{6,5},{7,4},{8,11},{9,10},{10,... | collective-permute-start | bytes 786440 | tf_op jit(solution)/shard_map/ppermute | solution.py:292
  24.4 10.7 %collective-permute-start.6 = (bf16[64,2048]{1,0:T(8,128)(2,1)S(1)}, bf16[64,2048]{1,0:T(8,128)(2,1)S(1)}, u32[]{:S(2)}, u32[]{:S(2)}) collective-permute-start(bf16[64,2048]{1,0:T(8,128)(2,1)S(1)} %get-tuple-element.66), channel_id=1, source_target_pairs={{0,1},{1,0},{2,3},{3,2},{4,5},{5,4},{6,7},{7,6},{8,9},{9,8},{10,11... | collective-permute-start | bytes 786440 | tf_op jit(solution)/shard_map/ppermute | solution.py:292
  24.7 11.4 %collective-permute-start.2 = (bf16[1,2,256,128]{3,2,1,0:T(8,128)(2,1)S(1)}, bf16[1,2,256,128]{3,2,1,0:T(8,128)(2,1)S(1)}, u32[]{:S(2)}, u32[]{:S(2)}) collective-permute-start(bf16[1,2,256,128]{3,2,1,0:T(8,128)(2,1)S(1)} %get-tuple-element.60), channel_id=1, source_target_pairs={{0,8},{4,12},{8,0},{12,4},{1,9},{5,13},{9,1},{13,5},{2,10},{6,14},... | collective-permute-start | bytes 393224 | tf_op jit(solution)/shard_map/ppermute | solution.py:292
  33.1 7.6 %collective-permute-start.3 = (bf16[1,2,256,128]{3,2,1,0:T(8,128)(2,1)S(1)}, bf16[1,2,256,128]{3,2,1,0:T(8,128)(2,1)S(1)}, u32[]{:S(2)}, u32[]{:S(2)}) collective-permute-start(bf16[1,2,256,128]{3,2,1,0:T(8,128)(2,1)S(1)} %get-tuple-element.61), channel_id=1, source_target_pairs={{0,8},{4,12},{8,0},{12,4},{1,9},{5,13},{9,1},{13,5},{2,10},{6,14},... | collective-permute-start | bytes 393224 | tf_op jit(solution)/shard_map/ppermute | solution.py:292

commit v17 on v16

--- a/solution.py
+++ b/solution.py
@@ -260,12 +260,21 @@
 
 
 def cart_kernel(kv_local, *refs):
-    part_refs, got_refs, out_ref = refs[:kv_local], refs[kv_local:-1], refs[-1]
-    part_rows = part_refs[0].shape[2]
-    for kv_index in range(kv_local):
-        for kind in range(2):
-            total = part_refs[kv_index][0, kind] + got_refs[kv_index][0, kind].astype(f32)
-            out_ref[pl.ds(kind * kv_local + kv_index, part_rows, stride=2 * kv_local), :] = total
+    part_refs, got_refs, (out_ref, *buffers, sems) = refs[:kv_local], refs[kv_local : 2 * kv_local], refs[2 * kv_local :]
+    spread = 2 * kv_local
+    rows = part_refs[0].shape[2] // len(buffers)
+    copies = []
+    for index, buffer in enumerate(buffers):
+        here = slice(index * rows, (index + 1) * rows)
+        for kv_index in range(kv_local):
+            for kind in range(2):
+                total = part_refs[kv_index][0, kind, here, :] + got_refs[kv_index][0, kind, here, :].astype(f32)
+                buffer[pl.ds(kind * kv_local + kv_index, rows, stride=spread), :] = total
+        at = slice(index * rows * spread, (index + 1) * rows * spread)
+        copies.append(pltpu.make_async_copy(buffer, out_ref.at[at, :], sems.at[index]))
+        copies[-1].start()
+    for copy in copies:
+        copy.wait()
 
 
 def place_kernel(heads_size, kv_local, *refs):
@@ -319,7 +328,7 @@
     width = heads_local // kv_local
     block_tokens = 64
     chunk = 512
-    fine = 128
+    fine = 64
     sub = 16
     all_keys = cart_rows + tokens
     rows = block_tokens * width
@@ -424,6 +433,13 @@
     cart_grads = pl.pallas_call(
         functools.partial(cart_kernel, kv_local),
         out_shape=jax.ShapeDtypeStruct((part_rows * 2 * kv_local, head_dim), f32),
+        in_specs=[pl.BlockSpec(memory_space=pltpu.VMEM)] * (2 * kv_local),
+        out_specs=anywhere,
+        scratch_shapes=[
+            pltpu.VMEM((part_rows * kv_local, head_dim), f32),
+            pltpu.VMEM((part_rows * kv_local, head_dim), f32),
+            pltpu.SemaphoreType.DMA((2,)),
+        ],
         compiler_params=pltpu.CompilerParams(vmem_limit_bytes=small_vmem_bytes),
         cost_estimate=pl.CostEstimate(flops=2**20, bytes_accessed=2 * 2**20, transcendentals=0),
         name="cart_grads",

time: 41.7 us -> 41.7 us (level)
  transfers between devices with their start and end apart: 7 -> 7, of which waited for: 3 -> 3; matrix products, arithmetic and copies ran while one was open for 0% -> 0% of each run, Pallas kernels for 25% -> 24%
where the time goes in v17:
time: 41.7 us; the launch traced here: 41.5 us
  Pallas kernels  20.5 us (49%)
  waiting for transfers between devices  10.5 us (25%)
  starting transfers between devices  9.64 us (23%)
  between operations  0.83 us (2%)
    pallas_call x2, Pallas kernels, on_device(): pl.pallas_call(functools.partial(head_kernel, dp_size, heads_size, kv_ind...  18.6 us
    ppermute x7, waiting for transfers between devices, swap(): lax.ppermute(values, axis, [(source, source ^ step) for source in range(s...  10.5 us
    ppermute x7, starting transfers between devices, swap(): lax.ppermute(values, axis, [(source, source ^ step) for source in range(s...  9.64 us
    pallas_call x1, Pallas kernels, on_device(): pl.pallas_call(functools.partial(place_kernel, heads_size, kv_local), out...  0.99 us
    pallas_call x1, Pallas kernels, on_device(): pl.pallas_call(functools.partial(cart_kernel, kv_local), out_shape=jax.Sh...  0.84 us
  transfers between devices with their start and end apart: 7, of which 3 were waited for; matrix products, arithmetic and copies ran while one was open for 0% of the time, Pallas kernels for 24%

profile of v17, /device:TPU:0, one launch (start us, length us, event | category | flops | bytes accessed | tf_op | source)
XLA Modules:
  0.0 41.5 jit_solution(10968497824306220138)
XLA Ops:
  0.6 9.6 %head_grads.2 = (f32[2,2,256,128]{3,2,1,0:T(8,128)S(1)}, bf16[2,2,256,128]{3,2,1,0:T(8,128)(2,1)S(1)}, bf16[64,1024]{1,0:T(8,128)(2,1)S(1)}, bf16[64,1024]{1,0:T...) custom-call(bf16[4096,128]{1,0:T(8,128)(2,1)} %bitcast.9, ...), custom_call_target="tpu_custom_call" | custom-call | flops 6710886400 | bytes 5242880 | tf_op jit(solution)/shard_map/head_grads/pallas_call | solution.py:374
  10.2 3.1 %collective-permute-start = (bf16[2,2,256,128]{3,2,1,0:T(8,128)(2,1)S(1)}, bf16[2,2,256,128]{3,2,1,0:T(8,128)(2,1)S(1)}, u32[]{:S(2)}, u32[]{:S(2)}) collective-permute-start(bf16[2,2,256,128]{3,2,1,0:T(8,128)(2,1)S(1)} %get-tuple-element.53), channel_id=1, source_target_pairs={{0,4},{4,0},{8,12},{12,8},{1,5},{5,1},{9,13},{13,9},{2,6},{6,2},{1... | collective-permute-start | bytes 786440 | tf_op jit(solution)/shard_map/ppermute | solution.py:301
  13.3 9.0 %head_grads.3 = (f32[2,2,256,128]{3,2,1,0:T(8,128)S(1)}, bf16[2,2,256,128]{3,2,1,0:T(8,128)(2,1)S(1)}, bf16[64,2048]{1,0:T(8,128)(2,1)S(1)}, bf16[64,2048]{1,0:T...) custom-call(bf16[1280,128]{1,0:T(8,128)(2,1)S(1)} %get-tuple-element.35.refs, ...), custom_call_target="tpu_custom_call" | custom-call | flops 6710886400 | bytes 5242880 | tf_op jit(solution)/shard_map/head_grads/pallas_call | solution.py:374
  22.3 0.0 collective-permute-done.got_ref
  22.3 0.0 collective-permute-start.1
  22.3 1.9 %collective-permute-start.4 = (bf16[64,2048]{1,0:T(8,128)(2,1)S(1)}, bf16[64,2048]{1,0:T(8,128)(2,1)S(1)}, u32[]{:S(2)}, u32[]{:S(2)}) collective-permute-start(bf16[64,2048]{1,0:T(8,128)(2,1)S(1)} %get-tuple-element.64), channel_id=1, source_target_pairs={{0,2},{1,3},{2,0},{3,1},{4,6},{5,7},{6,4},{7,5},{8,10},{9,11},{10,... | collective-permute-start | bytes 786440 | tf_op jit(solution)/shard_map/ppermute | solution.py:301
  24.2 0.0 collective-permute-start.5
  24.2 0.2 collective-permute-start.6
  24.5 3.1 %collective-permute-start.2 = (bf16[1,2,256,128]{3,2,1,0:T(8,128)(2,1)S(1)}, bf16[1,2,256,128]{3,2,1,0:T(8,128)(2,1)S(1)}, u32[]{:S(2)}, u32[]{:S(2)}) collective-permute-start(bf16[1,2,256,128]{3,2,1,0:T(8,128)(2,1)S(1)} %get-tuple-element.60), channel_id=1, source_target_pairs={{0,8},{4,12},{8,0},{12,4},{1,9},{5,13},{9,1},{13,5},{2,10},{6,14},... | collective-permute-start | bytes 393224 | tf_op jit(solution)/shard_map/ppermute | solution.py:301
  27.6 5.3 %collective-permute-done.1.got_ref = bf16[2,2,256,128]{3,2,1,0:T(8,128)(2,1)S(1)} collective-permute-done((bf16[2,2,256,128]{3,2,1,0:T(8,128)(2,1)S(1)}, bf16[2,2,256,128]{3,2,1,0:T(8,128)(2,1)S(1)}, u32[]{:S(2)}, u32[]{:S(2)}) %collective-permute-start.1) | collective-permute-done | bytes 262176 | tf_op jit(solution)/shard_map/ppermute | solution.py:301
  32.9 0.1 cart_fold.3
  32.9 1.3 %collective-permute-start.3 = (bf16[1,2,256,128]{3,2,1,0:T(8,128)(2,1)S(1)}, bf16[1,2,256,128]{3,2,1,0:T(8,128)(2,1)S(1)}, u32[]{:S(2)}, u32[]{:S(2)}) collective-permute-start(bf16[1,2,256,128]{3,2,1,0:T(8,128)(2,1)S(1)} %get-tuple-element.61), channel_id=1, source_target_pairs={{0,8},{4,12},{8,0},{12,4},{1,9},{5,13},{9,1},{13,5},{2,10},{6,14},... | collective-permute-start | bytes 393224 | tf_op jit(solution)/shard_map/ppermute | solution.py:301
  34.3 0.0 collective-permute-done.4.refs_1_
  34.3 0.6 %collective-permute-done.5.refs_2_ = bf16[64,2048]{1,0:T(8,128)(2,1)S(1)} collective-permute-done((bf16[64,2048]{1,0:T(8,128)(2,1)S(1)}, bf16[64,2048]{1,0:T(8,128)(2,1)S(1)}, u32[]{:S(2)}, u32[]{:S(2)}) %collective-permute-start.5) | collective-permute-done | bytes 262176 | tf_op jit(solution)/shard_map/ppermute | solution.py:301
  34.9 0.0 collective-permute-done.6.refs_3_
  34.9 1.0 %place_queries.1 = bf16[64,8192]{1,0:T(8,128)(2,1)} custom-call(bf16[64,2048]{1,0:T(8,128)(2,1)S(1)} %get-tuple-element.63.refs_0_, bf16[64,2048]{1,0:T(8,128)(2,1)S(1)} %collective-permute-done.4.refs_1_, bf16[64,2048]{1,0:T(8,128)(2,1)S(1)} %collective-permute-done.5.refs_2_, bf16[64,2048]{1,0:T(8,128)(2,1)S(1)} %collective-permute-done.6.refs_3_), custom_call_target="tpu_custom_call" | custom-call | flops 1048576 | bytes 2097152 | tf_op jit(solution)/shard_map/place_queries/pallas_call | solution.py:423
  35.9 0.0 collective-permute-done.2.refs_2_
  35.9 4.6 %collective-permute-done.3.refs_3_ = bf16[1,2,256,128]{3,2,1,0:T(8,128)(2,1)S(1)} collective-permute-done((bf16[1,2,256,128]{3,2,1,0:T(8,128)(2,1)S(1)}, bf16[1,2,256,128]{3,2,1,0:T(8,128)(2,1)S(1)}, u32[]{:S(2)}, u32[]{:S(2)}) %collective-permute-start.3) | collective-permute-done | bytes 131104 | tf_op jit(solution)/shard_map/ppermute | solution.py:301
  40.5 0.8 %cart_grads.1 = f32[1024,128]{1,0:T(8,128)} custom-call(f32[1,2,256,128]{3,2,1,0:T(8,128)S(1)} %get-tuple-element.56.refs_0_, f32[1,2,256,128]{3,2,1,0:T(8,128)S(1)} %get-tuple-element.59.refs_1_, bf16[1,2,256,128]{3,2,1,0:T(8,128)(2,1)S(1)} %collective-permute-done.2.refs_2_, bf16[1,2,256,128]{3,2,1,0:T(8,128)(2,1)S(1)} %collective-permute-done.3.refs_3_), custom_call_target="tpu_custom_call" | custom-call | flops 1048576 | bytes 2097152 | tf_op jit(solution)/shard_map/cart_grads/pallas_call | solution.py:433
  (1 shorter events, 0.0 us)
Async XLA Ops:
  10.2 12.1 %collective-permute-start = (bf16[2,2,256,128]{3,2,1,0:T(8,128)(2,1)S(1)}, bf16[2,2,256,128]{3,2,1,0:T(8,128)(2,1)S(1)}, u32[]{:S(2)}, u32[]{:S(2)}) collective-permute-start(bf16[2,2,256,128]{3,2,1,0:T(8,128)(2,1)S(1)} %get-tuple-element.53), channel_id=1, source_target_pairs={{0,4},{4,0},{8,12},{12,8},{1,5},{5,1},{9,13},{13,9},{2,6},{6,2},{1... | collective-permute-start | bytes 786440 | tf_op jit(solution)/shard_map/ppermute | solution.py:301
  22.3 10.6 %collective-permute-start.1 = (bf16[2,2,256,128]{3,2,1,0:T(8,128)(2,1)S(1)}, bf16[2,2,256,128]{3,2,1,0:T(8,128)(2,1)S(1)}, u32[]{:S(2)}, u32[]{:S(2)}) collective-permute-start(bf16[2,2,256,128]{3,2,1,0:T(8,128)(2,1)S(1)} %get-tuple-element.58), channel_id=1, source_target_pairs={{0,4},{4,0},{8,12},{12,8},{1,5},{5,1},{9,13},{13,9},{2,6},{6,2},{1... | collective-permute-start | bytes 786440 | tf_op jit(solution)/shard_map/ppermute | solution.py:301
  22.3 11.9 %collective-permute-start.4 = (bf16[64,2048]{1,0:T(8,128)(2,1)S(1)}, bf16[64,2048]{1,0:T(8,128)(2,1)S(1)}, u32[]{:S(2)}, u32[]{:S(2)}) collective-permute-start(bf16[64,2048]{1,0:T(8,128)(2,1)S(1)} %get-tuple-element.64), channel_id=1, source_target_pairs={{0,2},{1,3},{2,0},{3,1},{4,6},{5,7},{6,4},{7,5},{8,10},{9,11},{10,... | collective-permute-start | bytes 786440 | tf_op jit(solution)/shard_map/ppermute | solution.py:301
  24.2 10.6 %collective-permute-start.5 = (bf16[64,2048]{1,0:T(8,128)(2,1)S(1)}, bf16[64,2048]{1,0:T(8,128)(2,1)S(1)}, u32[]{:S(2)}, u32[]{:S(2)}) collective-permute-start(bf16[64,2048]{1,0:T(8,128)(2,1)S(1)} %get-tuple-element.65), channel_id=1, source_target_pairs={{0,3},{1,2},{2,1},{3,0},{4,7},{5,6},{6,5},{7,4},{8,11},{9,10},{10,... | collective-permute-start | bytes 786440 | tf_op jit(solution)/shard_map/ppermute | solution.py:301
  24.2 10.6 %collective-permute-start.6 = (bf16[64,2048]{1,0:T(8,128)(2,1)S(1)}, bf16[64,2048]{1,0:T(8,128)(2,1)S(1)}, u32[]{:S(2)}, u32[]{:S(2)}) collective-permute-start(bf16[64,2048]{1,0:T(8,128)(2,1)S(1)} %get-tuple-element.66), channel_id=1, source_target_pairs={{0,1},{1,0},{2,3},{3,2},{4,5},{5,4},{6,7},{7,6},{8,9},{9,8},{10,11... | collective-permute-start | bytes 786440 | tf_op jit(solution)/shard_map/ppermute | solution.py:301
  24.5 11.4 %collective-permute-start.2 = (bf16[1,2,256,128]{3,2,1,0:T(8,128)(2,1)S(1)}, bf16[1,2,256,128]{3,2,1,0:T(8,128)(2,1)S(1)}, u32[]{:S(2)}, u32[]{:S(2)}) collective-permute-start(bf16[1,2,256,128]{3,2,1,0:T(8,128)(2,1)S(1)} %get-tuple-element.60), channel_id=1, source_target_pairs={{0,8},{4,12},{8,0},{12,4},{1,9},{5,13},{9,1},{13,5},{2,10},{6,14},... | collective-permute-start | bytes 393224 | tf_op jit(solution)/shard_map/ppermute | solution.py:301
  32.9 7.6 %collective-permute-start.3 = (bf16[1,2,256,128]{3,2,1,0:T(8,128)(2,1)S(1)}, bf16[1,2,256,128]{3,2,1,0:T(8,128)(2,1)S(1)}, u32[]{:S(2)}, u32[]{:S(2)}) collective-permute-start(bf16[1,2,256,128]{3,2,1,0:T(8,128)(2,1)S(1)} %get-tuple-element.61), channel_id=1, source_target_pairs={{0,8},{4,12},{8,0},{12,4},{1,9},{5,13},{9,1},{13,5},{2,10},{6,14},... | collective-permute-start | bytes 393224 | tf_op jit(solution)/shard_map/ppermute | solution.py:301

commit v18 on v16

--- a/solution.py
+++ b/solution.py
@@ -318,7 +318,7 @@
     cart_rows = cart_keys.shape[0]
     width = heads_local // kv_local
     block_tokens = 64
-    chunk = 512
+    chunk = 1024
     fine = 128
     sub = 16
     all_keys = cart_rows + tokens

time: 41.7 us -> 42.1 us (level)
    pallas_call x2, Pallas kernels: 18.7 us -> 19.2 us  [on_device(): pl.pallas_call(functools.partial(head_kernel, dp_size, heads_size, kv_ind...]
where the time goes in v18:
time: 42.1 us; the launch traced here: 42 us
  Pallas kernels  21.1 us (50%)
  waiting for transfers between devices  10.5 us (25%)
  starting transfers between devices  9.64 us (23%)
  between operations  0.67 us (2%)
    pallas_call x2, Pallas kernels, on_device(): pl.pallas_call(functools.partial(head_kernel, dp_size, heads_size, kv_ind...  19.2 us
    ppermute x7, waiting for transfers between devices, swap(): lax.ppermute(values, axis, [(source, source ^ step) for source in range(s...  10.5 us
    ppermute x7, starting transfers between devices, swap(): lax.ppermute(values, axis, [(source, source ^ step) for source in range(s...  9.64 us
    pallas_call x1, Pallas kernels, on_device(): pl.pallas_call(functools.partial(place_kernel, heads_size, kv_local), out...  0.99 us
    pallas_call x1, Pallas kernels, on_device(): pl.pallas_call(functools.partial(cart_kernel, kv_local), out_shape=jax.Sh...  0.87 us
  transfers between devices with their start and end apart: 7, of which 3 were waited for; matrix products, arithmetic and copies ran while one was open for 0% of the time, Pallas kernels for 25%

profile of v18, /device:TPU:0, one launch (start us, length us, event | category | flops | bytes accessed | tf_op | source)
XLA Modules:
  0.0 42.0 jit_solution(14042215597923233617)
XLA Ops:
  0.6 9.7 %head_grads.2 = (f32[2,2,256,128]{3,2,1,0:T(8,128)S(1)}, bf16[2,2,256,128]{3,2,1,0:T(8,128)(2,1)S(1)}, bf16[64,1024]{1,0:T(8,128)(2,1)S(1)}, bf16[64,1024]{1,0:T...) custom-call(bf16[4096,128]{1,0:T(8,128)(2,1)} %bitcast.9, ...), custom_call_target="tpu_custom_call" | custom-call | flops 6710886400 | bytes 5242880 | tf_op jit(solution)/shard_map/head_grads/pallas_call | solution.py:365
  10.3 3.1 %collective-permute-start = (bf16[2,2,256,128]{3,2,1,0:T(8,128)(2,1)S(1)}, bf16[2,2,256,128]{3,2,1,0:T(8,128)(2,1)S(1)}, u32[]{:S(2)}, u32[]{:S(2)}) collective-permute-start(bf16[2,2,256,128]{3,2,1,0:T(8,128)(2,1)S(1)} %get-tuple-element.53), channel_id=1, source_target_pairs={{0,4},{4,0},{8,12},{12,8},{1,5},{5,1},{9,13},{13,9},{2,6},{6,2},{1... | collective-permute-start | bytes 786440 | tf_op jit(solution)/shard_map/ppermute | solution.py:292
  13.4 9.5 %head_grads.3 = (f32[2,2,256,128]{3,2,1,0:T(8,128)S(1)}, bf16[2,2,256,128]{3,2,1,0:T(8,128)(2,1)S(1)}, bf16[64,2048]{1,0:T(8,128)(2,1)S(1)}, bf16[64,2048]{1,0:T...) custom-call(bf16[1280,128]{1,0:T(8,128)(2,1)S(1)} %get-tuple-element.35.refs, ...), custom_call_target="tpu_custom_call" | custom-call | flops 6710886400 | bytes 5242880 | tf_op jit(solution)/shard_map/head_grads/pallas_call | solution.py:365
  22.9 0.0 collective-permute-done.got_ref
  22.9 0.0 collective-permute-start.1
  22.9 1.9 %collective-permute-start.4 = (bf16[64,2048]{1,0:T(8,128)(2,1)S(1)}, bf16[64,2048]{1,0:T(8,128)(2,1)S(1)}, u32[]{:S(2)}, u32[]{:S(2)}) collective-permute-start(bf16[64,2048]{1,0:T(8,128)(2,1)S(1)} %get-tuple-element.64), channel_id=1, source_target_pairs={{0,2},{1,3},{2,0},{3,1},{4,6},{5,7},{6,4},{7,5},{8,10},{9,11},{10,... | collective-permute-start | bytes 786440 | tf_op jit(solution)/shard_map/ppermute | solution.py:292
  24.8 0.0 collective-permute-start.5
  24.8 0.2 collective-permute-start.6
  25.1 3.1 %collective-permute-start.2 = (bf16[1,2,256,128]{3,2,1,0:T(8,128)(2,1)S(1)}, bf16[1,2,256,128]{3,2,1,0:T(8,128)(2,1)S(1)}, u32[]{:S(2)}, u32[]{:S(2)}) collective-permute-start(bf16[1,2,256,128]{3,2,1,0:T(8,128)(2,1)S(1)} %get-tuple-element.60), channel_id=1, source_target_pairs={{0,8},{4,12},{8,0},{12,4},{1,9},{5,13},{9,1},{13,5},{2,10},{6,14},... | collective-permute-start | bytes 393224 | tf_op jit(solution)/shard_map/ppermute | solution.py:292
  28.2 5.3 %collective-permute-done.1.got_ref = bf16[2,2,256,128]{3,2,1,0:T(8,128)(2,1)S(1)} collective-permute-done((bf16[2,2,256,128]{3,2,1,0:T(8,128)(2,1)S(1)}, bf16[2,2,256,128]{3,2,1,0:T(8,128)(2,1)S(1)}, u32[]{:S(2)}, u32[]{:S(2)}) %collective-permute-start.1) | collective-permute-done | bytes 262176 | tf_op jit(solution)/shard_map/ppermute | solution.py:292
  33.5 0.1 cart_fold.3
  33.5 1.3 %collective-permute-start.3 = (bf16[1,2,256,128]{3,2,1,0:T(8,128)(2,1)S(1)}, bf16[1,2,256,128]{3,2,1,0:T(8,128)(2,1)S(1)}, u32[]{:S(2)}, u32[]{:S(2)}) collective-permute-start(bf16[1,2,256,128]{3,2,1,0:T(8,128)(2,1)S(1)} %get-tuple-element.61), channel_id=1, source_target_pairs={{0,8},{4,12},{8,0},{12,4},{1,9},{5,13},{9,1},{13,5},{2,10},{6,14},... | collective-permute-start | bytes 393224 | tf_op jit(solution)/shard_map/ppermute | solution.py:292
  34.8 0.0 collective-permute-done.4.refs_1_
  34.8 0.6 %collective-permute-done.5.refs_2_ = bf16[64,2048]{1,0:T(8,128)(2,1)S(1)} collective-permute-done((bf16[64,2048]{1,0:T(8,128)(2,1)S(1)}, bf16[64,2048]{1,0:T(8,128)(2,1)S(1)}, u32[]{:S(2)}, u32[]{:S(2)}) %collective-permute-start.5) | collective-permute-done | bytes 262176 | tf_op jit(solution)/shard_map/ppermute | solution.py:292
  35.5 0.0 collective-permute-done.6.refs_3_
  35.5 1.0 %place_queries.1 = bf16[64,8192]{1,0:T(8,128)(2,1)} custom-call(bf16[64,2048]{1,0:T(8,128)(2,1)S(1)} %get-tuple-element.63.refs_0_, bf16[64,2048]{1,0:T(8,128)(2,1)S(1)} %collective-permute-done.4.refs_1_, bf16[64,2048]{1,0:T(8,128)(2,1)S(1)} %collective-permute-done.5.refs_2_, bf16[64,2048]{1,0:T(8,128)(2,1)S(1)} %collective-permute-done.6.refs_3_), custom_call_target="tpu_custom_call" | custom-call | flops 1048576 | bytes 2097152 | tf_op jit(solution)/shard_map/place_queries/pallas_call | solution.py:414
  36.5 0.0 collective-permute-done.2.refs_2_
  36.5 4.6 %collective-permute-done.3.refs_3_ = bf16[1,2,256,128]{3,2,1,0:T(8,128)(2,1)S(1)} collective-permute-done((bf16[1,2,256,128]{3,2,1,0:T(8,128)(2,1)S(1)}, bf16[1,2,256,128]{3,2,1,0:T(8,128)(2,1)S(1)}, u32[]{:S(2)}, u32[]{:S(2)}) %collective-permute-start.3) | collective-permute-done | bytes 131104 | tf_op jit(solution)/shard_map/ppermute | solution.py:292
  41.1 0.9 %cart_grads.1 = f32[1024,128]{1,0:T(8,128)} custom-call(f32[1,2,256,128]{3,2,1,0:T(8,128)S(1)} %get-tuple-element.56.refs_0_, f32[1,2,256,128]{3,2,1,0:T(8,128)S(1)} %get-tuple-element.59.refs_1_, bf16[1,2,256,128]{3,2,1,0:T(8,128)(2,1)S(1)} %collective-permute-done.2.refs_2_, bf16[1,2,256,128]{3,2,1,0:T(8,128)(2,1)S(1)} %collective-permute-done.3.refs_3_), custom_call_target="tpu_custom_call" | custom-call | flops 1048576 | bytes 2097152 | tf_op jit(solution)/shard_map/cart_grads/pallas_call | solution.py:424
  (1 shorter events, 0.0 us)
Async XLA Ops:
  10.3 12.5 %collective-permute-start = (bf16[2,2,256,128]{3,2,1,0:T(8,128)(2,1)S(1)}, bf16[2,2,256,128]{3,2,1,0:T(8,128)(2,1)S(1)}, u32[]{:S(2)}, u32[]{:S(2)}) collective-permute-start(bf16[2,2,256,128]{3,2,1,0:T(8,128)(2,1)S(1)} %get-tuple-element.53), channel_id=1, source_target_pairs={{0,4},{4,0},{8,12},{12,8},{1,5},{5,1},{9,13},{13,9},{2,6},{6,2},{1... | collective-permute-start | bytes 786440 | tf_op jit(solution)/shard_map/ppermute | solution.py:292
  22.9 10.6 %collective-permute-start.1 = (bf16[2,2,256,128]{3,2,1,0:T(8,128)(2,1)S(1)}, bf16[2,2,256,128]{3,2,1,0:T(8,128)(2,1)S(1)}, u32[]{:S(2)}, u32[]{:S(2)}) collective-permute-start(bf16[2,2,256,128]{3,2,1,0:T(8,128)(2,1)S(1)} %get-tuple-element.58), channel_id=1, source_target_pairs={{0,4},{4,0},{8,12},{12,8},{1,5},{5,1},{9,13},{13,9},{2,6},{6,2},{1... | collective-permute-start | bytes 786440 | tf_op jit(solution)/shard_map/ppermute | solution.py:292
  22.9 11.9 %collective-permute-start.4 = (bf16[64,2048]{1,0:T(8,128)(2,1)S(1)}, bf16[64,2048]{1,0:T(8,128)(2,1)S(1)}, u32[]{:S(2)}, u32[]{:S(2)}) collective-permute-start(bf16[64,2048]{1,0:T(8,128)(2,1)S(1)} %get-tuple-element.64), channel_id=1, source_target_pairs={{0,2},{1,3},{2,0},{3,1},{4,6},{5,7},{6,4},{7,5},{8,10},{9,11},{10,... | collective-permute-start | bytes 786440 | tf_op jit(solution)/shard_map/ppermute | solution.py:292
  24.8 10.6 %collective-permute-start.5 = (bf16[64,2048]{1,0:T(8,128)(2,1)S(1)}, bf16[64,2048]{1,0:T(8,128)(2,1)S(1)}, u32[]{:S(2)}, u32[]{:S(2)}) collective-permute-start(bf16[64,2048]{1,0:T(8,128)(2,1)S(1)} %get-tuple-element.65), channel_id=1, source_target_pairs={{0,3},{1,2},{2,1},{3,0},{4,7},{5,6},{6,5},{7,4},{8,11},{9,10},{10,... | collective-permute-start | bytes 786440 | tf_op jit(solution)/shard_map/ppermute | solution.py:292
  24.8 10.6 %collective-permute-start.6 = (bf16[64,2048]{1,0:T(8,128)(2,1)S(1)}, bf16[64,2048]{1,0:T(8,128)(2,1)S(1)}, u32[]{:S(2)}, u32[]{:S(2)}) collective-permute-start(bf16[64,2048]{1,0:T(8,128)(2,1)S(1)} %get-tuple-element.66), channel_id=1, source_target_pairs={{0,1},{1,0},{2,3},{3,2},{4,5},{5,4},{6,7},{7,6},{8,9},{9,8},{10,11... | collective-permute-start | bytes 786440 | tf_op jit(solution)/shard_map/ppermute | solution.py:292
  25.1 11.4 %collective-permute-start.2 = (bf16[1,2,256,128]{3,2,1,0:T(8,128)(2,1)S(1)}, bf16[1,2,256,128]{3,2,1,0:T(8,128)(2,1)S(1)}, u32[]{:S(2)}, u32[]{:S(2)}) collective-permute-start(bf16[1,2,256,128]{3,2,1,0:T(8,128)(2,1)S(1)} %get-tuple-element.60), channel_id=1, source_target_pairs={{0,8},{4,12},{8,0},{12,4},{1,9},{5,13},{9,1},{13,5},{2,10},{6,14},... | collective-permute-start | bytes 393224 | tf_op jit(solution)/shard_map/ppermute | solution.py:292
  33.5 7.6 %collective-permute-start.3 = (bf16[1,2,256,128]{3,2,1,0:T(8,128)(2,1)S(1)}, bf16[1,2,256,128]{3,2,1,0:T(8,128)(2,1)S(1)}, u32[]{:S(2)}, u32[]{:S(2)}) collective-permute-start(bf16[1,2,256,128]{3,2,1,0:T(8,128)(2,1)S(1)} %get-tuple-element.61), channel_id=1, source_target_pairs={{0,8},{4,12},{8,0},{12,4},{1,9},{5,13},{9,1},{13,5},{2,10},{6,14},... | collective-permute-start | bytes 393224 | tf_op jit(solution)/shard_map/ppermute | solution.py:292
